TPU v7x, 32 devices: a whole 2x2x4 slice. The times are simulated.
32 devices in a mesh: dp: 2 (over core), ctx: 4 (over z), head: 4 (over y, x).
Axes of the slice: x: 2, y: 2, z: 4, core: 2. Of those that a mesh axis runs over, the one named last changes fastest.
Arguments:
- queries: bfloat16 [2, 512, 2560], P('dp', 'ctx', 'head'), may hold values from -25 to 25
- keys: bfloat16 [2, 512, 2560], P('dp', 'ctx', 'head'), may hold values from -25 to 25
- values: bfloat16 [2, 512, 2560], P('dp', 'ctx', 'head'), may hold values from -6 to 6
- grad_y: bfloat16 [2, 512, 2560], P('dp', 'ctx', 'head'), may hold values from -6 to 6
- out_gain: float32 [2560], P('head'), may hold values from 0.1 to 1.9
- offsets: int32 [2, 20], P(None, 'head'), may hold values from 0 to 7, as said below
Outputs:
- attended: bfloat16 [2, 512, 2560], P('dp', 'ctx', 'head')
- query_grad: bfloat16 [2, 512, 2560], P('dp', 'ctx', 'head')
- key_grad: bfloat16 [2, 512, 2560], P('dp', 'ctx', 'head')
- value_grad: bfloat16 [2, 512, 2560], P('dp', 'ctx', 'head')
- gain_grad: float32 [2560], P('head')
Inputs may be any that keep to these rules, and one draw needn't show every extreme that they name: Row 0 holds offsets below 8, row 1 offsets below 4.
All inputs are finite; a program needn't handle non-finite values.
Results may differ from a plain program's by a relative error of at most 0.011.
Values may be sent and summed in bfloat16 or wider, within the bound.
No kernel may reach another device: no remote copies, remote signals or barrier semaphores. Data moves between devices by JAX's collectives and lax.ppermute only.
A program may use at most 64 MiB of HBM per device.

v0:
```python
import math

import jax
import jax.numpy as jnp
from jax import lax
from jax.sharding import PartitionSpec as P

HEAD_DIM = 128
SPAN = 4
R1 = 8


EPS = 1e-06


def swapped(block, axis, bit):
    count = lax.axis_size(axis)
    route = []
    for low in range(count):
        high = low | 1 << bit
        if high != low and high < count:
            route += [(low, high), (high, low)]
    return lax.ppermute(block, axis, route)


def pick_rows(source_rows, dilation, shifts):
    row_count, head_count, head_width = source_rows.shape
    grouped = source_rows.reshape(row_count // dilation, dilation, head_count, head_width)
    hit_mask = jnp.arange(dilation, dtype=jnp.int32).reshape(1, dilation, 1, 1) == shifts.reshape(
        1, 1, head_count, 1
    )
    chosen = jnp.where(hit_mask, grouped, jnp.zeros((), source_rows.dtype))
    return jnp.sum(chosen, axis=1, dtype=source_rows.dtype)


def place_rows(row_values, dilation, shifts):
    row_count, head_count, head_width = row_values.shape
    hit_mask = jnp.arange(dilation, dtype=jnp.int32).reshape(1, dilation, 1, 1) == shifts.reshape(
        1, 1, head_count, 1
    )
    spread = jnp.where(hit_mask, row_values[:, None], jnp.zeros((), row_values.dtype))
    return spread.reshape(row_count * dilation, head_count, head_width)


def level_scores(q_rows, k_rows):
    score_scale = 1.0 / math.sqrt(q_rows.shape[-1])
    return (
        jnp.einsum("qhe,khe->hqk", q_rows, k_rows, preferred_element_type=jnp.float32) * score_scale
    )


def attend(q_rows, k_rows, v_rows):
    scores = level_scores(q_rows, k_rows)
    row_max = jnp.max(scores, axis=-1, keepdims=True)
    log_total = row_max[..., 0] + jnp.log(jnp.sum(jnp.exp(scores - row_max), axis=-1))
    soft_rows = jnp.exp(scores - log_total[..., None]).astype(jnp.bfloat16)
    level_out = jnp.einsum("hqk,khe->qhe", soft_rows, v_rows, preferred_element_type=jnp.float32)
    return (level_out, log_total.T)


def score_grads(q_rows, k_rows, v_rows, log_total, grad_low, row_shift):
    score_scale = 1.0 / math.sqrt(q_rows.shape[-1])
    scores = level_scores(q_rows, k_rows)
    exact_soft = jnp.exp(scores - log_total.T[..., None])
    prob_grad = jnp.einsum("qhe,khe->hqk", grad_low, v_rows, preferred_element_type=jnp.float32)
    score_grad = (exact_soft * (prob_grad + row_shift.T[..., None]) * score_scale).astype(
        jnp.bfloat16
    )
    return (score_grad, exact_soft.astype(jnp.bfloat16))


def key_parts(score_grad, soft_low, q_rows, grad_low):
    k_part = jnp.einsum("hqk,qhe->khe", score_grad, q_rows, preferred_element_type=jnp.float32)
    v_part = jnp.einsum("hqk,qhe->khe", soft_low, grad_low, preferred_element_type=jnp.float32)
    return (k_part, v_part)


def query_part(score_grad, k_rows):
    return jnp.einsum("hqk,khe->qhe", score_grad, k_rows, preferred_element_type=jnp.float32)


def shards(queries, keys, values, grad_y, out_gain, offsets):
    tokens = queries.shape[1]
    flat_width = queries.shape[2]
    head_count = flat_width // HEAD_DIM
    row_shape = (tokens, head_count, HEAD_DIM)
    q_own = queries[0].reshape(row_shape)
    k_own = keys[0].reshape(row_shape)
    v_own = values[0].reshape(row_shape)
    ctx_size = lax.axis_size("ctx")
    span_bits = SPAN.bit_length() - 1
    my_place = lax.axis_index("ctx")
    mid_shift = offsets[0]
    top_shift = offsets[1]
    positions = jnp.arange(tokens, dtype=jnp.int32)
    mid_hit = (positions % R1)[:, None] == mid_shift[None, :]
    top_hit = (positions % ctx_size)[:, None] == top_shift[None, :]
    mid_q = pick_rows(q_own, R1, mid_shift)
    mid_k = pick_rows(k_own, R1, mid_shift)
    mid_v = pick_rows(v_own, R1, mid_shift)
    top_q = pick_rows(q_own, ctx_size, top_shift)
    top_k = pick_rows(k_own, ctx_size, top_shift)
    top_v = pick_rows(v_own, ctx_size, top_shift)
    mid_keys = mid_k.reshape(-1, flat_width)
    mid_vals = mid_v.reshape(-1, flat_width)
    top_keys = top_k.reshape(-1, flat_width)
    top_vals = top_v.reshape(-1, flat_width)

    def append_peer(mine, received, level_bit):
        upper_side = my_place >> level_bit & 1 == 1
        return jnp.where(
            upper_side, jnp.concatenate([received, mine], 0), jnp.concatenate([mine, received], 0)
        )

    for level_bit in range(span_bits):
        received = swapped((mid_keys, mid_vals), "ctx", level_bit)
        mid_keys = append_peer(mid_keys, received[0], level_bit)
        mid_vals = append_peer(mid_vals, received[1], level_bit)
    top_keys, top_vals = (
        lax.all_gather(top_keys, "ctx", axis=0, tiled=True),
        lax.all_gather(top_vals, "ctx", axis=0, tiled=True),
    )
    mid_keys = mid_keys.reshape(-1, head_count, HEAD_DIM)
    mid_vals = mid_vals.reshape(-1, head_count, HEAD_DIM)
    top_keys = top_keys.reshape(-1, head_count, HEAD_DIM)
    top_vals = top_vals.reshape(-1, head_count, HEAD_DIM)
    base_out, base_total = attend(q_own, k_own, v_own)
    mid_out, mid_total = attend(mid_q, mid_keys, mid_vals)
    top_out, top_total = attend(top_q, top_keys, top_vals)
    mid_full = place_rows(mid_total[..., None], R1, mid_shift)[..., 0]
    top_full = place_rows(top_total[..., None], ctx_size, top_shift)[..., 0]
    row_max = jnp.maximum(base_total, jnp.where(mid_hit, mid_full, base_total))
    row_max = jnp.maximum(row_max, jnp.where(top_hit, top_full, base_total))
    base_expo = jnp.exp(base_total - row_max)
    mid_expo = jnp.where(mid_hit, jnp.exp(mid_full - row_max), 0.0)
    top_expo = jnp.where(top_hit, jnp.exp(top_full - row_max), 0.0)
    denom = base_expo + mid_expo + top_expo
    base_share = base_expo / denom
    mid_share = mid_expo / denom
    top_share = top_expo / denom
    attn = (
        base_share[..., None] * base_out
        + mid_share[..., None] * place_rows(mid_out, R1, mid_shift)
        + top_share[..., None] * place_rows(top_out, ctx_size, top_shift)
    )
    inv_rms = lax.rsqrt(jnp.mean(attn * attn, axis=-1, keepdims=True) + EPS)
    normed = attn * inv_rms
    gain_rows = out_gain.reshape(head_count, HEAD_DIM)
    attended = (normed * gain_rows).astype(jnp.bfloat16).reshape(1, tokens, flat_width)
    grad_full = grad_y[0].reshape(row_shape).astype(jnp.float32)
    gain_part = jnp.sum(grad_full * normed, axis=0).reshape(flat_width)
    gain_grad = lax.psum(gain_part, ("dp", "ctx"))
    grad_norm = grad_full * gain_rows
    grad_attn = inv_rms * (
        grad_norm - normed * jnp.mean(grad_norm * normed, axis=-1, keepdims=True)
    )
    inner = jnp.sum(grad_attn * attn, axis=-1)
    base_low = (base_share[..., None] * grad_attn).astype(jnp.bfloat16)
    base_shift = -(base_share * inner)
    base_grad, base_soft = score_grads(q_own, k_own, v_own, base_total, base_low, base_shift)
    base_dq = query_part(base_grad, k_own)
    base_dk, base_dv = key_parts(base_grad, base_soft, q_own, base_low)
    mid_sel = pick_rows(mid_share[..., None], R1, mid_shift)[..., 0]
    mid_low = (mid_sel[..., None] * pick_rows(grad_attn, R1, mid_shift)).astype(jnp.bfloat16)
    mid_row_shift = -(mid_sel * pick_rows(inner[..., None], R1, mid_shift)[..., 0])
    mid_grad, mid_soft = score_grads(mid_q, mid_keys, mid_vals, mid_total, mid_low, mid_row_shift)
    mid_dq = query_part(mid_grad, mid_keys)
    mid_dk, mid_dv = key_parts(mid_grad, mid_soft, mid_q, mid_low)
    mid_dk = mid_dk.reshape(-1, flat_width)
    mid_dv = mid_dv.reshape(-1, flat_width)
    for level_bit in reversed(range(span_bits)):
        half_rows = mid_dk.shape[0] // 2
        upper_side = my_place >> level_bit & 1 == 1
        keep_k = jnp.where(upper_side, mid_dk[half_rows:], mid_dk[:half_rows])
        keep_v = jnp.where(upper_side, mid_dv[half_rows:], mid_dv[:half_rows])
        send_k = jnp.where(upper_side, mid_dk[:half_rows], mid_dk[half_rows:])
        send_v = jnp.where(upper_side, mid_dv[:half_rows], mid_dv[half_rows:])
        received = (
            swapped(send_k.astype(jnp.bfloat16), "ctx", level_bit).astype(send_k.dtype),
            swapped(send_v.astype(jnp.bfloat16), "ctx", level_bit).astype(send_v.dtype),
        )
        mid_dk = keep_k + received[0]
        mid_dv = keep_v + received[1]
    mid_dk = mid_dk.reshape(-1, head_count, HEAD_DIM)
    mid_dv = mid_dv.reshape(-1, head_count, HEAD_DIM)
    top_sel = pick_rows(top_share[..., None], ctx_size, top_shift)[..., 0]
    top_low = (top_sel[..., None] * pick_rows(grad_attn, ctx_size, top_shift)).astype(jnp.bfloat16)
    top_row_shift = -(top_sel * pick_rows(inner[..., None], ctx_size, top_shift)[..., 0])
    top_grad, top_soft = score_grads(top_q, top_keys, top_vals, top_total, top_low, top_row_shift)
    top_dq = query_part(top_grad, top_keys)
    gathered_dk, gathered_dv = key_parts(top_grad, top_soft, top_q, top_low)
    summed = (
        lax.psum_scatter(
            gathered_dk.reshape(-1, flat_width), "ctx", scatter_dimension=0, tiled=True
        ),
        lax.psum_scatter(
            gathered_dv.reshape(-1, flat_width), "ctx", scatter_dimension=0, tiled=True
        ),
    )
    top_dk = summed[0].reshape(-1, head_count, HEAD_DIM)
    top_dv = summed[1].reshape(-1, head_count, HEAD_DIM)
    query_grad = (
        base_dq + place_rows(mid_dq, R1, mid_shift) + place_rows(top_dq, ctx_size, top_shift)
    )
    key_grad = base_dk + place_rows(mid_dk, R1, mid_shift) + place_rows(top_dk, ctx_size, top_shift)
    value_grad = (
        base_dv + place_rows(mid_dv, R1, mid_shift) + place_rows(top_dv, ctx_size, top_shift)
    )
    out_shape = (1, tokens, flat_width)
    return (
        attended,
        query_grad.astype(jnp.bfloat16).reshape(out_shape),
        key_grad.astype(jnp.bfloat16).reshape(out_shape),
        value_grad.astype(jnp.bfloat16).reshape(out_shape),
        gain_grad,
    )


def solution(mesh):
    in_specs = (
        P("dp", "ctx", "head"),
        P("dp", "ctx", "head"),
        P("dp", "ctx", "head"),
        P("dp", "ctx", "head"),
        P("head"),
        P(None, "head"),
    )
    out_specs = (
        P("dp", "ctx", "head"),
        P("dp", "ctx", "head"),
        P("dp", "ctx", "head"),
        P("dp", "ctx", "head"),
        P("head"),
    )
    return jax.shard_map(shards, mesh=mesh, in_specs=in_specs, out_specs=out_specs, check_vma=False)
```

profile of v0, /device:TPU:0, one launch (start us, length us, event | category | flops | bytes accessed | tf_op | source)
XLA Modules:
  0.0 112.3 jit_solution(5425909164242358926)
XLA Ops:
  7.2 0.8 slice_bitcast_fusion.1
  8.0 1.5 %fusion.25 = (bf16[16,5,128]{2,0,1:T(8,128)(2,1)S(1)}, bf16[16,5,128]{2,0,1:T(8,128)(2,1)S(1)}, bf16[16,5,128]{2,0,1:T(8,128)(2,1)S(1)}) fusion(pred[8,5]{0,1:T(8,128)(4,1)S(1)} %iota_compare_fusion, bf16[1,128,640]{2,1,0:T(8,128)(2,1)} %param.6, bf16[1,128,640]{2,1,0:T(8,128)(2,1)} %param.7, bf16[1,128,640]{2,1,0:T(8,128)(2,1)} %param.8), kind=kLoop, calls=%fused_computation.60 | loop fusion | flops 460800 | bytes 553000 | tf_op jit(solution)/shard_map/reduce_sum | solution.py:33
  9.6 3.1 %collective-permute-start = (bf16[16,640]{1,0:T(8,128)(2,1)S(1)}, bf16[16,640]{1,0:T(8,128)(2,1)S(1)}, u32[]{:S(2)}, u32[]{:S(2)}) collective-permute-start(bf16[16,640]{1,0:T(8,128)(2,1)S(1)} %copy_bitcast_fusion.9), channel_id=1, source_target_pairs={{0,4},{4,0},{8,12},{12,8},{1,5},{5,1},{9,13},{13,9},{2,6},{6,2},{1... | collective-permute-start | bytes 61448 | tf_op jit(solution)/shard_map/ppermute | solution.py:23
  12.9 0.6 copy-done.1
  14.2 0.7 copy-done.2
  15.1 0.4 select_reduce_fusion.2
  15.5 13.8 %all_gather.7 = bf16[128,640]{1,0:T(8,128)(2,1)S(1)} all-gather(bf16[32,640]{1,0:T(8,128)(2,1)S(1)} %bitcast.265), channel_id=1, replica_groups=mesh['dp'=2,'ctx'=4,'head'=4] {'ctx'}, dimensions={0}, use_global_device_ids=true | all-gather | bytes 204800 | tf_op jit(solution)/shard_map/all_gather | solution.py:121
  29.5 13.6 %all_gather.6 = bf16[128,640]{1,0:T(8,128)(2,1)S(1)} all-gather(bf16[32,640]{1,0:T(8,128)(2,1)S(1)} %bitcast.264), channel_id=1, replica_groups=mesh['dp'=2,'ctx'=4,'head'=4] {'ctx'}, dimensions={0}, use_global_device_ids=true | all-gather | bytes 204800 | tf_op jit(solution)/shard_map/all_gather | solution.py:120
  44.8 0.5 copy-done.3
  45.9 0.7 collective-permute-start.1
  46.6 2.4 %collective-permute-start.3 = (bf16[32,640]{1,0:T(8,128)(2,1)S(1)}, bf16[32,640]{1,0:T(8,128)(2,1)S(1)}, u32[]{:S(2)}, u32[]{:S(2)}) collective-permute-start(bf16[32,640]{1,0:T(8,128)(2,1)S(1)} %maximum_select_fusion.4), channel_id=1, source_target_pairs={{0,8},{8,0},{4,12},{12,4},{1,9},{9,1},{5,13},{13,5},{2,10},{10,2},... | collective-permute-start | bytes 122888 | tf_op jit(solution)/shard_map/ppermute | solution.py:23
  49.0 1.9 %collective-permute-done.1 = bf16[32,640]{1,0:T(8,128)(2,1)S(1)} collective-permute-done((bf16[32,640]{1,0:T(8,128)(2,1)S(1)}, bf16[32,640]{1,0:T(8,128)(2,1)S(1)}, u32[]{:S(2)}, u32[]{:S(2)}) %collective-permute-start.1) | collective-permute-done | bytes 40992 | tf_op jit(solution)/shard_map/ppermute | solution.py:23
  52.1 0.7 multiply_reduce_fusion.3
  52.8 0.7 copy-done.4
  54.6 0.3 convolution_bitcast_fusion.4
  57.0 2.2 %collective-permute-start.6 = (bf16[32,640]{1,0:T(8,128)(2,1)S(1)}, bf16[32,640]{1,0:T(8,128)(2,1)S(1)}, u32[]{:S(2)}, u32[]{:S(2)}) collective-permute-start(bf16[32,640]{1,0:T(8,128)(2,1)S(1)} %copy_bitcast_fusion.2), channel_id=1, source_target_pairs={{0,8},{8,0},{4,12},{12,4},{1,9},{9,1},{5,13},{13,5},{2,10},{10,2},... | collective-permute-start | bytes 122888 | tf_op jit(solution)/shard_map/ppermute | solution.py:23
  59.2 0.9 collective-permute-start.4
  60.0 0.9 copy.224
  61.0 0.4 fusion.14
  61.5 0.3 fusion.11
  62.0 0.8 copy.203
  62.8 0.9 copy.226
  63.9 0.8 copy.204
  64.7 18.1 %psum.7 = f32[640]{0:T(1024)} all-reduce(f32[640]{0:T(1024)S(1)} %bitcast.270), channel_id=1, replica_groups=mesh['dp'=2,'ctx'=4,'head'=4] {'dp','ctx'}, use_global_device_ids=true, to_apply=%region_24.25 | all-reduce | flops 640 | bytes 5120 | tf_op jit(solution)/shard_map/psum | solution.py:152
  82.9 2.1 %collective-permute-start.5 = (bf16[16,640]{1,0:T(8,128)(2,1)S(1)}, bf16[16,640]{1,0:T(8,128)(2,1)S(1)}, u32[]{:S(2)}, u32[]{:S(2)}) collective-permute-start(bf16[16,640]{1,0:T(8,128)(2,1)S(1)} %select_convert_fusion.3), channel_id=1, source_target_pairs={{0,4},{4,0},{8,12},{12,8},{1,5},{5,1},{9,13},{13,9},{2,6},{6,2},{1... | collective-permute-start | bytes 61448 | tf_op jit(solution)/shard_map/ppermute | solution.py:23
  85.0 1.7 %collective-permute-done.7 = bf16[16,640]{1,0:T(8,128)(2,1)S(1)} collective-permute-done((bf16[16,640]{1,0:T(8,128)(2,1)S(1)}, bf16[16,640]{1,0:T(8,128)(2,1)S(1)}, u32[]{:S(2)}, u32[]{:S(2)}) %collective-permute-start.7) | collective-permute-done | bytes 20512 | tf_op jit(solution)/shard_map/ppermute | solution.py:23
  86.9 1.0 copy.225
  88.6 0.8 copy.205
  89.5 13.4 %reduce-scatter.9.cloned.1.call-done = f32[32,640]{1,0:T(8,128)} async-done(((f32[128,640]{1,0:T(8,128)}), f32[32,640]{1,0:T(8,128)}) %reduce-scatter.9.cloned.1.call-update) | async-done | bytes 81936
  102.9 1.0 copy.227
  104.2 0.3 fusion.13
  104.7 0.8 copy.206
  (107 shorter events, 9.7 us)
Async XLA Ops:
  7.2 79.7 %reduce-scatter.7.cloned.1.call-start = ((), (), s32[]{:S(2)}) async-start(), calls=%async_computation.2 | async-start | bytes 409600
  8.0 4.7 %copy-start = (bf16[1,128,640]{2,1,0:T(8,128)(2,1)S(1)}, bf16[1,128,640]{2,1,0:T(8,128)(2,1)}, u32[]{:S(2)}) copy-start(bf16[1,128,640]{2,1,0:T(8,128)(2,1)} %param.6) | copy-start | bytes 491524
  9.6 36.2 %collective-permute-start = (bf16[16,640]{1,0:T(8,128)(2,1)S(1)}, bf16[16,640]{1,0:T(8,128)(2,1)S(1)}, u32[]{:S(2)}, u32[]{:S(2)}) collective-permute-start(bf16[16,640]{1,0:T(8,128)(2,1)S(1)} %copy_bitcast_fusion.9), channel_id=1, source_target_pairs={{0,4},{4,0},{8,12},{12,8},{1,5},{5,1},{9,13},{13,9},{2,6},{6,2},{1... | collective-permute-start | bytes 61448 | tf_op jit(solution)/shard_map/ppermute | solution.py:23
  12.7 0.9 copy-start.1
  12.7 33.2 %collective-permute-start.2 = (bf16[16,640]{1,0:T(8,128)(2,1)S(1)}, bf16[16,640]{1,0:T(8,128)(2,1)S(1)}, u32[]{:S(2)}, u32[]{:S(2)}) collective-permute-start(bf16[16,640]{1,0:T(8,128)(2,1)S(1)} %copy_bitcast_fusion.8), channel_id=1, source_target_pairs={{0,4},{4,0},{8,12},{12,8},{1,5},{5,1},{9,13},{13,9},{2,6},{6,2},{1... | collective-permute-start | bytes 61448 | tf_op jit(solution)/shard_map/ppermute | solution.py:23
  14.0 0.9 copy-start.2
  44.4 0.9 copy-start.3
  45.9 5.0 %collective-permute-start.1 = (bf16[32,640]{1,0:T(8,128)(2,1)S(1)}, bf16[32,640]{1,0:T(8,128)(2,1)S(1)}, u32[]{:S(2)}, u32[]{:S(2)}) collective-permute-start(bf16[32,640]{1,0:T(8,128)(2,1)S(1)} %maximum_select_fusion.2), channel_id=1, source_target_pairs={{0,8},{8,0},{4,12},{12,4},{1,9},{9,1},{5,13},{13,5},{2,10},{10,2},... | collective-permute-start | bytes 122888 | tf_op jit(solution)/shard_map/ppermute | solution.py:23
  46.6 5.2 %collective-permute-start.3 = (bf16[32,640]{1,0:T(8,128)(2,1)S(1)}, bf16[32,640]{1,0:T(8,128)(2,1)S(1)}, u32[]{:S(2)}, u32[]{:S(2)}) collective-permute-start(bf16[32,640]{1,0:T(8,128)(2,1)S(1)} %maximum_select_fusion.4), channel_id=1, source_target_pairs={{0,8},{8,0},{4,12},{12,4},{1,9},{9,1},{5,13},{13,5},{2,10},{10,2},... | collective-permute-start | bytes 122888 | tf_op jit(solution)/shard_map/ppermute | solution.py:23
  52.8 0.7 copy-start.4
  57.0 25.8 %collective-permute-start.6 = (bf16[32,640]{1,0:T(8,128)(2,1)S(1)}, bf16[32,640]{1,0:T(8,128)(2,1)S(1)}, u32[]{:S(2)}, u32[]{:S(2)}) collective-permute-start(bf16[32,640]{1,0:T(8,128)(2,1)S(1)} %copy_bitcast_fusion.2), channel_id=1, source_target_pairs={{0,8},{8,0},{4,12},{12,4},{1,9},{9,1},{5,13},{13,5},{2,10},{10,2},... | collective-permute-start | bytes 122888 | tf_op jit(solution)/shard_map/ppermute | solution.py:23
  59.2 23.7 %collective-permute-start.4 = (bf16[32,640]{1,0:T(8,128)(2,1)S(1)}, bf16[32,640]{1,0:T(8,128)(2,1)S(1)}, u32[]{:S(2)}, u32[]{:S(2)}) collective-permute-start(bf16[32,640]{1,0:T(8,128)(2,1)S(1)} %copy_bitcast_fusion.3), channel_id=1, source_target_pairs={{0,8},{8,0},{4,12},{12,4},{1,9},{9,1},{5,13},{13,5},{2,10},{10,2},... | collective-permute-start | bytes 122888 | tf_op jit(solution)/shard_map/ppermute | solution.py:23
  60.9 41.9 %reduce-scatter.9.cloned.1.call-start = ((), (), s32[]{:S(2)}) async-start(), calls=%async_computation.3 | async-start | bytes 409600
  82.8 3.8 %collective-permute-start.7 = (bf16[16,640]{1,0:T(8,128)(2,1)S(1)}, bf16[16,640]{1,0:T(8,128)(2,1)S(1)}, u32[]{:S(2)}, u32[]{:S(2)}) collective-permute-start(bf16[16,640]{1,0:T(8,128)(2,1)S(1)} %select_convert_fusion.2), channel_id=1, source_target_pairs={{0,4},{4,0},{8,12},{12,8},{1,5},{5,1},{9,13},{13,9},{2,6},{6,2},{1... | collective-permute-start | bytes 61448 | tf_op jit(solution)/shard_map/ppermute | solution.py:23
  82.9 3.9 %collective-permute-start.5 = (bf16[16,640]{1,0:T(8,128)(2,1)S(1)}, bf16[16,640]{1,0:T(8,128)(2,1)S(1)}, u32[]{:S(2)}, u32[]{:S(2)}) collective-permute-start(bf16[16,640]{1,0:T(8,128)(2,1)S(1)} %select_convert_fusion.3), channel_id=1, source_target_pairs={{0,4},{4,0},{8,12},{12,8},{1,5},{5,1},{9,13},{13,9},{2,6},{6,2},{1... | collective-permute-start | bytes 61448 | tf_op jit(solution)/shard_map/ppermute | solution.py:23
Sparse Core Ops, SparseCore 0:
  61.1 21.1 reduce-scatter.6
  84.5 18.3 reduce-scatter.8
where the time goes:
time: 113 us; the launch traced here: 112 us
  blocking collectives  45.4 us (40%)
  waiting for transfers between devices  17.3 us (15%)
  between operations  14.6 us (13%)
  local copies, waits for them, and re-layouts  14.5 us (13%)
  starting transfers between devices  11.5 us (10%)
  matrix products  5.13 us (5%)
  other arithmetic  3.94 us (3%)
    psum x1, blocking collectives, shards(): gain_grad = lax.psum(gain_part, ('dp', 'ctx'))  18.1 us
    all_gather x1, blocking collectives, shards(): lax.all_gather(top_vals, 'ctx', axis=0, tiled=True)  13.8 us
    all_gather x1, blocking collectives, shards(): lax.all_gather(top_keys, 'ctx', axis=0, tiled=True)  13.6 us
    unnamed x4, waiting for transfers between devices  13.5 us
    ppermute x8, starting transfers between devices, swapped(): return lax.ppermute(block, axis, route)  11.4 us
    unnamed x24, local copies, waits for them, and re-layouts  10.4 us
    ppermute x8, waiting for transfers between devices, swapped(): return lax.ppermute(block, axis, route)  3.77 us
    reduce_sum x6, other arithmetic, pick_rows(): return jnp.sum(chosen, axis=1, dtype=source_rows.dtype)  2.6 us
  transfers between devices with their start and end apart: 10, of which 4 were waited for; matrix products, arithmetic and copies ran while one was open for 10% of the time, Pallas kernels for 0%

commit v1 on v0

--- a/solution.py
+++ b/solution.py
@@ -1,8 +1,11 @@
+import functools
 import math
 
 import jax
 import jax.numpy as jnp
 from jax import lax
+from jax.experimental import pallas as pl
+from jax.experimental.pallas import tpu as pltpu
 from jax.sharding import PartitionSpec as P
 
 HEAD_DIM = 128
@@ -79,7 +82,7 @@
     return jnp.einsum("hqk,khe->qhe", score_grad, k_rows, preferred_element_type=jnp.float32)
 
 
-def shards(queries, keys, values, grad_y, out_gain, offsets):
+def general_shards(queries, keys, values, grad_y, out_gain, offsets):
     tokens = queries.shape[1]
     flat_width = queries.shape[2]
     head_count = flat_width // HEAD_DIM
@@ -216,6 +219,191 @@
     )
 
 
+VMEM_SPEC = pl.BlockSpec(memory_space=pltpu.VMEM)
+SMEM_SPEC = pl.BlockSpec(memory_space=pltpu.SMEM)
+
+
+def contract(left, right, left_dim, right_dim):
+    return lax.dot_general(
+        left, right, (((left_dim,), (right_dim,)), ((), ())), preferred_element_type=jnp.float32
+    )
+
+
+def pick_matrix(offsets_ref, head, top_rows, mid_rows, tokens, top_step):
+    shape = (top_rows + mid_rows, tokens)
+    row = lax.broadcasted_iota(jnp.int32, shape, 0)
+    position = lax.broadcasted_iota(jnp.int32, shape, 1)
+    wanted = jnp.where(
+        row < top_rows,
+        row * top_step + offsets_ref[1, head],
+        (row - top_rows) * R1 + offsets_ref[0, head],
+    )
+    return jnp.where(position == wanted, 1.0, 0.0).astype(jnp.bfloat16)
+
+
+def pack_kernel(top_step, offsets_ref, k_ref, v_ref, packed_ref):
+    tokens = k_ref.shape[1]
+    top_rows, mid_rows = tokens // top_step, tokens // R1
+    picked = top_rows + mid_rows
+    for head in range(k_ref.shape[2] // HEAD_DIM):
+        cols = pl.ds(head * HEAD_DIM, HEAD_DIM)
+        picks = pick_matrix(offsets_ref, head, top_rows, mid_rows, tokens, top_step)
+        packed_ref[:picked, cols] = contract(picks, k_ref[0, :, cols], 1, 0).astype(jnp.bfloat16)
+        packed_ref[picked:, cols] = contract(picks, v_ref[0, :, cols], 1, 0).astype(jnp.bfloat16)
+
+
+def attend_kernel(
+    top_step,
+    offsets_ref,
+    q_ref,
+    k_ref,
+    v_ref,
+    grad_ref,
+    gain_ref,
+    *refs,
+):
+    packed_refs = refs[:SPAN]
+    attended_ref, dq_ref, dk_ref, dv_ref, gain_part_ref = refs[SPAN : SPAN + 5]
+    part_refs = refs[SPAN + 5 :]
+    tokens = q_ref.shape[1]
+    top_rows, mid_rows = tokens // top_step, tokens // R1
+    picked = top_rows + mid_rows
+    key_count = tokens + SPAN * picked
+    score_scale = 1.0 / math.sqrt(HEAD_DIM)
+    row = lax.broadcasted_iota(jnp.int32, (tokens, 1), 0)
+    column = lax.broadcasted_iota(jnp.int32, (1, key_count), 1)
+    is_base = column < tokens
+    is_top = (column - tokens) % picked < top_rows
+    for head in range(q_ref.shape[2] // HEAD_DIM):
+        cols = pl.ds(head * HEAD_DIM, HEAD_DIM)
+        q_rows = q_ref[0, :, cols]
+        k_all = jnp.concatenate(
+            [k_ref[0, :, cols]] + [packed[:picked, cols] for packed in packed_refs], 0
+        )
+        v_all = jnp.concatenate(
+            [v_ref[0, :, cols]] + [packed[picked:, cols] for packed in packed_refs], 0
+        )
+        top_hit = jnp.where(row % top_step == offsets_ref[1, head], 1.0, 0.0)
+        mid_hit = jnp.where(row % R1 == offsets_ref[0, head], 1.0, 0.0)
+        seen = jnp.where(is_base, 1.0, jnp.where(is_top, top_hit, mid_hit))
+        scores = jnp.where(seen > 0.5, contract(q_rows, k_all, 1, 1) * score_scale, -1e30)
+        expo = jnp.exp(scores - jnp.max(scores, axis=1, keepdims=True))
+        soft = expo / jnp.sum(expo, axis=1, keepdims=True)
+        soft_low = soft.astype(jnp.bfloat16)
+        attn = contract(soft_low, v_all, 1, 0)
+        inv_rms = lax.rsqrt(jnp.mean(attn * attn, axis=1, keepdims=True) + EPS)
+        normed = attn * inv_rms
+        gain_row = gain_ref[:, cols]
+        attended_ref[0, :, cols] = (normed * gain_row).astype(jnp.bfloat16)
+        grad_rows = grad_ref[0, :, cols].astype(jnp.float32)
+        gain_part_ref[:, cols] = jnp.sum(grad_rows * normed, axis=0, keepdims=True)
+        grad_norm = grad_rows * gain_row
+        grad_attn = inv_rms * (
+            grad_norm - normed * jnp.mean(grad_norm * normed, axis=1, keepdims=True)
+        )
+        inner = jnp.sum(grad_attn * attn, axis=1, keepdims=True)
+        grad_low = grad_attn.astype(jnp.bfloat16)
+        prob_grad = contract(grad_low, v_all, 1, 1)
+        score_grad = (soft * (prob_grad - inner) * score_scale).astype(jnp.bfloat16)
+        dq_ref[0, :, cols] = contract(score_grad, k_all, 1, 0).astype(jnp.bfloat16)
+        dk_all = contract(score_grad, q_rows, 0, 0)
+        dv_all = contract(soft_low, grad_low, 0, 0)
+        dk_ref[:, cols] = dk_all[:tokens]
+        dv_ref[:, cols] = dv_all[:tokens]
+        for place, part_ref in enumerate(part_refs):
+            start = tokens + place * picked
+            part_ref[:picked, cols] = dk_all[start : start + picked].astype(part_ref.dtype)
+            part_ref[picked:, cols] = dv_all[start : start + picked].astype(part_ref.dtype)
+
+
+def finish_kernel(top_step, offsets_ref, dk_ref, dv_ref, *refs):
+    part_refs = refs[:SPAN]
+    gain_refs = refs[SPAN : 2 * SPAN]
+    dk_out_ref, dv_out_ref, gain_out_ref = refs[2 * SPAN :]
+    tokens = dk_ref.shape[0]
+    top_rows, mid_rows = tokens // top_step, tokens // R1
+    picked = top_rows + mid_rows
+    first, second, third, fourth = [gain_ref[...] for gain_ref in gain_refs]
+    gain_out_ref[...] = (first + second) + (third + fourth)
+    for head in range(dk_ref.shape[1] // HEAD_DIM):
+        cols = pl.ds(head * HEAD_DIM, HEAD_DIM)
+        picks = pick_matrix(offsets_ref, head, top_rows, mid_rows, tokens, top_step)
+        total = part_refs[0][:, cols]
+        for part_ref in part_refs[1:]:
+            total = total + part_ref[:, cols].astype(jnp.float32)
+        total = total.astype(jnp.bfloat16)
+        dk_out_ref[0, :, cols] = (
+            dk_ref[:, cols] + contract(picks, total[:picked], 0, 0)
+        ).astype(jnp.bfloat16)
+        dv_out_ref[0, :, cols] = (
+            dv_ref[:, cols] + contract(picks, total[picked:], 0, 0)
+        ).astype(jnp.bfloat16)
+
+
+def across(block, axis, distance):
+    route = [(place, place ^ distance) for place in range(lax.axis_size(axis))]
+    return lax.ppermute(block, axis, route)
+
+
+def one_segment_shards(queries, keys, values, grad_y, out_gain, offsets):
+    tokens, width = queries.shape[1:]
+    top_step = lax.axis_size("ctx")
+    packed_rows = 2 * (tokens // top_step + tokens // R1)
+    row_block = jax.ShapeDtypeStruct((1, tokens, width), jnp.bfloat16)
+    wide_block = jax.ShapeDtypeStruct((tokens, width), jnp.float32)
+    low_part = jax.ShapeDtypeStruct((packed_rows, width), jnp.bfloat16)
+    own_part = jax.ShapeDtypeStruct((packed_rows, width), jnp.float32)
+    gain_row = jax.ShapeDtypeStruct((1, width), jnp.float32)
+    distances = range(1, SPAN)
+    packed = pl.pallas_call(
+        functools.partial(pack_kernel, top_step),
+        out_shape=low_part,
+        in_specs=[SMEM_SPEC, VMEM_SPEC, VMEM_SPEC],
+        out_specs=VMEM_SPEC,
+        name="pack",
+    )(offsets, keys, values)
+    received = {distance: across(packed, "ctx", distance) for distance in reversed(distances)}
+    attended, query_grad, dk_base, dv_base, gain_part, own, *parts = pl.pallas_call(
+        functools.partial(attend_kernel, top_step),
+        out_shape=[row_block, row_block, wide_block, wide_block, gain_row, own_part]
+        + [low_part] * (SPAN - 1),
+        in_specs=[SMEM_SPEC] + [VMEM_SPEC] * (5 + SPAN),
+        out_specs=[VMEM_SPEC] * (5 + SPAN),
+        compiler_params=pltpu.CompilerParams(vmem_limit_bytes=32 * 1024 * 1024),
+        name="attend",
+    )(
+        offsets,
+        queries,
+        keys,
+        values,
+        grad_y,
+        out_gain.reshape(1, width),
+        packed,
+        *[received[distance] for distance in distances],
+    )
+    returned = {
+        distance: across(parts[distance - 1], "ctx", distance) for distance in reversed(distances)
+    }
+    gain_pair = gain_part + across(gain_part, "dp", 1)
+    gains = [gain_pair] + [across(gain_pair, "ctx", distance) for distance in distances]
+    key_grad, value_grad, gain_grad = pl.pallas_call(
+        functools.partial(finish_kernel, top_step),
+        out_shape=[row_block, row_block, gain_row],
+        in_specs=[SMEM_SPEC] + [VMEM_SPEC] * (2 + 2 * SPAN),
+        out_specs=[VMEM_SPEC] * 3,
+        compiler_params=pltpu.CompilerParams(vmem_limit_bytes=32 * 1024 * 1024),
+        name="finish",
+    )(
+        offsets,
+        dk_base,
+        dv_base,
+        own,
+        *[returned[distance] for distance in distances],
+        *gains,
+    )
+    return attended, query_grad, key_grad, value_grad, gain_grad.reshape(width)
+
+
 def solution(mesh):
     in_specs = (
         P("dp", "ctx", "head"),
@@ -232,4 +420,5 @@
         P("dp", "ctx", "head"),
         P("head"),
     )
-    return jax.shard_map(shards, mesh=mesh, in_specs=in_specs, out_specs=out_specs, check_vma=False)
+    body = one_segment_shards if mesh.shape["ctx"] == SPAN else general_shards
+    return jax.shard_map(body, mesh=mesh, in_specs=in_specs, out_specs=out_specs, check_vma=False)

time: 113 us -> 44.4 us (0.39)
  blocking collectives: 45.4 us -> 0 us
  between operations: 14.6 us -> 0.7 us
  local copies, waits for them, and re-layouts: 14.5 us -> 2.75 us
  Pallas kernels: 0 us -> 8.98 us
  matrix products: 5.13 us -> 0 us
  starting transfers between devices: 11.5 us -> 15.4 us
  other arithmetic: 3.94 us -> 0.61 us
  waiting for transfers between devices: 17.3 us -> 15.8 us
    all_gather x2 -> x0, blocking collectives: 27.4 us -> none  [the longest x1 13.8 us: shards(): lax.all_gather(top_vals, 'ctx', axis=0, tiled=True)]
    psum x1 -> x0, blocking collectives: 18.1 us -> none  [shards(): gain_grad = lax.psum(gain_part, ('dp', 'ctx'))]
    unnamed x4 -> x0, waiting for transfers between devices: 13.5 us -> none
    ppermute x8 -> x10, waiting for transfers between devices: 3.77 us -> 15.8 us  [across(): return lax.ppermute(block, axis, route)]
    pallas_call x0 -> x3, Pallas kernels: none -> 8.98 us  [the longest x1 5.48 us: one_segment_shards(): pl.pallas_call(functools.partial(attend_kernel, top_step), out_shape=[row...]
    unnamed x24 -> x14, local copies, waits for them, and re-layouts: 10.4 us -> 2.74 us
    dot_general x18 -> x0, matrix products: 5.13 us -> none  [the longest x3 1.14 us: attend(): jnp.einsum('hqk,khe->qhe', soft_rows, v_rows, preferred_element_type=jnp....]
    ppermute x8 -> x10, starting transfers between devices: 11.4 us -> 15.4 us  [across(): return lax.ppermute(block, axis, route)]
  transfers between devices with their start and end apart: 10 -> 10, of which waited for: 4 -> 5; matrix products, arithmetic and copies ran while one was open for 10% -> 0% of each run, Pallas kernels for 0% -> 0%
where the time goes in v1:
time: 44.4 us; the launch traced here: 44.2 us
  waiting for transfers between devices  15.8 us (36%)
  starting transfers between devices  15.4 us (35%)
  Pallas kernels  8.98 us (20%)
  local copies, waits for them, and re-layouts  2.75 us (6%)
  between operations  0.7 us (2%)
  other arithmetic  0.61 us (1%)
    ppermute x10, waiting for transfers between devices, across(): return lax.ppermute(block, axis, route)  15.8 us
    ppermute x10, starting transfers between devices, across(): return lax.ppermute(block, axis, route)  15.4 us
    pallas_call x1, Pallas kernels, one_segment_shards(): pl.pallas_call(functools.partial(attend_kernel, top_step), out_shape=[row...  5.48 us
    unnamed x14, local copies, waits for them, and re-layouts  2.74 us
    pallas_call x1, Pallas kernels, one_segment_shards(): pl.pallas_call(functools.partial(pack_kernel, top_step), out_shape=low_pa...  1.95 us
    pallas_call x1, Pallas kernels, one_segment_shards(): pl.pallas_call(functools.partial(finish_kernel, top_step), out_shape=[row...  1.56 us
  transfers between devices with their start and end apart: 10, of which 5 were waited for; matrix products, arithmetic and copies ran while one was open for 0% of the time, Pallas kernels for 0%

profile of v1, /device:TPU:0, one launch (start us, length us, event | category | flops | bytes accessed | tf_op | source)
XLA Modules:
  0.0 44.2 jit_solution(5336824716222566981)
XLA Ops:
  0.6 0.0 copy-start.1
  0.6 0.0 copy-start
  0.7 0.0 copy-start.6
  0.7 1.9 %pack.1.refs_0_ = bf16[96,640]{1,0:T(8,128)(2,1)} custom-call(s32[2,5]{1,0:T(2,128)} %offsets_ref.5, bf16[1,128,640]{2,1,0:T(8,128)(2,1)} %k_ref.3, bf16[1,128,640]{2,1,0:T(8,128)(2,1)} %v_ref.3), custom_call_target="tpu_custom_call" | custom-call | tf_op jit(solution)/shard_map/pack/pallas_call | solution.py:358
  2.6 5.0 %collective-permute-start.2 = (bf16[96,640]{1,0:T(8,128)(2,1)}, bf16[96,640]{1,0:T(8,128)(2,1)S(1)}, u32[]{:S(2)}, u32[]{:S(2)}) collective-permute-start(bf16[96,640]{1,0:T(8,128)(2,1)} %pack.1.refs_0_), channel_id=1, source_target_pairs={{0,12},{4,8},{8,4},{12,0},{1,13},{5,9},{9,5},{13,1},{2,14},{6,10},... | collective-permute-start | bytes 368648 | tf_op jit(solution)/shard_map/ppermute | solution.py:345
  7.7 0.0 collective-permute-start.1
  7.7 0.6 %collective-permute-start = (bf16[96,640]{1,0:T(8,128)(2,1)}, bf16[96,640]{1,0:T(8,128)(2,1)S(1)}, u32[]{:S(2)}, u32[]{:S(2)}) collective-permute-start(bf16[96,640]{1,0:T(8,128)(2,1)} %pack.1.refs_0_), channel_id=1, source_target_pairs={{0,4},{4,0},{8,12},{12,8},{1,5},{5,1},{9,13},{13,9},{2,6},{6,2},{1... | collective-permute-start | bytes 368648 | tf_op jit(solution)/shard_map/ppermute | solution.py:345
  8.2 0.0 copy-done.6
  8.2 3.9 %collective-permute-done.2.refs_3_ = bf16[96,640]{1,0:T(8,128)(2,1)S(1)} collective-permute-done((bf16[96,640]{1,0:T(8,128)(2,1)}, bf16[96,640]{1,0:T(8,128)(2,1)S(1)}, u32[]{:S(2)}, u32[]{:S(2)}) %collective-permute-start.2) | collective-permute-done | bytes 122912 | tf_op jit(solution)/shard_map/ppermute | solution.py:345
  12.1 6.1 %collective-permute-done.1.refs_2_ = bf16[96,640]{1,0:T(8,128)(2,1)S(1)} collective-permute-done((bf16[96,640]{1,0:T(8,128)(2,1)}, bf16[96,640]{1,0:T(8,128)(2,1)S(1)}, u32[]{:S(2)}, u32[]{:S(2)}) %collective-permute-start.1) | collective-permute-done | bytes 122912 | tf_op jit(solution)/shard_map/ppermute | solution.py:345
  18.2 0.0 collective-permute-done.refs_1_
  18.3 0.0 copy-start.2
  18.3 0.9 %copy-done.2 = bf16[96,640]{1,0:T(8,128)(2,1)S(1)} copy-done((bf16[96,640]{1,0:T(8,128)(2,1)S(1)}, bf16[96,640]{1,0:T(8,128)(2,1)}, u32[]{:S(2)}) %copy-start.2) | copy-done | bytes 122904
  19.2 0.9 %copy-done.3 = bf16[1,128,640]{2,1,0:T(8,128)(2,1)S(1)} copy-done((bf16[1,128,640]{2,1,0:T(8,128)(2,1)S(1)}, bf16[1,128,640]{2,1,0:T(8,128)(2,1)}, u32[]{:S(2)}) %copy-start.3) | copy-done | bytes 163864
  20.1 0.9 %copy-done.4 = bf16[1,128,640]{2,1,0:T(8,128)(2,1)S(1)} copy-done((bf16[1,128,640]{2,1,0:T(8,128)(2,1)S(1)}, bf16[1,128,640]{2,1,0:T(8,128)(2,1)}, u32[]{:S(2)}) %copy-start.4) | copy-done | bytes 163864
  21.0 5.5 %attend.1 = (bf16[1,128,640]{2,1,0:T(8,128)(2,1)}, bf16[1,128,640]{2,1,0:T(8,128)(2,1)}, f32[128,640]{1,0:T(8,128)S(1)}, f32[128,640]{1,0:T(8,128)S(1)}, f32[1,6...) custom-call(s32[2,5]{1,0:T(2,128)S(1)} %copy-done.5, ...), custom_call_target="tpu_custom_call" | custom-call | tf_op jit(solution)/shard_map/attend/pallas_call | solution.py:366
  26.5 0.0 collective-permute-start.3
  26.5 3.0 %collective-permute-start.4 = (bf16[96,640]{1,0:T(8,128)(2,1)S(1)}, bf16[96,640]{1,0:T(8,128)(2,1)S(1)}, u32[]{:S(2)}, u32[]{:S(2)}) collective-permute-start(bf16[96,640]{1,0:T(8,128)(2,1)S(1)} %get-tuple-element.23), channel_id=1, source_target_pairs={{0,8},{4,12},{8,0},{12,4},{1,9},{5,13},{9,1},{13,5},{2,10},{6,14},... | collective-permute-start | bytes 368648 | tf_op jit(solution)/shard_map/ppermute | solution.py:345
  29.5 1.3 %collective-permute-start.5 = (bf16[96,640]{1,0:T(8,128)(2,1)S(1)}, bf16[96,640]{1,0:T(8,128)(2,1)S(1)}, u32[]{:S(2)}, u32[]{:S(2)}) collective-permute-start(bf16[96,640]{1,0:T(8,128)(2,1)S(1)} %get-tuple-element.24), channel_id=1, source_target_pairs={{0,12},{4,8},{8,4},{12,0},{1,13},{5,9},{9,5},{13,1},{2,14},{6,10},... | collective-permute-start | bytes 368648 | tf_op jit(solution)/shard_map/ppermute | solution.py:345
  30.9 0.0 collective-permute-start.6
  30.9 1.2 %collective-permute-done.6 = f32[1,640]{1,0:T(1,128)S(1)} collective-permute-done((f32[1,640]{1,0:T(1,128)S(1)}, f32[1,640]{1,0:T(1,128)S(1)}, u32[]{:S(2)}, u32[]{:S(2)}) %collective-permute-start.6) | collective-permute-done | bytes 2592 | tf_op jit(solution)/shard_map/ppermute | solution.py:345
  32.0 2.5 %collective-permute-start.9 = (f32[1,640]{1,0:T(1,128)S(1)}, f32[1,640]{1,0:T(1,128)S(1)}, u32[]{:S(2)}, u32[]{:S(2)}) collective-permute-start(f32[1,640]{1,0:T(1,128)S(1)} %add.3.refs_4_), channel_id=1, source_target_pairs={{0,12},{4,8},{8,4},{12,0},{1,13},{5,9},{9,5},{13,1},{2,14},{6,10},... | collective-permute-start | bytes 7688 | tf_op jit(solution)/shard_map/ppermute | solution.py:345
  34.5 0.0 collective-permute-start.8
  34.5 3.0 %collective-permute-done.9.refs_7_ = f32[1,640]{1,0:T(1,128)S(1)} collective-permute-done((f32[1,640]{1,0:T(1,128)S(1)}, f32[1,640]{1,0:T(1,128)S(1)}, u32[]{:S(2)}, u32[]{:S(2)}) %collective-permute-start.9) | collective-permute-done | bytes 2592 | tf_op jit(solution)/shard_map/ppermute | solution.py:345
  37.5 2.9 %collective-permute-start.7 = (f32[1,640]{1,0:T(1,128)S(1)}, f32[1,640]{1,0:T(1,128)S(1)}, u32[]{:S(2)}, u32[]{:S(2)}) collective-permute-start(f32[1,640]{1,0:T(1,128)S(1)} %add.3.refs_4_), channel_id=1, source_target_pairs={{0,4},{4,0},{8,12},{12,8},{1,5},{5,1},{9,13},{13,9},{2,6},{6,2},{1... | collective-permute-start | bytes 7688 | tf_op jit(solution)/shard_map/ppermute | solution.py:345
  40.5 0.0 collective-permute-done.8.refs_6_
  40.5 1.6 %collective-permute-done.7.refs_5_ = f32[1,640]{1,0:T(1,128)S(1)} collective-permute-done((f32[1,640]{1,0:T(1,128)S(1)}, f32[1,640]{1,0:T(1,128)S(1)}, u32[]{:S(2)}, u32[]{:S(2)}) %collective-permute-start.7) | collective-permute-done | bytes 2592 | tf_op jit(solution)/shard_map/ppermute | solution.py:345
  42.0 0.0 collective-permute-done.3.refs_1_
  42.0 0.0 collective-permute-done.4.refs_2_
  42.0 0.0 collective-permute-done.5.refs_3_
  42.0 1.6 %finish.1 = (bf16[1,128,640]{2,1,0:T(8,128)(2,1)}, bf16[1,128,640]{2,1,0:T(8,128)(2,1)}, f32[1,640]{1,0:T(1,128)S(1)}) custom-call(s32[2,5]{1,0:T(2,128)S(1)} %copy-done.5, f32[128,640]{1,0:T(8,128)S(1)} %get-tuple-element.19.dk_ref, f32[128,640]{1,0:T(8,128)S(1)} %get-tuple-element.20.dv_ref, f32[96,640]{1,0:T(8,128)S(1)} %get-tuple-element.21.refs_0_, ...), custom_call_target="tpu_custom_call" | custom-call | tf_op jit(solution)/shard_map/finish/pallas_call | solution.py:389
  43.6 0.6 %reduce = f32[640]{0:T(1024)} reduce(f32[1,640]{1,0:T(1,128)S(1)} %get-tuple-element.28, f32[]{:T(128)} %constant.5), dimensions={0}, to_apply=%get-tuple-element.28.reduce_sub_computation | reduce | bytes 5124 | tf_op jit(solution)/shard_map/finish/pallas_call | solution.py:389
  (8 shorter events, 0.0 us)
Async XLA Ops:
  0.6 17.6 %copy-start.1 = (bf16[1,128,640]{2,1,0:T(8,128)(2,1)S(1)}, bf16[1,128,640]{2,1,0:T(8,128)(2,1)}, u32[]{:S(2)}) copy-start(bf16[1,128,640]{2,1,0:T(8,128)(2,1)} %v_ref.3) | copy-start | bytes 491524
  0.6 17.6 %copy-start = (bf16[1,128,640]{2,1,0:T(8,128)(2,1)S(1)}, bf16[1,128,640]{2,1,0:T(8,128)(2,1)}, u32[]{:S(2)}) copy-start(bf16[1,128,640]{2,1,0:T(8,128)(2,1)} %k_ref.3) | copy-start | bytes 491524
  0.7 7.6 %copy-start.6 = (f32[640]{0:T(1024)S(1)}, f32[640]{0:T(1024)}, u32[]{:S(2)}) copy-start(f32[640]{0:T(1024)} %param.10) | copy-start | bytes 7684
  2.6 15.6 %copy-start.5 = (s32[2,5]{1,0:T(2,128)S(1)}, s32[2,5]{1,0:T(2,128)}, u32[]{:S(2)}) copy-start(s32[2,5]{1,0:T(2,128)} %offsets_ref.5) | copy-start | bytes 124
  2.6 9.5 %collective-permute-start.2 = (bf16[96,640]{1,0:T(8,128)(2,1)}, bf16[96,640]{1,0:T(8,128)(2,1)S(1)}, u32[]{:S(2)}, u32[]{:S(2)}) collective-permute-start(bf16[96,640]{1,0:T(8,128)(2,1)} %pack.1.refs_0_), channel_id=1, source_target_pairs={{0,12},{4,8},{8,4},{12,0},{1,13},{5,9},{9,5},{13,1},{2,14},{6,10},... | collective-permute-start | bytes 368648 | tf_op jit(solution)/shard_map/ppermute | solution.py:345
  7.7 10.6 %collective-permute-start.1 = (bf16[96,640]{1,0:T(8,128)(2,1)}, bf16[96,640]{1,0:T(8,128)(2,1)S(1)}, u32[]{:S(2)}, u32[]{:S(2)}) collective-permute-start(bf16[96,640]{1,0:T(8,128)(2,1)} %pack.1.refs_0_), channel_id=1, source_target_pairs={{0,8},{4,12},{8,0},{12,4},{1,9},{5,13},{9,1},{13,5},{2,10},{6,14},... | collective-permute-start | bytes 368648 | tf_op jit(solution)/shard_map/ppermute | solution.py:345
  7.7 10.6 %collective-permute-start = (bf16[96,640]{1,0:T(8,128)(2,1)}, bf16[96,640]{1,0:T(8,128)(2,1)S(1)}, u32[]{:S(2)}, u32[]{:S(2)}) collective-permute-start(bf16[96,640]{1,0:T(8,128)(2,1)} %pack.1.refs_0_), channel_id=1, source_target_pairs={{0,4},{4,0},{8,12},{12,8},{1,5},{5,1},{9,13},{13,9},{2,6},{6,2},{1... | collective-permute-start | bytes 368648 | tf_op jit(solution)/shard_map/ppermute | solution.py:345
  18.3 0.9 %copy-start.2 = (bf16[96,640]{1,0:T(8,128)(2,1)S(1)}, bf16[96,640]{1,0:T(8,128)(2,1)}, u32[]{:S(2)}) copy-start(bf16[96,640]{1,0:T(8,128)(2,1)} %pack.1.refs_0_) | copy-start | bytes 368644
  19.2 0.9 %copy-start.3 = (bf16[1,128,640]{2,1,0:T(8,128)(2,1)S(1)}, bf16[1,128,640]{2,1,0:T(8,128)(2,1)}, u32[]{:S(2)}) copy-start(bf16[1,128,640]{2,1,0:T(8,128)(2,1)} %q_ref.1) | copy-start | bytes 491524
  20.1 0.9 %copy-start.4 = (bf16[1,128,640]{2,1,0:T(8,128)(2,1)S(1)}, bf16[1,128,640]{2,1,0:T(8,128)(2,1)}, u32[]{:S(2)}) copy-start(bf16[1,128,640]{2,1,0:T(8,128)(2,1)} %grad_ref.1) | copy-start | bytes 491524
  26.5 15.6 %collective-permute-start.3 = (bf16[96,640]{1,0:T(8,128)(2,1)S(1)}, bf16[96,640]{1,0:T(8,128)(2,1)S(1)}, u32[]{:S(2)}, u32[]{:S(2)}) collective-permute-start(bf16[96,640]{1,0:T(8,128)(2,1)S(1)} %get-tuple-element.22), channel_id=1, source_target_pairs={{0,4},{4,0},{8,12},{12,8},{1,5},{5,1},{9,13},{13,9},{2,6},{6,2},{1... | collective-permute-start | bytes 368648 | tf_op jit(solution)/shard_map/ppermute | solution.py:345
  26.5 15.6 %collective-permute-start.4 = (bf16[96,640]{1,0:T(8,128)(2,1)S(1)}, bf16[96,640]{1,0:T(8,128)(2,1)S(1)}, u32[]{:S(2)}, u32[]{:S(2)}) collective-permute-start(bf16[96,640]{1,0:T(8,128)(2,1)S(1)} %get-tuple-element.23), channel_id=1, source_target_pairs={{0,8},{4,12},{8,0},{12,4},{1,9},{5,13},{9,1},{13,5},{2,10},{6,14},... | collective-permute-start | bytes 368648 | tf_op jit(solution)/shard_map/ppermute | solution.py:345
  29.5 12.5 %collective-permute-start.5 = (bf16[96,640]{1,0:T(8,128)(2,1)S(1)}, bf16[96,640]{1,0:T(8,128)(2,1)S(1)}, u32[]{:S(2)}, u32[]{:S(2)}) collective-permute-start(bf16[96,640]{1,0:T(8,128)(2,1)S(1)} %get-tuple-element.24), channel_id=1, source_target_pairs={{0,12},{4,8},{8,4},{12,0},{1,13},{5,9},{9,5},{13,1},{2,14},{6,10},... | collective-permute-start | bytes 368648 | tf_op jit(solution)/shard_map/ppermute | solution.py:345
  30.9 1.2 %collective-permute-start.6 = (f32[1,640]{1,0:T(1,128)S(1)}, f32[1,640]{1,0:T(1,128)S(1)}, u32[]{:S(2)}, u32[]{:S(2)}) collective-permute-start(f32[1,640]{1,0:T(1,128)S(1)} %get-tuple-element.25), channel_id=1, source_target_pairs={{0,16},{16,0},{1,17},{17,1},{2,18},{18,2},{3,19},{19,3},{4,20},{20... | collective-permute-start | bytes 7688 | tf_op jit(solution)/shard_map/ppermute | solution.py:345
  32.0 5.5 %collective-permute-start.9 = (f32[1,640]{1,0:T(1,128)S(1)}, f32[1,640]{1,0:T(1,128)S(1)}, u32[]{:S(2)}, u32[]{:S(2)}) collective-permute-start(f32[1,640]{1,0:T(1,128)S(1)} %add.3.refs_4_), channel_id=1, source_target_pairs={{0,12},{4,8},{8,4},{12,0},{1,13},{5,9},{9,5},{13,1},{2,14},{6,10},... | collective-permute-start | bytes 7688 | tf_op jit(solution)/shard_map/ppermute | solution.py:345
  34.5 6.0 %collective-permute-start.8 = (f32[1,640]{1,0:T(1,128)S(1)}, f32[1,640]{1,0:T(1,128)S(1)}, u32[]{:S(2)}, u32[]{:S(2)}) collective-permute-start(f32[1,640]{1,0:T(1,128)S(1)} %add.3.refs_4_), channel_id=1, source_target_pairs={{0,8},{4,12},{8,0},{12,4},{1,9},{5,13},{9,1},{13,5},{2,10},{6,14},... | collective-permute-start | bytes 7688 | tf_op jit(solution)/shard_map/ppermute | solution.py:345
  37.5 4.5 %collective-permute-start.7 = (f32[1,640]{1,0:T(1,128)S(1)}, f32[1,640]{1,0:T(1,128)S(1)}, u32[]{:S(2)}, u32[]{:S(2)}) collective-permute-start(f32[1,640]{1,0:T(1,128)S(1)} %add.3.refs_4_), channel_id=1, source_target_pairs={{0,4},{4,0},{8,12},{12,8},{1,5},{5,1},{9,13},{13,9},{2,6},{6,2},{1... | collective-permute-start | bytes 7688 | tf_op jit(solution)/shard_map/ppermute | solution.py:345

commit v2 on v0

--- a/solution.py
+++ b/solution.py
@@ -1,8 +1,11 @@
+import functools
 import math
 
 import jax
 import jax.numpy as jnp
 from jax import lax
+from jax.experimental import pallas as pl
+from jax.experimental.pallas import tpu as pltpu
 from jax.sharding import PartitionSpec as P
 
 HEAD_DIM = 128
@@ -79,7 +82,7 @@
     return jnp.einsum("hqk,khe->qhe", score_grad, k_rows, preferred_element_type=jnp.float32)
 
 
-def shards(queries, keys, values, grad_y, out_gain, offsets):
+def general_shards(queries, keys, values, grad_y, out_gain, offsets):
     tokens = queries.shape[1]
     flat_width = queries.shape[2]
     head_count = flat_width // HEAD_DIM
@@ -216,6 +219,333 @@
     )
 
 
+VMEM_SPEC = pl.BlockSpec(memory_space=pltpu.VMEM)
+SMEM_SPEC = pl.BlockSpec(memory_space=pltpu.SMEM)
+LANES = 128
+PIECES = 3
+LOW = jnp.bfloat16
+WIDE = jnp.float32
+
+
+def contract(left, right, left_dim, right_dim):
+    return lax.dot_general(
+        left, right, (((left_dim,), (right_dim,)), ((), ())), preferred_element_type=WIDE
+    )
+
+
+def head_cols(head):
+    return pl.ds(head * HEAD_DIM, HEAD_DIM)
+
+
+def picked_counts(tokens, top_step):
+    return tokens // top_step, tokens // R1
+
+
+def pick_matrix(offsets_ref, head, tokens, top_step):
+    top_rows, mid_rows = picked_counts(tokens, top_step)
+    shape = (top_rows + mid_rows, tokens)
+    row = lax.broadcasted_iota(jnp.int32, shape, 0)
+    position = lax.broadcasted_iota(jnp.int32, shape, 1)
+    wanted = jnp.where(
+        row < top_rows,
+        row * top_step + offsets_ref[1, head],
+        (row - top_rows) * R1 + offsets_ref[0, head],
+    )
+    return jnp.where(position == wanted, 1.0, 0.0).astype(LOW)
+
+
+def level_hits(offsets_ref, head, shape, axis, top_step):
+    position = lax.broadcasted_iota(jnp.int32, shape, axis)
+    top_hit = jnp.where(position % top_step == offsets_ref[1, head], 1.0, 0.0)
+    mid_hit = jnp.where(position % R1 == offsets_ref[0, head], 1.0, 0.0)
+    return top_hit, mid_hit
+
+
+def picked_mask(offsets_ref, head, tokens, top_step, picked_total):
+    top_rows, mid_rows = picked_counts(tokens, top_step)
+    top_hit, mid_hit = level_hits(offsets_ref, head, (tokens, 1), 0, top_step)
+    column = lax.broadcasted_iota(jnp.int32, (1, picked_total), 1)
+    return jnp.where(column % (top_rows + mid_rows) < top_rows, top_hit, mid_hit) > 0.5
+
+
+def stacked(refs, rows, cols):
+    return jnp.concatenate([ref[rows, cols] for ref in refs], 0)
+
+
+def pack_kernel(top_step, offsets_ref, k_ref, v_ref, packed_ref):
+    tokens, width = k_ref.shape[1:]
+    picked = sum(picked_counts(tokens, top_step))
+    for head in range(width // HEAD_DIM):
+        cols = head_cols(head)
+        both = jnp.concatenate([k_ref[0, :, cols], v_ref[0, :, cols]], 1)
+        rows = contract(pick_matrix(offsets_ref, head, tokens, top_step), both, 1, 0).astype(LOW)
+        packed_ref[:picked, cols] = rows[:, :HEAD_DIM]
+        packed_ref[picked:, cols] = rows[:, HEAD_DIM:]
+
+
+def base_kernel(
+    top_step, offsets_ref, q_ref, k_ref, v_ref, picked_q_ref, expo_ref, out_ref, stats_ref
+):
+    tokens, width = q_ref.shape[1:]
+    heads = width // HEAD_DIM
+    score_scale = 1.0 / math.sqrt(HEAD_DIM)
+    for head in range(heads):
+        cols = head_cols(head)
+        q_rows = q_ref[0, :, cols]
+        picks = pick_matrix(offsets_ref, head, tokens, top_step)
+        picked_q_ref[:, cols] = contract(picks, q_rows, 1, 0).astype(LOW)
+        top_row, mid_row = level_hits(offsets_ref, head, (tokens, 1), 0, top_step)
+        top_col, mid_col = level_hits(offsets_ref, head, (1, tokens), 1, top_step)
+        times = 1.0 + top_row * top_col + mid_row * mid_col
+        scores = contract(q_rows, k_ref[0, :, cols], 1, 1) * score_scale
+        row_max = jnp.max(scores, axis=1, keepdims=True)
+        expo = times * jnp.exp(scores - row_max)
+        expo_low = expo.astype(LOW)
+        expo_ref[:, cols] = expo_low
+        out_ref[:, cols] = contract(expo_low, v_ref[0, :, cols], 1, 0)
+        stats_ref[:, head : head + 1] = row_max
+        stats_ref[:, heads + head : heads + head + 1] = jnp.sum(expo, axis=1, keepdims=True)
+
+
+def low_pieces(values):
+    pieces = []
+    for _ in range(PIECES):
+        piece = values.astype(LOW).astype(WIDE)
+        pieces.append(piece)
+        values = values - piece
+    return pieces
+
+
+def attend_kernel(
+    top_step,
+    offsets_ref,
+    q_ref,
+    grad_ref,
+    gain_ref,
+    base_out_ref,
+    base_stats_ref,
+    *refs,
+):
+    peers = SPAN - 1
+    packed_refs = refs[:peers]
+    attended_ref, gain_part_ref, sent_ref, grad_low_ref, soft_ref, stats_ref = refs[peers:]
+    tokens, width = q_ref.shape[1:]
+    heads = width // HEAD_DIM
+    picked = sum(picked_counts(tokens, top_step))
+    score_scale = 1.0 / math.sqrt(HEAD_DIM)
+    lane = lax.broadcasted_iota(jnp.int32, (1, LANES), 1)
+    sent_stats = jnp.zeros((picked, LANES), WIDE)
+    for head in range(heads):
+        cols = head_cols(head)
+        k_peers = stacked(packed_refs, pl.ds(0, picked), cols)
+        v_peers = stacked(packed_refs, pl.ds(picked, picked), cols)
+        seen = picked_mask(offsets_ref, head, tokens, top_step, peers * picked)
+        scores = contract(q_ref[0, :, cols], k_peers, 1, 1) * score_scale
+        scores = jnp.where(seen, scores, -1e30)
+        base_max = base_stats_ref[:, head : head + 1]
+        base_total = base_stats_ref[:, heads + head : heads + head + 1]
+        row_max = jnp.maximum(base_max, jnp.max(scores, axis=1, keepdims=True))
+        base_factor = jnp.exp(base_max - row_max)
+        expo = jnp.exp(scores - row_max)
+        total = base_factor * base_total + jnp.sum(expo, axis=1, keepdims=True)
+        inv_total = 1.0 / total
+        soft_low = (expo * inv_total).astype(LOW)
+        soft_ref[:, pl.ds(head * 2 * LANES, peers * picked)] = soft_low
+        base_factor = base_factor * inv_total
+        attn = base_factor * base_out_ref[:, cols] + contract(soft_low, v_peers, 1, 0)
+        inv_rms = lax.rsqrt(jnp.mean(attn * attn, axis=1, keepdims=True) + EPS)
+        normed = attn * inv_rms
+        gain_row = gain_ref[:, cols]
+        attended_ref[0, :, cols] = (normed * gain_row).astype(LOW)
+        grad_rows = grad_ref[0, :, cols].astype(WIDE)
+        gain_part_ref[:, cols] = jnp.sum(grad_rows * normed, axis=0, keepdims=True)
+        grad_norm = grad_rows * gain_row
+        grad_attn = inv_rms * (
+            grad_norm - normed * jnp.mean(grad_norm * normed, axis=1, keepdims=True)
+        )
+        inner = jnp.sum(grad_attn * attn, axis=1, keepdims=True)
+        grad_low = grad_attn.astype(LOW)
+        grad_low_ref[:, cols] = grad_low
+        stats_ref[:, head : head + 1] = base_factor
+        stats_ref[:, heads + head : heads + head + 1] = inner
+        log_total = (row_max + jnp.log(total)) * (1.0 / score_scale)
+        columns = jnp.zeros((tokens, LANES), WIDE)
+        for place, piece in enumerate(low_pieces(log_total) + low_pieces(inner)):
+            columns = jnp.where(lane == 2 * PIECES * head + place, piece, columns)
+        picks = pick_matrix(offsets_ref, head, tokens, top_step)
+        rows = contract(picks, jnp.concatenate([grad_low, columns.astype(LOW)], 1), 1, 0)
+        sent_ref[:, cols] = rows[:, :HEAD_DIM].astype(LOW)
+        sent_stats = sent_stats + rows[:, HEAD_DIM:]
+    sent_ref[:, pl.ds(width, LANES)] = sent_stats.astype(LOW)
+
+
+def local_grad_kernel(
+    top_step, q_ref, k_ref, v_ref, expo_ref, grad_low_ref, soft_ref, stats_ref, *refs
+):
+    peers = SPAN - 1
+    packed_refs = refs[:peers]
+    dq_ref, dk_ref, dv_ref = refs[peers:]
+    tokens, width = q_ref.shape[1:]
+    heads = width // HEAD_DIM
+    picked = sum(picked_counts(tokens, top_step))
+    score_scale = 1.0 / math.sqrt(HEAD_DIM)
+    for head in range(heads):
+        cols = head_cols(head)
+        k_rows = k_ref[0, :, cols]
+        k_peers = stacked(packed_refs, pl.ds(0, picked), cols)
+        v_peers = stacked(packed_refs, pl.ds(picked, picked), cols)
+        grad_low = grad_low_ref[:, cols]
+        inner = stats_ref[:, heads + head : heads + head + 1]
+        soft = expo_ref[:, cols].astype(WIDE) * stats_ref[:, head : head + 1]
+        prob_grad = contract(grad_low, v_ref[0, :, cols], 1, 1)
+        score_grad = (soft * (prob_grad - inner) * score_scale).astype(LOW)
+        peer_soft = soft_ref[:, pl.ds(head * 2 * LANES, peers * picked)].astype(WIDE)
+        peer_prob_grad = contract(grad_low, v_peers, 1, 1)
+        peer_score_grad = (peer_soft * (peer_prob_grad - inner) * score_scale).astype(LOW)
+        dq_ref[0, :, cols] = (
+            contract(score_grad, k_rows, 1, 0) + contract(peer_score_grad, k_peers, 1, 0)
+        ).astype(LOW)
+        dk_ref[:, cols] = contract(score_grad, q_ref[0, :, cols], 0, 0)
+        dv_ref[:, cols] = contract(soft.astype(LOW), grad_low, 0, 0)
+
+
+def finish_kernel(top_step, offsets_ref, k_ref, v_ref, dk_ref, dv_ref, *refs):
+    peers = SPAN - 1
+    q_refs, sent_refs = refs[:peers], refs[peers : 2 * peers]
+    dk_out_ref, dv_out_ref = refs[2 * peers :]
+    tokens, width = k_ref.shape[1:]
+    picked = sum(picked_counts(tokens, top_step))
+    score_scale = 1.0 / math.sqrt(HEAD_DIM)
+    every = pl.ds(0, picked)
+    stats = stacked(sent_refs, every, pl.ds(width, LANES))
+    lane = lax.broadcasted_iota(jnp.int32, (tokens, LANES), 1)
+    for head in range(width // HEAD_DIM):
+        cols = head_cols(head)
+        q_peers = stacked(q_refs, every, cols)
+        grad_peers = stacked(sent_refs, every, cols)
+        first = 2 * PIECES * head
+        is_total = (lane >= first) & (lane < first + PIECES)
+        is_inner = (lane >= first + PIECES) & (lane < first + 2 * PIECES)
+        less_total = jnp.where(is_total, -1.0, 0.0).astype(LOW)
+        less_inner = jnp.where(is_inner, -1.0, 0.0).astype(LOW)
+        seen = picked_mask(offsets_ref, head, tokens, top_step, peers * picked)
+        logs = contract(
+            jnp.concatenate([k_ref[0, :, cols], less_total], 1),
+            jnp.concatenate([q_peers, stats], 1),
+            1,
+            1,
+        )
+        soft = jnp.exp(jnp.where(seen, logs * score_scale, -1e30))
+        shifted = contract(
+            jnp.concatenate([v_ref[0, :, cols], less_inner], 1),
+            jnp.concatenate([grad_peers, stats], 1),
+            1,
+            1,
+        )
+        score_grad = (soft * shifted * score_scale).astype(LOW)
+        dk_out_ref[0, :, cols] = (
+            dk_ref[:, cols] + contract(score_grad, q_peers, 1, 0)
+        ).astype(LOW)
+        dv_out_ref[0, :, cols] = (
+            dv_ref[:, cols] + contract(soft.astype(LOW), grad_peers, 1, 0)
+        ).astype(LOW)
+
+
+def across(block, axis, distance):
+    route = [(place, place ^ distance) for place in range(lax.axis_size(axis))]
+    return lax.ppermute(block, axis, route)
+
+
+def to_peers(block):
+    farthest_first = [across(block, "ctx", distance) for distance in range(SPAN - 1, 0, -1)]
+    return farthest_first[::-1]
+
+
+def call(kernel, name, operands, results, microseconds):
+    return pl.pallas_call(
+        kernel,
+        out_shape=results,
+        in_specs=[SMEM_SPEC if block.dtype == jnp.int32 else VMEM_SPEC for block in operands],
+        out_specs=[VMEM_SPEC] * len(results),
+        compiler_params=pltpu.CompilerParams(vmem_limit_bytes=16 * 1024 * 1024),
+        cost_estimate=pl.CostEstimate(
+            flops=microseconds * 10**9, bytes_accessed=10**6, transcendentals=0
+        ),
+        name=name,
+    )(*operands)
+
+
+def one_segment_shards(queries, keys, values, grad_y, out_gain, offsets):
+    tokens, width = queries.shape[1:]
+    heads = width // HEAD_DIM
+    top_step = lax.axis_size("ctx")
+    picked = sum(picked_counts(tokens, top_step))
+    shape = jax.ShapeDtypeStruct
+    row_block = shape((1, tokens, width), LOW)
+    low_block = shape((tokens, width), LOW)
+    wide_block = shape((tokens, width), WIDE)
+    stats_block = shape((tokens, LANES), WIDE)
+    bind = functools.partial
+    (packed,) = call(
+        bind(pack_kernel, top_step),
+        "pack",
+        (offsets, keys, values),
+        [shape((2 * picked, width), LOW)],
+        1,
+    )
+    packed_peers = to_peers(packed)
+    picked_q, expo, base_out, base_stats = call(
+        bind(base_kernel, top_step),
+        "base",
+        (offsets, queries, keys, values),
+        [shape((picked, width), LOW), low_block, wide_block, stats_block],
+        2,
+    )
+    q_peers = to_peers(picked_q)
+    attended, gain_part, sent, grad_low, soft, stats = call(
+        bind(attend_kernel, top_step),
+        "attend",
+        (
+            offsets,
+            queries,
+            grad_y,
+            out_gain.reshape(1, width),
+            base_out,
+            base_stats,
+            *packed_peers,
+        ),
+        [
+            row_block,
+            shape((1, width), WIDE),
+            shape((picked, width + LANES), LOW),
+            low_block,
+            shape((tokens, heads * 2 * LANES), LOW),
+            stats_block,
+        ],
+        3,
+    )
+    sent_peers = to_peers(sent)
+    gain_part = gain_part.reshape(width)
+    gain_pair = gain_part + across(gain_part, "dp", 1)
+    gain_peers = to_peers(gain_pair)
+    gain_grad = (gain_pair + gain_peers[0]) + (gain_peers[1] + gain_peers[2])
+    query_grad, dk_base, dv_base = call(
+        bind(local_grad_kernel, top_step),
+        "local_grad",
+        (queries, keys, values, expo, grad_low, soft, stats, *packed_peers),
+        [row_block, wide_block, wide_block],
+        3,
+    )
+    key_grad, value_grad = call(
+        bind(finish_kernel, top_step),
+        "finish",
+        (offsets, keys, values, dk_base, dv_base, *q_peers, *sent_peers),
+        [row_block, row_block],
+        2,
+    )
+    return attended, query_grad, key_grad, value_grad, gain_grad
+
+
 def solution(mesh):
     in_specs = (
         P("dp", "ctx", "head"),
@@ -232,4 +562,5 @@
         P("dp", "ctx", "head"),
         P("head"),
     )
-    return jax.shard_map(shards, mesh=mesh, in_specs=in_specs, out_specs=out_specs, check_vma=False)
+    body = one_segment_shards if mesh.shape["ctx"] == SPAN else general_shards
+    return jax.shard_map(body, mesh=mesh, in_specs=in_specs, out_specs=out_specs, check_vma=False)

time: 113 us -> 48.5 us (0.43)
  blocking collectives: 45.4 us -> 0 us
  between operations: 14.6 us -> 0.71 us
  Pallas kernels: 0 us -> 11.3 us
  local copies, waits for them, and re-layouts: 14.5 us -> 3.25 us
  starting transfers between devices: 11.5 us -> 18.8 us
  matrix products: 5.13 us -> 0 us
  waiting for transfers between devices: 17.3 us -> 13.6 us
  other arithmetic: 3.94 us -> 0.61 us
    all_gather x2 -> x0, blocking collectives: 27.4 us -> none  [the longest x1 13.8 us: shards(): lax.all_gather(top_vals, 'ctx', axis=0, tiled=True)]
    psum x1 -> x0, blocking collectives: 18.1 us -> none  [shards(): gain_grad = lax.psum(gain_part, ('dp', 'ctx'))]
    unnamed x4 -> x0, waiting for transfers between devices: 13.5 us -> none
    pallas_call x0 -> x5, Pallas kernels: none -> 11.3 us  [call(): pl.pallas_call(kernel, out_shape=results, in_specs=[SMEM_SPEC if block.dt...]
    ppermute x8 -> x13, waiting for transfers between devices: 3.77 us -> 13.6 us  [across(): return lax.ppermute(block, axis, route)]
    ppermute x8 -> x13, starting transfers between devices: 11.4 us -> 18.8 us  [across(): return lax.ppermute(block, axis, route)]
    unnamed x24 -> x18, local copies, waits for them, and re-layouts: 10.4 us -> 3.25 us
    dot_general x18 -> x0, matrix products: 5.13 us -> none  [the longest x3 1.14 us: attend(): jnp.einsum('hqk,khe->qhe', soft_rows, v_rows, preferred_element_type=jnp....]
  transfers between devices with their start and end apart: 10 -> 13, of which waited for: 4 -> 4; matrix products, arithmetic and copies ran while one was open for 10% -> 1% of each run, Pallas kernels for 0% -> 6%
where the time goes in v2:
time: 48.5 us; the launch traced here: 48.3 us
  starting transfers between devices  18.8 us (39%)
  waiting for transfers between devices  13.6 us (28%)
  Pallas kernels  11.3 us (23%)
  local copies, waits for them, and re-layouts  3.25 us (7%)
  between operations  0.71 us (1%)
  other arithmetic  0.61 us (1%)
    ppermute x13, starting transfers between devices, across(): return lax.ppermute(block, axis, route)  18.8 us
    ppermute x13, waiting for transfers between devices, across(): return lax.ppermute(block, axis, route)  13.6 us
    pallas_call x5, Pallas kernels, call(): pl.pallas_call(kernel, out_shape=results, in_specs=[SMEM_SPEC if block.dt...  11.3 us
    unnamed x18, local copies, waits for them, and re-layouts  3.25 us
  transfers between devices with their start and end apart: 13, of which 4 were waited for; matrix products, arithmetic and copies ran while one was open for 1% of the time, Pallas kernels for 6%

profile of v2, /device:TPU:0, one launch (start us, length us, event | category | flops | bytes accessed | tf_op | source)
XLA Modules:
  0.0 48.3 jit_solution(13388809536890749213)
XLA Ops:
  0.6 0.0 copy-start.2
  0.7 0.9 %copy-done.2 = bf16[1,128,640]{2,1,0:T(8,128)(2,1)S(1)} copy-done((bf16[1,128,640]{2,1,0:T(8,128)(2,1)S(1)}, bf16[1,128,640]{2,1,0:T(8,128)(2,1)}, u32[]{:S(2)}) %copy-start.2) | copy-done | bytes 163864
  1.6 0.9 %copy-done.4 = bf16[1,128,640]{2,1,0:T(8,128)(2,1)S(1)} copy-done((bf16[1,128,640]{2,1,0:T(8,128)(2,1)S(1)}, bf16[1,128,640]{2,1,0:T(8,128)(2,1)}, u32[]{:S(2)}) %copy-start.4) | copy-done | bytes 163864
  2.5 0.7 %copy-done.6 = s32[2,5]{1,0:T(2,128)S(1)} copy-done((s32[2,5]{1,0:T(2,128)S(1)}, s32[2,5]{1,0:T(2,128)}, u32[]{:S(2)}) %copy-start.6) | copy-done | bytes 64
  3.2 0.7 %pack.1 = bf16[96,640]{1,0:T(8,128)(2,1)S(1)} custom-call(s32[2,5]{1,0:T(2,128)S(1)} %copy-done.6, bf16[1,128,640]{2,1,0:T(8,128)(2,1)S(1)} %copy-done.2, bf16[1,128,640]{2,1,0:T(8,128)(2,1)S(1)} %copy-done.4), custom_call_target="tpu_custom_call" | custom-call | flops 1000000000 | bytes 1000000 | tf_op jit(solution)/shard_map/pack/pallas_call | solution.py:465
  3.9 3.1 %collective-permute-start = (bf16[96,640]{1,0:T(8,128)(2,1)S(1)}, bf16[96,640]{1,0:T(8,128)(2,1)S(1)}, u32[]{:S(2)}, u32[]{:S(2)}) collective-permute-start(bf16[96,640]{1,0:T(8,128)(2,1)S(1)} %pack.1), channel_id=1, source_target_pairs={{0,4},{4,0},{8,12},{12,8},{1,5},{5,1},{9,13},{13,9},{2,6},{6,2},{1... | collective-permute-start | bytes 368648 | tf_op jit(solution)/shard_map/ppermute | solution.py:456
  7.0 2.6 %collective-permute-start.1 = (bf16[96,640]{1,0:T(8,128)(2,1)S(1)}, bf16[96,640]{1,0:T(8,128)(2,1)S(1)}, u32[]{:S(2)}, u32[]{:S(2)}) collective-permute-start(bf16[96,640]{1,0:T(8,128)(2,1)S(1)} %pack.1), channel_id=1, source_target_pairs={{0,8},{4,12},{8,0},{12,4},{1,9},{5,13},{9,1},{13,5},{2,10},{6,14},... | collective-permute-start | bytes 368648 | tf_op jit(solution)/shard_map/ppermute | solution.py:456
  9.6 0.0 collective-permute-start.2
  9.6 0.0 copy-start
  9.6 1.1 %base.1 = (bf16[48,640]{1,0:T(8,128)(2,1)S(1)}, bf16[128,640]{1,0:T(8,128)(2,1)S(1)}, f32[128,640]{1,0:T(8,128)S(1)}, f32[128,128]{1,0:T(8,128)S(1)}) custom-call(s32[2,5]{1,0:T(2,128)S(1)} %copy-done.6, bf16[1,128,640]{2,1,0:T(8,128)(2,1)S(1)} %copy-done.1, bf16[1,128,640]{2,1,0:T(8,128)(2,1)S(1)} %copy-done.2, bf16[1,128,640]{2,1,0:T(8,128)(2,1)S(1)} %copy-done.4), custom_call_target="tpu_custom_call" | custom-call | flops 2000000000 | bytes 1000000 | tf_op jit(solution)/shard_map/base/pallas_call | solution.py:465
  10.7 1.0 %collective-permute-done.refs_0_ = bf16[96,640]{1,0:T(8,128)(2,1)S(1)} collective-permute-done((bf16[96,640]{1,0:T(8,128)(2,1)S(1)}, bf16[96,640]{1,0:T(8,128)(2,1)S(1)}, u32[]{:S(2)}, u32[]{:S(2)}) %collective-permute-start) | collective-permute-done | bytes 122912 | tf_op jit(solution)/shard_map/ppermute | solution.py:456
  11.7 7.7 %collective-permute-done.1.refs_1_ = bf16[96,640]{1,0:T(8,128)(2,1)S(1)} collective-permute-done((bf16[96,640]{1,0:T(8,128)(2,1)S(1)}, bf16[96,640]{1,0:T(8,128)(2,1)S(1)}, u32[]{:S(2)}, u32[]{:S(2)}) %collective-permute-start.1) | collective-permute-done | bytes 122912 | tf_op jit(solution)/shard_map/ppermute | solution.py:456
  19.3 0.0 copy-start.5
  19.4 5.3 %attend.1 = (bf16[1,128,640]{2,1,0:T(8,128)(2,1)}, f32[1,640]{1,0:T(1,128)S(1)}, bf16[48,768]{1,0:T(8,128)(2,1)S(1)}, bf16[128,640]{1,0:T(8,128)(2,1)S(1)}, bf16...) custom-call(s32[2,5]{1,0:T(2,128)S(1)} %copy-done.6, bf16[1,128,640]{2,1,0:T(8,128)(2,1)S(1)} %copy-done.1, ...), custom_call_target="tpu_custom_call" | custom-call | flops 3000000000 | bytes 1000000 | tf_op jit(solution)/shard_map/attend/pallas_call | solution.py:465
  24.7 0.1 collective-permute-start.9
  24.7 1.9 %collective-permute-start.3 = (bf16[48,640]{1,0:T(8,128)(2,1)S(1)}, bf16[48,640]{1,0:T(8,128)(2,1)S(1)}, u32[]{:S(2)}, u32[]{:S(2)}) collective-permute-start(bf16[48,640]{1,0:T(8,128)(2,1)S(1)} %get-tuple-element.30), channel_id=1, source_target_pairs={{0,4},{4,0},{8,12},{12,8},{1,5},{5,1},{9,13},{13,9},{2,6},{6,2},{1... | collective-permute-start | bytes 184328 | tf_op jit(solution)/shard_map/ppermute | solution.py:456
  26.7 1.1 %collective-permute-start.4 = (bf16[48,640]{1,0:T(8,128)(2,1)S(1)}, bf16[48,640]{1,0:T(8,128)(2,1)S(1)}, u32[]{:S(2)}, u32[]{:S(2)}) collective-permute-start(bf16[48,640]{1,0:T(8,128)(2,1)S(1)} %get-tuple-element.30), channel_id=1, source_target_pairs={{0,8},{4,12},{8,0},{12,4},{1,9},{5,13},{9,1},{13,5},{2,10},{6,14},... | collective-permute-start | bytes 184328 | tf_op jit(solution)/shard_map/ppermute | solution.py:456
  27.8 1.8 %collective-permute-start.11 = (f32[640]{0:T(1024)S(1)}, f32[640]{0:T(1024)S(1)}, u32[]{:S(2)}, u32[]{:S(2)}) collective-permute-start(f32[640]{0:T(1024)S(1)} %add.12), channel_id=1, source_target_pairs={{0,8},{4,12},{8,0},{12,4},{1,9},{5,13},{9,1},{13,5},{2,10},{6,14},... | collective-permute-start | bytes 7688 | tf_op jit(solution)/shard_map/ppermute | solution.py:456
  29.6 2.5 %collective-permute-start.12 = (f32[640]{0:T(1024)S(1)}, f32[640]{0:T(1024)S(1)}, u32[]{:S(2)}, u32[]{:S(2)}) collective-permute-start(f32[640]{0:T(1024)S(1)} %add.12), channel_id=1, source_target_pairs={{0,12},{4,8},{8,4},{12,0},{1,13},{5,9},{9,5},{13,1},{2,14},{6,10},... | collective-permute-start | bytes 7688 | tf_op jit(solution)/shard_map/ppermute | solution.py:456
  32.1 1.9 %local_grad.1 = (bf16[1,128,640]{2,1,0:T(8,128)(2,1)}, f32[128,640]{1,0:T(8,128)S(1)}, f32[128,640]{1,0:T(8,128)S(1)}) custom-call(bf16[1,128,640]{2,1,0:T(8,128)(2,1)S(1)} %copy-done.1, bf16[1,128,640]{2,1,0:T(8,128)(2,1)S(1)} %copy-done.3, bf16[1,128,640]{2,1,0:T(8,128)(2,1)S(1)} %copy-done.5, bf16[128,640]{1,0:T(8,128)(2,1)S(1)} %get-tuple-element.23.expo_ref, ...), custom_call_target="tpu_custom_call" | custom-call | flops 3000000000 | bytes 1000000 | tf_op jit(solution)/shard_map/local_grad/pallas_call | solution.py:465
  34.0 0.0 collective-permute-done.3.refs_0_
  34.0 1.3 %collective-permute-start.5 = (bf16[48,640]{1,0:T(8,128)(2,1)S(1)}, bf16[48,640]{1,0:T(8,128)(2,1)S(1)}, u32[]{:S(2)}, u32[]{:S(2)}) collective-permute-start(bf16[48,640]{1,0:T(8,128)(2,1)S(1)} %get-tuple-element.30), channel_id=1, source_target_pairs={{0,12},{4,8},{8,4},{12,0},{1,13},{5,9},{9,5},{13,1},{2,14},{6,10},... | collective-permute-start | bytes 184328 | tf_op jit(solution)/shard_map/ppermute | solution.py:456
  35.3 1.1 %collective-permute-start.6 = (bf16[48,768]{1,0:T(8,128)(2,1)S(1)}, bf16[48,768]{1,0:T(8,128)(2,1)S(1)}, u32[]{:S(2)}, u32[]{:S(2)}) collective-permute-start(bf16[48,768]{1,0:T(8,128)(2,1)S(1)} %get-tuple-element.31), channel_id=1, source_target_pairs={{0,4},{4,0},{8,12},{12,8},{1,5},{5,1},{9,13},{13,9},{2,6},{6,2},{1... | collective-permute-start | bytes 221192 | tf_op jit(solution)/shard_map/ppermute | solution.py:456
  36.4 0.0 collective-permute-done.12
  36.4 1.9 %collective-permute-start.7 = (bf16[48,768]{1,0:T(8,128)(2,1)S(1)}, bf16[48,768]{1,0:T(8,128)(2,1)S(1)}, u32[]{:S(2)}, u32[]{:S(2)}) collective-permute-start(bf16[48,768]{1,0:T(8,128)(2,1)S(1)} %get-tuple-element.31), channel_id=1, source_target_pairs={{0,8},{4,12},{8,0},{12,4},{1,9},{5,13},{9,1},{13,5},{2,10},{6,14},... | collective-permute-start | bytes 221192 | tf_op jit(solution)/shard_map/ppermute | solution.py:456
  38.4 0.0 collective-permute-done.10
  38.4 1.3 %collective-permute-start.8 = (bf16[48,768]{1,0:T(8,128)(2,1)S(1)}, bf16[48,768]{1,0:T(8,128)(2,1)S(1)}, u32[]{:S(2)}, u32[]{:S(2)}) collective-permute-start(bf16[48,768]{1,0:T(8,128)(2,1)S(1)} %get-tuple-element.31), channel_id=1, source_target_pairs={{0,12},{4,8},{8,4},{12,0},{1,13},{5,9},{9,5},{13,1},{2,14},{6,10},... | collective-permute-start | bytes 221192 | tf_op jit(solution)/shard_map/ppermute | solution.py:456
  39.7 0.6 %add_add_fusion = f32[640]{0:T(1024)} fusion(f32[640]{0:T(1024)S(1)} %collective-permute-done.11, f32[640]{0:T(1024)S(1)} %collective-permute-done.12, f32[640]{0:T(1024)S(1)} %add.12, f32[640]{0:T(1024)S(1)} %collective-permute-done.10), kind=kLoop, calls=%fused_computation | loop fusion | flops 1920 | bytes 12800 | tf_op jit(solution)/shard_map/add | solution.py:531
  40.3 0.4 collective-permute-done.5.refs_2_
  40.7 4.6 %collective-permute-done.7.refs_4_ = bf16[48,768]{1,0:T(8,128)(2,1)S(1)} collective-permute-done((bf16[48,768]{1,0:T(8,128)(2,1)S(1)}, bf16[48,768]{1,0:T(8,128)(2,1)S(1)}, u32[]{:S(2)}, u32[]{:S(2)}) %collective-permute-start.7) | collective-permute-done | bytes 73760 | tf_op jit(solution)/shard_map/ppermute | solution.py:456
  45.3 0.7 %copy-done.7 = s32[2,5]{1,0:T(2,128)S(1)} copy-done((s32[2,5]{1,0:T(2,128)S(1)}, s32[2,5]{1,0:T(2,128)}, u32[]{:S(2)}) %copy-start.7) | copy-done | bytes 64
  45.9 2.3 %finish.1 = (bf16[1,128,640]{2,1,0:T(8,128)(2,1)}, bf16[1,128,640]{2,1,0:T(8,128)(2,1)}) custom-call(s32[2,5]{1,0:T(2,128)S(1)} %copy-done.7, bf16[1,128,640]{2,1,0:T(8,128)(2,1)S(1)} %copy-done.3, bf16[1,128,640]{2,1,0:T(8,128)(2,1)S(1)} %copy-done.5, f32[128,640]{1,0:T(8,128)S(1)} %get-tuple-element.28.dk_ref, f32[128,640]{1,0:T(8,128)S(1)} %get-tuple-element.29.dv_ref, ...), custom_call_target="tpu_custom_call" | custom-call | flops 2000000000 | bytes 1000000 | tf_op jit(solution)/shard_map/finish/pallas_call | solution.py:465
  (21 shorter events, 0.1 us)
Async XLA Ops:
  0.6 9.0 %copy-start.1 = (bf16[1,128,640]{2,1,0:T(8,128)(2,1)S(1)}, bf16[1,128,640]{2,1,0:T(8,128)(2,1)}, u32[]{:S(2)}) copy-start(bf16[1,128,640]{2,1,0:T(8,128)(2,1)} %q_ref.5) | copy-start | bytes 491524
  0.6 1.0 %copy-start.2 = (bf16[1,128,640]{2,1,0:T(8,128)(2,1)S(1)}, bf16[1,128,640]{2,1,0:T(8,128)(2,1)}, u32[]{:S(2)}) copy-start(bf16[1,128,640]{2,1,0:T(8,128)(2,1)} %k_ref.7) | copy-start | bytes 491524
  1.6 0.9 %copy-start.4 = (bf16[1,128,640]{2,1,0:T(8,128)(2,1)S(1)}, bf16[1,128,640]{2,1,0:T(8,128)(2,1)}, u32[]{:S(2)}) copy-start(bf16[1,128,640]{2,1,0:T(8,128)(2,1)} %v_ref.7) | copy-start | bytes 491524
  2.5 0.7 %copy-start.6 = (s32[2,5]{1,0:T(2,128)S(1)}, s32[2,5]{1,0:T(2,128)}, u32[]{:S(2)}) copy-start(s32[2,5]{1,0:T(2,128)} %offsets_ref.7) | copy-start | bytes 124
  3.2 6.4 %copy-start.8 = (f32[640]{0:T(1024)S(1)}, f32[640]{0:T(1024)}, u32[]{:S(2)}) copy-start(f32[640]{0:T(1024)} %param.10) | copy-start | bytes 7684
  3.9 7.7 %collective-permute-start = (bf16[96,640]{1,0:T(8,128)(2,1)S(1)}, bf16[96,640]{1,0:T(8,128)(2,1)S(1)}, u32[]{:S(2)}, u32[]{:S(2)}) collective-permute-start(bf16[96,640]{1,0:T(8,128)(2,1)S(1)} %pack.1), channel_id=1, source_target_pairs={{0,4},{4,0},{8,12},{12,8},{1,5},{5,1},{9,13},{13,9},{2,6},{6,2},{1... | collective-permute-start | bytes 368648 | tf_op jit(solution)/shard_map/ppermute | solution.py:456
  7.0 12.3 %collective-permute-start.1 = (bf16[96,640]{1,0:T(8,128)(2,1)S(1)}, bf16[96,640]{1,0:T(8,128)(2,1)S(1)}, u32[]{:S(2)}, u32[]{:S(2)}) collective-permute-start(bf16[96,640]{1,0:T(8,128)(2,1)S(1)} %pack.1), channel_id=1, source_target_pairs={{0,8},{4,12},{8,0},{12,4},{1,9},{5,13},{9,1},{13,5},{2,10},{6,14},... | collective-permute-start | bytes 368648 | tf_op jit(solution)/shard_map/ppermute | solution.py:456
  9.6 9.7 %collective-permute-start.2 = (bf16[96,640]{1,0:T(8,128)(2,1)S(1)}, bf16[96,640]{1,0:T(8,128)(2,1)S(1)}, u32[]{:S(2)}, u32[]{:S(2)}) collective-permute-start(bf16[96,640]{1,0:T(8,128)(2,1)S(1)} %pack.1), channel_id=1, source_target_pairs={{0,12},{4,8},{8,4},{12,0},{1,13},{5,9},{9,5},{13,1},{2,14},{6,10},... | collective-permute-start | bytes 368648 | tf_op jit(solution)/shard_map/ppermute | solution.py:456
  9.6 9.7 %copy-start = (bf16[1,128,640]{2,1,0:T(8,128)(2,1)S(1)}, bf16[1,128,640]{2,1,0:T(8,128)(2,1)}, u32[]{:S(2)}) copy-start(bf16[1,128,640]{2,1,0:T(8,128)(2,1)} %grad_ref.1) | copy-start | bytes 491524
  19.3 12.7 %copy-start.3 = (bf16[1,128,640]{2,1,0:T(8,128)(2,1)S(1)}, bf16[1,128,640]{2,1,0:T(8,128)(2,1)}, u32[]{:S(2)}) copy-start(bf16[1,128,640]{2,1,0:T(8,128)(2,1)} %k_ref.7) | copy-start | bytes 491524
  19.3 12.7 %copy-start.5 = (bf16[1,128,640]{2,1,0:T(8,128)(2,1)S(1)}, bf16[1,128,640]{2,1,0:T(8,128)(2,1)}, u32[]{:S(2)}) copy-start(bf16[1,128,640]{2,1,0:T(8,128)(2,1)} %v_ref.7) | copy-start | bytes 491524
  24.7 3.1 %collective-permute-start.9 = (f32[640]{0:T(1024)S(1)}, f32[640]{0:T(1024)S(1)}, u32[]{:S(2)}, u32[]{:S(2)}) collective-permute-start(f32[640]{0:T(1024)S(1)} %reduce), channel_id=1, source_target_pairs={{0,16},{16,0},{1,17},{17,1},{2,18},{18,2},{3,19},{19,3},{4,20},{20... | collective-permute-start | bytes 7688 | tf_op jit(solution)/shard_map/ppermute | solution.py:456
  24.7 9.2 %collective-permute-start.3 = (bf16[48,640]{1,0:T(8,128)(2,1)S(1)}, bf16[48,640]{1,0:T(8,128)(2,1)S(1)}, u32[]{:S(2)}, u32[]{:S(2)}) collective-permute-start(bf16[48,640]{1,0:T(8,128)(2,1)S(1)} %get-tuple-element.30), channel_id=1, source_target_pairs={{0,4},{4,0},{8,12},{12,8},{1,5},{5,1},{9,13},{13,9},{2,6},{6,2},{1... | collective-permute-start | bytes 184328 | tf_op jit(solution)/shard_map/ppermute | solution.py:456
  26.7 13.7 %collective-permute-start.4 = (bf16[48,640]{1,0:T(8,128)(2,1)S(1)}, bf16[48,640]{1,0:T(8,128)(2,1)S(1)}, u32[]{:S(2)}, u32[]{:S(2)}) collective-permute-start(bf16[48,640]{1,0:T(8,128)(2,1)S(1)} %get-tuple-element.30), channel_id=1, source_target_pairs={{0,8},{4,12},{8,0},{12,4},{1,9},{5,13},{9,1},{13,5},{2,10},{6,14},... | collective-permute-start | bytes 184328 | tf_op jit(solution)/shard_map/ppermute | solution.py:456
  27.8 7.6 %collective-permute-start.11 = (f32[640]{0:T(1024)S(1)}, f32[640]{0:T(1024)S(1)}, u32[]{:S(2)}, u32[]{:S(2)}) collective-permute-start(f32[640]{0:T(1024)S(1)} %add.12), channel_id=1, source_target_pairs={{0,8},{4,12},{8,0},{12,4},{1,9},{5,13},{9,1},{13,5},{2,10},{6,14},... | collective-permute-start | bytes 7688 | tf_op jit(solution)/shard_map/ppermute | solution.py:456
  29.6 6.8 %collective-permute-start.12 = (f32[640]{0:T(1024)S(1)}, f32[640]{0:T(1024)S(1)}, u32[]{:S(2)}, u32[]{:S(2)}) collective-permute-start(f32[640]{0:T(1024)S(1)} %add.12), channel_id=1, source_target_pairs={{0,12},{4,8},{8,4},{12,0},{1,13},{5,9},{9,5},{13,1},{2,14},{6,10},... | collective-permute-start | bytes 7688 | tf_op jit(solution)/shard_map/ppermute | solution.py:456
  32.1 6.3 %collective-permute-start.10 = (f32[640]{0:T(1024)S(1)}, f32[640]{0:T(1024)S(1)}, u32[]{:S(2)}, u32[]{:S(2)}) collective-permute-start(f32[640]{0:T(1024)S(1)} %add.12), channel_id=1, source_target_pairs={{0,4},{4,0},{8,12},{12,8},{1,5},{5,1},{9,13},{13,9},{2,6},{6,2},{1... | collective-permute-start | bytes 7688 | tf_op jit(solution)/shard_map/ppermute | solution.py:456
  34.0 6.7 %collective-permute-start.5 = (bf16[48,640]{1,0:T(8,128)(2,1)S(1)}, bf16[48,640]{1,0:T(8,128)(2,1)S(1)}, u32[]{:S(2)}, u32[]{:S(2)}) collective-permute-start(bf16[48,640]{1,0:T(8,128)(2,1)S(1)} %get-tuple-element.30), channel_id=1, source_target_pairs={{0,12},{4,8},{8,4},{12,0},{1,13},{5,9},{9,5},{13,1},{2,14},{6,10},... | collective-permute-start | bytes 184328 | tf_op jit(solution)/shard_map/ppermute | solution.py:456
  35.3 5.4 %collective-permute-start.6 = (bf16[48,768]{1,0:T(8,128)(2,1)S(1)}, bf16[48,768]{1,0:T(8,128)(2,1)S(1)}, u32[]{:S(2)}, u32[]{:S(2)}) collective-permute-start(bf16[48,768]{1,0:T(8,128)(2,1)S(1)} %get-tuple-element.31), channel_id=1, source_target_pairs={{0,4},{4,0},{8,12},{12,8},{1,5},{5,1},{9,13},{13,9},{2,6},{6,2},{1... | collective-permute-start | bytes 221192 | tf_op jit(solution)/shard_map/ppermute | solution.py:456
  36.4 8.8 %collective-permute-start.7 = (bf16[48,768]{1,0:T(8,128)(2,1)S(1)}, bf16[48,768]{1,0:T(8,128)(2,1)S(1)}, u32[]{:S(2)}, u32[]{:S(2)}) collective-permute-start(bf16[48,768]{1,0:T(8,128)(2,1)S(1)} %get-tuple-element.31), channel_id=1, source_target_pairs={{0,8},{4,12},{8,0},{12,4},{1,9},{5,13},{9,1},{13,5},{2,10},{6,14},... | collective-permute-start | bytes 221192 | tf_op jit(solution)/shard_map/ppermute | solution.py:456
  38.4 6.9 %collective-permute-start.8 = (bf16[48,768]{1,0:T(8,128)(2,1)S(1)}, bf16[48,768]{1,0:T(8,128)(2,1)S(1)}, u32[]{:S(2)}, u32[]{:S(2)}) collective-permute-start(bf16[48,768]{1,0:T(8,128)(2,1)S(1)} %get-tuple-element.31), channel_id=1, source_target_pairs={{0,12},{4,8},{8,4},{12,0},{1,13},{5,9},{9,5},{13,1},{2,14},{6,10},... | collective-permute-start | bytes 221192 | tf_op jit(solution)/shard_map/ppermute | solution.py:456
  45.3 0.7 %copy-start.7 = (s32[2,5]{1,0:T(2,128)S(1)}, s32[2,5]{1,0:T(2,128)}, u32[]{:S(2)}) copy-start(s32[2,5]{1,0:T(2,128)} %offsets_ref.7) | copy-start | bytes 124

commit v3 on v0

--- a/solution.py
+++ b/solution.py
@@ -1,8 +1,11 @@
+import functools
 import math
 
 import jax
 import jax.numpy as jnp
 from jax import lax
+from jax.experimental import pallas as pl
+from jax.experimental.pallas import tpu as pltpu
 from jax.sharding import PartitionSpec as P
 
 HEAD_DIM = 128
@@ -79,7 +82,7 @@
     return jnp.einsum("hqk,khe->qhe", score_grad, k_rows, preferred_element_type=jnp.float32)
 
 
-def shards(queries, keys, values, grad_y, out_gain, offsets):
+def general_shards(queries, keys, values, grad_y, out_gain, offsets):
     tokens = queries.shape[1]
     flat_width = queries.shape[2]
     head_count = flat_width // HEAD_DIM
@@ -216,6 +219,367 @@
     )
 
 
+VMEM_SPEC = pl.BlockSpec(memory_space=pltpu.VMEM)
+SMEM_SPEC = pl.BlockSpec(memory_space=pltpu.SMEM)
+HBM_SPEC = pl.BlockSpec(memory_space=pltpu.HBM)
+PEERS = SPAN - 1
+STATS_ROWS = 8
+NEVER = -1e30
+LOW = jnp.bfloat16
+WIDE = jnp.float32
+HEAD_GROUPS = ((0, 5),)
+
+
+def contract(left, right, left_dim, right_dim):
+    return lax.dot_general(
+        left, right, (((left_dim,), (right_dim,)), ((), ())), preferred_element_type=WIDE
+    )
+
+
+def head_cols(head):
+    return pl.ds(head * HEAD_DIM, HEAD_DIM)
+
+
+def picked_counts(tokens, top_step):
+    return tokens // top_step, tokens // R1
+
+
+def pick_matrix(offsets_ref, head, tokens, top_step, picked_axis):
+    top_rows, mid_rows = picked_counts(tokens, top_step)
+    shape = (top_rows + mid_rows, tokens) if picked_axis == 0 else (tokens, top_rows + mid_rows)
+    row = lax.broadcasted_iota(jnp.int32, shape, picked_axis)
+    position = lax.broadcasted_iota(jnp.int32, shape, 1 - picked_axis)
+    wanted = jnp.where(
+        row < top_rows,
+        row * top_step + offsets_ref[1, head],
+        (row - top_rows) * R1 + offsets_ref[0, head],
+    )
+    return jnp.where(position == wanted, 1.0, 0.0).astype(LOW)
+
+
+def stacked(refs, rows, cols):
+    return jnp.concatenate([ref[rows, cols] for ref in refs], 0)
+
+
+def pack_kernel(top_step, groups, offsets_ref, k_hbm, v_hbm, *refs):
+    packed_refs, (k_ref, v_ref, sems) = refs[: len(groups)], refs[len(groups) :]
+    tokens, width = k_ref.shape
+    picked = sum(picked_counts(tokens, top_step))
+    copies = []
+    for head in range(width // HEAD_DIM):
+        cols = head_cols(head)
+        pair = [
+            pltpu.make_async_copy(source.at[0, :, cols], held.at[:, cols], sems.at[which, head])
+            for which, (source, held) in enumerate(((k_hbm, k_ref), (v_hbm, v_ref)))
+        ]
+        for copy in pair:
+            copy.start()
+        copies.append(pair)
+    for (first, last), packed_ref in zip(groups, packed_refs):
+        for head in range(first, last):
+            cols = head_cols(head)
+            picks = pick_matrix(offsets_ref, head, tokens, top_step, 0)
+            for copy in copies[head]:
+                copy.wait()
+            both = jnp.concatenate([k_ref[:, cols], v_ref[:, cols]], 1)
+            rows = contract(picks, both, 1, 0).astype(LOW)
+            packed_ref[:picked, head_cols(head - first)] = rows[:, :HEAD_DIM]
+            packed_ref[picked:, head_cols(head - first)] = rows[:, HEAD_DIM:]
+
+
+def fetch(sources, held, sems):
+    copies = [
+        pltpu.make_async_copy(source.at[0] if len(source.shape) == 3 else source, block, sems.at[i])
+        for i, (source, block) in enumerate(zip(sources, held))
+    ]
+    for copy in copies:
+        copy.start()
+    for copy in copies:
+        copy.wait()
+
+
+def base_kernel(top_step, offsets_ref, *refs):
+    sources, refs = refs[:5], refs[5:]
+    held, sems = refs[-6:-1], refs[-1]
+    expo_ref, out_ref, grad_norm_ref, q_copy_ref, inv_gain_ref, place_ref, stats_ref = refs[:-6]
+    fetch(sources, held, sems)
+    q_ref, k_ref, v_ref, grad_ref, gain_ref = held
+    tokens, width = q_ref.shape
+    picked = sum(picked_counts(tokens, top_step))
+    score_scale = 1.0 / math.sqrt(HEAD_DIM)
+    key_row = lax.broadcasted_iota(jnp.int32, (tokens, 1), 0)
+    query_col = lax.broadcasted_iota(jnp.int32, (1, tokens), 1)
+    q_copy_ref[...] = q_ref[...]
+    inv_gain_ref[...] = 1.0 / gain_ref[...]
+    for head in range(width // HEAD_DIM):
+        cols = head_cols(head)
+        times = 1.0
+        for level, step in ((0, R1), (1, top_step)):
+            offset = offsets_ref[level, head]
+            hit_row = jnp.where(key_row % step == offset, 1.0, 0.0)
+            hit_col = jnp.where(query_col % step == offset, 1.0, 0.0)
+            times = times + hit_row * hit_col
+            bias_row = (2 + level) * STATS_ROWS + head
+            stats_ref[bias_row : bias_row + 1, :] = (1.0 - hit_col) * NEVER
+        place_ref[:, pl.ds(head * HEAD_DIM, picked)] = pick_matrix(
+            offsets_ref, head, tokens, top_step, 1
+        )
+        scores = contract(k_ref[:, cols], q_ref[:, cols], 1, 1) * score_scale
+        top_score = jnp.max(scores, axis=0, keepdims=True)
+        expo = times * jnp.exp(scores - top_score)
+        expo_low = expo.astype(LOW)
+        expo_ref[:, cols] = expo_low
+        out_ref[:, cols] = contract(v_ref[:, cols], expo_low, 0, 0)
+        stats_ref[head : head + 1, :] = top_score
+        stats_ref[STATS_ROWS + head : STATS_ROWS + head + 1, :] = jnp.sum(
+            expo, axis=0, keepdims=True
+        )
+        grad_norm_ref[:, cols] = (grad_ref[:, cols].astype(WIDE) * gain_ref[:, cols]).T
+
+
+def attend_kernel(
+    top_step,
+    first,
+    last,
+    q_ref,
+    base_out_ref,
+    grad_norm_ref,
+    inv_gain_ref,
+    base_stats_ref,
+    *refs,
+):
+    packed_refs = refs[:PEERS]
+    gain_part_ref, normed_ref, grad_low_ref, score_grad_ref, stats_ref = refs[PEERS : PEERS + 5]
+    part_refs = refs[PEERS + 5 :]
+    tokens = q_ref.shape[0]
+    top_rows, mid_rows = picked_counts(tokens, top_step)
+    picked = top_rows + mid_rows
+    score_scale = 1.0 / math.sqrt(HEAD_DIM)
+    ones = jnp.ones((STATS_ROWS, tokens), LOW)
+    for head in range(first, last):
+        cols = head_cols(head)
+        own = head_cols(head - first)
+        q_rows = q_ref[:, cols]
+        k_peers = stacked(packed_refs, pl.ds(0, picked), own)
+        v_peers = stacked(packed_refs, pl.ds(picked, picked), own)
+        mid_bias, top_bias = [
+            base_stats_ref[row + head : row + head + 1, :]
+            for row in (2 * STATS_ROWS, 3 * STATS_ROWS)
+        ]
+        bias = jnp.concatenate(
+            [
+                jnp.broadcast_to(top_bias, (top_rows, tokens)),
+                jnp.broadcast_to(mid_bias, (mid_rows, tokens)),
+            ]
+            * PEERS,
+            0,
+        )
+        scores = contract(k_peers, q_rows, 1, 1) * score_scale + bias
+        base_top = base_stats_ref[head : head + 1, :]
+        base_total = base_stats_ref[STATS_ROWS + head : STATS_ROWS + head + 1, :]
+        top_score = jnp.maximum(base_top, jnp.max(scores, axis=0, keepdims=True))
+        base_factor = jnp.exp(base_top - top_score)
+        expo = jnp.exp(scores - top_score)
+        inv_total = 1.0 / (base_factor * base_total + jnp.sum(expo, axis=0, keepdims=True))
+        soft = expo * inv_total
+        soft_low = soft.astype(LOW)
+        base_factor = base_factor * inv_total
+        attn = base_factor * base_out_ref[:, cols] + contract(v_peers, soft_low, 0, 0)
+        inv_rms = lax.rsqrt(jnp.mean(attn * attn, axis=0, keepdims=True) + EPS)
+        normed = attn * inv_rms
+        normed_ref[:, own] = normed
+        grad_norm = grad_norm_ref[:, cols]
+        product = grad_norm * normed
+        grad_attn = inv_rms * (grad_norm - normed * jnp.mean(product, axis=0, keepdims=True))
+        product_high = product.astype(LOW)
+        product_rest = (product - product_high.astype(WIDE)).astype(LOW)
+        gain_rows = contract(ones, product_high, 1, 1) + contract(ones, product_rest, 1, 1)
+        gain_part_ref[:, own] = gain_rows[:1] * inv_gain_ref[:, cols]
+        inner = jnp.sum(grad_attn * attn, axis=0, keepdims=True)
+        grad_low = grad_attn.astype(LOW)
+        grad_low_ref[:, own] = grad_low
+        stats_ref[head - first : head - first + 1, :] = base_factor
+        stats_ref[STATS_ROWS + head - first : STATS_ROWS + head - first + 1, :] = inner
+        prob_grad = contract(v_peers, grad_low, 1, 0)
+        score_grad = (soft * (prob_grad - inner) * score_scale).astype(LOW)
+        score_grad_ref[:, own] = score_grad
+        dk_peers = contract(score_grad, q_rows, 1, 0).astype(LOW)
+        dv_peers = contract(soft_low, grad_low, 1, 1).astype(LOW)
+        for place, part_ref in enumerate(part_refs):
+            part_ref[:picked, own] = dk_peers[place * picked : (place + 1) * picked]
+            part_ref[picked:, own] = dv_peers[place * picked : (place + 1) * picked]
+
+
+def local_grad_kernel(top_step, groups, *refs):
+    sources, expo_ref, refs = refs[:4], refs[4], refs[5:]
+    held, sems = refs[-5:-1], refs[-1]
+    per_group = 4 + PEERS
+    group_refs = refs[: per_group * len(groups)]
+    attended_ref, dq_ref, dk_ref, dv_ref = refs[per_group * len(groups) : -5]
+    fetch(sources, held, sems)
+    q_ref, k_ref, v_ref, gain_ref = held
+    picked = sum(picked_counts(q_ref.shape[0], top_step))
+    score_scale = 1.0 / math.sqrt(HEAD_DIM)
+    for place, (first, last) in enumerate(groups):
+        normed_ref, grad_low_ref, peer_score_grad_ref, stats_ref, *packed_refs = group_refs[
+            place * per_group : (place + 1) * per_group
+        ]
+        for head in range(first, last):
+            cols = head_cols(head)
+            own = head_cols(head - first)
+            normed = normed_ref[:, own].T
+            attended_ref[0, :, cols] = (normed * gain_ref[:, cols]).astype(LOW)
+            k_rows = k_ref[:, cols]
+            k_peers = stacked(packed_refs, pl.ds(0, picked), own)
+            grad_low = grad_low_ref[:, own]
+            base_factor = stats_ref[head - first : head - first + 1, :]
+            inner = stats_ref[STATS_ROWS + head - first : STATS_ROWS + head - first + 1, :]
+            soft = expo_ref[:, cols].astype(WIDE) * base_factor
+            prob_grad = contract(v_ref[:, cols], grad_low, 1, 0)
+            score_grad = (soft * (prob_grad - inner) * score_scale).astype(LOW)
+            dk_ref[:, cols] = contract(score_grad, q_ref[:, cols], 1, 0)
+            dv_ref[:, cols] = contract(soft.astype(LOW), grad_low, 1, 1)
+            dq_ref[0, :, cols] = (
+                contract(score_grad, k_rows, 0, 0)
+                + contract(peer_score_grad_ref[:, own], k_peers, 0, 0)
+            ).astype(LOW)
+
+
+def finish_kernel(top_step, groups, place_ref, dk_ref, dv_ref, *refs):
+    dk_out_ref, dv_out_ref = refs[PEERS * len(groups) :]
+    tokens = dk_ref.shape[0]
+    picked = sum(picked_counts(tokens, top_step))
+    for place, (first, last) in enumerate(groups):
+        part_refs = refs[place * PEERS : (place + 1) * PEERS]
+        for head in range(first, last):
+            cols = head_cols(head)
+            own = head_cols(head - first)
+            total = sum(part_ref[:, own].astype(WIDE) for part_ref in part_refs).astype(LOW)
+            both = jnp.concatenate([total[:picked], total[picked:]], 1)
+            placed = contract(place_ref[:, pl.ds(head * HEAD_DIM, picked)], both, 1, 0)
+            dk_out_ref[0, :, cols] = (dk_ref[:, cols] + placed[:, :HEAD_DIM]).astype(LOW)
+            dv_out_ref[0, :, cols] = (dv_ref[:, cols] + placed[:, HEAD_DIM:]).astype(LOW)
+
+
+def across(block, axis, distance):
+    route = [(place, place ^ distance) for place in range(lax.axis_size(axis))]
+    return lax.ppermute(block, axis, route)
+
+
+def to_peers(blocks):
+    farthest_first = [
+        across(blocks[distance - 1], "ctx", distance) for distance in range(PEERS, 0, -1)
+    ]
+    return farthest_first[::-1]
+
+
+def call(kernel, name, operands, results, microseconds, **options):
+    options.setdefault(
+        "in_specs", [SMEM_SPEC if block.dtype == jnp.int32 else VMEM_SPEC for block in operands]
+    )
+    options.setdefault(
+        "compiler_params", pltpu.CompilerParams(vmem_limit_bytes=16 * 1024 * 1024)
+    )
+    return pl.pallas_call(
+        kernel,
+        out_shape=results,
+        out_specs=[VMEM_SPEC] * len(results),
+        cost_estimate=pl.CostEstimate(
+            flops=microseconds * 10**9, bytes_accessed=10**6, transcendentals=0
+        ),
+        name=name,
+        **options,
+    )(*operands)
+
+
+def one_segment_shards(queries, keys, values, grad_y, out_gain, offsets):
+    tokens, width = queries.shape[1:]
+    heads = width // HEAD_DIM
+    top_step = lax.axis_size("ctx")
+    picked = sum(picked_counts(tokens, top_step))
+    shape = jax.ShapeDtypeStruct
+    row_block = shape((1, tokens, width), LOW)
+    low_block = shape((tokens, width), LOW)
+    wide_block = shape((tokens, width), WIDE)
+    groups = HEAD_GROUPS
+    widths = [(last - first) * HEAD_DIM for first, last in groups]
+    bind = functools.partial
+    gain_row = out_gain.reshape(1, width)
+    packed = call(
+        bind(pack_kernel, top_step, groups),
+        "pack",
+        (offsets, keys, values),
+        [shape((2 * picked, group_width), LOW) for group_width in widths],
+        1,
+        in_specs=[SMEM_SPEC, HBM_SPEC, HBM_SPEC],
+        compiler_params=None,
+        scratch_shapes=[
+            pltpu.VMEM((tokens, width), LOW),
+            pltpu.VMEM((tokens, width), LOW),
+            pltpu.SemaphoreType.DMA((2, heads)),
+        ],
+    )
+    packed_peers = [to_peers([block] * PEERS) for block in packed]
+    row_scratch, gain_scratch = pltpu.VMEM((tokens, width), LOW), pltpu.VMEM((1, width), WIDE)
+    expo, base_out, grad_norm, q_copy, inv_gain, place, base_stats = call(
+        bind(base_kernel, top_step),
+        "base",
+        (offsets, queries, keys, values, grad_y, gain_row),
+        [
+            low_block,
+            wide_block,
+            wide_block,
+            low_block,
+            shape((1, width), WIDE),
+            low_block,
+            shape((4 * STATS_ROWS, tokens), WIDE),
+        ],
+        2,
+        in_specs=[SMEM_SPEC] + [HBM_SPEC] * 5,
+        scratch_shapes=[row_scratch] * 4 + [gain_scratch, pltpu.SemaphoreType.DMA((5,))],
+    )
+    kept, returned, gain_parts = [], [], []
+    for (first, last), group_width, peers in zip(groups, widths, packed_peers):
+        gain_part, normed, grad_low, score_grad, stats, *parts = call(
+            bind(attend_kernel, top_step, first, last),
+            "attend",
+            (q_copy, base_out, grad_norm, inv_gain, base_stats, *peers),
+            [
+                shape((1, group_width), WIDE),
+                shape((tokens, group_width), WIDE),
+                shape((tokens, group_width), LOW),
+                shape((PEERS * picked, group_width), LOW),
+                shape((2 * STATS_ROWS, tokens), WIDE),
+            ]
+            + [shape((2 * picked, group_width), LOW)] * PEERS,
+            last - first,
+        )
+        gain_parts.append(gain_part.reshape(group_width))
+        kept += [normed, grad_low, score_grad, stats, *peers]
+        returned += to_peers(parts)
+    gain_part = jnp.concatenate(gain_parts) if len(groups) > 1 else gain_parts[0]
+    gain_pair = gain_part + across(gain_part, "dp", 1)
+    gain_peers = to_peers([gain_pair] * PEERS)
+    gain_grad = (gain_pair + gain_peers[0]) + (gain_peers[1] + gain_peers[2])
+    attended, query_grad, dk_base, dv_base = call(
+        bind(local_grad_kernel, top_step, groups),
+        "local_grad",
+        (queries, keys, values, gain_row, expo, *kept),
+        [row_block, row_block, wide_block, wide_block],
+        3,
+        in_specs=[HBM_SPEC] * 4 + [VMEM_SPEC] * (1 + len(kept)),
+        scratch_shapes=[row_scratch] * 3 + [gain_scratch, pltpu.SemaphoreType.DMA((4,))],
+    )
+    key_grad, value_grad = call(
+        bind(finish_kernel, top_step, groups),
+        "finish",
+        (place, dk_base, dv_base, *returned),
+        [row_block, row_block],
+        2,
+    )
+    return attended, query_grad, key_grad, value_grad, gain_grad
+
+
 def solution(mesh):
     in_specs = (
         P("dp", "ctx", "head"),
@@ -232,4 +596,5 @@
         P("dp", "ctx", "head"),
         P("head"),
     )
-    return jax.shard_map(shards, mesh=mesh, in_specs=in_specs, out_specs=out_specs, check_vma=False)
+    body = one_segment_shards if mesh.shape["ctx"] == SPAN else general_shards
+    return jax.shard_map(body, mesh=mesh, in_specs=in_specs, out_specs=out_specs, check_vma=False)

time: 113 us -> 40.6 us (0.36)
  blocking collectives: 45.4 us -> 0 us
  local copies, waits for them, and re-layouts: 14.5 us -> 0.03 us
  between operations: 14.6 us -> 0.78 us
  Pallas kernels: 0 us -> 12.1 us
  waiting for transfers between devices: 17.3 us -> 12.1 us
  matrix products: 5.13 us -> 0 us
  other arithmetic: 3.94 us -> 0.62 us
  starting transfers between devices: 11.5 us -> 14.7 us
    all_gather x2 -> x0, blocking collectives: 27.4 us -> none  [the longest x1 13.8 us: shards(): lax.all_gather(top_vals, 'ctx', axis=0, tiled=True)]
    psum x1 -> x0, blocking collectives: 18.1 us -> none  [shards(): gain_grad = lax.psum(gain_part, ('dp', 'ctx'))]
    unnamed x4 -> x0, waiting for transfers between devices: 13.5 us -> none
    pallas_call x0 -> x5, Pallas kernels: none -> 12.1 us  [call(): pl.pallas_call(kernel, out_shape=results, out_specs=[VMEM_SPEC] * len(res...]
    unnamed x24 -> x12, local copies, waits for them, and re-layouts: 10.4 us -> 0.03 us
    ppermute x8 -> x10, waiting for transfers between devices: 3.77 us -> 12.1 us  [across(): return lax.ppermute(block, axis, route)]
    dot_general x18 -> x0, matrix products: 5.13 us -> none  [the longest x3 1.14 us: attend(): jnp.einsum('hqk,khe->qhe', soft_rows, v_rows, preferred_element_type=jnp....]
    reduce_sum x11 -> x0, other arithmetic: 3.49 us -> none  [the longest x6 2.6 us: pick_rows(): return jnp.sum(chosen, axis=1, dtype=source_rows.dtype)]
  transfers between devices with their start and end apart: 10 -> 10, of which waited for: 4 -> 3; matrix products, arithmetic and copies ran while one was open for 10% -> 1% of each run, Pallas kernels for 0% -> 12%
where the time goes in v3:
time: 40.6 us; the launch traced here: 40.4 us
  starting transfers between devices  14.7 us (36%)
  Pallas kernels  12.1 us (30%)
  waiting for transfers between devices  12.1 us (30%)
  between operations  0.78 us (2%)
  other arithmetic  0.62 us (2%)
    ppermute x10, starting transfers between devices, across(): return lax.ppermute(block, axis, route)  14.7 us
    pallas_call x5, Pallas kernels, call(): pl.pallas_call(kernel, out_shape=results, out_specs=[VMEM_SPEC] * len(res...  12.1 us
    ppermute x10, waiting for transfers between devices, across(): return lax.ppermute(block, axis, route)  12.1 us
  transfers between devices with their start and end apart: 10, of which 3 were waited for; matrix products, arithmetic and copies ran while one was open for 1% of the time, Pallas kernels for 12%

profile of v3, /device:TPU:0, one launch (start us, length us, event | category | flops | bytes accessed | tf_op | source)
XLA Modules:
  0.0 40.4 jit_solution(18024315580779120597)
XLA Ops:
  0.6 0.0 copy-start.3
  0.6 0.0 copy-start.2
  0.7 0.0 copy-start.5
  0.7 0.0 copy-start.1
  0.7 3.0 %pack.1 = bf16[96,640]{1,0:T(8,128)(2,1)} custom-call(s32[2,5]{1,0:T(2,128)} %offsets_ref.3, bf16[1,128,640]{2,1,0:T(8,128)(2,1)} %refs_1_.3, bf16[1,128,640]{2,1,0:T(8,128)(2,1)} %refs_2_.3), custom_call_target="tpu_custom_call" | custom-call | flops 1000000000 | bytes 1000000 | tf_op jit(solution)/shard_map/pack/pallas_call | solution.py:483
  3.7 0.0 copy-start.4
  3.8 5.1 %collective-permute-start.2 = (bf16[96,640]{1,0:T(8,128)(2,1)}, bf16[96,640]{1,0:T(8,128)(2,1)S(1)}, u32[]{:S(2)}, u32[]{:S(2)}) collective-permute-start(bf16[96,640]{1,0:T(8,128)(2,1)} %pack.1), channel_id=1, source_target_pairs={{0,12},{4,8},{8,4},{12,0},{1,13},{5,9},{9,5},{13,1},{2,14},{6,10},... | collective-permute-start | bytes 368648 | tf_op jit(solution)/shard_map/ppermute | solution.py:466
  8.9 0.0 collective-permute-start.1
  8.9 0.6 %collective-permute-start = (bf16[96,640]{1,0:T(8,128)(2,1)}, bf16[96,640]{1,0:T(8,128)(2,1)S(1)}, u32[]{:S(2)}, u32[]{:S(2)}) collective-permute-start(bf16[96,640]{1,0:T(8,128)(2,1)} %pack.1), channel_id=1, source_target_pairs={{0,4},{4,0},{8,12},{12,8},{1,5},{5,1},{9,13},{13,9},{2,6},{6,2},{1... | collective-permute-start | bytes 368648 | tf_op jit(solution)/shard_map/ppermute | solution.py:466
  9.5 0.0 copy-done.5
  9.6 2.6 %base.1 = (bf16[128,640]{1,0:T(8,128)(2,1)S(1)}, f32[128,640]{1,0:T(8,128)S(1)}, f32[128,640]{1,0:T(8,128)S(1)}, bf16[128,640]{1,0:T(8,128)(2,1)S(1)}, f32[1,640...) custom-call(s32[2,5]{1,0:T(2,128)S(1)} %copy-done.4, bf16[1,128,640]{2,1,0:T(8,128)(2,1)S(1)} %copy-done.1, ...), custom_call_target="tpu_custom_call" | custom-call | flops 2000000000 | bytes 1000000 | tf_op jit(solution)/shard_map/base/pallas_call | solution.py:483
  12.2 1.2 %collective-permute-done.2.refs_2_.refs_11_ = bf16[96,640]{1,0:T(8,128)(2,1)S(1)} collective-permute-done((bf16[96,640]{1,0:T(8,128)(2,1)}, bf16[96,640]{1,0:T(8,128)(2,1)S(1)}, u32[]{:S(2)}, u32[]{:S(2)}) %collective-permute-start.2) | collective-permute-done | bytes 122912 | tf_op jit(solution)/shard_map/ppermute | solution.py:466
  13.3 6.1 %collective-permute-done.1.refs_1_.refs_10_ = bf16[96,640]{1,0:T(8,128)(2,1)S(1)} collective-permute-done((bf16[96,640]{1,0:T(8,128)(2,1)}, bf16[96,640]{1,0:T(8,128)(2,1)S(1)}, u32[]{:S(2)}, u32[]{:S(2)}) %collective-permute-start.1) | collective-permute-done | bytes 122912 | tf_op jit(solution)/shard_map/ppermute | solution.py:466
  19.4 0.0 collective-permute-done.refs_0_.refs_9_
  19.5 3.2 %attend.1 = (f32[1,640]{1,0:T(1,128)S(1)}, f32[128,640]{1,0:T(8,128)S(1)}, bf16[128,640]{1,0:T(8,128)(2,1)S(1)}, bf16[144,640]{1,0:T(8,128)(2,1)S(1)}, f32[16,12...) custom-call(bf16[128,640]{1,0:T(8,128)(2,1)S(1)} %get-tuple-element.27.q_, ...), custom_call_target="tpu_custom_call" | custom-call | flops 5000000000 | bytes 1000000 | tf_op jit(solution)/shard_map/attend/pallas_call | solution.py:483
  22.6 0.1 collective-permute-start.6
  22.7 0.1 collective-permute-start.3
  22.8 3.0 %collective-permute-start.4 = (bf16[96,640]{1,0:T(8,128)(2,1)S(1)}, bf16[96,640]{1,0:T(8,128)(2,1)S(1)}, u32[]{:S(2)}, u32[]{:S(2)}) collective-permute-start(bf16[96,640]{1,0:T(8,128)(2,1)S(1)} %get-tuple-element.42), channel_id=1, source_target_pairs={{0,8},{4,12},{8,0},{12,4},{1,9},{5,13},{9,1},{13,5},{2,10},{6,14},... | collective-permute-start | bytes 368648 | tf_op jit(solution)/shard_map/ppermute | solution.py:466
  25.8 0.0 collective-permute-done.6
  25.8 1.3 %collective-permute-start.9 = (f32[640]{0:T(1024)S(1)}, f32[640]{0:T(1024)S(1)}, u32[]{:S(2)}, u32[]{:S(2)}) collective-permute-start(f32[640]{0:T(1024)S(1)} %add.12), channel_id=1, source_target_pairs={{0,12},{4,8},{8,4},{12,0},{1,13},{5,9},{9,5},{13,1},{2,14},{6,10},... | collective-permute-start | bytes 7688 | tf_op jit(solution)/shard_map/ppermute | solution.py:466
  27.2 0.2 collective-permute-start.8
  27.4 2.8 %collective-permute-start.7 = (f32[640]{0:T(1024)S(1)}, f32[640]{0:T(1024)S(1)}, u32[]{:S(2)}, u32[]{:S(2)}) collective-permute-start(f32[640]{0:T(1024)S(1)} %add.12), channel_id=1, source_target_pairs={{0,4},{4,0},{8,12},{12,8},{1,5},{5,1},{9,13},{13,9},{2,6},{6,2},{1... | collective-permute-start | bytes 7688 | tf_op jit(solution)/shard_map/ppermute | solution.py:466
  30.2 2.4 %local_grad.1 = (bf16[1,128,640]{2,1,0:T(8,128)(2,1)}, bf16[1,128,640]{2,1,0:T(8,128)(2,1)}, f32[128,640]{1,0:T(8,128)S(1)}, f32[128,640]{1,0:T(8,128)S(1)}) custom-call(bf16[1,128,640]{2,1,0:T(8,128)(2,1)S(1)} %copy-done.1, bf16[1,128,640]{2,1,0:T(8,128)(2,1)S(1)} %copy-done.2, bf16[1,128,640]{2,1,0:T(8,128)(2,1)S(1)} %copy-done.3, ...), custom_call_target="tpu_custom_call" | custom-call | flops 3000000000 | bytes 1000000 | tf_op jit(solution)/shard_map/local_grad/pallas_call | solution.py:483
  32.6 0.0 collective-permute-done.9
  32.6 1.4 %collective-permute-start.5 = (bf16[96,640]{1,0:T(8,128)(2,1)S(1)}, bf16[96,640]{1,0:T(8,128)(2,1)S(1)}, u32[]{:S(2)}, u32[]{:S(2)}) collective-permute-start(bf16[96,640]{1,0:T(8,128)(2,1)S(1)} %get-tuple-element.43), channel_id=1, source_target_pairs={{0,12},{4,8},{8,4},{12,0},{1,13},{5,9},{9,5},{13,1},{2,14},{6,10},... | collective-permute-start | bytes 368648 | tf_op jit(solution)/shard_map/ppermute | solution.py:466
  34.0 0.0 collective-permute-done.8
  34.0 0.0 collective-permute-done.7
  34.0 0.6 %add_add_fusion = f32[640]{0:T(1024)} fusion(f32[640]{0:T(1024)S(1)} %collective-permute-done.8, f32[640]{0:T(1024)S(1)} %collective-permute-done.9, f32[640]{0:T(1024)S(1)} %add.12, f32[640]{0:T(1024)S(1)} %collective-permute-done.7), kind=kLoop, calls=%fused_computation | loop fusion | flops 1920 | bytes 12800 | tf_op jit(solution)/shard_map/add | solution.py:563
  34.6 0.0 collective-permute-done.3.refs_0_
  34.6 0.0 collective-permute-done.4.refs_1_
  34.6 4.8 %collective-permute-done.5.refs_2_ = bf16[96,640]{1,0:T(8,128)(2,1)S(1)} collective-permute-done((bf16[96,640]{1,0:T(8,128)(2,1)S(1)}, bf16[96,640]{1,0:T(8,128)(2,1)S(1)}, u32[]{:S(2)}, u32[]{:S(2)}) %collective-permute-start.5) | collective-permute-done | bytes 122912 | tf_op jit(solution)/shard_map/ppermute | solution.py:466
  39.5 1.0 %finish.1 = (bf16[1,128,640]{2,1,0:T(8,128)(2,1)}, bf16[1,128,640]{2,1,0:T(8,128)(2,1)}) custom-call(bf16[128,640]{1,0:T(8,128)(2,1)S(1)} %get-tuple-element.38.place_ref, f32[128,640]{1,0:T(8,128)S(1)} %get-tuple-element.39.dk_ref, f32[128,640]{1,0:T(8,128)S(1)} %get-tuple-element.40.dv_ref, bf16[96,640]{1,0:T(8,128)(2,1)S(1)} %collective-permute-done.3.refs_0_, ...), custom_call_target="tpu_custom_call" | custom-call | flops 2000000000 | bytes 1000000 | tf_op jit(solution)/shard_map/finish/pallas_call | solution.py:483
  (9 shorter events, 0.0 us)
Async XLA Ops:
  0.6 8.9 %copy-start.3 = (bf16[1,128,640]{2,1,0:T(8,128)(2,1)S(1)}, bf16[1,128,640]{2,1,0:T(8,128)(2,1)}, u32[]{:S(2)}) copy-start(bf16[1,128,640]{2,1,0:T(8,128)(2,1)} %refs_2_.3) | copy-start | bytes 491524
  0.6 8.9 %copy-start.2 = (bf16[1,128,640]{2,1,0:T(8,128)(2,1)S(1)}, bf16[1,128,640]{2,1,0:T(8,128)(2,1)}, u32[]{:S(2)}) copy-start(bf16[1,128,640]{2,1,0:T(8,128)(2,1)} %refs_1_.3) | copy-start | bytes 491524
  0.7 8.9 %copy-start.5 = (f32[640]{0:T(1024)S(1)}, f32[640]{0:T(1024)}, u32[]{:S(2)}) copy-start(f32[640]{0:T(1024)} %param.10) | copy-start | bytes 7684
  0.7 8.9 %copy-start.1 = (bf16[1,128,640]{2,1,0:T(8,128)(2,1)S(1)}, bf16[1,128,640]{2,1,0:T(8,128)(2,1)}, u32[]{:S(2)}) copy-start(bf16[1,128,640]{2,1,0:T(8,128)(2,1)} %refs_0_.3) | copy-start | bytes 491524
  0.7 8.9 %copy-start = (bf16[1,128,640]{2,1,0:T(8,128)(2,1)S(1)}, bf16[1,128,640]{2,1,0:T(8,128)(2,1)}, u32[]{:S(2)}) copy-start(bf16[1,128,640]{2,1,0:T(8,128)(2,1)} %refs_3_.1) | copy-start | bytes 491524
  3.7 5.8 %copy-start.4 = (s32[2,5]{1,0:T(2,128)S(1)}, s32[2,5]{1,0:T(2,128)}, u32[]{:S(2)}) copy-start(s32[2,5]{1,0:T(2,128)} %offsets_ref.3) | copy-start | bytes 124
  3.8 9.6 %collective-permute-start.2 = (bf16[96,640]{1,0:T(8,128)(2,1)}, bf16[96,640]{1,0:T(8,128)(2,1)S(1)}, u32[]{:S(2)}, u32[]{:S(2)}) collective-permute-start(bf16[96,640]{1,0:T(8,128)(2,1)} %pack.1), channel_id=1, source_target_pairs={{0,12},{4,8},{8,4},{12,0},{1,13},{5,9},{9,5},{13,1},{2,14},{6,10},... | collective-permute-start | bytes 368648 | tf_op jit(solution)/shard_map/ppermute | solution.py:466
  8.9 10.6 %collective-permute-start.1 = (bf16[96,640]{1,0:T(8,128)(2,1)}, bf16[96,640]{1,0:T(8,128)(2,1)S(1)}, u32[]{:S(2)}, u32[]{:S(2)}) collective-permute-start(bf16[96,640]{1,0:T(8,128)(2,1)} %pack.1), channel_id=1, source_target_pairs={{0,8},{4,12},{8,0},{12,4},{1,9},{5,13},{9,1},{13,5},{2,10},{6,14},... | collective-permute-start | bytes 368648 | tf_op jit(solution)/shard_map/ppermute | solution.py:466
  8.9 10.6 %collective-permute-start = (bf16[96,640]{1,0:T(8,128)(2,1)}, bf16[96,640]{1,0:T(8,128)(2,1)S(1)}, u32[]{:S(2)}, u32[]{:S(2)}) collective-permute-start(bf16[96,640]{1,0:T(8,128)(2,1)} %pack.1), channel_id=1, source_target_pairs={{0,4},{4,0},{8,12},{12,8},{1,5},{5,1},{9,13},{13,9},{2,6},{6,2},{1... | collective-permute-start | bytes 368648 | tf_op jit(solution)/shard_map/ppermute | solution.py:466
  22.6 3.2 %collective-permute-start.6 = (f32[640]{0:T(1024)S(1)}, f32[640]{0:T(1024)S(1)}, u32[]{:S(2)}, u32[]{:S(2)}) collective-permute-start(f32[640]{0:T(1024)S(1)} %reduce), channel_id=1, source_target_pairs={{0,16},{16,0},{1,17},{17,1},{2,18},{18,2},{3,19},{19,3},{4,20},{20... | collective-permute-start | bytes 7688 | tf_op jit(solution)/shard_map/ppermute | solution.py:466
  22.7 11.9 %collective-permute-start.3 = (bf16[96,640]{1,0:T(8,128)(2,1)S(1)}, bf16[96,640]{1,0:T(8,128)(2,1)S(1)}, u32[]{:S(2)}, u32[]{:S(2)}) collective-permute-start(bf16[96,640]{1,0:T(8,128)(2,1)S(1)} %get-tuple-element.41), channel_id=1, source_target_pairs={{0,4},{4,0},{8,12},{12,8},{1,5},{5,1},{9,13},{13,9},{2,6},{6,2},{1... | collective-permute-start | bytes 368648 | tf_op jit(solution)/shard_map/ppermute | solution.py:466
  22.8 11.8 %collective-permute-start.4 = (bf16[96,640]{1,0:T(8,128)(2,1)S(1)}, bf16[96,640]{1,0:T(8,128)(2,1)S(1)}, u32[]{:S(2)}, u32[]{:S(2)}) collective-permute-start(bf16[96,640]{1,0:T(8,128)(2,1)S(1)} %get-tuple-element.42), channel_id=1, source_target_pairs={{0,8},{4,12},{8,0},{12,4},{1,9},{5,13},{9,1},{13,5},{2,10},{6,14},... | collective-permute-start | bytes 368648 | tf_op jit(solution)/shard_map/ppermute | solution.py:466
  25.8 6.8 %collective-permute-start.9 = (f32[640]{0:T(1024)S(1)}, f32[640]{0:T(1024)S(1)}, u32[]{:S(2)}, u32[]{:S(2)}) collective-permute-start(f32[640]{0:T(1024)S(1)} %add.12), channel_id=1, source_target_pairs={{0,12},{4,8},{8,4},{12,0},{1,13},{5,9},{9,5},{13,1},{2,14},{6,10},... | collective-permute-start | bytes 7688 | tf_op jit(solution)/shard_map/ppermute | solution.py:466
  27.2 6.8 %collective-permute-start.8 = (f32[640]{0:T(1024)S(1)}, f32[640]{0:T(1024)S(1)}, u32[]{:S(2)}, u32[]{:S(2)}) collective-permute-start(f32[640]{0:T(1024)S(1)} %add.12), channel_id=1, source_target_pairs={{0,8},{4,12},{8,0},{12,4},{1,9},{5,13},{9,1},{13,5},{2,10},{6,14},... | collective-permute-start | bytes 7688 | tf_op jit(solution)/shard_map/ppermute | solution.py:466
  27.4 6.7 %collective-permute-start.7 = (f32[640]{0:T(1024)S(1)}, f32[640]{0:T(1024)S(1)}, u32[]{:S(2)}, u32[]{:S(2)}) collective-permute-start(f32[640]{0:T(1024)S(1)} %add.12), channel_id=1, source_target_pairs={{0,4},{4,0},{8,12},{12,8},{1,5},{5,1},{9,13},{13,9},{2,6},{6,2},{1... | collective-permute-start | bytes 7688 | tf_op jit(solution)/shard_map/ppermute | solution.py:466
  32.6 6.8 %collective-permute-start.5 = (bf16[96,640]{1,0:T(8,128)(2,1)S(1)}, bf16[96,640]{1,0:T(8,128)(2,1)S(1)}, u32[]{:S(2)}, u32[]{:S(2)}) collective-permute-start(bf16[96,640]{1,0:T(8,128)(2,1)S(1)} %get-tuple-element.43), channel_id=1, source_target_pairs={{0,12},{4,8},{8,4},{12,0},{1,13},{5,9},{9,5},{13,1},{2,14},{6,10},... | collective-permute-start | bytes 368648 | tf_op jit(solution)/shard_map/ppermute | solution.py:466

commit v4 on v3

--- a/solution.py
+++ b/solution.py
@@ -228,6 +228,7 @@
 LOW = jnp.bfloat16
 WIDE = jnp.float32
 HEAD_GROUPS = ((0, 5),)
+PACK_VMEM = 65408 * 1024
 
 
 def contract(left, right, left_dim, right_dim):
@@ -410,15 +411,15 @@
             part_ref[picked:, own] = dv_peers[place * picked : (place + 1) * picked]
 
 
-def local_grad_kernel(top_step, groups, *refs):
-    sources, expo_ref, refs = refs[:4], refs[4], refs[5:]
-    held, sems = refs[-5:-1], refs[-1]
+def query_grad_kernel(top_step, groups, *refs):
+    sources, expo_ref, refs = refs[:3], refs[3], refs[4:]
+    held, sems = refs[-4:-1], refs[-1]
     per_group = 4 + PEERS
     group_refs = refs[: per_group * len(groups)]
-    attended_ref, dq_ref, dk_ref, dv_ref = refs[per_group * len(groups) : -5]
+    attended_ref, dq_ref, score_grad_ref, soft_ref = refs[per_group * len(groups) : -4]
     fetch(sources, held, sems)
-    q_ref, k_ref, v_ref, gain_ref = held
-    picked = sum(picked_counts(q_ref.shape[0], top_step))
+    k_ref, v_ref, gain_ref = held
+    picked = sum(picked_counts(k_ref.shape[0], top_step))
     score_scale = 1.0 / math.sqrt(HEAD_DIM)
     for place, (first, last) in enumerate(groups):
         normed_ref, grad_low_ref, peer_score_grad_ref, stats_ref, *packed_refs = group_refs[
@@ -427,22 +428,30 @@
         for head in range(first, last):
             cols = head_cols(head)
             own = head_cols(head - first)
-            normed = normed_ref[:, own].T
-            attended_ref[0, :, cols] = (normed * gain_ref[:, cols]).astype(LOW)
-            k_rows = k_ref[:, cols]
+            attended_ref[0, :, cols] = (normed_ref[:, own].T * gain_ref[:, cols]).astype(LOW)
             k_peers = stacked(packed_refs, pl.ds(0, picked), own)
-            grad_low = grad_low_ref[:, own]
             base_factor = stats_ref[head - first : head - first + 1, :]
             inner = stats_ref[STATS_ROWS + head - first : STATS_ROWS + head - first + 1, :]
             soft = expo_ref[:, cols].astype(WIDE) * base_factor
-            prob_grad = contract(v_ref[:, cols], grad_low, 1, 0)
+            prob_grad = contract(v_ref[:, cols], grad_low_ref[:, own], 1, 0)
             score_grad = (soft * (prob_grad - inner) * score_scale).astype(LOW)
-            dk_ref[:, cols] = contract(score_grad, q_ref[:, cols], 1, 0)
-            dv_ref[:, cols] = contract(soft.astype(LOW), grad_low, 1, 1)
+            score_grad_ref[:, cols] = score_grad
+            soft_ref[:, cols] = soft.astype(LOW)
             dq_ref[0, :, cols] = (
-                contract(score_grad, k_rows, 0, 0)
+                contract(score_grad, k_ref[:, cols], 0, 0)
                 + contract(peer_score_grad_ref[:, own], k_peers, 0, 0)
             ).astype(LOW)
+
+
+def key_grad_kernel(groups, q_ref, score_grad_ref, soft_ref, *refs):
+    grad_low_refs, (dk_ref, dv_ref) = refs[: len(groups)], refs[len(groups) :]
+    for (first, last), grad_low_ref in zip(groups, grad_low_refs):
+        for head in range(first, last):
+            cols = head_cols(head)
+            dk_ref[:, cols] = contract(score_grad_ref[:, cols], q_ref[:, cols], 1, 0)
+            dv_ref[:, cols] = contract(
+                soft_ref[:, cols], grad_low_ref[:, head_cols(head - first)], 1, 1
+            )
 
 
 def finish_kernel(top_step, groups, place_ref, dk_ref, dv_ref, *refs):
@@ -512,7 +521,7 @@
         [shape((2 * picked, group_width), LOW) for group_width in widths],
         1,
         in_specs=[SMEM_SPEC, HBM_SPEC, HBM_SPEC],
-        compiler_params=None,
+        compiler_params=pltpu.CompilerParams(vmem_limit_bytes=PACK_VMEM),
         scratch_shapes=[
             pltpu.VMEM((tokens, width), LOW),
             pltpu.VMEM((tokens, width), LOW),
@@ -538,7 +547,7 @@
         in_specs=[SMEM_SPEC] + [HBM_SPEC] * 5,
         scratch_shapes=[row_scratch] * 4 + [gain_scratch, pltpu.SemaphoreType.DMA((5,))],
     )
-    kept, returned, gain_parts = [], [], []
+    kept, returned, gain_parts, grad_lows = [], [], [], []
     for (first, last), group_width, peers in zip(groups, widths, packed_peers):
         gain_part, normed, grad_low, score_grad, stats, *parts = call(
             bind(attend_kernel, top_step, first, last),
@@ -555,20 +564,28 @@
             last - first,
         )
         gain_parts.append(gain_part.reshape(group_width))
+        grad_lows.append(grad_low)
         kept += [normed, grad_low, score_grad, stats, *peers]
         returned += to_peers(parts)
     gain_part = jnp.concatenate(gain_parts) if len(groups) > 1 else gain_parts[0]
-    gain_pair = gain_part + across(gain_part, "dp", 1)
-    gain_peers = to_peers([gain_pair] * PEERS)
-    gain_grad = (gain_pair + gain_peers[0]) + (gain_peers[1] + gain_peers[2])
-    attended, query_grad, dk_base, dv_base = call(
-        bind(local_grad_kernel, top_step, groups),
-        "local_grad",
-        (queries, keys, values, gain_row, expo, *kept),
-        [row_block, row_block, wide_block, wide_block],
-        3,
-        in_specs=[HBM_SPEC] * 4 + [VMEM_SPEC] * (1 + len(kept)),
-        scratch_shapes=[row_scratch] * 3 + [gain_scratch, pltpu.SemaphoreType.DMA((4,))],
+    gain_grad = gain_part + across(gain_part, "dp", 1)
+    for distance in (1, 2):
+        gain_grad = gain_grad + across(gain_grad, "ctx", distance)
+    attended, query_grad, score_grad, soft = call(
+        bind(query_grad_kernel, top_step, groups),
+        "query_grad",
+        (keys, values, gain_row, expo, *kept),
+        [row_block, row_block, low_block, low_block],
+        20,
+        in_specs=[HBM_SPEC] * 3 + [VMEM_SPEC] * (1 + len(kept)),
+        scratch_shapes=[row_scratch] * 2 + [gain_scratch, pltpu.SemaphoreType.DMA((3,))],
+    )
+    dk_base, dv_base = call(
+        bind(key_grad_kernel, groups),
+        "key_grad",
+        (q_copy, score_grad, soft, *grad_lows),
+        [wide_block, wide_block],
+        20,
     )
     key_grad, value_grad = call(
         bind(finish_kernel, top_step, groups),

time: 40.6 us -> 39.4 us (0.970)
  waiting for transfers between devices: 12.1 us -> 7.91 us
  local copies, waits for them, and re-layouts: 0.03 us -> 3.68 us
  starting transfers between devices: 14.7 us -> 13.8 us
    ppermute x10 -> x9, waiting for transfers between devices: 12.1 us -> 7.91 us  [across(): return lax.ppermute(block, axis, route)]
    unnamed x12 -> x16, local copies, waits for them, and re-layouts: 0.03 us -> 3.67 us
    ppermute x10 -> x9, starting transfers between devices: 14.7 us -> 13.8 us  [across(): return lax.ppermute(block, axis, route)]
    pallas_call x5 -> x6, Pallas kernels: 12.1 us -> 12.3 us  [call(): pl.pallas_call(kernel, out_shape=results, out_specs=[VMEM_SPEC] * len(res...]
  transfers between devices with their start and end apart: 10 -> 9, of which waited for: 3 -> 3; matrix products, arithmetic and copies ran while one was open for 1% -> 2% of each run, Pallas kernels for 12% -> 13%
where the time goes in v4:
time: 39.4 us; the launch traced here: 39.1 us
  starting transfers between devices  13.8 us (35%)
  Pallas kernels  12.3 us (31%)
  waiting for transfers between devices  7.91 us (20%)
  local copies, waits for them, and re-layouts  3.68 us (9%)
  between operations  0.76 us (2%)
  other arithmetic  0.62 us (2%)
    ppermute x9, starting transfers between devices, across(): return lax.ppermute(block, axis, route)  13.8 us
    pallas_call x6, Pallas kernels, call(): pl.pallas_call(kernel, out_shape=results, out_specs=[VMEM_SPEC] * len(res...  12.3 us
    ppermute x9, waiting for transfers between devices, across(): return lax.ppermute(block, axis, route)  7.91 us
    unnamed x16, local copies, waits for them, and re-layouts  3.67 us
  transfers between devices with their start and end apart: 9, of which 3 were waited for; matrix products, arithmetic and copies ran while one was open for 2% of the time, Pallas kernels for 13%

profile of v4, /device:TPU:0, one launch (start us, length us, event | category | flops | bytes accessed | tf_op | source)
XLA Modules:
  0.0 39.1 jit_solution(10618714526109321836)
XLA Ops:
  0.6 3.0 %pack.1 = bf16[96,640]{1,0:T(8,128)(2,1)} custom-call(s32[2,5]{1,0:T(2,128)} %offsets_ref.3, bf16[1,128,640]{2,1,0:T(8,128)(2,1)} %refs_0_.3, bf16[1,128,640]{2,1,0:T(8,128)(2,1)} %refs_1_.3), custom_call_target="tpu_custom_call" | custom-call | flops 1000000000 | bytes 1000000 | tf_op jit(solution)/shard_map/pack/pallas_call | solution.py:492
  3.7 0.0 copy-start.6
  3.7 5.1 %collective-permute-start.2 = (bf16[96,640]{1,0:T(8,128)(2,1)}, bf16[96,640]{1,0:T(8,128)(2,1)S(1)}, u32[]{:S(2)}, u32[]{:S(2)}) collective-permute-start(bf16[96,640]{1,0:T(8,128)(2,1)} %pack.1), channel_id=1, source_target_pairs={{0,12},{4,8},{8,4},{12,0},{1,13},{5,9},{9,5},{13,1},{2,14},{6,10},... | collective-permute-start | bytes 368648 | tf_op jit(solution)/shard_map/ppermute | solution.py:475
  8.8 0.0 collective-permute-start.1
  8.8 0.6 %collective-permute-start = (bf16[96,640]{1,0:T(8,128)(2,1)}, bf16[96,640]{1,0:T(8,128)(2,1)S(1)}, u32[]{:S(2)}, u32[]{:S(2)}) collective-permute-start(bf16[96,640]{1,0:T(8,128)(2,1)} %pack.1), channel_id=1, source_target_pairs={{0,4},{4,0},{8,12},{12,8},{1,5},{5,1},{9,13},{13,9},{2,6},{6,2},{1... | collective-permute-start | bytes 368648 | tf_op jit(solution)/shard_map/ppermute | solution.py:475
  9.5 0.0 copy-done.7
  9.5 0.0 copy-start
  9.5 0.9 %copy-done = bf16[1,128,640]{2,1,0:T(8,128)(2,1)S(1)} copy-done((bf16[1,128,640]{2,1,0:T(8,128)(2,1)S(1)}, bf16[1,128,640]{2,1,0:T(8,128)(2,1)}, u32[]{:S(2)}) %copy-start) | copy-done | bytes 163864
  10.4 0.9 %copy-done.1 = bf16[1,128,640]{2,1,0:T(8,128)(2,1)S(1)} copy-done((bf16[1,128,640]{2,1,0:T(8,128)(2,1)S(1)}, bf16[1,128,640]{2,1,0:T(8,128)(2,1)}, u32[]{:S(2)}) %copy-start.1) | copy-done | bytes 163864
  11.3 0.9 %copy-done.2 = bf16[1,128,640]{2,1,0:T(8,128)(2,1)S(1)} copy-done((bf16[1,128,640]{2,1,0:T(8,128)(2,1)S(1)}, bf16[1,128,640]{2,1,0:T(8,128)(2,1)}, u32[]{:S(2)}) %copy-start.2) | copy-done | bytes 163864
  12.2 0.9 %copy-done.4 = bf16[1,128,640]{2,1,0:T(8,128)(2,1)S(1)} copy-done((bf16[1,128,640]{2,1,0:T(8,128)(2,1)S(1)}, bf16[1,128,640]{2,1,0:T(8,128)(2,1)}, u32[]{:S(2)}) %copy-start.4) | copy-done | bytes 163864
  13.1 2.6 %base.1 = (bf16[128,640]{1,0:T(8,128)(2,1)S(1)}, f32[128,640]{1,0:T(8,128)S(1)}, f32[128,640]{1,0:T(8,128)S(1)}, bf16[128,640]{1,0:T(8,128)(2,1)S(1)}, f32[1,640...) custom-call(s32[2,5]{1,0:T(2,128)S(1)} %copy-done.6, bf16[1,128,640]{2,1,0:T(8,128)(2,1)S(1)} %copy-done, ...), custom_call_target="tpu_custom_call" | custom-call | flops 2000000000 | bytes 1000000 | tf_op jit(solution)/shard_map/base/pallas_call | solution.py:492
  15.8 0.0 collective-permute-done.2.refs_2_.refs_10_
  15.8 3.6 %collective-permute-done.1.refs_1_.refs_9_ = bf16[96,640]{1,0:T(8,128)(2,1)S(1)} collective-permute-done((bf16[96,640]{1,0:T(8,128)(2,1)}, bf16[96,640]{1,0:T(8,128)(2,1)S(1)}, u32[]{:S(2)}, u32[]{:S(2)}) %collective-permute-start.1) | collective-permute-done | bytes 122912 | tf_op jit(solution)/shard_map/ppermute | solution.py:475
  19.4 0.0 collective-permute-done.refs_0_.refs_8_
  19.4 3.2 %attend.1 = (f32[1,640]{1,0:T(1,128)S(1)}, f32[128,640]{1,0:T(8,128)S(1)}, bf16[128,640]{1,0:T(8,128)(2,1)S(1)}, bf16[144,640]{1,0:T(8,128)(2,1)S(1)}, f32[16,12...) custom-call(bf16[128,640]{1,0:T(8,128)(2,1)S(1)} %get-tuple-element.29.q_, ...), custom_call_target="tpu_custom_call" | custom-call | flops 5000000000 | bytes 1000000 | tf_op jit(solution)/shard_map/attend/pallas_call | solution.py:492
  22.6 0.1 collective-permute-start.6
  22.7 0.1 collective-permute-start.3
  22.8 3.0 %collective-permute-start.4 = (bf16[96,640]{1,0:T(8,128)(2,1)S(1)}, bf16[96,640]{1,0:T(8,128)(2,1)S(1)}, u32[]{:S(2)}, u32[]{:S(2)}) collective-permute-start(bf16[96,640]{1,0:T(8,128)(2,1)S(1)} %get-tuple-element.46), channel_id=1, source_target_pairs={{0,8},{4,12},{8,0},{12,4},{1,9},{5,13},{9,1},{13,5},{2,10},{6,14},... | collective-permute-start | bytes 368648 | tf_op jit(solution)/shard_map/ppermute | solution.py:475
  25.8 1.4 %collective-permute-start.5 = (bf16[96,640]{1,0:T(8,128)(2,1)S(1)}, bf16[96,640]{1,0:T(8,128)(2,1)S(1)}, u32[]{:S(2)}, u32[]{:S(2)}) collective-permute-start(bf16[96,640]{1,0:T(8,128)(2,1)S(1)} %get-tuple-element.47), channel_id=1, source_target_pairs={{0,12},{4,8},{8,4},{12,0},{1,13},{5,9},{9,5},{13,1},{2,14},{6,10},... | collective-permute-start | bytes 368648 | tf_op jit(solution)/shard_map/ppermute | solution.py:475
  27.1 0.0 collective-permute-done.6
  27.1 0.0 collective-permute-start.7
  27.2 2.3 %query_grad.1 = (bf16[1,128,640]{2,1,0:T(8,128)(2,1)}, bf16[1,128,640]{2,1,0:T(8,128)(2,1)}, bf16[128,640]{1,0:T(8,128)(2,1)S(1)}, bf16[128,640]{1,0:T(8,128)(2,1)S(1)}) custom-call(bf16[1,128,640]{2,1,0:T(8,128)(2,1)S(1)} %copy-done.3, bf16[1,128,640]{2,1,0:T(8,128)(2,1)S(1)} %copy-done.5, f32[1,640]{1,0:T(1,128)S(1)} %reshape.16.refs_4_.refs_2_, ...), custom_call_target="tpu_custom_call" | custom-call | flops 20000000000 | bytes 1000000 | tf_op jit(solution)/shard_map/query_grad/pallas_call | solution.py:492
  29.5 2.1 %collective-permute-done.7 = f32[640]{0:T(1024)S(1)} collective-permute-done((f32[640]{0:T(1024)S(1)}, f32[640]{0:T(1024)S(1)}, u32[]{:S(2)}, u32[]{:S(2)}) %collective-permute-start.7) | collective-permute-done | bytes 2592 | tf_op jit(solution)/shard_map/ppermute | solution.py:475
  31.6 3.5 %collective-permute-start.8 = (f32[640]{0:T(1024)S(1)}, f32[640]{0:T(1024)S(1)}, u32[]{:S(2)}, u32[]{:S(2)}) collective-permute-start(f32[640]{0:T(1024)S(1)} %add.10), channel_id=1, source_target_pairs={{0,8},{4,12},{8,0},{12,4},{1,9},{5,13},{9,1},{13,5},{2,10},{6,14},... | collective-permute-start | bytes 7688 | tf_op jit(solution)/shard_map/ppermute | solution.py:475
  35.1 0.3 key_grad.1
  35.4 2.1 %collective-permute-done.8 = f32[640]{0:T(1024)S(1)} collective-permute-done((f32[640]{0:T(1024)S(1)}, f32[640]{0:T(1024)S(1)}, u32[]{:S(2)}, u32[]{:S(2)}) %collective-permute-start.8) | collective-permute-done | bytes 2592 | tf_op jit(solution)/shard_map/ppermute | solution.py:475
  37.5 0.6 %add.11 = f32[640]{0:T(1024)} add(f32[640]{0:T(1024)S(1)} %add.10, f32[640]{0:T(1024)S(1)} %collective-permute-done.8) | non-fusion elementwise | flops 640 | bytes 7680 | tf_op jit(solution)/shard_map/add | solution.py:573
  38.1 0.0 collective-permute-done.3.refs_0_
  38.1 0.0 collective-permute-done.4.refs_1_
  38.1 0.0 collective-permute-done.5.refs_2_
  38.1 1.0 %finish.1 = (bf16[1,128,640]{2,1,0:T(8,128)(2,1)}, bf16[1,128,640]{2,1,0:T(8,128)(2,1)}) custom-call(bf16[128,640]{1,0:T(8,128)(2,1)S(1)} %get-tuple-element.40.place_ref, f32[128,640]{1,0:T(8,128)S(1)} %get-tuple-element.43.dk_ref, f32[128,640]{1,0:T(8,128)S(1)} %get-tuple-element.44.dv_ref, bf16[96,640]{1,0:T(8,128)(2,1)S(1)} %collective-permute-done.3.refs_0_, ...), custom_call_target="tpu_custom_call" | custom-call | flops 2000000000 | bytes 1000000 | tf_op jit(solution)/shard_map/finish/pallas_call | solution.py:492
  (13 shorter events, 0.0 us)
Async XLA Ops:
  0.6 8.8 %copy-start.7 = (f32[640]{0:T(1024)S(1)}, f32[640]{0:T(1024)}, u32[]{:S(2)}) copy-start(f32[640]{0:T(1024)} %param.10) | copy-start | bytes 7684
  3.7 5.8 %copy-start.6 = (s32[2,5]{1,0:T(2,128)S(1)}, s32[2,5]{1,0:T(2,128)}, u32[]{:S(2)}) copy-start(s32[2,5]{1,0:T(2,128)} %offsets_ref.3) | copy-start | bytes 124
  3.7 12.1 %collective-permute-start.2 = (bf16[96,640]{1,0:T(8,128)(2,1)}, bf16[96,640]{1,0:T(8,128)(2,1)S(1)}, u32[]{:S(2)}, u32[]{:S(2)}) collective-permute-start(bf16[96,640]{1,0:T(8,128)(2,1)} %pack.1), channel_id=1, source_target_pairs={{0,12},{4,8},{8,4},{12,0},{1,13},{5,9},{9,5},{13,1},{2,14},{6,10},... | collective-permute-start | bytes 368648 | tf_op jit(solution)/shard_map/ppermute | solution.py:475
  8.8 10.6 %collective-permute-start.1 = (bf16[96,640]{1,0:T(8,128)(2,1)}, bf16[96,640]{1,0:T(8,128)(2,1)S(1)}, u32[]{:S(2)}, u32[]{:S(2)}) collective-permute-start(bf16[96,640]{1,0:T(8,128)(2,1)} %pack.1), channel_id=1, source_target_pairs={{0,8},{4,12},{8,0},{12,4},{1,9},{5,13},{9,1},{13,5},{2,10},{6,14},... | collective-permute-start | bytes 368648 | tf_op jit(solution)/shard_map/ppermute | solution.py:475
  8.8 10.6 %collective-permute-start = (bf16[96,640]{1,0:T(8,128)(2,1)}, bf16[96,640]{1,0:T(8,128)(2,1)S(1)}, u32[]{:S(2)}, u32[]{:S(2)}) collective-permute-start(bf16[96,640]{1,0:T(8,128)(2,1)} %pack.1), channel_id=1, source_target_pairs={{0,4},{4,0},{8,12},{12,8},{1,5},{5,1},{9,13},{13,9},{2,6},{6,2},{1... | collective-permute-start | bytes 368648 | tf_op jit(solution)/shard_map/ppermute | solution.py:475
  9.5 0.9 %copy-start = (bf16[1,128,640]{2,1,0:T(8,128)(2,1)S(1)}, bf16[1,128,640]{2,1,0:T(8,128)(2,1)}, u32[]{:S(2)}) copy-start(bf16[1,128,640]{2,1,0:T(8,128)(2,1)} %refs_0_.2) | copy-start | bytes 491524
  10.4 0.9 %copy-start.1 = (bf16[1,128,640]{2,1,0:T(8,128)(2,1)S(1)}, bf16[1,128,640]{2,1,0:T(8,128)(2,1)}, u32[]{:S(2)}) copy-start(bf16[1,128,640]{2,1,0:T(8,128)(2,1)} %refs_3_.1) | copy-start | bytes 491524
  11.3 0.9 %copy-start.2 = (bf16[1,128,640]{2,1,0:T(8,128)(2,1)S(1)}, bf16[1,128,640]{2,1,0:T(8,128)(2,1)}, u32[]{:S(2)}) copy-start(bf16[1,128,640]{2,1,0:T(8,128)(2,1)} %refs_0_.3) | copy-start | bytes 491524
  12.2 0.9 %copy-start.4 = (bf16[1,128,640]{2,1,0:T(8,128)(2,1)S(1)}, bf16[1,128,640]{2,1,0:T(8,128)(2,1)}, u32[]{:S(2)}) copy-start(bf16[1,128,640]{2,1,0:T(8,128)(2,1)} %refs_1_.3) | copy-start | bytes 491524
  19.4 7.7 %copy-start.3 = (bf16[1,128,640]{2,1,0:T(8,128)(2,1)S(1)}, bf16[1,128,640]{2,1,0:T(8,128)(2,1)}, u32[]{:S(2)}) copy-start(bf16[1,128,640]{2,1,0:T(8,128)(2,1)} %refs_0_.3) | copy-start | bytes 491524
  19.4 7.7 %copy-start.5 = (bf16[1,128,640]{2,1,0:T(8,128)(2,1)S(1)}, bf16[1,128,640]{2,1,0:T(8,128)(2,1)}, u32[]{:S(2)}) copy-start(bf16[1,128,640]{2,1,0:T(8,128)(2,1)} %refs_1_.3) | copy-start | bytes 491524
  22.6 4.5 %collective-permute-start.6 = (f32[640]{0:T(1024)S(1)}, f32[640]{0:T(1024)S(1)}, u32[]{:S(2)}, u32[]{:S(2)}) collective-permute-start(f32[640]{0:T(1024)S(1)} %reduce), channel_id=1, source_target_pairs={{0,16},{16,0},{1,17},{17,1},{2,18},{18,2},{3,19},{19,3},{4,20},{20... | collective-permute-start | bytes 7688 | tf_op jit(solution)/shard_map/ppermute | solution.py:475
  22.7 15.4 %collective-permute-start.3 = (bf16[96,640]{1,0:T(8,128)(2,1)S(1)}, bf16[96,640]{1,0:T(8,128)(2,1)S(1)}, u32[]{:S(2)}, u32[]{:S(2)}) collective-permute-start(bf16[96,640]{1,0:T(8,128)(2,1)S(1)} %get-tuple-element.45), channel_id=1, source_target_pairs={{0,4},{4,0},{8,12},{12,8},{1,5},{5,1},{9,13},{13,9},{2,6},{6,2},{1... | collective-permute-start | bytes 368648 | tf_op jit(solution)/shard_map/ppermute | solution.py:475
  22.8 15.4 %collective-permute-start.4 = (bf16[96,640]{1,0:T(8,128)(2,1)S(1)}, bf16[96,640]{1,0:T(8,128)(2,1)S(1)}, u32[]{:S(2)}, u32[]{:S(2)}) collective-permute-start(bf16[96,640]{1,0:T(8,128)(2,1)S(1)} %get-tuple-element.46), channel_id=1, source_target_pairs={{0,8},{4,12},{8,0},{12,4},{1,9},{5,13},{9,1},{13,5},{2,10},{6,14},... | collective-permute-start | bytes 368648 | tf_op jit(solution)/shard_map/ppermute | solution.py:475
  25.8 12.3 %collective-permute-start.5 = (bf16[96,640]{1,0:T(8,128)(2,1)S(1)}, bf16[96,640]{1,0:T(8,128)(2,1)S(1)}, u32[]{:S(2)}, u32[]{:S(2)}) collective-permute-start(bf16[96,640]{1,0:T(8,128)(2,1)S(1)} %get-tuple-element.47), channel_id=1, source_target_pairs={{0,12},{4,8},{8,4},{12,0},{1,13},{5,9},{9,5},{13,1},{2,14},{6,10},... | collective-permute-start | bytes 368648 | tf_op jit(solution)/shard_map/ppermute | solution.py:475
  27.1 4.5 %collective-permute-start.7 = (f32[640]{0:T(1024)S(1)}, f32[640]{0:T(1024)S(1)}, u32[]{:S(2)}, u32[]{:S(2)}) collective-permute-start(f32[640]{0:T(1024)S(1)} %add.9), channel_id=1, source_target_pairs={{0,4},{4,0},{8,12},{12,8},{1,5},{5,1},{9,13},{13,9},{2,6},{6,2},{1... | collective-permute-start | bytes 7688 | tf_op jit(solution)/shard_map/ppermute | solution.py:475
  31.6 5.9 %collective-permute-start.8 = (f32[640]{0:T(1024)S(1)}, f32[640]{0:T(1024)S(1)}, u32[]{:S(2)}, u32[]{:S(2)}) collective-permute-start(f32[640]{0:T(1024)S(1)} %add.10), channel_id=1, source_target_pairs={{0,8},{4,12},{8,0},{12,4},{1,9},{5,13},{9,1},{13,5},{2,10},{6,14},... | collective-permute-start | bytes 7688 | tf_op jit(solution)/shard_map/ppermute | solution.py:475

commit v5 on v4

--- a/solution.py
+++ b/solution.py
@@ -228,6 +228,7 @@
 LOW = jnp.bfloat16
 WIDE = jnp.float32
 HEAD_GROUPS = ((0, 5),)
+LOAD_PIECES = 4
 PACK_VMEM = 65408 * 1024
 
 
@@ -266,22 +267,24 @@
     packed_refs, (k_ref, v_ref, sems) = refs[: len(groups)], refs[len(groups) :]
     tokens, width = k_ref.shape
     picked = sum(picked_counts(tokens, top_step))
-    copies = []
-    for head in range(width // HEAD_DIM):
-        cols = head_cols(head)
-        pair = [
-            pltpu.make_async_copy(source.at[0, :, cols], held.at[:, cols], sems.at[which, head])
-            for which, (source, held) in enumerate(((k_hbm, k_ref), (v_hbm, v_ref)))
-        ]
-        for copy in pair:
-            copy.start()
-        copies.append(pair)
+    step = tokens // LOAD_PIECES
+    copies = [
+        pltpu.make_async_copy(
+            source.at[0, pl.ds(piece * step, step)],
+            held.at[pl.ds(piece * step, step)],
+            sems.at[which, piece],
+        )
+        for which, (source, held) in enumerate(((k_hbm, k_ref), (v_hbm, v_ref)))
+        for piece in range(LOAD_PIECES)
+    ]
+    for copy in copies:
+        copy.start()
+    for copy in copies:
+        copy.wait()
     for (first, last), packed_ref in zip(groups, packed_refs):
         for head in range(first, last):
             cols = head_cols(head)
             picks = pick_matrix(offsets_ref, head, tokens, top_step, 0)
-            for copy in copies[head]:
-                copy.wait()
             both = jnp.concatenate([k_ref[:, cols], v_ref[:, cols]], 1)
             rows = contract(picks, both, 1, 0).astype(LOW)
             packed_ref[:picked, head_cols(head - first)] = rows[:, :HEAD_DIM]
@@ -454,8 +457,9 @@
             )
 
 
-def finish_kernel(top_step, groups, place_ref, dk_ref, dv_ref, *refs):
-    dk_out_ref, dv_out_ref = refs[PEERS * len(groups) :]
+def finish_kernel(top_step, groups, gain_ref, place_ref, dk_ref, dv_ref, *refs):
+    dk_out_ref, dv_out_ref, gain_out_ref = refs[PEERS * len(groups) :]
+    gain_out_ref[...] = gain_ref[...]
     tokens = dk_ref.shape[0]
     picked = sum(picked_counts(tokens, top_step))
     for place, (first, last) in enumerate(groups):
@@ -494,7 +498,7 @@
         out_shape=results,
         out_specs=[VMEM_SPEC] * len(results),
         cost_estimate=pl.CostEstimate(
-            flops=microseconds * 10**9, bytes_accessed=10**6, transcendentals=0
+            flops=int(microseconds * 10**9), bytes_accessed=0, transcendentals=0
         ),
         name=name,
         **options,
@@ -525,7 +529,7 @@
         scratch_shapes=[
             pltpu.VMEM((tokens, width), LOW),
             pltpu.VMEM((tokens, width), LOW),
-            pltpu.SemaphoreType.DMA((2, heads)),
+            pltpu.SemaphoreType.DMA((2, LOAD_PIECES)),
         ],
     )
     packed_peers = [to_peers([block] * PEERS) for block in packed]
@@ -563,20 +567,20 @@
             + [shape((2 * picked, group_width), LOW)] * PEERS,
             last - first,
         )
-        gain_parts.append(gain_part.reshape(group_width))
+        gain_parts.append(gain_part)
         grad_lows.append(grad_low)
         kept += [normed, grad_low, score_grad, stats, *peers]
-        returned += to_peers(parts)
-    gain_part = jnp.concatenate(gain_parts) if len(groups) > 1 else gain_parts[0]
+        returned += to_peers(parts)[::-1]
+    gain_part = jnp.concatenate(gain_parts, 1) if len(groups) > 1 else gain_parts[0]
     gain_grad = gain_part + across(gain_part, "dp", 1)
-    for distance in (1, 2):
-        gain_grad = gain_grad + across(gain_grad, "ctx", distance)
+    gain_grad = gain_grad + across(gain_grad, "ctx", 1)
+    gain_rest = across(gain_grad, "ctx", 2)
     attended, query_grad, score_grad, soft = call(
         bind(query_grad_kernel, top_step, groups),
         "query_grad",
         (keys, values, gain_row, expo, *kept),
         [row_block, row_block, low_block, low_block],
-        20,
+        0.5,
         in_specs=[HBM_SPEC] * 3 + [VMEM_SPEC] * (1 + len(kept)),
         scratch_shapes=[row_scratch] * 2 + [gain_scratch, pltpu.SemaphoreType.DMA((3,))],
     )
@@ -585,15 +589,16 @@
         "key_grad",
         (q_copy, score_grad, soft, *grad_lows),
         [wide_block, wide_block],
-        20,
-    )
-    key_grad, value_grad = call(
+        0.5,
+    )
+    key_grad, value_grad, gain_grad = call(
         bind(finish_kernel, top_step, groups),
         "finish",
-        (place, dk_base, dv_base, *returned),
-        [row_block, row_block],
-        2,
-    )
+        (gain_grad, place, dk_base, dv_base, *returned),
+        [row_block, row_block, shape((1, width), WIDE)],
+        1,
+    )
+    gain_grad = (gain_grad + gain_rest).reshape(width)
     return attended, query_grad, key_grad, value_grad, gain_grad
 
 

time: 39.4 us -> 38.3 us (0.972)
  starting transfers between devices: 13.8 us -> 11.9 us
  waiting for transfers between devices: 7.91 us -> 9.15 us
  Pallas kernels: 12.3 us -> 11.9 us
    ppermute x9, starting transfers between devices: 13.8 us -> 11.9 us  [across(): return lax.ppermute(block, axis, route)]
    ppermute x9, waiting for transfers between devices: 7.91 us -> 9.15 us  [across(): return lax.ppermute(block, axis, route)]
    pallas_call x6, Pallas kernels: 12.3 us -> 11.9 us  [call(): pl.pallas_call(kernel, out_shape=results, out_specs=[VMEM_SPEC] * len(res...]
  transfers between devices with their start and end apart: 9 -> 9, of which waited for: 3 -> 4; matrix products, arithmetic and copies ran while one was open for 2% -> 0% of each run, Pallas kernels for 13% -> 16%
where the time goes in v5:
time: 38.3 us; the launch traced here: 38 us
  Pallas kernels  11.9 us (31%)
  starting transfers between devices  11.9 us (31%)
  waiting for transfers between devices  9.15 us (24%)
  local copies, waits for them, and re-layouts  3.68 us (10%)
  between operations  0.73 us (2%)
  other arithmetic  0.62 us (2%)
    pallas_call x6, Pallas kernels, call(): pl.pallas_call(kernel, out_shape=results, out_specs=[VMEM_SPEC] * len(res...  11.9 us
    ppermute x9, starting transfers between devices, across(): return lax.ppermute(block, axis, route)  11.9 us
    ppermute x9, waiting for transfers between devices, across(): return lax.ppermute(block, axis, route)  9.15 us
    unnamed x16, local copies, waits for them, and re-layouts  3.67 us
  transfers between devices with their start and end apart: 9, of which 4 were waited for; matrix products, arithmetic and copies ran while one was open for 0% of the time, Pallas kernels for 16%

profile of v5, /device:TPU:0, one launch (start us, length us, event | category | flops | bytes accessed | tf_op | source)
XLA Modules:
  0.0 38.0 jit_solution(401184007201651117)
XLA Ops:
  0.6 2.6 %pack.1 = bf16[96,640]{1,0:T(8,128)(2,1)} custom-call(s32[2,5]{1,0:T(2,128)} %offsets_ref.3, bf16[1,128,640]{2,1,0:T(8,128)(2,1)} %refs_0_.3, bf16[1,128,640]{2,1,0:T(8,128)(2,1)} %refs_1_.3), custom_call_target="tpu_custom_call" | custom-call | flops 1000000000 | tf_op jit(solution)/shard_map/pack/pallas_call | solution.py:496
  3.3 0.0 copy-start.6
  3.3 5.1 %collective-permute-start.2 = (bf16[96,640]{1,0:T(8,128)(2,1)}, bf16[96,640]{1,0:T(8,128)(2,1)S(1)}, u32[]{:S(2)}, u32[]{:S(2)}) collective-permute-start(bf16[96,640]{1,0:T(8,128)(2,1)} %pack.1), channel_id=1, source_target_pairs={{0,12},{4,8},{8,4},{12,0},{1,13},{5,9},{9,5},{13,1},{2,14},{6,10},... | collective-permute-start | bytes 368648 | tf_op jit(solution)/shard_map/ppermute | solution.py:479
  8.4 0.0 collective-permute-start.1
  8.4 0.6 %collective-permute-start = (bf16[96,640]{1,0:T(8,128)(2,1)}, bf16[96,640]{1,0:T(8,128)(2,1)S(1)}, u32[]{:S(2)}, u32[]{:S(2)}) collective-permute-start(bf16[96,640]{1,0:T(8,128)(2,1)} %pack.1), channel_id=1, source_target_pairs={{0,4},{4,0},{8,12},{12,8},{1,5},{5,1},{9,13},{13,9},{2,6},{6,2},{1... | collective-permute-start | bytes 368648 | tf_op jit(solution)/shard_map/ppermute | solution.py:479
  9.1 0.0 copy-done.6
  9.1 0.0 copy-start
  9.1 0.9 %copy-done = bf16[1,128,640]{2,1,0:T(8,128)(2,1)S(1)} copy-done((bf16[1,128,640]{2,1,0:T(8,128)(2,1)S(1)}, bf16[1,128,640]{2,1,0:T(8,128)(2,1)}, u32[]{:S(2)}) %copy-start) | copy-done | bytes 163864
  10.0 0.9 %copy-done.1 = bf16[1,128,640]{2,1,0:T(8,128)(2,1)S(1)} copy-done((bf16[1,128,640]{2,1,0:T(8,128)(2,1)S(1)}, bf16[1,128,640]{2,1,0:T(8,128)(2,1)}, u32[]{:S(2)}) %copy-start.1) | copy-done | bytes 163864
  10.9 0.9 %copy-done.2 = bf16[1,128,640]{2,1,0:T(8,128)(2,1)S(1)} copy-done((bf16[1,128,640]{2,1,0:T(8,128)(2,1)S(1)}, bf16[1,128,640]{2,1,0:T(8,128)(2,1)}, u32[]{:S(2)}) %copy-start.2) | copy-done | bytes 163864
  11.8 0.9 %copy-done.4 = bf16[1,128,640]{2,1,0:T(8,128)(2,1)S(1)} copy-done((bf16[1,128,640]{2,1,0:T(8,128)(2,1)S(1)}, bf16[1,128,640]{2,1,0:T(8,128)(2,1)}, u32[]{:S(2)}) %copy-start.4) | copy-done | bytes 163864
  12.7 2.6 %base.1 = (bf16[128,640]{1,0:T(8,128)(2,1)S(1)}, f32[128,640]{1,0:T(8,128)S(1)}, f32[128,640]{1,0:T(8,128)S(1)}, bf16[128,640]{1,0:T(8,128)(2,1)S(1)}, f32[1,640...) custom-call(s32[2,5]{1,0:T(2,128)S(1)} %copy-done.6, bf16[1,128,640]{2,1,0:T(8,128)(2,1)S(1)} %copy-done, ...), custom_call_target="tpu_custom_call" | custom-call | flops 2000000000 | tf_op jit(solution)/shard_map/base/pallas_call | solution.py:496
  15.4 0.0 collective-permute-done.2.refs_2_.refs_10_
  15.4 3.6 %collective-permute-done.1.refs_1_.refs_9_ = bf16[96,640]{1,0:T(8,128)(2,1)S(1)} collective-permute-done((bf16[96,640]{1,0:T(8,128)(2,1)}, bf16[96,640]{1,0:T(8,128)(2,1)S(1)}, u32[]{:S(2)}, u32[]{:S(2)}) %collective-permute-start.1) | collective-permute-done | bytes 122912 | tf_op jit(solution)/shard_map/ppermute | solution.py:479
  19.0 0.0 collective-permute-done.refs_0_.refs_8_
  19.0 3.2 %attend.1 = (f32[1,640]{1,0:T(1,128)S(1)}, f32[128,640]{1,0:T(8,128)S(1)}, bf16[128,640]{1,0:T(8,128)(2,1)S(1)}, bf16[144,640]{1,0:T(8,128)(2,1)S(1)}, f32[16,12...) custom-call(bf16[128,640]{1,0:T(8,128)(2,1)S(1)} %get-tuple-element.30.q_, ...), custom_call_target="tpu_custom_call" | custom-call | flops 5000000000 | tf_op jit(solution)/shard_map/attend/pallas_call | solution.py:496
  22.2 2.5 %collective-permute-start.5 = (bf16[96,640]{1,0:T(8,128)(2,1)S(1)}, bf16[96,640]{1,0:T(8,128)(2,1)S(1)}, u32[]{:S(2)}, u32[]{:S(2)}) collective-permute-start(bf16[96,640]{1,0:T(8,128)(2,1)S(1)} %get-tuple-element.47), channel_id=1, source_target_pairs={{0,12},{4,8},{8,4},{12,0},{1,13},{5,9},{9,5},{13,1},{2,14},{6,10},... | collective-permute-start | bytes 368648 | tf_op jit(solution)/shard_map/ppermute | solution.py:479
  24.7 0.0 collective-permute-start.6
  24.7 1.9 %collective-permute-start.7 = (bf16[96,640]{1,0:T(8,128)(2,1)S(1)}, bf16[96,640]{1,0:T(8,128)(2,1)S(1)}, u32[]{:S(2)}, u32[]{:S(2)}) collective-permute-start(bf16[96,640]{1,0:T(8,128)(2,1)S(1)} %get-tuple-element.49), channel_id=1, source_target_pairs={{0,4},{4,0},{8,12},{12,8},{1,5},{5,1},{9,13},{13,9},{2,6},{6,2},{1... | collective-permute-start | bytes 368648 | tf_op jit(solution)/shard_map/ppermute | solution.py:479
  26.6 0.0 collective-permute-start.3
  26.6 2.3 %query_grad.1 = (bf16[1,128,640]{2,1,0:T(8,128)(2,1)}, bf16[1,128,640]{2,1,0:T(8,128)(2,1)}, bf16[128,640]{1,0:T(8,128)(2,1)S(1)}, bf16[128,640]{1,0:T(8,128)(2,1)S(1)}) custom-call(bf16[1,128,640]{2,1,0:T(8,128)(2,1)S(1)} %copy-done.3, bf16[1,128,640]{2,1,0:T(8,128)(2,1)S(1)} %copy-done.5, f32[1,640]{1,0:T(1,128)S(1)} %reshape.16.refs_4_.refs_2_, ...), custom_call_target="tpu_custom_call" | custom-call | flops 500000000 | tf_op jit(solution)/shard_map/query_grad/pallas_call | solution.py:496
  28.9 0.0 collective-permute-done.3
  29.0 0.2 collective-permute-start.4
  29.1 0.3 key_grad.1
  29.4 3.4 %collective-permute-done.4 = f32[1,640]{1,0:T(1,128)S(1)} collective-permute-done((f32[1,640]{1,0:T(1,128)S(1)}, f32[1,640]{1,0:T(1,128)S(1)}, u32[]{:S(2)}, u32[]{:S(2)}) %collective-permute-start.4) | collective-permute-done | bytes 2592 | tf_op jit(solution)/shard_map/ppermute | solution.py:479
  32.9 1.5 %collective-permute-start.8 = (f32[1,640]{1,0:T(1,128)S(1)}, f32[1,640]{1,0:T(1,128)S(1)}, u32[]{:S(2)}, u32[]{:S(2)}) collective-permute-start(f32[1,640]{1,0:T(1,128)S(1)} %add.10.gain_ref), channel_id=1, source_target_pairs={{0,8},{4,12},{8,0},{12,4},{1,9},{5,13},{9,1},{13,5},{2,10},{6,14},... | collective-permute-start | bytes 7688 | tf_op jit(solution)/shard_map/ppermute | solution.py:479
  34.4 0.0 collective-permute-done.5.refs_0_
  34.4 0.1 collective-permute-done.6.refs_1_
  34.5 0.0 collective-permute-done.7.refs_2_
  34.5 1.0 %finish.1 = (bf16[1,128,640]{2,1,0:T(8,128)(2,1)}, bf16[1,128,640]{2,1,0:T(8,128)(2,1)}, f32[1,640]{1,0:T(1,128)S(1)}) custom-call(f32[1,640]{1,0:T(1,128)S(1)} %add.10.gain_ref, bf16[128,640]{1,0:T(8,128)(2,1)S(1)} %get-tuple-element.42.place_ref, f32[128,640]{1,0:T(8,128)S(1)} %get-tuple-element.45.dk_ref, f32[128,640]{1,0:T(8,128)S(1)} %get-tuple-element.46.dv_ref, ...), custom_call_target="tpu_custom_call" | custom-call | flops 1000000000 | tf_op jit(solution)/shard_map/finish/pallas_call | solution.py:496
  35.4 1.9 %collective-permute-done.8 = f32[1,640]{1,0:T(1,128)S(1)} collective-permute-done((f32[1,640]{1,0:T(1,128)S(1)}, f32[1,640]{1,0:T(1,128)S(1)}, u32[]{:S(2)}, u32[]{:S(2)}) %collective-permute-start.8) | collective-permute-done | bytes 2592 | tf_op jit(solution)/shard_map/ppermute | solution.py:479
  37.4 0.6 %add_reduce_fusion = f32[640]{0:T(1024)} fusion(f32[1,640]{1,0:T(1,128)S(1)} %get-tuple-element.52, f32[1,640]{1,0:T(1,128)S(1)} %collective-permute-done.8), kind=kLoop, calls=%fused_computation | loop fusion | flops 640 | bytes 7680 | tf_op jit(solution)/shard_map/add | solution.py:601
  (12 shorter events, 0.0 us)
Async XLA Ops:
  0.6 8.4 %copy-start.7 = (f32[640]{0:T(1024)S(1)}, f32[640]{0:T(1024)}, u32[]{:S(2)}) copy-start(f32[640]{0:T(1024)} %param.10) | copy-start | bytes 7684
  3.3 5.8 %copy-start.6 = (s32[2,5]{1,0:T(2,128)S(1)}, s32[2,5]{1,0:T(2,128)}, u32[]{:S(2)}) copy-start(s32[2,5]{1,0:T(2,128)} %offsets_ref.3) | copy-start | bytes 124
  3.3 12.1 %collective-permute-start.2 = (bf16[96,640]{1,0:T(8,128)(2,1)}, bf16[96,640]{1,0:T(8,128)(2,1)S(1)}, u32[]{:S(2)}, u32[]{:S(2)}) collective-permute-start(bf16[96,640]{1,0:T(8,128)(2,1)} %pack.1), channel_id=1, source_target_pairs={{0,12},{4,8},{8,4},{12,0},{1,13},{5,9},{9,5},{13,1},{2,14},{6,10},... | collective-permute-start | bytes 368648 | tf_op jit(solution)/shard_map/ppermute | solution.py:479
  8.4 10.6 %collective-permute-start.1 = (bf16[96,640]{1,0:T(8,128)(2,1)}, bf16[96,640]{1,0:T(8,128)(2,1)S(1)}, u32[]{:S(2)}, u32[]{:S(2)}) collective-permute-start(bf16[96,640]{1,0:T(8,128)(2,1)} %pack.1), channel_id=1, source_target_pairs={{0,8},{4,12},{8,0},{12,4},{1,9},{5,13},{9,1},{13,5},{2,10},{6,14},... | collective-permute-start | bytes 368648 | tf_op jit(solution)/shard_map/ppermute | solution.py:479
  8.4 10.6 %collective-permute-start = (bf16[96,640]{1,0:T(8,128)(2,1)}, bf16[96,640]{1,0:T(8,128)(2,1)S(1)}, u32[]{:S(2)}, u32[]{:S(2)}) collective-permute-start(bf16[96,640]{1,0:T(8,128)(2,1)} %pack.1), channel_id=1, source_target_pairs={{0,4},{4,0},{8,12},{12,8},{1,5},{5,1},{9,13},{13,9},{2,6},{6,2},{1... | collective-permute-start | bytes 368648 | tf_op jit(solution)/shard_map/ppermute | solution.py:479
  9.1 0.9 %copy-start = (bf16[1,128,640]{2,1,0:T(8,128)(2,1)S(1)}, bf16[1,128,640]{2,1,0:T(8,128)(2,1)}, u32[]{:S(2)}) copy-start(bf16[1,128,640]{2,1,0:T(8,128)(2,1)} %refs_0_.2) | copy-start | bytes 491524
  10.0 0.9 %copy-start.1 = (bf16[1,128,640]{2,1,0:T(8,128)(2,1)S(1)}, bf16[1,128,640]{2,1,0:T(8,128)(2,1)}, u32[]{:S(2)}) copy-start(bf16[1,128,640]{2,1,0:T(8,128)(2,1)} %refs_3_.1) | copy-start | bytes 491524
  10.9 0.9 %copy-start.2 = (bf16[1,128,640]{2,1,0:T(8,128)(2,1)S(1)}, bf16[1,128,640]{2,1,0:T(8,128)(2,1)}, u32[]{:S(2)}) copy-start(bf16[1,128,640]{2,1,0:T(8,128)(2,1)} %refs_0_.3) | copy-start | bytes 491524
  11.8 0.9 %copy-start.4 = (bf16[1,128,640]{2,1,0:T(8,128)(2,1)S(1)}, bf16[1,128,640]{2,1,0:T(8,128)(2,1)}, u32[]{:S(2)}) copy-start(bf16[1,128,640]{2,1,0:T(8,128)(2,1)} %refs_1_.3) | copy-start | bytes 491524
  19.0 7.6 %copy-start.3 = (bf16[1,128,640]{2,1,0:T(8,128)(2,1)S(1)}, bf16[1,128,640]{2,1,0:T(8,128)(2,1)}, u32[]{:S(2)}) copy-start(bf16[1,128,640]{2,1,0:T(8,128)(2,1)} %refs_0_.3) | copy-start | bytes 491524
  19.0 7.6 %copy-start.5 = (bf16[1,128,640]{2,1,0:T(8,128)(2,1)S(1)}, bf16[1,128,640]{2,1,0:T(8,128)(2,1)}, u32[]{:S(2)}) copy-start(bf16[1,128,640]{2,1,0:T(8,128)(2,1)} %refs_1_.3) | copy-start | bytes 491524
  22.2 12.2 %collective-permute-start.5 = (bf16[96,640]{1,0:T(8,128)(2,1)S(1)}, bf16[96,640]{1,0:T(8,128)(2,1)S(1)}, u32[]{:S(2)}, u32[]{:S(2)}) collective-permute-start(bf16[96,640]{1,0:T(8,128)(2,1)S(1)} %get-tuple-element.47), channel_id=1, source_target_pairs={{0,12},{4,8},{8,4},{12,0},{1,13},{5,9},{9,5},{13,1},{2,14},{6,10},... | collective-permute-start | bytes 368648 | tf_op jit(solution)/shard_map/ppermute | solution.py:479
  24.7 9.8 %collective-permute-start.6 = (bf16[96,640]{1,0:T(8,128)(2,1)S(1)}, bf16[96,640]{1,0:T(8,128)(2,1)S(1)}, u32[]{:S(2)}, u32[]{:S(2)}) collective-permute-start(bf16[96,640]{1,0:T(8,128)(2,1)S(1)} %get-tuple-element.48), channel_id=1, source_target_pairs={{0,8},{4,12},{8,0},{12,4},{1,9},{5,13},{9,1},{13,5},{2,10},{6,14},... | collective-permute-start | bytes 368648 | tf_op jit(solution)/shard_map/ppermute | solution.py:479
  24.7 9.8 %collective-permute-start.7 = (bf16[96,640]{1,0:T(8,128)(2,1)S(1)}, bf16[96,640]{1,0:T(8,128)(2,1)S(1)}, u32[]{:S(2)}, u32[]{:S(2)}) collective-permute-start(bf16[96,640]{1,0:T(8,128)(2,1)S(1)} %get-tuple-element.49), channel_id=1, source_target_pairs={{0,4},{4,0},{8,12},{12,8},{1,5},{5,1},{9,13},{13,9},{2,6},{6,2},{1... | collective-permute-start | bytes 368648 | tf_op jit(solution)/shard_map/ppermute | solution.py:479
  26.6 2.3 %collective-permute-start.3 = (f32[1,640]{1,0:T(1,128)S(1)}, f32[1,640]{1,0:T(1,128)S(1)}, u32[]{:S(2)}, u32[]{:S(2)}) collective-permute-start(f32[1,640]{1,0:T(1,128)S(1)} %get-tuple-element.41), channel_id=1, source_target_pairs={{0,16},{16,0},{1,17},{17,1},{2,18},{18,2},{3,19},{19,3},{4,20},{20... | collective-permute-start | bytes 7688 | tf_op jit(solution)/shard_map/ppermute | solution.py:479
  29.0 3.9 %collective-permute-start.4 = (f32[1,640]{1,0:T(1,128)S(1)}, f32[1,640]{1,0:T(1,128)S(1)}, u32[]{:S(2)}, u32[]{:S(2)}) collective-permute-start(f32[1,640]{1,0:T(1,128)S(1)} %add.9), channel_id=1, source_target_pairs={{0,4},{4,0},{8,12},{12,8},{1,5},{5,1},{9,13},{13,9},{2,6},{6,2},{1... | collective-permute-start | bytes 7688 | tf_op jit(solution)/shard_map/ppermute | solution.py:479
  32.9 4.5 %collective-permute-start.8 = (f32[1,640]{1,0:T(1,128)S(1)}, f32[1,640]{1,0:T(1,128)S(1)}, u32[]{:S(2)}, u32[]{:S(2)}) collective-permute-start(f32[1,640]{1,0:T(1,128)S(1)} %add.10.gain_ref), channel_id=1, source_target_pairs={{0,8},{4,12},{8,0},{12,4},{1,9},{5,13},{9,1},{13,5},{2,10},{6,14},... | collective-permute-start | bytes 7688 | tf_op jit(solution)/shard_map/ppermute | solution.py:479

commit v6 on v5

--- a/solution.py
+++ b/solution.py
@@ -228,7 +228,7 @@
 LOW = jnp.bfloat16
 WIDE = jnp.float32
 HEAD_GROUPS = ((0, 5),)
-LOAD_PIECES = 4
+LOAD_PIECES = 1
 PACK_VMEM = 65408 * 1024
 
 
@@ -279,16 +279,18 @@
     ]
     for copy in copies:
         copy.start()
+    heads = range(width // HEAD_DIM)
+    picks = [pick_matrix(offsets_ref, head, tokens, top_step, 0) for head in heads]
     for copy in copies:
         copy.wait()
+    both = [
+        jnp.concatenate([k_ref[:, head_cols(head)], v_ref[:, head_cols(head)]], 1) for head in heads
+    ]
+    rows = [contract(picks[head], both[head], 1, 0).astype(LOW) for head in heads]
     for (first, last), packed_ref in zip(groups, packed_refs):
         for head in range(first, last):
-            cols = head_cols(head)
-            picks = pick_matrix(offsets_ref, head, tokens, top_step, 0)
-            both = jnp.concatenate([k_ref[:, cols], v_ref[:, cols]], 1)
-            rows = contract(picks, both, 1, 0).astype(LOW)
-            packed_ref[:picked, head_cols(head - first)] = rows[:, :HEAD_DIM]
-            packed_ref[picked:, head_cols(head - first)] = rows[:, HEAD_DIM:]
+            packed_ref[:picked, head_cols(head - first)] = rows[head][:, :HEAD_DIM]
+            packed_ref[picked:, head_cols(head - first)] = rows[head][:, HEAD_DIM:]
 
 
 def fetch(sources, held, sems):
@@ -360,58 +362,71 @@
     picked = top_rows + mid_rows
     score_scale = 1.0 / math.sqrt(HEAD_DIM)
     ones = jnp.ones((STATS_ROWS, tokens), LOW)
-    for head in range(first, last):
-        cols = head_cols(head)
-        own = head_cols(head - first)
-        q_rows = q_ref[:, cols]
-        k_peers = stacked(packed_refs, pl.ds(0, picked), own)
-        v_peers = stacked(packed_refs, pl.ds(picked, picked), own)
-        mid_bias, top_bias = [
-            base_stats_ref[row + head : row + head + 1, :]
-            for row in (2 * STATS_ROWS, 3 * STATS_ROWS)
-        ]
+    heads = range(last - first)
+    every = [head_cols(head) for head in range(first, last)]
+    own = [head_cols(head) for head in heads]
+
+    def stat(block, head):
+        row = block * STATS_ROWS + first + head
+        return base_stats_ref[row : row + 1, :]
+
+    q_rows = [q_ref[:, cols] for cols in every]
+    k_peers = [stacked(packed_refs, pl.ds(0, picked), cols) for cols in own]
+    v_peers = [stacked(packed_refs, pl.ds(picked, picked), cols) for cols in own]
+    products = [contract(k_peers[head], q_rows[head], 1, 1) for head in heads]
+    expos, factors, inv_totals = [], [], []
+    for head in heads:
         bias = jnp.concatenate(
             [
-                jnp.broadcast_to(top_bias, (top_rows, tokens)),
-                jnp.broadcast_to(mid_bias, (mid_rows, tokens)),
+                jnp.broadcast_to(stat(3, head), (top_rows, tokens)),
+                jnp.broadcast_to(stat(2, head), (mid_rows, tokens)),
             ]
             * PEERS,
             0,
         )
-        scores = contract(k_peers, q_rows, 1, 1) * score_scale + bias
-        base_top = base_stats_ref[head : head + 1, :]
-        base_total = base_stats_ref[STATS_ROWS + head : STATS_ROWS + head + 1, :]
-        top_score = jnp.maximum(base_top, jnp.max(scores, axis=0, keepdims=True))
-        base_factor = jnp.exp(base_top - top_score)
-        expo = jnp.exp(scores - top_score)
-        inv_total = 1.0 / (base_factor * base_total + jnp.sum(expo, axis=0, keepdims=True))
-        soft = expo * inv_total
-        soft_low = soft.astype(LOW)
-        base_factor = base_factor * inv_total
-        attn = base_factor * base_out_ref[:, cols] + contract(v_peers, soft_low, 0, 0)
+        scores = products[head] * score_scale + bias
+        top_score = jnp.maximum(stat(0, head), jnp.max(scores, axis=0, keepdims=True))
+        expos.append(jnp.exp(scores - top_score))
+        factors.append(jnp.exp(stat(0, head) - top_score))
+    for head in heads:
+        total = factors[head] * stat(1, head) + jnp.sum(expos[head], axis=0, keepdims=True)
+        inv_totals.append(1.0 / total)
+        factors[head] = factors[head] * inv_totals[head]
+        stats_ref[head : head + 1, :] = factors[head]
+    softs = [expos[head] * inv_totals[head] for head in heads]
+    soft_lows = [soft.astype(LOW) for soft in softs]
+    mixed = [contract(v_peers[head], soft_lows[head], 0, 0) for head in heads]
+    grad_lows, inners, gain_products = [], [], []
+    for head in heads:
+        attn = factors[head] * base_out_ref[:, every[head]] + mixed[head]
         inv_rms = lax.rsqrt(jnp.mean(attn * attn, axis=0, keepdims=True) + EPS)
         normed = attn * inv_rms
-        normed_ref[:, own] = normed
-        grad_norm = grad_norm_ref[:, cols]
+        normed_ref[:, own[head]] = normed
+        grad_norm = grad_norm_ref[:, every[head]]
         product = grad_norm * normed
+        gain_products.append(product)
         grad_attn = inv_rms * (grad_norm - normed * jnp.mean(product, axis=0, keepdims=True))
-        product_high = product.astype(LOW)
-        product_rest = (product - product_high.astype(WIDE)).astype(LOW)
+        inners.append(jnp.sum(grad_attn * attn, axis=0, keepdims=True))
+        stats_ref[STATS_ROWS + head : STATS_ROWS + head + 1, :] = inners[head]
+        grad_lows.append(grad_attn.astype(LOW))
+        grad_low_ref[:, own[head]] = grad_lows[head]
+    prob_grads = [contract(v_peers[head], grad_lows[head], 1, 0) for head in heads]
+    dv_peers = [contract(soft_lows[head], grad_lows[head], 1, 1).astype(LOW) for head in heads]
+    score_grads = [
+        (softs[head] * (prob_grads[head] - inners[head]) * score_scale).astype(LOW)
+        for head in heads
+    ]
+    dk_peers = [contract(score_grads[head], q_rows[head], 1, 0).astype(LOW) for head in heads]
+    for head in heads:
+        score_grad_ref[:, own[head]] = score_grads[head]
+        product_high = gain_products[head].astype(LOW)
+        product_rest = (gain_products[head] - product_high.astype(WIDE)).astype(LOW)
         gain_rows = contract(ones, product_high, 1, 1) + contract(ones, product_rest, 1, 1)
-        gain_part_ref[:, own] = gain_rows[:1] * inv_gain_ref[:, cols]
-        inner = jnp.sum(grad_attn * attn, axis=0, keepdims=True)
-        grad_low = grad_attn.astype(LOW)
-        grad_low_ref[:, own] = grad_low
-        stats_ref[head - first : head - first + 1, :] = base_factor
-        stats_ref[STATS_ROWS + head - first : STATS_ROWS + head - first + 1, :] = inner
-        prob_grad = contract(v_peers, grad_low, 1, 0)
-        score_grad = (soft * (prob_grad - inner) * score_scale).astype(LOW)
-        score_grad_ref[:, own] = score_grad
-        dk_peers = contract(score_grad, q_rows, 1, 0).astype(LOW)
-        dv_peers = contract(soft_low, grad_low, 1, 1).astype(LOW)
+        gain_part_ref[:, own[head]] = gain_rows[:1] * inv_gain_ref[:, every[head]]
         for place, part_ref in enumerate(part_refs):
-            part_ref[:picked, own] = dk_peers[place * picked : (place + 1) * picked]
-            part_ref[picked:, own] = dv_peers[place * picked : (place + 1) * picked]
+            start = place * picked
+            part_ref[:picked, own[head]] = dk_peers[head][start : start + picked]
+            part_ref[picked:, own[head]] = dv_peers[head][start : start + picked]
 
 
 def query_grad_kernel(top_step, groups, *refs):
@@ -572,15 +587,15 @@
         kept += [normed, grad_low, score_grad, stats, *peers]
         returned += to_peers(parts)[::-1]
     gain_part = jnp.concatenate(gain_parts, 1) if len(groups) > 1 else gain_parts[0]
-    gain_grad = gain_part + across(gain_part, "dp", 1)
-    gain_grad = gain_grad + across(gain_grad, "ctx", 1)
-    gain_rest = across(gain_grad, "ctx", 2)
+    gain_grad = gain_part + across(gain_part, "ctx", 2)
+    gain_grad = gain_grad + across(gain_grad, "dp", 1)
+    gain_rest = across(gain_grad, "ctx", 1)
     attended, query_grad, score_grad, soft = call(
         bind(query_grad_kernel, top_step, groups),
         "query_grad",
         (keys, values, gain_row, expo, *kept),
         [row_block, row_block, low_block, low_block],
-        0.5,
+        20,
         in_specs=[HBM_SPEC] * 3 + [VMEM_SPEC] * (1 + len(kept)),
         scratch_shapes=[row_scratch] * 2 + [gain_scratch, pltpu.SemaphoreType.DMA((3,))],
     )
@@ -589,7 +604,7 @@
         "key_grad",
         (q_copy, score_grad, soft, *grad_lows),
         [wide_block, wide_block],
-        0.5,
+        20,
     )
     key_grad, value_grad, gain_grad = call(
         bind(finish_kernel, top_step, groups),

time: 38.3 us -> 36.2 us (0.945)
  Pallas kernels: 11.9 us -> 9.96 us
    pallas_call x6, Pallas kernels: 11.9 us -> 9.96 us  [call(): pl.pallas_call(kernel, out_shape=results, out_specs=[VMEM_SPEC] * len(res...]
  transfers between devices with their start and end apart: 9 -> 9, of which waited for: 4 -> 4; matrix products, arithmetic and copies ran while one was open for 0% -> 0% of each run, Pallas kernels for 16% -> 17%
where the time goes in v6:
time: 36.2 us; the launch traced here: 36 us
  starting transfers between devices  11.9 us (33%)
  Pallas kernels  9.96 us (28%)
  waiting for transfers between devices  9.12 us (25%)
  local copies, waits for them, and re-layouts  3.68 us (10%)
  between operations  0.71 us (2%)
  other arithmetic  0.61 us (2%)
    ppermute x9, starting transfers between devices, across(): return lax.ppermute(block, axis, route)  11.9 us
    pallas_call x6, Pallas kernels, call(): pl.pallas_call(kernel, out_shape=results, out_specs=[VMEM_SPEC] * len(res...  9.96 us
    ppermute x9, waiting for transfers between devices, across(): return lax.ppermute(block, axis, route)  9.12 us
    unnamed x16, local copies, waits for them, and re-layouts  3.67 us
  transfers between devices with their start and end apart: 9, of which 4 were waited for; matrix products, arithmetic and copies ran while one was open for 0% of the time, Pallas kernels for 17%

profile of v6, /device:TPU:0, one launch (start us, length us, event | category | flops | bytes accessed | tf_op | source)
XLA Modules:
  0.0 36.0 jit_solution(14662621447269542347)
XLA Ops:
  0.6 0.0 copy-start.7
  0.6 2.7 %pack.1 = bf16[96,640]{1,0:T(8,128)(2,1)} custom-call(s32[2,5]{1,0:T(2,128)} %offsets_ref.3, bf16[1,128,640]{2,1,0:T(8,128)(2,1)} %refs_0_.3, bf16[1,128,640]{2,1,0:T(8,128)(2,1)} %refs_1_.3), custom_call_target="tpu_custom_call" | custom-call | flops 1000000000 | tf_op jit(solution)/shard_map/pack/pallas_call | solution.py:511
  3.3 0.0 copy-start.6
  3.3 5.1 %collective-permute-start.2 = (bf16[96,640]{1,0:T(8,128)(2,1)}, bf16[96,640]{1,0:T(8,128)(2,1)S(1)}, u32[]{:S(2)}, u32[]{:S(2)}) collective-permute-start(bf16[96,640]{1,0:T(8,128)(2,1)} %pack.1), channel_id=1, source_target_pairs={{0,12},{4,8},{8,4},{12,0},{1,13},{5,9},{9,5},{13,1},{2,14},{6,10},... | collective-permute-start | bytes 368648 | tf_op jit(solution)/shard_map/ppermute | solution.py:494
  8.4 0.0 collective-permute-start.1
  8.4 0.6 %collective-permute-start = (bf16[96,640]{1,0:T(8,128)(2,1)}, bf16[96,640]{1,0:T(8,128)(2,1)S(1)}, u32[]{:S(2)}, u32[]{:S(2)}) collective-permute-start(bf16[96,640]{1,0:T(8,128)(2,1)} %pack.1), channel_id=1, source_target_pairs={{0,4},{4,0},{8,12},{12,8},{1,5},{5,1},{9,13},{13,9},{2,6},{6,2},{1... | collective-permute-start | bytes 368648 | tf_op jit(solution)/shard_map/ppermute | solution.py:494
  9.1 0.0 copy-start
  9.1 0.9 %copy-done = bf16[1,128,640]{2,1,0:T(8,128)(2,1)S(1)} copy-done((bf16[1,128,640]{2,1,0:T(8,128)(2,1)S(1)}, bf16[1,128,640]{2,1,0:T(8,128)(2,1)}, u32[]{:S(2)}) %copy-start) | copy-done | bytes 163864
  10.0 0.9 %copy-done.1 = bf16[1,128,640]{2,1,0:T(8,128)(2,1)S(1)} copy-done((bf16[1,128,640]{2,1,0:T(8,128)(2,1)S(1)}, bf16[1,128,640]{2,1,0:T(8,128)(2,1)}, u32[]{:S(2)}) %copy-start.1) | copy-done | bytes 163864
  10.9 0.9 %copy-done.2 = bf16[1,128,640]{2,1,0:T(8,128)(2,1)S(1)} copy-done((bf16[1,128,640]{2,1,0:T(8,128)(2,1)S(1)}, bf16[1,128,640]{2,1,0:T(8,128)(2,1)}, u32[]{:S(2)}) %copy-start.2) | copy-done | bytes 163864
  11.9 0.9 %copy-done.4 = bf16[1,128,640]{2,1,0:T(8,128)(2,1)S(1)} copy-done((bf16[1,128,640]{2,1,0:T(8,128)(2,1)S(1)}, bf16[1,128,640]{2,1,0:T(8,128)(2,1)}, u32[]{:S(2)}) %copy-start.4) | copy-done | bytes 163864
  12.8 2.6 %base.1 = (bf16[128,640]{1,0:T(8,128)(2,1)S(1)}, f32[128,640]{1,0:T(8,128)S(1)}, f32[128,640]{1,0:T(8,128)S(1)}, bf16[128,640]{1,0:T(8,128)(2,1)S(1)}, f32[1,640...) custom-call(s32[2,5]{1,0:T(2,128)S(1)} %copy-done.6, bf16[1,128,640]{2,1,0:T(8,128)(2,1)S(1)} %copy-done, ...), custom_call_target="tpu_custom_call" | custom-call | flops 2000000000 | tf_op jit(solution)/shard_map/base/pallas_call | solution.py:511
  15.4 0.0 collective-permute-done.2.refs_2_.refs_10_
  15.4 3.6 %collective-permute-done.1.refs_1_.refs_9_ = bf16[96,640]{1,0:T(8,128)(2,1)S(1)} collective-permute-done((bf16[96,640]{1,0:T(8,128)(2,1)}, bf16[96,640]{1,0:T(8,128)(2,1)S(1)}, u32[]{:S(2)}, u32[]{:S(2)}) %collective-permute-start.1) | collective-permute-done | bytes 122912 | tf_op jit(solution)/shard_map/ppermute | solution.py:494
  19.0 0.0 collective-permute-done.refs_0_.refs_8_
  19.0 1.2 %attend.1 = (f32[1,640]{1,0:T(1,128)S(1)}, f32[128,640]{1,0:T(8,128)S(1)}, bf16[128,640]{1,0:T(8,128)(2,1)S(1)}, bf16[144,640]{1,0:T(8,128)(2,1)S(1)}, f32[16,12...) custom-call(bf16[128,640]{1,0:T(8,128)(2,1)S(1)} %get-tuple-element.30.q_, ...), custom_call_target="tpu_custom_call" | custom-call | flops 5000000000 | tf_op jit(solution)/shard_map/attend/pallas_call | solution.py:511
  20.2 0.1 collective-permute-start.3
  20.3 2.4 %collective-permute-start.5 = (bf16[96,640]{1,0:T(8,128)(2,1)S(1)}, bf16[96,640]{1,0:T(8,128)(2,1)S(1)}, u32[]{:S(2)}, u32[]{:S(2)}) collective-permute-start(bf16[96,640]{1,0:T(8,128)(2,1)S(1)} %get-tuple-element.47), channel_id=1, source_target_pairs={{0,12},{4,8},{8,4},{12,0},{1,13},{5,9},{9,5},{13,1},{2,14},{6,10},... | collective-permute-start | bytes 368648 | tf_op jit(solution)/shard_map/ppermute | solution.py:494
  22.7 2.0 %collective-permute-start.6 = (bf16[96,640]{1,0:T(8,128)(2,1)S(1)}, bf16[96,640]{1,0:T(8,128)(2,1)S(1)}, u32[]{:S(2)}, u32[]{:S(2)}) collective-permute-start(bf16[96,640]{1,0:T(8,128)(2,1)S(1)} %get-tuple-element.48), channel_id=1, source_target_pairs={{0,8},{4,12},{8,0},{12,4},{1,9},{5,13},{9,1},{13,5},{2,10},{6,14},... | collective-permute-start | bytes 368648 | tf_op jit(solution)/shard_map/ppermute | solution.py:494
  24.7 0.0 collective-permute-start.7
  24.7 2.3 %query_grad.1 = (bf16[1,128,640]{2,1,0:T(8,128)(2,1)}, bf16[1,128,640]{2,1,0:T(8,128)(2,1)}, bf16[128,640]{1,0:T(8,128)(2,1)S(1)}, bf16[128,640]{1,0:T(8,128)(2,1)S(1)}) custom-call(bf16[1,128,640]{2,1,0:T(8,128)(2,1)S(1)} %copy-done.3, bf16[1,128,640]{2,1,0:T(8,128)(2,1)S(1)} %copy-done.5, f32[1,640]{1,0:T(1,128)S(1)} %reshape.16.refs_4_.refs_2_, ...), custom_call_target="tpu_custom_call" | custom-call | flops 20000000000 | tf_op jit(solution)/shard_map/query_grad/pallas_call | solution.py:511
  27.0 0.5 %collective-permute-done.3 = f32[1,640]{1,0:T(1,128)S(1)} collective-permute-done((f32[1,640]{1,0:T(1,128)S(1)}, f32[1,640]{1,0:T(1,128)S(1)}, u32[]{:S(2)}, u32[]{:S(2)}) %collective-permute-start.3) | collective-permute-done | bytes 2592 | tf_op jit(solution)/shard_map/ppermute | solution.py:494
  27.5 0.0 collective-permute-start.4
  27.5 0.3 key_grad.1
  27.8 0.9 %collective-permute-done.4 = f32[1,640]{1,0:T(1,128)S(1)} collective-permute-done((f32[1,640]{1,0:T(1,128)S(1)}, f32[1,640]{1,0:T(1,128)S(1)}, u32[]{:S(2)}, u32[]{:S(2)}) %collective-permute-start.4) | collective-permute-done | bytes 2592 | tf_op jit(solution)/shard_map/ppermute | solution.py:494
  28.7 1.6 %collective-permute-start.8 = (f32[1,640]{1,0:T(1,128)S(1)}, f32[1,640]{1,0:T(1,128)S(1)}, u32[]{:S(2)}, u32[]{:S(2)}) collective-permute-start(f32[1,640]{1,0:T(1,128)S(1)} %add.10.gain_ref), channel_id=1, source_target_pairs={{0,4},{4,0},{8,12},{12,8},{1,5},{5,1},{9,13},{13,9},{2,6},{6,2},{1... | collective-permute-start | bytes 7688 | tf_op jit(solution)/shard_map/ppermute | solution.py:494
  30.3 0.0 collective-permute-done.5.refs_0_
  30.3 4.1 %collective-permute-done.6.refs_1_ = bf16[96,640]{1,0:T(8,128)(2,1)S(1)} collective-permute-done((bf16[96,640]{1,0:T(8,128)(2,1)S(1)}, bf16[96,640]{1,0:T(8,128)(2,1)S(1)}, u32[]{:S(2)}, u32[]{:S(2)}) %collective-permute-start.6) | collective-permute-done | bytes 122912 | tf_op jit(solution)/shard_map/ppermute | solution.py:494
  34.4 0.0 collective-permute-done.7.refs_2_
  34.4 1.0 %finish.1 = (bf16[1,128,640]{2,1,0:T(8,128)(2,1)}, bf16[1,128,640]{2,1,0:T(8,128)(2,1)}, f32[1,640]{1,0:T(1,128)S(1)}) custom-call(f32[1,640]{1,0:T(1,128)S(1)} %add.10.gain_ref, bf16[128,640]{1,0:T(8,128)(2,1)S(1)} %get-tuple-element.42.place_ref, f32[128,640]{1,0:T(8,128)S(1)} %get-tuple-element.45.dk_ref, f32[128,640]{1,0:T(8,128)S(1)} %get-tuple-element.46.dv_ref, ...), custom_call_target="tpu_custom_call" | custom-call | flops 1000000000 | tf_op jit(solution)/shard_map/finish/pallas_call | solution.py:511
  35.4 0.0 collective-permute-done.8
  35.4 0.6 %add_reduce_fusion = f32[640]{0:T(1024)} fusion(f32[1,640]{1,0:T(1,128)S(1)} %get-tuple-element.52, f32[1,640]{1,0:T(1,128)S(1)} %collective-permute-done.8), kind=kLoop, calls=%fused_computation | loop fusion | flops 640 | bytes 7680 | tf_op jit(solution)/shard_map/add | solution.py:616
  (12 shorter events, 0.0 us)
Async XLA Ops:
  0.6 8.5 %copy-start.7 = (f32[640]{0:T(1024)S(1)}, f32[640]{0:T(1024)}, u32[]{:S(2)}) copy-start(f32[640]{0:T(1024)} %param.10) | copy-start | bytes 7684
  3.3 5.8 %copy-start.6 = (s32[2,5]{1,0:T(2,128)S(1)}, s32[2,5]{1,0:T(2,128)}, u32[]{:S(2)}) copy-start(s32[2,5]{1,0:T(2,128)} %offsets_ref.3) | copy-start | bytes 124
  3.3 12.1 %collective-permute-start.2 = (bf16[96,640]{1,0:T(8,128)(2,1)}, bf16[96,640]{1,0:T(8,128)(2,1)S(1)}, u32[]{:S(2)}, u32[]{:S(2)}) collective-permute-start(bf16[96,640]{1,0:T(8,128)(2,1)} %pack.1), channel_id=1, source_target_pairs={{0,12},{4,8},{8,4},{12,0},{1,13},{5,9},{9,5},{13,1},{2,14},{6,10},... | collective-permute-start | bytes 368648 | tf_op jit(solution)/shard_map/ppermute | solution.py:494
  8.4 10.6 %collective-permute-start.1 = (bf16[96,640]{1,0:T(8,128)(2,1)}, bf16[96,640]{1,0:T(8,128)(2,1)S(1)}, u32[]{:S(2)}, u32[]{:S(2)}) collective-permute-start(bf16[96,640]{1,0:T(8,128)(2,1)} %pack.1), channel_id=1, source_target_pairs={{0,8},{4,12},{8,0},{12,4},{1,9},{5,13},{9,1},{13,5},{2,10},{6,14},... | collective-permute-start | bytes 368648 | tf_op jit(solution)/shard_map/ppermute | solution.py:494
  8.4 10.6 %collective-permute-start = (bf16[96,640]{1,0:T(8,128)(2,1)}, bf16[96,640]{1,0:T(8,128)(2,1)S(1)}, u32[]{:S(2)}, u32[]{:S(2)}) collective-permute-start(bf16[96,640]{1,0:T(8,128)(2,1)} %pack.1), channel_id=1, source_target_pairs={{0,4},{4,0},{8,12},{12,8},{1,5},{5,1},{9,13},{13,9},{2,6},{6,2},{1... | collective-permute-start | bytes 368648 | tf_op jit(solution)/shard_map/ppermute | solution.py:494
  9.1 0.9 %copy-start = (bf16[1,128,640]{2,1,0:T(8,128)(2,1)S(1)}, bf16[1,128,640]{2,1,0:T(8,128)(2,1)}, u32[]{:S(2)}) copy-start(bf16[1,128,640]{2,1,0:T(8,128)(2,1)} %refs_0_.2) | copy-start | bytes 491524
  10.0 0.9 %copy-start.1 = (bf16[1,128,640]{2,1,0:T(8,128)(2,1)S(1)}, bf16[1,128,640]{2,1,0:T(8,128)(2,1)}, u32[]{:S(2)}) copy-start(bf16[1,128,640]{2,1,0:T(8,128)(2,1)} %refs_3_.1) | copy-start | bytes 491524
  10.9 0.9 %copy-start.2 = (bf16[1,128,640]{2,1,0:T(8,128)(2,1)S(1)}, bf16[1,128,640]{2,1,0:T(8,128)(2,1)}, u32[]{:S(2)}) copy-start(bf16[1,128,640]{2,1,0:T(8,128)(2,1)} %refs_0_.3) | copy-start | bytes 491524
  11.9 0.9 %copy-start.4 = (bf16[1,128,640]{2,1,0:T(8,128)(2,1)S(1)}, bf16[1,128,640]{2,1,0:T(8,128)(2,1)}, u32[]{:S(2)}) copy-start(bf16[1,128,640]{2,1,0:T(8,128)(2,1)} %refs_1_.3) | copy-start | bytes 491524
  19.0 5.7 %copy-start.3 = (bf16[1,128,640]{2,1,0:T(8,128)(2,1)S(1)}, bf16[1,128,640]{2,1,0:T(8,128)(2,1)}, u32[]{:S(2)}) copy-start(bf16[1,128,640]{2,1,0:T(8,128)(2,1)} %refs_0_.3) | copy-start | bytes 491524
  19.0 5.7 %copy-start.5 = (bf16[1,128,640]{2,1,0:T(8,128)(2,1)S(1)}, bf16[1,128,640]{2,1,0:T(8,128)(2,1)}, u32[]{:S(2)}) copy-start(bf16[1,128,640]{2,1,0:T(8,128)(2,1)} %refs_1_.3) | copy-start | bytes 491524
  20.2 7.3 %collective-permute-start.3 = (f32[1,640]{1,0:T(1,128)S(1)}, f32[1,640]{1,0:T(1,128)S(1)}, u32[]{:S(2)}, u32[]{:S(2)}) collective-permute-start(f32[1,640]{1,0:T(1,128)S(1)} %get-tuple-element.41), channel_id=1, source_target_pairs={{0,8},{4,12},{8,0},{12,4},{1,9},{5,13},{9,1},{13,5},{2,10},{6,14},... | collective-permute-start | bytes 7688 | tf_op jit(solution)/shard_map/ppermute | solution.py:494
  20.3 10.0 %collective-permute-start.5 = (bf16[96,640]{1,0:T(8,128)(2,1)S(1)}, bf16[96,640]{1,0:T(8,128)(2,1)S(1)}, u32[]{:S(2)}, u32[]{:S(2)}) collective-permute-start(bf16[96,640]{1,0:T(8,128)(2,1)S(1)} %get-tuple-element.47), channel_id=1, source_target_pairs={{0,12},{4,8},{8,4},{12,0},{1,13},{5,9},{9,5},{13,1},{2,14},{6,10},... | collective-permute-start | bytes 368648 | tf_op jit(solution)/shard_map/ppermute | solution.py:494
  22.7 11.7 %collective-permute-start.6 = (bf16[96,640]{1,0:T(8,128)(2,1)S(1)}, bf16[96,640]{1,0:T(8,128)(2,1)S(1)}, u32[]{:S(2)}, u32[]{:S(2)}) collective-permute-start(bf16[96,640]{1,0:T(8,128)(2,1)S(1)} %get-tuple-element.48), channel_id=1, source_target_pairs={{0,8},{4,12},{8,0},{12,4},{1,9},{5,13},{9,1},{13,5},{2,10},{6,14},... | collective-permute-start | bytes 368648 | tf_op jit(solution)/shard_map/ppermute | solution.py:494
  24.7 9.7 %collective-permute-start.7 = (bf16[96,640]{1,0:T(8,128)(2,1)S(1)}, bf16[96,640]{1,0:T(8,128)(2,1)S(1)}, u32[]{:S(2)}, u32[]{:S(2)}) collective-permute-start(bf16[96,640]{1,0:T(8,128)(2,1)S(1)} %get-tuple-element.49), channel_id=1, source_target_pairs={{0,4},{4,0},{8,12},{12,8},{1,5},{5,1},{9,13},{13,9},{2,6},{6,2},{1... | collective-permute-start | bytes 368648 | tf_op jit(solution)/shard_map/ppermute | solution.py:494
  27.5 1.2 %collective-permute-start.4 = (f32[1,640]{1,0:T(1,128)S(1)}, f32[1,640]{1,0:T(1,128)S(1)}, u32[]{:S(2)}, u32[]{:S(2)}) collective-permute-start(f32[1,640]{1,0:T(1,128)S(1)} %add.9), channel_id=1, source_target_pairs={{0,16},{16,0},{1,17},{17,1},{2,18},{18,2},{3,19},{19,3},{4,20},{20... | collective-permute-start | bytes 7688 | tf_op jit(solution)/shard_map/ppermute | solution.py:494
  28.7 6.7 %collective-permute-start.8 = (f32[1,640]{1,0:T(1,128)S(1)}, f32[1,640]{1,0:T(1,128)S(1)}, u32[]{:S(2)}, u32[]{:S(2)}) collective-permute-start(f32[1,640]{1,0:T(1,128)S(1)} %add.10.gain_ref), channel_id=1, source_target_pairs={{0,4},{4,0},{8,12},{12,8},{1,5},{5,1},{9,13},{13,9},{2,6},{6,2},{1... | collective-permute-start | bytes 7688 | tf_op jit(solution)/shard_map/ppermute | solution.py:494

commit v7 on v6

--- a/solution.py
+++ b/solution.py
@@ -228,7 +228,6 @@
 LOW = jnp.bfloat16
 WIDE = jnp.float32
 HEAD_GROUPS = ((0, 5),)
-LOAD_PIECES = 1
 PACK_VMEM = 65408 * 1024
 
 
@@ -263,30 +262,15 @@
     return jnp.concatenate([ref[rows, cols] for ref in refs], 0)
 
 
-def pack_kernel(top_step, groups, offsets_ref, k_hbm, v_hbm, *refs):
-    packed_refs, (k_ref, v_ref, sems) = refs[: len(groups)], refs[len(groups) :]
-    tokens, width = k_ref.shape
+def pack_kernel(top_step, groups, offsets_ref, k_ref, v_ref, *packed_refs):
+    tokens, width = k_ref.shape[1:]
     picked = sum(picked_counts(tokens, top_step))
-    step = tokens // LOAD_PIECES
-    copies = [
-        pltpu.make_async_copy(
-            source.at[0, pl.ds(piece * step, step)],
-            held.at[pl.ds(piece * step, step)],
-            sems.at[which, piece],
-        )
-        for which, (source, held) in enumerate(((k_hbm, k_ref), (v_hbm, v_ref)))
-        for piece in range(LOAD_PIECES)
+    every = [head_cols(head) for head in range(width // HEAD_DIM)]
+    picks = [
+        pick_matrix(offsets_ref, head, tokens, top_step, 0) for head in range(width // HEAD_DIM)
     ]
-    for copy in copies:
-        copy.start()
-    heads = range(width // HEAD_DIM)
-    picks = [pick_matrix(offsets_ref, head, tokens, top_step, 0) for head in heads]
-    for copy in copies:
-        copy.wait()
-    both = [
-        jnp.concatenate([k_ref[:, head_cols(head)], v_ref[:, head_cols(head)]], 1) for head in heads
-    ]
-    rows = [contract(picks[head], both[head], 1, 0).astype(LOW) for head in heads]
+    both = [jnp.concatenate([k_ref[0, :, cols], v_ref[0, :, cols]], 1) for cols in every]
+    rows = [contract(pick, block, 1, 0).astype(LOW) for pick, block in zip(picks, both)]
     for (first, last), packed_ref in zip(groups, packed_refs):
         for head in range(first, last):
             packed_ref[:picked, head_cols(head - first)] = rows[head][:, :HEAD_DIM]
@@ -472,21 +456,24 @@
             )
 
 
-def finish_kernel(top_step, groups, gain_ref, place_ref, dk_ref, dv_ref, *refs):
-    dk_out_ref, dv_out_ref, gain_out_ref = refs[PEERS * len(groups) :]
-    gain_out_ref[...] = gain_ref[...]
-    tokens = dk_ref.shape[0]
-    picked = sum(picked_counts(tokens, top_step))
+def finish_kernel(groups, place_ref, dk_ref, dv_ref, *refs):
+    dk_out_ref, dv_out_ref = refs[PEERS * len(groups) :]
+    picked = refs[0].shape[0] // 2
+    everyone = []
     for place, (first, last) in enumerate(groups):
         part_refs = refs[place * PEERS : (place + 1) * PEERS]
         for head in range(first, last):
-            cols = head_cols(head)
             own = head_cols(head - first)
             total = sum(part_ref[:, own].astype(WIDE) for part_ref in part_refs).astype(LOW)
-            both = jnp.concatenate([total[:picked], total[picked:]], 1)
-            placed = contract(place_ref[:, pl.ds(head * HEAD_DIM, picked)], both, 1, 0)
-            dk_out_ref[0, :, cols] = (dk_ref[:, cols] + placed[:, :HEAD_DIM]).astype(LOW)
-            dv_out_ref[0, :, cols] = (dv_ref[:, cols] + placed[:, HEAD_DIM:]).astype(LOW)
+            everyone.append(jnp.concatenate([total[:picked], total[picked:]], 1))
+    placed = [
+        contract(place_ref[:, pl.ds(head * HEAD_DIM, picked)], both, 1, 0)
+        for head, both in enumerate(everyone)
+    ]
+    for head, rows in enumerate(placed):
+        cols = head_cols(head)
+        dk_out_ref[0, :, cols] = (dk_ref[:, cols] + rows[:, :HEAD_DIM]).astype(LOW)
+        dv_out_ref[0, :, cols] = (dv_ref[:, cols] + rows[:, HEAD_DIM:]).astype(LOW)
 
 
 def across(block, axis, distance):
@@ -539,13 +526,7 @@
         (offsets, keys, values),
         [shape((2 * picked, group_width), LOW) for group_width in widths],
         1,
-        in_specs=[SMEM_SPEC, HBM_SPEC, HBM_SPEC],
         compiler_params=pltpu.CompilerParams(vmem_limit_bytes=PACK_VMEM),
-        scratch_shapes=[
-            pltpu.VMEM((tokens, width), LOW),
-            pltpu.VMEM((tokens, width), LOW),
-            pltpu.SemaphoreType.DMA((2, LOAD_PIECES)),
-        ],
     )
     packed_peers = [to_peers([block] * PEERS) for block in packed]
     row_scratch, gain_scratch = pltpu.VMEM((tokens, width), LOW), pltpu.VMEM((1, width), WIDE)
@@ -589,7 +570,7 @@
     gain_part = jnp.concatenate(gain_parts, 1) if len(groups) > 1 else gain_parts[0]
     gain_grad = gain_part + across(gain_part, "ctx", 2)
     gain_grad = gain_grad + across(gain_grad, "dp", 1)
-    gain_rest = across(gain_grad, "ctx", 1)
+    gain_grad = (gain_grad + across(gain_grad, "ctx", 1)).reshape(width)
     attended, query_grad, score_grad, soft = call(
         bind(query_grad_kernel, top_step, groups),
         "query_grad",
@@ -606,14 +587,13 @@
         [wide_block, wide_block],
         20,
     )
-    key_grad, value_grad, gain_grad = call(
-        bind(finish_kernel, top_step, groups),
+    key_grad, value_grad = call(
+        bind(finish_kernel, groups),
         "finish",
-        (gain_grad, place, dk_base, dv_base, *returned),
-        [row_block, row_block, shape((1, width), WIDE)],
+        (place, dk_base, dv_base, *returned),
+        [row_block, row_block],
         1,
     )
-    gain_grad = (gain_grad + gain_rest).reshape(width)
     return attended, query_grad, key_grad, value_grad, gain_grad
 
 

time: 36.2 us -> 34.7 us (0.959)
  starting transfers between devices: 11.9 us -> 10.2 us
  waiting for transfers between devices: 9.12 us -> 10.1 us
  Pallas kernels: 9.96 us -> 9.16 us
    ppermute x9, starting transfers between devices: 11.9 us -> 10.2 us  [across(): return lax.ppermute(block, axis, route)]
    ppermute x9, waiting for transfers between devices: 9.12 us -> 10.1 us  [across(): return lax.ppermute(block, axis, route)]
    pallas_call x6, Pallas kernels: 9.96 us -> 9.16 us  [call(): pl.pallas_call(kernel, out_shape=results, out_specs=[VMEM_SPEC] * len(res...]
  transfers between devices with their start and end apart: 9 -> 9, of which waited for: 4 -> 4; matrix products, arithmetic and copies ran while one was open for 0% -> 2% of each run, Pallas kernels for 17% -> 15%
where the time goes in v7:
time: 34.7 us; the launch traced here: 34.5 us
  starting transfers between devices  10.2 us (29%)
  waiting for transfers between devices  10.1 us (29%)
  Pallas kernels  9.16 us (26%)
  local copies, waits for them, and re-layouts  3.67 us (11%)
  between operations  0.73 us (2%)
  other arithmetic  0.62 us (2%)
    ppermute x9, starting transfers between devices, across(): return lax.ppermute(block, axis, route)  10.2 us
    ppermute x9, waiting for transfers between devices, across(): return lax.ppermute(block, axis, route)  10.1 us
    pallas_call x6, Pallas kernels, call(): pl.pallas_call(kernel, out_shape=results, out_specs=[VMEM_SPEC] * len(res...  9.16 us
    unnamed x16, local copies, waits for them, and re-layouts  3.67 us
  transfers between devices with their start and end apart: 9, of which 4 were waited for; matrix products, arithmetic and copies ran while one was open for 2% of the time, Pallas kernels for 15%

profile of v7, /device:TPU:0, one launch (start us, length us, event | category | flops | bytes accessed | tf_op | source)
XLA Modules:
  0.0 34.5 jit_solution(6218729191214198290)
XLA Ops:
  0.6 0.0 copy-start.7
  0.6 1.8 %pack.1 = bf16[96,640]{1,0:T(8,128)(2,1)} custom-call(s32[2,5]{1,0:T(2,128)} %offsets_ref.3, bf16[1,128,640]{2,1,0:T(8,128)(2,1)} %refs_0_.3, bf16[1,128,640]{2,1,0:T(8,128)(2,1)} %refs_1_.3), custom_call_target="tpu_custom_call" | custom-call | flops 1000000000 | tf_op jit(solution)/shard_map/pack/pallas_call | solution.py:498
  2.5 5.0 %collective-permute-start.2 = (bf16[96,640]{1,0:T(8,128)(2,1)}, bf16[96,640]{1,0:T(8,128)(2,1)S(1)}, u32[]{:S(2)}, u32[]{:S(2)}) collective-permute-start(bf16[96,640]{1,0:T(8,128)(2,1)} %pack.1), channel_id=1, source_target_pairs={{0,12},{4,8},{8,4},{12,0},{1,13},{5,9},{9,5},{13,1},{2,14},{6,10},... | collective-permute-start | bytes 368648 | tf_op jit(solution)/shard_map/ppermute | solution.py:481
  7.5 0.0 collective-permute-start.1
  7.5 0.6 %collective-permute-start = (bf16[96,640]{1,0:T(8,128)(2,1)}, bf16[96,640]{1,0:T(8,128)(2,1)S(1)}, u32[]{:S(2)}, u32[]{:S(2)}) collective-permute-start(bf16[96,640]{1,0:T(8,128)(2,1)} %pack.1), channel_id=1, source_target_pairs={{0,4},{4,0},{8,12},{12,8},{1,5},{5,1},{9,13},{13,9},{2,6},{6,2},{1... | collective-permute-start | bytes 368648 | tf_op jit(solution)/shard_map/ppermute | solution.py:481
  8.1 0.0 copy-done.7
  8.1 0.0 copy-start
  8.1 0.9 %copy-done = bf16[1,128,640]{2,1,0:T(8,128)(2,1)S(1)} copy-done((bf16[1,128,640]{2,1,0:T(8,128)(2,1)S(1)}, bf16[1,128,640]{2,1,0:T(8,128)(2,1)}, u32[]{:S(2)}) %copy-start) | copy-done | bytes 163864
  9.0 0.9 %copy-done.1 = bf16[1,128,640]{2,1,0:T(8,128)(2,1)S(1)} copy-done((bf16[1,128,640]{2,1,0:T(8,128)(2,1)S(1)}, bf16[1,128,640]{2,1,0:T(8,128)(2,1)}, u32[]{:S(2)}) %copy-start.1) | copy-done | bytes 163864
  10.0 0.9 %copy-done.2 = bf16[1,128,640]{2,1,0:T(8,128)(2,1)S(1)} copy-done((bf16[1,128,640]{2,1,0:T(8,128)(2,1)S(1)}, bf16[1,128,640]{2,1,0:T(8,128)(2,1)}, u32[]{:S(2)}) %copy-start.2) | copy-done | bytes 163864
  10.9 0.9 %copy-done.4 = bf16[1,128,640]{2,1,0:T(8,128)(2,1)S(1)} copy-done((bf16[1,128,640]{2,1,0:T(8,128)(2,1)S(1)}, bf16[1,128,640]{2,1,0:T(8,128)(2,1)}, u32[]{:S(2)}) %copy-start.4) | copy-done | bytes 163864
  11.8 2.6 %base.1 = (bf16[128,640]{1,0:T(8,128)(2,1)S(1)}, f32[128,640]{1,0:T(8,128)S(1)}, f32[128,640]{1,0:T(8,128)S(1)}, bf16[128,640]{1,0:T(8,128)(2,1)S(1)}, f32[1,640...) custom-call(s32[2,5]{1,0:T(2,128)S(1)} %copy-done.6, bf16[1,128,640]{2,1,0:T(8,128)(2,1)S(1)} %copy-done, ...), custom_call_target="tpu_custom_call" | custom-call | flops 2000000000 | tf_op jit(solution)/shard_map/base/pallas_call | solution.py:498
  14.4 0.0 collective-permute-done.2.refs_2_.refs_10_
  14.4 3.7 %collective-permute-done.1.refs_1_.refs_9_ = bf16[96,640]{1,0:T(8,128)(2,1)S(1)} collective-permute-done((bf16[96,640]{1,0:T(8,128)(2,1)}, bf16[96,640]{1,0:T(8,128)(2,1)S(1)}, u32[]{:S(2)}, u32[]{:S(2)}) %collective-permute-start.1) | collective-permute-done | bytes 122912 | tf_op jit(solution)/shard_map/ppermute | solution.py:481
  18.1 0.0 collective-permute-done.refs_0_.refs_8_
  18.1 1.2 %attend.1 = (f32[1,640]{1,0:T(1,128)S(1)}, f32[128,640]{1,0:T(8,128)S(1)}, bf16[128,640]{1,0:T(8,128)(2,1)S(1)}, bf16[144,640]{1,0:T(8,128)(2,1)S(1)}, f32[16,12...) custom-call(bf16[128,640]{1,0:T(8,128)(2,1)S(1)} %get-tuple-element.29.q_, ...), custom_call_target="tpu_custom_call" | custom-call | flops 5000000000 | tf_op jit(solution)/shard_map/attend/pallas_call | solution.py:498
  19.3 0.1 collective-permute-start.6
  19.4 2.4 %collective-permute-start.3 = (bf16[96,640]{1,0:T(8,128)(2,1)S(1)}, bf16[96,640]{1,0:T(8,128)(2,1)S(1)}, u32[]{:S(2)}, u32[]{:S(2)}) collective-permute-start(bf16[96,640]{1,0:T(8,128)(2,1)S(1)} %get-tuple-element.45), channel_id=1, source_target_pairs={{0,12},{4,8},{8,4},{12,0},{1,13},{5,9},{9,5},{13,1},{2,14},{6,10},... | collective-permute-start | bytes 368648 | tf_op jit(solution)/shard_map/ppermute | solution.py:481
  21.8 2.0 %collective-permute-start.4 = (bf16[96,640]{1,0:T(8,128)(2,1)S(1)}, bf16[96,640]{1,0:T(8,128)(2,1)S(1)}, u32[]{:S(2)}, u32[]{:S(2)}) collective-permute-start(bf16[96,640]{1,0:T(8,128)(2,1)S(1)} %get-tuple-element.46), channel_id=1, source_target_pairs={{0,8},{4,12},{8,0},{12,4},{1,9},{5,13},{9,1},{13,5},{2,10},{6,14},... | collective-permute-start | bytes 368648 | tf_op jit(solution)/shard_map/ppermute | solution.py:481
  23.8 0.0 collective-permute-start.5
  23.8 2.8 %collective-permute-done.6 = f32[1,640]{1,0:T(1,128)S(1)} collective-permute-done((f32[1,640]{1,0:T(1,128)S(1)}, f32[1,640]{1,0:T(1,128)S(1)}, u32[]{:S(2)}, u32[]{:S(2)}) %collective-permute-start.6) | collective-permute-done | bytes 2592 | tf_op jit(solution)/shard_map/ppermute | solution.py:481
  26.6 0.0 collective-permute-start.7
  26.7 2.3 %query_grad.1 = (bf16[1,128,640]{2,1,0:T(8,128)(2,1)}, bf16[1,128,640]{2,1,0:T(8,128)(2,1)}, bf16[128,640]{1,0:T(8,128)(2,1)S(1)}, bf16[128,640]{1,0:T(8,128)(2,1)S(1)}) custom-call(bf16[1,128,640]{2,1,0:T(8,128)(2,1)S(1)} %copy-done.3, bf16[1,128,640]{2,1,0:T(8,128)(2,1)S(1)} %copy-done.5, f32[1,640]{1,0:T(1,128)S(1)} %reshape.16.refs_4_.refs_2_, ...), custom_call_target="tpu_custom_call" | custom-call | flops 20000000000 | tf_op jit(solution)/shard_map/query_grad/pallas_call | solution.py:498
  29.0 0.0 collective-permute-done.7
  29.0 0.1 collective-permute-start.8
  29.1 0.3 key_grad.1
  29.3 3.5 %collective-permute-done.8 = f32[1,640]{1,0:T(1,128)S(1)} collective-permute-done((f32[1,640]{1,0:T(1,128)S(1)}, f32[1,640]{1,0:T(1,128)S(1)}, u32[]{:S(2)}, u32[]{:S(2)}) %collective-permute-start.8) | collective-permute-done | bytes 2592 | tf_op jit(solution)/shard_map/ppermute | solution.py:481
  32.8 0.6 %add_reduce_fusion = f32[640]{0:T(1024)} fusion(f32[1,640]{1,0:T(1,128)S(1)} %add.10, f32[1,640]{1,0:T(1,128)S(1)} %collective-permute-done.8), kind=kLoop, calls=%fused_computation | loop fusion | flops 640 | bytes 7680 | tf_op jit(solution)/shard_map/add | solution.py:573
  33.4 0.0 collective-permute-done.3.refs_0_
  33.4 0.1 collective-permute-done.4.refs_1_
  33.5 0.0 collective-permute-done.5.refs_2_
  33.5 1.0 %finish.1 = (bf16[1,128,640]{2,1,0:T(8,128)(2,1)}, bf16[1,128,640]{2,1,0:T(8,128)(2,1)}) custom-call(bf16[128,640]{1,0:T(8,128)(2,1)S(1)} %get-tuple-element.40.place_ref, f32[128,640]{1,0:T(8,128)S(1)} %get-tuple-element.43.dk_ref, f32[128,640]{1,0:T(8,128)S(1)} %get-tuple-element.44.dv_ref, bf16[96,640]{1,0:T(8,128)(2,1)S(1)} %collective-permute-done.3.refs_0_, ...), custom_call_target="tpu_custom_call" | custom-call | flops 1000000000 | tf_op jit(solution)/shard_map/finish/pallas_call | solution.py:498
  (12 shorter events, 0.0 us)
Async XLA Ops:
  0.6 7.5 %copy-start.7 = (f32[640]{0:T(1024)S(1)}, f32[640]{0:T(1024)}, u32[]{:S(2)}) copy-start(f32[640]{0:T(1024)} %param.10) | copy-start | bytes 7684
  2.5 5.6 %copy-start.6 = (s32[2,5]{1,0:T(2,128)S(1)}, s32[2,5]{1,0:T(2,128)}, u32[]{:S(2)}) copy-start(s32[2,5]{1,0:T(2,128)} %offsets_ref.3) | copy-start | bytes 124
  2.5 11.9 %collective-permute-start.2 = (bf16[96,640]{1,0:T(8,128)(2,1)}, bf16[96,640]{1,0:T(8,128)(2,1)S(1)}, u32[]{:S(2)}, u32[]{:S(2)}) collective-permute-start(bf16[96,640]{1,0:T(8,128)(2,1)} %pack.1), channel_id=1, source_target_pairs={{0,12},{4,8},{8,4},{12,0},{1,13},{5,9},{9,5},{13,1},{2,14},{6,10},... | collective-permute-start | bytes 368648 | tf_op jit(solution)/shard_map/ppermute | solution.py:481
  7.5 10.6 %collective-permute-start.1 = (bf16[96,640]{1,0:T(8,128)(2,1)}, bf16[96,640]{1,0:T(8,128)(2,1)S(1)}, u32[]{:S(2)}, u32[]{:S(2)}) collective-permute-start(bf16[96,640]{1,0:T(8,128)(2,1)} %pack.1), channel_id=1, source_target_pairs={{0,8},{4,12},{8,0},{12,4},{1,9},{5,13},{9,1},{13,5},{2,10},{6,14},... | collective-permute-start | bytes 368648 | tf_op jit(solution)/shard_map/ppermute | solution.py:481
  7.5 10.6 %collective-permute-start = (bf16[96,640]{1,0:T(8,128)(2,1)}, bf16[96,640]{1,0:T(8,128)(2,1)S(1)}, u32[]{:S(2)}, u32[]{:S(2)}) collective-permute-start(bf16[96,640]{1,0:T(8,128)(2,1)} %pack.1), channel_id=1, source_target_pairs={{0,4},{4,0},{8,12},{12,8},{1,5},{5,1},{9,13},{13,9},{2,6},{6,2},{1... | collective-permute-start | bytes 368648 | tf_op jit(solution)/shard_map/ppermute | solution.py:481
  8.1 0.9 %copy-start = (bf16[1,128,640]{2,1,0:T(8,128)(2,1)S(1)}, bf16[1,128,640]{2,1,0:T(8,128)(2,1)}, u32[]{:S(2)}) copy-start(bf16[1,128,640]{2,1,0:T(8,128)(2,1)} %refs_0_.2) | copy-start | bytes 491524
  9.0 0.9 %copy-start.1 = (bf16[1,128,640]{2,1,0:T(8,128)(2,1)S(1)}, bf16[1,128,640]{2,1,0:T(8,128)(2,1)}, u32[]{:S(2)}) copy-start(bf16[1,128,640]{2,1,0:T(8,128)(2,1)} %refs_3_.1) | copy-start | bytes 491524
  10.0 0.9 %copy-start.2 = (bf16[1,128,640]{2,1,0:T(8,128)(2,1)S(1)}, bf16[1,128,640]{2,1,0:T(8,128)(2,1)}, u32[]{:S(2)}) copy-start(bf16[1,128,640]{2,1,0:T(8,128)(2,1)} %refs_0_.3) | copy-start | bytes 491524
  10.9 0.9 %copy-start.4 = (bf16[1,128,640]{2,1,0:T(8,128)(2,1)S(1)}, bf16[1,128,640]{2,1,0:T(8,128)(2,1)}, u32[]{:S(2)}) copy-start(bf16[1,128,640]{2,1,0:T(8,128)(2,1)} %refs_1_.3) | copy-start | bytes 491524
  18.1 8.5 %copy-start.3 = (bf16[1,128,640]{2,1,0:T(8,128)(2,1)S(1)}, bf16[1,128,640]{2,1,0:T(8,128)(2,1)}, u32[]{:S(2)}) copy-start(bf16[1,128,640]{2,1,0:T(8,128)(2,1)} %refs_0_.3) | copy-start | bytes 491524
  18.1 8.5 %copy-start.5 = (bf16[1,128,640]{2,1,0:T(8,128)(2,1)S(1)}, bf16[1,128,640]{2,1,0:T(8,128)(2,1)}, u32[]{:S(2)}) copy-start(bf16[1,128,640]{2,1,0:T(8,128)(2,1)} %refs_1_.3) | copy-start | bytes 491524
  19.3 7.3 %collective-permute-start.6 = (f32[1,640]{1,0:T(1,128)S(1)}, f32[1,640]{1,0:T(1,128)S(1)}, u32[]{:S(2)}, u32[]{:S(2)}) collective-permute-start(f32[1,640]{1,0:T(1,128)S(1)} %get-tuple-element.50), channel_id=1, source_target_pairs={{0,8},{4,12},{8,0},{12,4},{1,9},{5,13},{9,1},{13,5},{2,10},{6,14},... | collective-permute-start | bytes 7688 | tf_op jit(solution)/shard_map/ppermute | solution.py:481
  19.4 14.0 %collective-permute-start.3 = (bf16[96,640]{1,0:T(8,128)(2,1)S(1)}, bf16[96,640]{1,0:T(8,128)(2,1)S(1)}, u32[]{:S(2)}, u32[]{:S(2)}) collective-permute-start(bf16[96,640]{1,0:T(8,128)(2,1)S(1)} %get-tuple-element.45), channel_id=1, source_target_pairs={{0,12},{4,8},{8,4},{12,0},{1,13},{5,9},{9,5},{13,1},{2,14},{6,10},... | collective-permute-start | bytes 368648 | tf_op jit(solution)/shard_map/ppermute | solution.py:481
  21.8 11.7 %collective-permute-start.4 = (bf16[96,640]{1,0:T(8,128)(2,1)S(1)}, bf16[96,640]{1,0:T(8,128)(2,1)S(1)}, u32[]{:S(2)}, u32[]{:S(2)}) collective-permute-start(bf16[96,640]{1,0:T(8,128)(2,1)S(1)} %get-tuple-element.46), channel_id=1, source_target_pairs={{0,8},{4,12},{8,0},{12,4},{1,9},{5,13},{9,1},{13,5},{2,10},{6,14},... | collective-permute-start | bytes 368648 | tf_op jit(solution)/shard_map/ppermute | solution.py:481
  23.8 9.7 %collective-permute-start.5 = (bf16[96,640]{1,0:T(8,128)(2,1)S(1)}, bf16[96,640]{1,0:T(8,128)(2,1)S(1)}, u32[]{:S(2)}, u32[]{:S(2)}) collective-permute-start(bf16[96,640]{1,0:T(8,128)(2,1)S(1)} %get-tuple-element.47), channel_id=1, source_target_pairs={{0,4},{4,0},{8,12},{12,8},{1,5},{5,1},{9,13},{13,9},{2,6},{6,2},{1... | collective-permute-start | bytes 368648 | tf_op jit(solution)/shard_map/ppermute | solution.py:481
  26.6 2.3 %collective-permute-start.7 = (f32[1,640]{1,0:T(1,128)S(1)}, f32[1,640]{1,0:T(1,128)S(1)}, u32[]{:S(2)}, u32[]{:S(2)}) collective-permute-start(f32[1,640]{1,0:T(1,128)S(1)} %add.9), channel_id=1, source_target_pairs={{0,16},{16,0},{1,17},{17,1},{2,18},{18,2},{3,19},{19,3},{4,20},{20... | collective-permute-start | bytes 7688 | tf_op jit(solution)/shard_map/ppermute | solution.py:481
  29.0 3.9 %collective-permute-start.8 = (f32[1,640]{1,0:T(1,128)S(1)}, f32[1,640]{1,0:T(1,128)S(1)}, u32[]{:S(2)}, u32[]{:S(2)}) collective-permute-start(f32[1,640]{1,0:T(1,128)S(1)} %add.10), channel_id=1, source_target_pairs={{0,4},{4,0},{8,12},{12,8},{1,5},{5,1},{9,13},{13,9},{2,6},{6,2},{1... | collective-permute-start | bytes 7688 | tf_op jit(solution)/shard_map/ppermute | solution.py:481

commit v8 on v0

--- a/solution.py
+++ b/solution.py
@@ -1,8 +1,11 @@
+import functools
 import math
 
 import jax
 import jax.numpy as jnp
 from jax import lax
+from jax.experimental import pallas as pl
+from jax.experimental.pallas import tpu as pltpu
 from jax.sharding import PartitionSpec as P
 
 HEAD_DIM = 128
@@ -79,7 +82,7 @@
     return jnp.einsum("hqk,khe->qhe", score_grad, k_rows, preferred_element_type=jnp.float32)
 
 
-def shards(queries, keys, values, grad_y, out_gain, offsets):
+def general_shards(queries, keys, values, grad_y, out_gain, offsets):
     tokens = queries.shape[1]
     flat_width = queries.shape[2]
     head_count = flat_width // HEAD_DIM
@@ -216,6 +219,566 @@
     )
 
 
+VMEM_SPEC = pl.BlockSpec(memory_space=pltpu.VMEM)
+SMEM_SPEC = pl.BlockSpec(memory_space=pltpu.SMEM)
+PEERS = SPAN - 1
+OWNED = SPAN
+TILE = 8
+STAT_TILES = 2 * TILE
+PIECES = 3
+NEVER = -1e30
+LOW = jnp.bfloat16
+WIDE = jnp.float32
+PACK_VMEM = 65408 * 1024
+PLAIN_VMEM = 16 * 1024 * 1024
+
+
+def contract(left, right, left_dim, right_dim):
+    return lax.dot_general(
+        left, right, (((left_dim,), (right_dim,)), ((), ())), preferred_element_type=WIDE
+    )
+
+
+def head_cols(head):
+    return pl.ds(head * HEAD_DIM, HEAD_DIM)
+
+
+def picked_counts(tokens, top_step):
+    return tokens // top_step, tokens // R1
+
+
+def pick_matrix(offsets_ref, head, tokens, top_step, picked_axis):
+    top_rows, mid_rows = picked_counts(tokens, top_step)
+    shape = (top_rows + mid_rows, tokens) if picked_axis == 0 else (tokens, top_rows + mid_rows)
+    row = lax.broadcasted_iota(jnp.int32, shape, picked_axis)
+    position = lax.broadcasted_iota(jnp.int32, shape, 1 - picked_axis)
+    wanted = jnp.where(
+        row < top_rows,
+        row * top_step + offsets_ref[1, head],
+        (row - top_rows) * R1 + offsets_ref[0, head],
+    )
+    return jnp.where(position == wanted, 1.0, 0.0).astype(LOW)
+
+
+def slot_matrix(offset, step, slot, tokens):
+    count = tokens // step
+    position = lax.broadcasted_iota(jnp.int32, (tokens, tokens), 0)
+    index = lax.broadcasted_iota(jnp.int32, (tokens, tokens), 1) - slot * count
+    inside = (index >= 0) & (index < count)
+    return jnp.where(inside & (position == index * step + offset), 1.0, 0.0).astype(LOW)
+
+
+def hit_row(offset, step, tokens):
+    position = lax.broadcasted_iota(jnp.int32, (1, tokens), 1)
+    return jnp.where(position % step == offset, 1.0, 0.0)
+
+
+def piece_rows(row):
+    pieces = []
+    for _ in range(PIECES):
+        piece = row.astype(LOW).astype(WIDE)
+        pieces.append(piece)
+        row = row - piece
+    return jnp.concatenate(pieces + [jnp.zeros((TILE - PIECES, row.shape[1]), WIDE)], 0)
+
+
+def joined_row(rows, first):
+    total = rows[first : first + 1]
+    for piece in range(1, PIECES):
+        total = total + rows[first + piece : first + piece + 1]
+    return total
+
+
+def gain_row_of(ones, product):
+    high = product.astype(LOW)
+    rest = (product - high.astype(WIDE)).astype(LOW)
+    return (contract(ones, high, 1, 1) + contract(ones, rest, 1, 1))[:1]
+
+
+def column_mean(block):
+    return jnp.mean(block, axis=0, keepdims=True)
+
+
+def norm_backward(attn, grad_norm):
+    inv_rms = lax.rsqrt(column_mean(attn * attn) + EPS)
+    normed = attn * inv_rms
+    product = grad_norm * normed
+    grad_attn = inv_rms * (grad_norm - normed * column_mean(product))
+    inner = jnp.sum(grad_attn * attn, axis=0, keepdims=True)
+    return normed, product, grad_attn.astype(LOW), inner
+
+
+def nearest_first(refs):
+    return [refs[0], *refs[:0:-1]]
+
+
+def pack_kernel(top_step, offsets_ref, q_ref, k_ref, v_ref, grad_ref, *refs):
+    payload_refs, (expo_ref, out_ref, stats_ref, held_ref) = refs[:SPAN], refs[SPAN:]
+    tokens, width = q_ref.shape[1:]
+    heads = range(width // HEAD_DIM)
+    owned = range(OWNED)
+    me = lax.axis_index("ctx")
+    picked = sum(picked_counts(tokens, top_step))
+    score_scale = 1.0 / math.sqrt(HEAD_DIM)
+    q_rows, k_rows, v_rows, grad_rows = [
+        [ref[0, :, head_cols(head)] for head in heads] for ref in (q_ref, k_ref, v_ref, grad_ref)
+    ]
+    picks = [pick_matrix(offsets_ref, head, tokens, top_step, 0) for head in heads]
+    scores = [contract(k_rows[head], q_rows[head], 1, 1) * score_scale for head in heads]
+    moved = [
+        contract(
+            picks[head],
+            jnp.concatenate([q_rows[head], k_rows[head], v_rows[head], grad_rows[head]], 1),
+            1,
+            0,
+        ).astype(LOW)
+        for head in owned
+    ]
+    shared = [
+        contract(picks[head], jnp.concatenate([k_rows[head], v_rows[head]], 1), 1, 0).astype(LOW)
+        for head in heads[OWNED:]
+    ]
+    top_scores = [jnp.max(block, axis=0, keepdims=True) for block in scores]
+    expos = [jnp.exp(scores[head] - top_scores[head]) for head in heads]
+    for head in heads[OWNED:]:
+        key_row = lax.broadcasted_iota(jnp.int32, (tokens, 1), 0)
+        times = 1.0
+        for level, step in ((0, R1), (1, top_step)):
+            offset = offsets_ref[level, head]
+            hit_column = jnp.where(key_row % step == offset, 1.0, 0.0)
+            times = times + hit_column * hit_row(offset, step, tokens)
+        expos[head] = times * expos[head]
+    expo_lows = [expo.astype(LOW) for expo in expos]
+    outs = [contract(v_rows[head], expo_lows[head], 0, 0) for head in heads]
+    totals = [jnp.sum(expo, axis=0, keepdims=True) for expo in expos]
+    for head in heads:
+        expo_ref[:, head_cols(head)] = expo_lows[head]
+        stats_ref[head : head + 1, :] = top_scores[head]
+        stats_ref[TILE + head : TILE + head + 1, :] = totals[head]
+    for head in owned:
+        outs[head] = outs[head] * (1.0 / totals[head])
+    picked_outs = [contract(picks[head], outs[head].astype(LOW), 1, 1).astype(LOW) for head in owned]
+    for head in heads:
+        out_ref[:, head_cols(head)] = outs[head]
+    for head in owned:
+        pieces = piece_rows(top_scores[head] + jnp.log(totals[head])).astype(LOW)
+        slot = me ^ head
+        stat_rows = [
+            contract(pieces, slot_matrix(offsets_ref[level, head], step, slot, tokens), 1, 0)
+            for level, step in ((1, top_step), (0, R1))
+        ]
+        blocks = [moved[head][:, block * HEAD_DIM : (block + 1) * HEAD_DIM] for block in range(4)]
+        blocks.append(picked_outs[head])
+        blocks += [shared[0][:, :HEAD_DIM], shared[0][:, HEAD_DIM:]]
+        blocks.append(jnp.concatenate(stat_rows, 0).astype(LOW))
+        held_ref[head] = jnp.concatenate(blocks, 0)
+    for distance, payload_ref in enumerate(payload_refs):
+        payload_ref[...] = held_ref[me ^ distance]
+
+
+def prepare_kernel(top_step, offsets_ref, grad_ref, gain_ref, out_ref, *refs):
+    grad_norm_ref, gain_part_ref, place_ref, slots_ref = refs
+    tokens, width = grad_ref.shape[1:]
+    heads = range(width // HEAD_DIM)
+    me = lax.axis_index("ctx")
+    picked = sum(picked_counts(tokens, top_step))
+    top_rows = tokens // top_step
+    ones = jnp.ones((TILE, tokens), LOW)
+    column = lax.broadcasted_iota(jnp.int32, (tokens, picked), 1)
+    gain_part_ref[...] = jnp.zeros(gain_part_ref.shape, WIDE)
+    grad_norms = [
+        (grad_ref[0, :, head_cols(head)].astype(WIDE) * gain_ref[:, head_cols(head)]).T
+        for head in heads
+    ]
+    for head in heads:
+        cols = head_cols(head)
+        grad_norm_ref[:, cols] = grad_norms[head]
+        picks = pick_matrix(offsets_ref, head, tokens, top_step, 1)
+        place_ref[:, pl.ds(head * HEAD_DIM, picked)] = picks
+    for head in range(OWNED):
+        cols = head_cols(head)
+        mid_offset, top_offset = offsets_ref[0, head], offsets_ref[1, head]
+        seen = jnp.maximum(
+            hit_row(top_offset, top_step, tokens), hit_row(mid_offset, R1, tokens)
+        )
+        attn = out_ref[:, cols]
+        normed = attn * lax.rsqrt(column_mean(attn * attn) + EPS)
+        product = grad_norms[head] * normed * (1.0 - seen)
+        gain_part_ref[:, cols] = gain_row_of(ones, product) / gain_ref[:, cols]
+        both = mid_offset % top_step == top_offset
+        kept = jnp.where(column < top_rows, 1.0, jnp.where(both, 0.0, 1.0)).astype(LOW)
+        picks = pick_matrix(offsets_ref, head, tokens, top_step, 1)
+        place_ref[:, pl.ds(width + head * HEAD_DIM, picked)] = picks * kept
+        for index, (offset, step) in enumerate(((top_offset, top_step), (mid_offset, R1))):
+            slots_ref[:, head_cols(2 * head + index)] = slot_matrix(
+                offset, step, me ^ head, tokens
+            )
+
+
+def owner_kernel(top_step, offsets_ref, q_ref, gain_ref, out_ref, grad_norm_ref, *refs):
+    stats_ref, gain_base_ref = refs[:2]
+    payload_refs, refs = nearest_first(refs[2 : 2 + SPAN]), refs[2 + SPAN :]
+    gain_part_ref, normed_ref, grad_low_ref, score_grad_ref, kept_ref = refs[:5]
+    return_refs = refs[5:]
+    tokens = q_ref.shape[1]
+    heads = q_ref.shape[2] // HEAD_DIM
+    top_rows, mid_rows = picked_counts(tokens, top_step)
+    picked = top_rows + mid_rows
+    top_all, mid_all = SPAN * top_rows, SPAN * mid_rows
+    queries = top_all + mid_all
+    score_scale = 1.0 / math.sqrt(HEAD_DIM)
+    me = lax.axis_index("ctx")
+    ones = jnp.ones((TILE, tokens), LOW)
+
+    def by_level(block):
+        start = block * picked
+        return jnp.concatenate(
+            [ref[start : start + top_rows] for ref in payload_refs]
+            + [ref[start + top_rows : start + picked] for ref in payload_refs],
+            0,
+        )
+
+    def per_level(top_row, mid_row):
+        return jnp.concatenate(
+            [
+                jnp.broadcast_to(top_row, (top_all, queries)),
+                jnp.broadcast_to(mid_row, (mid_all, queries)),
+            ],
+            0,
+        )
+
+    q_rows, k_rows, v_rows, grad_rows, base_rows = [by_level(block) for block in range(5)]
+    stat_start = 7 * picked
+    stat_rows = sum(
+        ref[stat_start : stat_start + STAT_TILES].astype(WIDE) for ref in payload_refs
+    )
+    base_log = jnp.concatenate(
+        [joined_row(stat_rows, 0), joined_row(stat_rows, TILE)[:, :mid_all]], 1
+    )
+    gain_row = jnp.zeros((1, HEAD_DIM), WIDE)
+    for head in range(OWNED):
+        gain_row = gain_row + jnp.where(me == head, 1.0, 0.0) * gain_ref[:, head_cols(head)]
+    mid_offset, top_offset = offsets_ref[0, me], offsets_ref[1, me]
+    both = mid_offset % top_step == top_offset
+    lane = lax.broadcasted_iota(jnp.int32, (1, queries), 1)
+    is_top = jnp.where(lane < top_all, 1.0, 0.0)
+    top_in_mid = jnp.where(((lane % top_rows) * top_step + top_offset) % R1 == mid_offset, 1.0, 0.0)
+    both_flag = jnp.where(both, 1.0, 0.0)
+    sees_top = is_top + (1.0 - is_top) * both_flag
+    sees_mid = is_top * top_in_mid + (1.0 - is_top)
+    bias = per_level((1.0 - sees_top) * NEVER, (1.0 - sees_mid) * NEVER)
+    same_level = per_level(is_top, 1.0 - is_top)
+    last = heads - 1
+    cols = head_cols(last)
+    peers = payload_refs[1:]
+    q_last = q_ref[0, :, cols]
+    k_peers = jnp.concatenate([ref[5 * picked : 6 * picked] for ref in peers], 0)
+    v_peers = jnp.concatenate([ref[6 * picked : 7 * picked] for ref in peers], 0)
+    last_biases = [
+        jnp.broadcast_to((1.0 - hit_row(offsets_ref[level, last], step, tokens)) * NEVER, shape)
+        for level, step, shape in (
+            (1, top_step, (top_rows, tokens)),
+            (0, R1, (mid_rows, tokens)),
+        )
+    ]
+    scores = contract(k_rows, q_rows, 1, 1) * score_scale + bias
+    scores_last = contract(k_peers, q_last, 1, 1) * score_scale + jnp.concatenate(
+        last_biases * PEERS, 0
+    )
+    base_attn = base_rows.astype(WIDE).T
+    grad_norm = (grad_rows.astype(WIDE) * gain_row).T
+    top_score = jnp.maximum(base_log, jnp.max(scores, axis=0, keepdims=True))
+    base_top, base_total = stats_ref[last : last + 1, :], stats_ref[TILE + last : TILE + last + 1, :]
+    top_last = jnp.maximum(base_top, jnp.max(scores_last, axis=0, keepdims=True))
+    expo = jnp.exp(scores - top_score)
+    expo_last = jnp.exp(scores_last - top_last)
+    factor = jnp.exp(base_log - top_score)
+    factor_last = jnp.exp(base_top - top_last)
+    total = factor + jnp.sum(expo, axis=0, keepdims=True)
+    total_last = factor_last * base_total + jnp.sum(expo_last, axis=0, keepdims=True)
+    inv_total, inv_last = 1.0 / total, 1.0 / total_last
+    soft, soft_last = expo * inv_total, expo_last * inv_last
+    soft_low, soft_last_low = soft.astype(LOW), soft_last.astype(LOW)
+    factor_last = factor_last * inv_last
+    attn = (factor * inv_total) * base_attn + contract(v_rows, soft_low, 0, 0)
+    attn_last = factor_last * out_ref[:, cols] + contract(v_peers, soft_last_low, 0, 0)
+    _, product, grad_low, inner = norm_backward(attn, grad_norm)
+    normed_last, product_last, grad_last_low, inner_last = norm_backward(
+        attn_last, grad_norm_ref[:, cols]
+    )
+    prob_grad = contract(v_rows, grad_low, 1, 0)
+    prob_grad_last = contract(v_peers, grad_last_low, 1, 0)
+    soft = soft * same_level
+    score_grad = (soft * (prob_grad - inner) * score_scale).astype(LOW)
+    score_grad_last = (soft_last * (prob_grad_last - inner_last) * score_scale).astype(LOW)
+    dk = contract(score_grad, q_rows, 1, 0).astype(LOW)
+    dk_last = contract(score_grad_last, q_last, 1, 0).astype(LOW)
+    dv = contract(soft.astype(LOW), grad_low, 1, 1).astype(LOW)
+    dv_last = contract(soft_last_low, grad_last_low, 1, 1).astype(LOW)
+    dq = contract(score_grad, k_rows, 0, 0).astype(LOW)
+    attn_rows = attn.T.astype(LOW)
+    log_total = top_score + jnp.log(total)
+    padding = jnp.zeros((1, top_all - mid_all), WIDE)
+    log_rows = jnp.concatenate(
+        [
+            piece_rows(log_total[:, :top_all]),
+            piece_rows(jnp.concatenate([log_total[:, top_all:], padding], 1)),
+        ],
+        0,
+    ).astype(LOW)
+    for distance, return_ref in enumerate(return_refs):
+        blocks = []
+        for rows in (dq, dk, dv, attn_rows):
+            mid_start = top_all + distance * mid_rows
+            blocks.append(rows[distance * top_rows : (distance + 1) * top_rows])
+            blocks.append(rows[mid_start : mid_start + mid_rows])
+        start = max(distance - 1, 0) * picked
+        blocks += [dk_last[start : start + picked], dv_last[start : start + picked], log_rows]
+        return_ref[...] = jnp.concatenate(blocks, 0)
+    normed_ref[...] = normed_last
+    grad_low_ref[...] = grad_last_low
+    score_grad_ref[...] = score_grad_last
+    kept_ref[0:1, :] = factor_last
+    kept_ref[1:2, :] = inner_last
+    once = is_top + (1.0 - is_top) * (1.0 - both_flag)
+    ones_all = jnp.ones((TILE, queries), LOW)
+    own_gain = gain_row_of(ones_all, product * once) / gain_row
+    last_gain = gain_row_of(ones, product_last) / gain_ref[:, cols]
+    for head in range(OWNED):
+        gain_part_ref[:, head_cols(head)] = gain_base_ref[:, head_cols(head)] + (
+            jnp.where(me == head, 1.0, 0.0) * own_gain
+        )
+    gain_part_ref[:, cols] = last_gain
+
+
+def last_head_kernel(top_step, *refs):
+    gain_part_ref, gain_peer_ref, q_ref, k_ref, v_ref, gain_ref, expo_ref, *refs = refs
+    normed_ref, grad_low_ref, peer_score_grad_ref, kept_ref, *peers = refs[: 4 + PEERS]
+    peers = peers[::-1]
+    attended_ref, dq_ref, dk_ref, dv_ref, gain_sum_ref = refs[4 + PEERS :]
+    gain_sum_ref[...] = gain_part_ref[...] + gain_peer_ref[...]
+    picked = sum(picked_counts(q_ref.shape[1], top_step))
+    score_scale = 1.0 / math.sqrt(HEAD_DIM)
+    cols = head_cols(q_ref.shape[2] // HEAD_DIM - 1)
+    attended_ref[...] = (normed_ref[...].T * gain_ref[:, cols]).astype(LOW)
+    k_peers = jnp.concatenate([ref[5 * picked : 6 * picked] for ref in peers], 0)
+    grad_low = grad_low_ref[...]
+    soft = expo_ref[:, cols].astype(WIDE) * kept_ref[0:1, :]
+    prob_grad = contract(v_ref[0, :, cols], grad_low, 1, 0)
+    score_grad = (soft * (prob_grad - kept_ref[1:2, :]) * score_scale).astype(LOW)
+    dk_ref[...] = contract(score_grad, q_ref[0, :, cols], 1, 0)
+    dv_ref[...] = contract(soft.astype(LOW), grad_low, 1, 1)
+    dq_ref[...] = (
+        contract(score_grad, k_ref[0, :, cols], 0, 0)
+        + contract(peer_score_grad_ref[...], k_peers, 0, 0)
+    ).astype(LOW)
+
+
+def finish_kernel(top_step, offsets_ref, q_ref, k_ref, v_ref, gain_ref, expo_ref, out_ref, *refs):
+    grad_norm_ref, stats_ref, place_ref, slots_ref = refs[:4]
+    gain_in_ref, last_attended_ref, last_dq_ref, last_dk_ref, last_dv_ref = refs[4:9]
+    return_refs, refs = nearest_first(refs[9 : 9 + SPAN]), refs[9 + SPAN :]
+    attended_ref, dq_ref, dk_ref, dv_ref, gain_out_ref, held_ref = refs
+    gain_out_ref[...] = gain_in_ref[...]
+    tokens, width = q_ref.shape[1:]
+    picked = sum(picked_counts(tokens, top_step))
+    score_scale = 1.0 / math.sqrt(HEAD_DIM)
+    me = lax.axis_index("ctx")
+    heads = range(OWNED)
+    every = [head_cols(head) for head in heads]
+    for distance, return_ref in enumerate(return_refs):
+        held_ref[me ^ distance] = return_ref[...]
+    blocks = [
+        [held_ref[head, block * picked : (block + 1) * picked] for block in range(4)]
+        for head in heads
+    ]
+    log_rows = [held_ref[head, 6 * picked : 6 * picked + STAT_TILES] for head in heads]
+    attn_parts = [
+        contract(blocks[head][3], place_ref[:, pl.ds(width + head * HEAD_DIM, picked)], 0, 1)
+        for head in heads
+    ]
+    log_parts = [
+        [contract(log_rows[head], slots_ref[:, head_cols(2 * head + level)], 1, 1) for level in (0, 1)]
+        for head in heads
+    ]
+    placed = [
+        contract(
+            place_ref[:, pl.ds(head * HEAD_DIM, picked)],
+            jnp.concatenate(blocks[head][:3], 1),
+            1,
+            0,
+        )
+        for head in heads
+    ]
+    factors, normeds, grad_lows, inners = [], [], [], []
+    for head in heads:
+        top_hit = hit_row(offsets_ref[1, head], top_step, tokens)
+        mid_hit = hit_row(offsets_ref[0, head], R1, tokens)
+        seen = jnp.maximum(top_hit, mid_hit) > 0.5
+        top_log, mid_log = joined_row(log_parts[head][0], 0), joined_row(log_parts[head][1], TILE)
+        top_score, total = stats_ref[head : head + 1, :], stats_ref[TILE + head : TILE + head + 1, :]
+        log_total = jnp.where(
+            top_hit > 0.5, top_log, jnp.where(mid_hit > 0.5, mid_log, top_score + jnp.log(total))
+        )
+        factors.append(jnp.exp(top_score - log_total))
+        attn = jnp.where(seen, attn_parts[head], out_ref[:, every[head]])
+        normed, _, grad_low, inner = norm_backward(attn, grad_norm_ref[:, every[head]])
+        normeds.append(normed)
+        grad_lows.append(grad_low)
+        inners.append(inner)
+    prob_grads = [contract(v_ref[0, :, every[head]], grad_lows[head], 1, 0) for head in heads]
+    softs = [expo_ref[:, every[head]].astype(WIDE) * factors[head] for head in heads]
+    dvs = [contract(softs[head].astype(LOW), grad_lows[head], 1, 1) for head in heads]
+    score_grads = [
+        (softs[head] * (prob_grads[head] - inners[head]) * score_scale).astype(LOW)
+        for head in heads
+    ]
+    dks = [contract(score_grads[head], q_ref[0, :, every[head]], 1, 0) for head in heads]
+    dqs = [contract(score_grads[head], k_ref[0, :, every[head]], 0, 0) for head in heads]
+    for head in heads:
+        cols = every[head]
+        attended_ref[0, :, cols] = (normeds[head].T * gain_ref[:, cols]).astype(LOW)
+        for which, (block, out_block_ref) in enumerate(
+            ((dqs[head], dq_ref), (dks[head], dk_ref), (dvs[head], dv_ref))
+        ):
+            part = placed[head][:, which * HEAD_DIM : (which + 1) * HEAD_DIM]
+            out_block_ref[0, :, cols] = (block + part).astype(LOW)
+    last = width // HEAD_DIM - 1
+    cols = head_cols(last)
+    total = sum(ref[4 * picked : 6 * picked].astype(WIDE) for ref in return_refs[1:]).astype(LOW)
+    rows = contract(
+        place_ref[:, pl.ds(last * HEAD_DIM, picked)],
+        jnp.concatenate([total[:picked], total[picked:]], 1),
+        1,
+        0,
+    )
+    attended_ref[0, :, cols] = last_attended_ref[...]
+    dq_ref[0, :, cols] = last_dq_ref[...]
+    dk_ref[0, :, cols] = (last_dk_ref[...] + rows[:, :HEAD_DIM]).astype(LOW)
+    dv_ref[0, :, cols] = (last_dv_ref[...] + rows[:, HEAD_DIM:]).astype(LOW)
+
+
+def across(block, axis, distance):
+    route = [(place, place ^ distance) for place in range(lax.axis_size(axis))]
+    return lax.ppermute(block, axis, route)
+
+
+def to_peers(blocks):
+    return [across(blocks[distance - 1], "ctx", distance) for distance in range(PEERS, 0, -1)]
+
+
+def call(kernel, name, operands, results, microseconds, vmem=PLAIN_VMEM, scratch=()):
+    return pl.pallas_call(
+        kernel,
+        out_shape=results,
+        in_specs=[SMEM_SPEC if block.dtype == jnp.int32 else VMEM_SPEC for block in operands],
+        out_specs=[VMEM_SPEC] * len(results),
+        scratch_shapes=scratch,
+        compiler_params=pltpu.CompilerParams(vmem_limit_bytes=vmem),
+        cost_estimate=pl.CostEstimate(
+            flops=int(microseconds * 10**9), bytes_accessed=0, transcendentals=0
+        ),
+        name=name,
+    )(*operands)
+
+
+def one_segment_shards(queries, keys, values, grad_y, out_gain, offsets):
+    tokens, width = queries.shape[1:]
+    heads = width // HEAD_DIM
+    top_step = lax.axis_size("ctx")
+    picked = sum(picked_counts(tokens, top_step))
+    shape = jax.ShapeDtypeStruct
+    row_block = shape((1, tokens, width), LOW)
+    low_block, wide_block = shape((tokens, width), LOW), shape((tokens, width), WIDE)
+    low_head, wide_head = shape((tokens, HEAD_DIM), LOW), shape((tokens, HEAD_DIM), WIDE)
+    gain_block = shape((1, width), WIDE)
+    stats_block = shape((2 * TILE, tokens), WIDE)
+    payload = shape((7 * picked + STAT_TILES, HEAD_DIM), LOW)
+    answer = shape((6 * picked + STAT_TILES, HEAD_DIM), LOW)
+    bind = functools.partial
+    gain_row = out_gain.reshape(1, width)
+    own, *sent, expo, base_out, stats = call(
+        bind(pack_kernel, top_step),
+        "pack",
+        (offsets, queries, keys, values, grad_y),
+        [payload] * SPAN + [low_block, wide_block, stats_block],
+        1,
+        vmem=PACK_VMEM,
+        scratch=[pltpu.VMEM((OWNED, *payload.shape), LOW)],
+    )
+    received = to_peers(sent)
+    grad_norm, gain_base, place, slots = call(
+        bind(prepare_kernel, top_step),
+        "prepare",
+        (offsets, grad_y, gain_row, base_out),
+        [wide_block, gain_block, shape((tokens, 2 * width), LOW), shape((tokens, 2 * OWNED * tokens), LOW)],
+        2,
+    )
+    gain_part, normed, grad_low, score_grad, kept, own_answer, *answers = call(
+        bind(owner_kernel, top_step),
+        "owner",
+        (offsets, queries, gain_row, base_out, grad_norm, stats, gain_base, own, *received),
+        [
+            gain_block,
+            wide_head,
+            low_head,
+            shape((PEERS * picked, HEAD_DIM), LOW),
+            shape((TILE, tokens), WIDE),
+        ]
+        + [answer] * SPAN,
+        3,
+    )
+    returned = to_peers(answers)
+    *last_results, gain_sum = call(
+        bind(last_head_kernel, top_step),
+        "last_head",
+        (
+            gain_part,
+            across(gain_part, "ctx", 2),
+            queries,
+            keys,
+            values,
+            gain_row,
+            expo,
+            normed,
+            grad_low,
+            score_grad,
+            kept,
+            *received,
+        ),
+        [low_head, low_head, wide_head, wide_head, gain_block],
+        20,
+    )
+    gain_sum = gain_sum + across(gain_sum, "dp", 1)
+    gain_rest = across(gain_sum, "ctx", 1)
+    attended, query_grad, key_grad, value_grad, gain_sum = call(
+        bind(finish_kernel, top_step),
+        "finish",
+        (
+            offsets,
+            queries,
+            keys,
+            values,
+            gain_row,
+            expo,
+            base_out,
+            grad_norm,
+            stats,
+            place,
+            slots,
+            gain_sum,
+            *last_results,
+            own_answer,
+            *returned,
+        ),
+        [row_block] * 4 + [gain_block],
+        1,
+        scratch=[pltpu.VMEM((OWNED, *answer.shape), LOW)],
+    )
+    gain_grad = (gain_sum + gain_rest).reshape(width)
+    return attended, query_grad, key_grad, value_grad, gain_grad
+
+
 def solution(mesh):
     in_specs = (
         P("dp", "ctx", "head"),
@@ -232,4 +795,5 @@
         P("dp", "ctx", "head"),
         P("head"),
     )
-    return jax.shard_map(shards, mesh=mesh, in_specs=in_specs, out_specs=out_specs, check_vma=False)
+    body = one_segment_shards if mesh.shape["ctx"] == SPAN else general_shards
+    return jax.shard_map(body, mesh=mesh, in_specs=in_specs, out_specs=out_specs, check_vma=False)

time: 113 us -> 31 us (0.27)
  blocking collectives: 45.4 us -> 0 us
  between operations: 14.6 us -> 0.72 us
  local copies, waits for them, and re-layouts: 14.5 us -> 2.61 us
  waiting for transfers between devices: 17.3 us -> 6.51 us
  Pallas kernels: 0 us -> 7.77 us
  matrix products: 5.13 us -> 0 us
  other arithmetic: 3.94 us -> 0.61 us
    all_gather x2 -> x0, blocking collectives: 27.4 us -> none  [the longest x1 13.8 us: shards(): lax.all_gather(top_vals, 'ctx', axis=0, tiled=True)]
    psum x1 -> x0, blocking collectives: 18.1 us -> none  [shards(): gain_grad = lax.psum(gain_part, ('dp', 'ctx'))]
    unnamed x4 -> x0, waiting for transfers between devices: 13.5 us -> none
    pallas_call x0 -> x5, Pallas kernels: none -> 7.77 us  [call(): pl.pallas_call(kernel, out_shape=results, in_specs=[SMEM_SPEC if block.dt...]
    unnamed x24 -> x22, local copies, waits for them, and re-layouts: 10.4 us -> 2.6 us
    dot_general x18 -> x0, matrix products: 5.13 us -> none  [the longest x3 1.14 us: attend(): jnp.einsum('hqk,khe->qhe', soft_rows, v_rows, preferred_element_type=jnp....]
    reduce_sum x11 -> x0, other arithmetic: 3.49 us -> none  [the longest x6 2.6 us: pick_rows(): return jnp.sum(chosen, axis=1, dtype=source_rows.dtype)]
    ppermute x8 -> x9, waiting for transfers between devices: 3.77 us -> 6.51 us  [across(): return lax.ppermute(block, axis, route)]
  transfers between devices with their start and end apart: 10 -> 9, of which waited for: 4 -> 3; matrix products, arithmetic and copies ran while one was open for 10% -> 0% of each run, Pallas kernels for 0% -> 12%
where the time goes in v8:
time: 31 us; the launch traced here: 30.7 us
  starting transfers between devices  12.5 us (40%)
  Pallas kernels  7.77 us (25%)
  waiting for transfers between devices  6.51 us (21%)
  local copies, waits for them, and re-layouts  2.61 us (8%)
  between operations  0.72 us (2%)
  other arithmetic  0.61 us (2%)
    ppermute x9, starting transfers between devices, across(): return lax.ppermute(block, axis, route)  12.5 us
    pallas_call x5, Pallas kernels, call(): pl.pallas_call(kernel, out_shape=results, in_specs=[SMEM_SPEC if block.dt...  7.77 us
    ppermute x9, waiting for transfers between devices, across(): return lax.ppermute(block, axis, route)  6.51 us
    unnamed x22, local copies, waits for them, and re-layouts  2.6 us
  transfers between devices with their start and end apart: 9, of which 3 were waited for; matrix products, arithmetic and copies ran while one was open for 0% of the time, Pallas kernels for 12%

profile of v8, /device:TPU:0, one launch (start us, length us, event | category | flops | bytes accessed | tf_op | source)
XLA Modules:
  0.0 30.7 jit_solution(10539954691999460391)
XLA Ops:
  0.6 2.6 %pack.1 = (bf16[352,128]{1,0:T(8,128)(2,1)}, bf16[352,128]{1,0:T(8,128)(2,1)}, bf16[352,128]{1,0:T(8,128)(2,1)}, bf16[352,128]{1,0:T(8,128)(2,1)}, bf16[128,640]...) custom-call(s32[2,5]{1,0:T(2,128)} %offsets_ref.7, bf16[1,128,640]{2,1,0:T(8,128)(2,1)} %q_ref.5, ...), custom_call_target="tpu_custom_call" | custom-call | flops 1000000000 | tf_op jit(solution)/shard_map/pack/pallas_call | solution.py:671
  3.2 5.1 %collective-permute-start = (bf16[352,128]{1,0:T(8,128)(2,1)}, bf16[352,128]{1,0:T(8,128)(2,1)S(1)}, u32[]{:S(2)}, u32[]{:S(2)}) collective-permute-start(bf16[352,128]{1,0:T(8,128)(2,1)} %get-tuple-element.43), channel_id=1, source_target_pairs={{0,12},{4,8},{8,4},{12,0},{1,13},{5,9},{9,5},{13,1},{2,14},{6,10},... | collective-permute-start | bytes 270344 | tf_op jit(solution)/shard_map/ppermute | solution.py:663
  8.3 0.0 collective-permute-start.1
  8.4 0.6 %collective-permute-start.2 = (bf16[352,128]{1,0:T(8,128)(2,1)}, bf16[352,128]{1,0:T(8,128)(2,1)S(1)}, u32[]{:S(2)}, u32[]{:S(2)}) collective-permute-start(bf16[352,128]{1,0:T(8,128)(2,1)} %get-tuple-element.45), channel_id=1, source_target_pairs={{0,4},{4,0},{8,12},{12,8},{1,5},{5,1},{9,13},{13,9},{2,6},{6,2},{1... | collective-permute-start | bytes 270344 | tf_op jit(solution)/shard_map/ppermute | solution.py:663
  9.0 0.0 copy-done.10
  9.0 0.7 %copy-done.4 = s32[2,5]{1,0:T(2,128)S(1)} copy-done((s32[2,5]{1,0:T(2,128)S(1)}, s32[2,5]{1,0:T(2,128)}, u32[]{:S(2)}) %copy-start.4) | copy-done | bytes 64
  9.7 0.9 %copy-done = bf16[1,128,640]{2,1,0:T(8,128)(2,1)S(1)} copy-done((bf16[1,128,640]{2,1,0:T(8,128)(2,1)S(1)}, bf16[1,128,640]{2,1,0:T(8,128)(2,1)}, u32[]{:S(2)}) %copy-start) | copy-done | bytes 163864
  10.6 1.0 %copy-done.5 = f32[128,640]{1,0:T(8,128)S(1)} copy-done((f32[128,640]{1,0:T(8,128)S(1)}, f32[128,640]{1,0:T(8,128)}, u32[]{:S(2)}) %copy-start.5) | copy-done | bytes 327704
  11.6 1.0 %prepare.1 = (f32[128,640]{1,0:T(8,128)S(1)}, f32[1,640]{1,0:T(1,128)S(1)}, bf16[128,1280]{1,0:T(8,128)(2,1)S(1)}, bf16[128,1024]{1,0:T(8,128)(2,1)S(1)}) custom-call(s32[2,5]{1,0:T(2,128)S(1)} %copy-done.4, bf16[1,128,640]{2,1,0:T(8,128)(2,1)S(1)} %copy-done, f32[1,640]{1,0:T(1,128)S(1)} %reshape.16.gain_ref.refs_5_, f32[128,640]{1,0:T(8,128)S(1)} %copy-done.5), custom_call_target="tpu_custom_call" | custom-call | flops 2000000000 | tf_op jit(solution)/shard_map/prepare/pallas_call | solution.py:671
  12.6 0.0 collective-permute-done.refs_3_.refs_11_
  12.6 3.5 %collective-permute-done.1.refs_4_.refs_12_ = bf16[352,128]{1,0:T(8,128)(2,1)S(1)} collective-permute-done((bf16[352,128]{1,0:T(8,128)(2,1)}, bf16[352,128]{1,0:T(8,128)(2,1)S(1)}, u32[]{:S(2)}, u32[]{:S(2)}) %collective-permute-start.1) | collective-permute-done | bytes 90144 | tf_op jit(solution)/shard_map/ppermute | solution.py:663
  16.1 0.0 collective-permute-done.2.refs_5_.refs_13_
  16.1 0.0 copy-done.1
  16.2 0.0 copy-start.2
  16.2 0.0 copy-start.3
  16.2 0.0 copy-start.7
  16.2 1.6 %owner.1 = (f32[1,640]{1,0:T(1,128)S(1)}, f32[128,128]{1,0:T(8,128)S(1)}, bf16[128,128]{1,0:T(8,128)(2,1)S(1)}, bf16[144,128]{1,0:T(8,128)(2,1)S(1)}, f32[8,128]...) custom-call(s32[2,5]{1,0:T(2,128)S(1)} %copy-done.4, ...), custom_call_target="tpu_custom_call" | custom-call | flops 3000000000 | tf_op jit(solution)/shard_map/owner/pallas_call | solution.py:671
  17.8 0.8 %collective-permute-start.3 = (f32[1,640]{1,0:T(1,128)S(1)}, f32[1,640]{1,0:T(1,128)S(1)}, u32[]{:S(2)}, u32[]{:S(2)}) collective-permute-start(f32[1,640]{1,0:T(1,128)S(1)} %get-tuple-element.46.refs_0_), channel_id=1, source_target_pairs={{0,8},{4,12},{8,0},{12,4},{1,9},{5,13},{9,1},{13,5},{2,10},{6,14},... | collective-permute-start | bytes 7688 | tf_op jit(solution)/shard_map/ppermute | solution.py:663
  18.6 2.3 %collective-permute-start.5 = (bf16[304,128]{1,0:T(8,128)(2,1)S(1)}, bf16[304,128]{1,0:T(8,128)(2,1)S(1)}, u32[]{:S(2)}, u32[]{:S(2)}) collective-permute-start(bf16[304,128]{1,0:T(8,128)(2,1)S(1)} %get-tuple-element.57), channel_id=1, source_target_pairs={{0,12},{4,8},{8,4},{12,0},{1,13},{5,9},{9,5},{13,1},{2,14},{6,10},... | collective-permute-start | bytes 233480 | tf_op jit(solution)/shard_map/ppermute | solution.py:663
  20.9 1.6 %collective-permute-start.6 = (bf16[304,128]{1,0:T(8,128)(2,1)S(1)}, bf16[304,128]{1,0:T(8,128)(2,1)S(1)}, u32[]{:S(2)}, u32[]{:S(2)}) collective-permute-start(bf16[304,128]{1,0:T(8,128)(2,1)S(1)} %get-tuple-element.58), channel_id=1, source_target_pairs={{0,8},{4,12},{8,0},{12,4},{1,9},{5,13},{9,1},{13,5},{2,10},{6,14},... | collective-permute-start | bytes 233480 | tf_op jit(solution)/shard_map/ppermute | solution.py:663
  22.4 0.5 %collective-permute-start.7 = (bf16[304,128]{1,0:T(8,128)(2,1)S(1)}, bf16[304,128]{1,0:T(8,128)(2,1)S(1)}, u32[]{:S(2)}, u32[]{:S(2)}) collective-permute-start(bf16[304,128]{1,0:T(8,128)(2,1)S(1)} %get-tuple-element.59), channel_id=1, source_target_pairs={{0,4},{4,0},{8,12},{12,8},{1,5},{5,1},{9,13},{13,9},{2,6},{6,2},{1... | collective-permute-start | bytes 233480 | tf_op jit(solution)/shard_map/ppermute | solution.py:663
  22.9 0.0 collective-permute-done.3.refs_1_
  23.0 0.3 %last_head.1 = (bf16[128,128]{1,0:T(8,128)(2,1)S(1)}, bf16[128,128]{1,0:T(8,128)(2,1)S(1)}, f32[128,128]{1,0:T(8,128)S(1)}, f32[128,128]{1,0:T(8,128)S(1)}, f32[1,640]{1,0:T(1,128)S(1)}) custom-call(f32[1,640]{1,0:T(1,128)S(1)} %get-tuple-element.46.refs_0_, f32[1,640]{1,0:T(1,128)S(1)} %collective-permute-done.3.refs_1_, ...), custom_call_target="tpu_custom_call" | custom-call | flops 20000000000 | tf_op jit(solution)/shard_map/last_head/pallas_call | solution.py:671
  23.3 0.1 collective-permute-start.4
  23.4 1.1 %collective-permute-done.4 = f32[1,640]{1,0:T(1,128)S(1)} collective-permute-done((f32[1,640]{1,0:T(1,128)S(1)}, f32[1,640]{1,0:T(1,128)S(1)}, u32[]{:S(2)}, u32[]{:S(2)}) %collective-permute-start.4) | collective-permute-done | bytes 2592 | tf_op jit(solution)/shard_map/ppermute | solution.py:663
  24.5 1.5 %collective-permute-start.8 = (f32[1,640]{1,0:T(1,128)S(1)}, f32[1,640]{1,0:T(1,128)S(1)}, u32[]{:S(2)}, u32[]{:S(2)}) collective-permute-start(f32[1,640]{1,0:T(1,128)S(1)} %add.6.refs_4_), channel_id=1, source_target_pairs={{0,4},{4,0},{8,12},{12,8},{1,5},{5,1},{9,13},{13,9},{2,6},{6,2},{1... | collective-permute-start | bytes 7688 | tf_op jit(solution)/shard_map/ppermute | solution.py:663
  26.1 0.0 collective-permute-done.5.refs_10_
  26.1 1.8 %collective-permute-done.6.refs_11_ = bf16[304,128]{1,0:T(8,128)(2,1)S(1)} collective-permute-done((bf16[304,128]{1,0:T(8,128)(2,1)S(1)}, bf16[304,128]{1,0:T(8,128)(2,1)S(1)}, u32[]{:S(2)}, u32[]{:S(2)}) %collective-permute-start.6) | collective-permute-done | bytes 77856 | tf_op jit(solution)/shard_map/ppermute | solution.py:663
  27.9 0.0 collective-permute-done.7.refs_12_
  27.9 2.2 %finish.1 = (bf16[1,128,640]{2,1,0:T(8,128)(2,1)}, bf16[1,128,640]{2,1,0:T(8,128)(2,1)}, bf16[1,128,640]{2,1,0:T(8,128)(2,1)}, bf16[1,128,640]{2,1,0:T(8,128)(2,1)}, f32[1,640]{1,0:T(1,128)S(1)}) custom-call(s32[2,5]{1,0:T(2,128)S(1)} %copy-done.4, bf16[1,128,640]{2,1,0:T(8,128)(2,1)S(1)} %copy-done.1, bf16[1,128,640]{2,1,0:T(8,128)(2,1)S(1)} %copy-done.2, ...), custom_call_target="tpu_custom_call" | custom-call | flops 1000000000 | tf_op jit(solution)/shard_map/finish/pallas_call | solution.py:671
  30.1 0.0 collective-permute-done.8
  30.1 0.6 %add_reduce_fusion = f32[640]{0:T(1024)} fusion(f32[1,640]{1,0:T(1,128)S(1)} %get-tuple-element.64, f32[1,640]{1,0:T(1,128)S(1)} %collective-permute-done.8), kind=kLoop, calls=%fused_computation | loop fusion | flops 640 | bytes 7680 | tf_op jit(solution)/shard_map/add | solution.py:778
  (16 shorter events, 0.0 us)
Async XLA Ops:
  3.2 5.8 %copy-start.10 = (f32[640]{0:T(1024)S(1)}, f32[640]{0:T(1024)}, u32[]{:S(2)}) copy-start(f32[640]{0:T(1024)} %param.10) | copy-start | bytes 7684
  3.2 9.4 %collective-permute-start = (bf16[352,128]{1,0:T(8,128)(2,1)}, bf16[352,128]{1,0:T(8,128)(2,1)S(1)}, u32[]{:S(2)}, u32[]{:S(2)}) collective-permute-start(bf16[352,128]{1,0:T(8,128)(2,1)} %get-tuple-element.43), channel_id=1, source_target_pairs={{0,12},{4,8},{8,4},{12,0},{1,13},{5,9},{9,5},{13,1},{2,14},{6,10},... | collective-permute-start | bytes 270344 | tf_op jit(solution)/shard_map/ppermute | solution.py:663
  8.3 7.8 %collective-permute-start.1 = (bf16[352,128]{1,0:T(8,128)(2,1)}, bf16[352,128]{1,0:T(8,128)(2,1)S(1)}, u32[]{:S(2)}, u32[]{:S(2)}) collective-permute-start(bf16[352,128]{1,0:T(8,128)(2,1)} %get-tuple-element.44), channel_id=1, source_target_pairs={{0,8},{4,12},{8,0},{12,4},{1,9},{5,13},{9,1},{13,5},{2,10},{6,14},... | collective-permute-start | bytes 270344 | tf_op jit(solution)/shard_map/ppermute | solution.py:663
  8.4 7.8 %collective-permute-start.2 = (bf16[352,128]{1,0:T(8,128)(2,1)}, bf16[352,128]{1,0:T(8,128)(2,1)S(1)}, u32[]{:S(2)}, u32[]{:S(2)}) collective-permute-start(bf16[352,128]{1,0:T(8,128)(2,1)} %get-tuple-element.45), channel_id=1, source_target_pairs={{0,4},{4,0},{8,12},{12,8},{1,5},{5,1},{9,13},{13,9},{2,6},{6,2},{1... | collective-permute-start | bytes 270344 | tf_op jit(solution)/shard_map/ppermute | solution.py:663
  9.0 0.7 %copy-start.4 = (s32[2,5]{1,0:T(2,128)S(1)}, s32[2,5]{1,0:T(2,128)}, u32[]{:S(2)}) copy-start(s32[2,5]{1,0:T(2,128)} %offsets_ref.7) | copy-start | bytes 124
  9.7 0.9 %copy-start = (bf16[1,128,640]{2,1,0:T(8,128)(2,1)S(1)}, bf16[1,128,640]{2,1,0:T(8,128)(2,1)}, u32[]{:S(2)}) copy-start(bf16[1,128,640]{2,1,0:T(8,128)(2,1)} %grad_ref.3) | copy-start | bytes 491524
  10.6 1.0 %copy-start.5 = (f32[128,640]{1,0:T(8,128)S(1)}, f32[128,640]{1,0:T(8,128)}, u32[]{:S(2)}) copy-start(f32[128,640]{1,0:T(8,128)} %get-tuple-element.36.out_ref) | copy-start | bytes 983044
  11.6 4.6 %copy-start.1 = (bf16[1,128,640]{2,1,0:T(8,128)(2,1)S(1)}, bf16[1,128,640]{2,1,0:T(8,128)(2,1)}, u32[]{:S(2)}) copy-start(bf16[1,128,640]{2,1,0:T(8,128)(2,1)} %q_ref.5) | copy-start | bytes 491524
  11.6 4.6 %copy-start.6 = (f32[128,640]{1,0:T(8,128)S(1)}, f32[128,640]{1,0:T(8,128)}, u32[]{:S(2)}) copy-start(f32[128,640]{1,0:T(8,128)} %get-tuple-element.36.out_ref) | copy-start | bytes 983044
  11.6 4.6 %copy-start.8 = (bf16[352,128]{1,0:T(8,128)(2,1)S(1)}, bf16[352,128]{1,0:T(8,128)(2,1)}, u32[]{:S(2)}) copy-start(bf16[352,128]{1,0:T(8,128)(2,1)} %get-tuple-element.42.refs_2_) | copy-start | bytes 270340
  11.6 4.6 %copy-start.9 = (f32[16,128]{1,0:T(8,128)S(1)}, f32[16,128]{1,0:T(8,128)}, u32[]{:S(2)}) copy-start(f32[16,128]{1,0:T(8,128)} %get-tuple-element.38.refs_0_.refs_1_) | copy-start | bytes 24580
  16.2 6.8 %copy-start.2 = (bf16[1,128,640]{2,1,0:T(8,128)(2,1)S(1)}, bf16[1,128,640]{2,1,0:T(8,128)(2,1)}, u32[]{:S(2)}) copy-start(bf16[1,128,640]{2,1,0:T(8,128)(2,1)} %k_ref.3) | copy-start | bytes 491524
  16.2 6.8 %copy-start.3 = (bf16[1,128,640]{2,1,0:T(8,128)(2,1)S(1)}, bf16[1,128,640]{2,1,0:T(8,128)(2,1)}, u32[]{:S(2)}) copy-start(bf16[1,128,640]{2,1,0:T(8,128)(2,1)} %v_ref.3) | copy-start | bytes 491524
  16.2 6.8 %copy-start.7 = (bf16[128,640]{1,0:T(8,128)(2,1)S(1)}, bf16[128,640]{1,0:T(8,128)(2,1)}, u32[]{:S(2)}) copy-start(bf16[128,640]{1,0:T(8,128)(2,1)} %get-tuple-element.35.refs_6_.expo_ref) | copy-start | bytes 491524
  17.8 5.2 %collective-permute-start.3 = (f32[1,640]{1,0:T(1,128)S(1)}, f32[1,640]{1,0:T(1,128)S(1)}, u32[]{:S(2)}, u32[]{:S(2)}) collective-permute-start(f32[1,640]{1,0:T(1,128)S(1)} %get-tuple-element.46.refs_0_), channel_id=1, source_target_pairs={{0,8},{4,12},{8,0},{12,4},{1,9},{5,13},{9,1},{13,5},{2,10},{6,14},... | collective-permute-start | bytes 7688 | tf_op jit(solution)/shard_map/ppermute | solution.py:663
  18.6 7.5 %collective-permute-start.5 = (bf16[304,128]{1,0:T(8,128)(2,1)S(1)}, bf16[304,128]{1,0:T(8,128)(2,1)S(1)}, u32[]{:S(2)}, u32[]{:S(2)}) collective-permute-start(bf16[304,128]{1,0:T(8,128)(2,1)S(1)} %get-tuple-element.57), channel_id=1, source_target_pairs={{0,12},{4,8},{8,4},{12,0},{1,13},{5,9},{9,5},{13,1},{2,14},{6,10},... | collective-permute-start | bytes 233480 | tf_op jit(solution)/shard_map/ppermute | solution.py:663
  20.9 7.0 %collective-permute-start.6 = (bf16[304,128]{1,0:T(8,128)(2,1)S(1)}, bf16[304,128]{1,0:T(8,128)(2,1)S(1)}, u32[]{:S(2)}, u32[]{:S(2)}) collective-permute-start(bf16[304,128]{1,0:T(8,128)(2,1)S(1)} %get-tuple-element.58), channel_id=1, source_target_pairs={{0,8},{4,12},{8,0},{12,4},{1,9},{5,13},{9,1},{13,5},{2,10},{6,14},... | collective-permute-start | bytes 233480 | tf_op jit(solution)/shard_map/ppermute | solution.py:663
  22.4 5.5 %collective-permute-start.7 = (bf16[304,128]{1,0:T(8,128)(2,1)S(1)}, bf16[304,128]{1,0:T(8,128)(2,1)S(1)}, u32[]{:S(2)}, u32[]{:S(2)}) collective-permute-start(bf16[304,128]{1,0:T(8,128)(2,1)S(1)} %get-tuple-element.59), channel_id=1, source_target_pairs={{0,4},{4,0},{8,12},{12,8},{1,5},{5,1},{9,13},{13,9},{2,6},{6,2},{1... | collective-permute-start | bytes 233480 | tf_op jit(solution)/shard_map/ppermute | solution.py:663
  23.3 1.2 %collective-permute-start.4 = (f32[1,640]{1,0:T(1,128)S(1)}, f32[1,640]{1,0:T(1,128)S(1)}, u32[]{:S(2)}, u32[]{:S(2)}) collective-permute-start(f32[1,640]{1,0:T(1,128)S(1)} %get-tuple-element.51), channel_id=1, source_target_pairs={{0,16},{16,0},{1,17},{17,1},{2,18},{18,2},{3,19},{19,3},{4,20},{20... | collective-permute-start | bytes 7688 | tf_op jit(solution)/shard_map/ppermute | solution.py:663
  24.5 5.6 %collective-permute-start.8 = (f32[1,640]{1,0:T(1,128)S(1)}, f32[1,640]{1,0:T(1,128)S(1)}, u32[]{:S(2)}, u32[]{:S(2)}) collective-permute-start(f32[1,640]{1,0:T(1,128)S(1)} %add.6.refs_4_), channel_id=1, source_target_pairs={{0,4},{4,0},{8,12},{12,8},{1,5},{5,1},{9,13},{13,9},{2,6},{6,2},{1... | collective-permute-start | bytes 7688 | tf_op jit(solution)/shard_map/ppermute | solution.py:663

commit v9 on v8

--- a/solution.py
+++ b/solution.py
@@ -221,6 +221,7 @@
 
 VMEM_SPEC = pl.BlockSpec(memory_space=pltpu.VMEM)
 SMEM_SPEC = pl.BlockSpec(memory_space=pltpu.SMEM)
+HBM_SPEC = pl.BlockSpec(memory_space=pltpu.HBM)
 PEERS = SPAN - 1
 OWNED = SPAN
 TILE = 8
@@ -313,7 +314,8 @@
 
 
 def pack_kernel(top_step, offsets_ref, q_ref, k_ref, v_ref, grad_ref, *refs):
-    payload_refs, (expo_ref, out_ref, stats_ref, held_ref) = refs[:SPAN], refs[SPAN:]
+    payload_refs, refs = refs[:SPAN], refs[SPAN:]
+    stats_ref, expo_hbm, out_hbm, held_ref, expo_ref, out_ref, sems = refs
     tokens, width = q_ref.shape[1:]
     heads = range(width // HEAD_DIM)
     owned = range(OWNED)
@@ -357,9 +359,15 @@
         stats_ref[TILE + head : TILE + head + 1, :] = totals[head]
     for head in owned:
         outs[head] = outs[head] * (1.0 / totals[head])
-    picked_outs = [contract(picks[head], outs[head].astype(LOW), 1, 1).astype(LOW) for head in owned]
     for head in heads:
         out_ref[:, head_cols(head)] = outs[head]
+    copies = [
+        pltpu.make_async_copy(expo_ref, expo_hbm, sems.at[0]),
+        pltpu.make_async_copy(out_ref, out_hbm, sems.at[1]),
+    ]
+    for copy in copies:
+        copy.start()
+    picked_outs = [contract(picks[head], outs[head].astype(LOW), 1, 1).astype(LOW) for head in owned]
     for head in owned:
         pieces = piece_rows(top_scores[head] + jnp.log(totals[head])).astype(LOW)
         slot = me ^ head
@@ -374,6 +382,8 @@
         held_ref[head] = jnp.concatenate(blocks, 0)
     for distance, payload_ref in enumerate(payload_refs):
         payload_ref[...] = held_ref[me ^ distance]
+    for copy in copies:
+        copy.wait()
 
 
 def prepare_kernel(top_step, offsets_ref, grad_ref, gain_ref, out_ref, *refs):
@@ -576,10 +586,16 @@
 
 def finish_kernel(top_step, offsets_ref, q_ref, k_ref, v_ref, gain_ref, expo_ref, out_ref, *refs):
     grad_norm_ref, stats_ref, place_ref, slots_ref = refs[:4]
-    gain_in_ref, last_attended_ref, last_dq_ref, last_dk_ref, last_dv_ref = refs[4:9]
-    return_refs, refs = nearest_first(refs[9 : 9 + SPAN]), refs[9 + SPAN :]
-    attended_ref, dq_ref, dk_ref, dv_ref, gain_out_ref, held_ref = refs
-    gain_out_ref[...] = gain_in_ref[...]
+    gain_refs, refs = refs[4:6], refs[6:]
+    last_attended_ref, last_dq_ref, last_dk_ref, last_dv_ref = refs[:4]
+    return_refs, refs = nearest_first(refs[4 : 4 + SPAN]), refs[4 + SPAN :]
+    gain_out_ref, *result_hbm = refs[:5]
+    held_ref, attended_ref, dq_ref, dk_ref, dv_ref, sems = refs[5:]
+    gain_out_ref[...] = (gain_refs[0][...] + gain_refs[1][...]).reshape(gain_out_ref.shape)
+    copies = [
+        pltpu.make_async_copy(ref, hbm.at[0], sems.at[which])
+        for which, (ref, hbm) in enumerate(zip((attended_ref, dq_ref, dk_ref, dv_ref), result_hbm))
+    ]
     tokens, width = q_ref.shape[1:]
     picked = sum(picked_counts(tokens, top_step))
     score_scale = 1.0 / math.sqrt(HEAD_DIM)
@@ -626,25 +642,13 @@
         normeds.append(normed)
         grad_lows.append(grad_low)
         inners.append(inner)
+    last = width // HEAD_DIM - 1
+    last_cols = head_cols(last)
     prob_grads = [contract(v_ref[0, :, every[head]], grad_lows[head], 1, 0) for head in heads]
-    softs = [expo_ref[:, every[head]].astype(WIDE) * factors[head] for head in heads]
-    dvs = [contract(softs[head].astype(LOW), grad_lows[head], 1, 1) for head in heads]
-    score_grads = [
-        (softs[head] * (prob_grads[head] - inners[head]) * score_scale).astype(LOW)
-        for head in heads
-    ]
-    dks = [contract(score_grads[head], q_ref[0, :, every[head]], 1, 0) for head in heads]
-    dqs = [contract(score_grads[head], k_ref[0, :, every[head]], 0, 0) for head in heads]
     for head in heads:
-        cols = every[head]
-        attended_ref[0, :, cols] = (normeds[head].T * gain_ref[:, cols]).astype(LOW)
-        for which, (block, out_block_ref) in enumerate(
-            ((dqs[head], dq_ref), (dks[head], dk_ref), (dvs[head], dv_ref))
-        ):
-            part = placed[head][:, which * HEAD_DIM : (which + 1) * HEAD_DIM]
-            out_block_ref[0, :, cols] = (block + part).astype(LOW)
-    last = width // HEAD_DIM - 1
-    cols = head_cols(last)
+        attended_ref[:, every[head]] = (normeds[head].T * gain_ref[:, every[head]]).astype(LOW)
+    attended_ref[:, last_cols] = last_attended_ref[...]
+    copies[0].start()
     total = sum(ref[4 * picked : 6 * picked].astype(WIDE) for ref in return_refs[1:]).astype(LOW)
     rows = contract(
         place_ref[:, pl.ds(last * HEAD_DIM, picked)],
@@ -652,10 +656,27 @@
         1,
         0,
     )
-    attended_ref[0, :, cols] = last_attended_ref[...]
-    dq_ref[0, :, cols] = last_dq_ref[...]
-    dk_ref[0, :, cols] = (last_dk_ref[...] + rows[:, :HEAD_DIM]).astype(LOW)
-    dv_ref[0, :, cols] = (last_dv_ref[...] + rows[:, HEAD_DIM:]).astype(LOW)
+    softs = [expo_ref[:, every[head]].astype(WIDE) * factors[head] for head in heads]
+
+    def put(block_ref, which, blocks, last_block):
+        for head in heads:
+            part = placed[head][:, which * HEAD_DIM : (which + 1) * HEAD_DIM]
+            block_ref[:, every[head]] = (blocks[head] + part).astype(LOW)
+        block_ref[:, last_cols] = last_block.astype(LOW)
+        copies[which + 1].start()
+
+    dvs = [contract(softs[head].astype(LOW), grad_lows[head], 1, 1) for head in heads]
+    put(dv_ref, 2, dvs, last_dv_ref[...] + rows[:, HEAD_DIM:])
+    score_grads = [
+        (softs[head] * (prob_grads[head] - inners[head]) * score_scale).astype(LOW)
+        for head in heads
+    ]
+    dks = [contract(score_grads[head], q_ref[0, :, every[head]], 1, 0) for head in heads]
+    put(dk_ref, 1, dks, last_dk_ref[...] + rows[:, :HEAD_DIM])
+    dqs = [contract(score_grads[head], k_ref[0, :, every[head]], 0, 0) for head in heads]
+    put(dq_ref, 0, dqs, last_dq_ref[...])
+    for copy in copies:
+        copy.wait()
 
 
 def across(block, axis, distance):
@@ -667,12 +688,14 @@
     return [across(blocks[distance - 1], "ctx", distance) for distance in range(PEERS, 0, -1)]
 
 
-def call(kernel, name, operands, results, microseconds, vmem=PLAIN_VMEM, scratch=()):
+def call(
+    kernel, name, operands, results, microseconds, vmem=PLAIN_VMEM, scratch=(), in_hbm=0
+):
     return pl.pallas_call(
         kernel,
         out_shape=results,
         in_specs=[SMEM_SPEC if block.dtype == jnp.int32 else VMEM_SPEC for block in operands],
-        out_specs=[VMEM_SPEC] * len(results),
+        out_specs=[VMEM_SPEC] * (len(results) - in_hbm) + [HBM_SPEC] * in_hbm,
         scratch_shapes=scratch,
         compiler_params=pltpu.CompilerParams(vmem_limit_bytes=vmem),
         cost_estimate=pl.CostEstimate(
@@ -697,14 +720,20 @@
     answer = shape((6 * picked + STAT_TILES, HEAD_DIM), LOW)
     bind = functools.partial
     gain_row = out_gain.reshape(1, width)
-    own, *sent, expo, base_out, stats = call(
+    own, *sent, stats, expo, base_out = call(
         bind(pack_kernel, top_step),
         "pack",
         (offsets, queries, keys, values, grad_y),
-        [payload] * SPAN + [low_block, wide_block, stats_block],
+        [payload] * SPAN + [stats_block, low_block, wide_block],
         1,
         vmem=PACK_VMEM,
-        scratch=[pltpu.VMEM((OWNED, *payload.shape), LOW)],
+        scratch=[
+            pltpu.VMEM((OWNED, *payload.shape), LOW),
+            pltpu.VMEM(low_block.shape, LOW),
+            pltpu.VMEM(wide_block.shape, WIDE),
+            pltpu.SemaphoreType.DMA((2,)),
+        ],
+        in_hbm=2,
     )
     received = to_peers(sent)
     grad_norm, gain_base, place, slots = call(
@@ -751,7 +780,7 @@
     )
     gain_sum = gain_sum + across(gain_sum, "dp", 1)
     gain_rest = across(gain_sum, "ctx", 1)
-    attended, query_grad, key_grad, value_grad, gain_sum = call(
+    gain_grad, attended, query_grad, key_grad, value_grad = call(
         bind(finish_kernel, top_step),
         "finish",
         (
@@ -767,15 +796,18 @@
             place,
             slots,
             gain_sum,
+            gain_rest,
             *last_results,
             own_answer,
             *returned,
         ),
-        [row_block] * 4 + [gain_block],
+        [shape((width,), WIDE)] + [row_block] * 4,
         1,
-        scratch=[pltpu.VMEM((OWNED, *answer.shape), LOW)],
-    )
-    gain_grad = (gain_sum + gain_rest).reshape(width)
+        scratch=[pltpu.VMEM((OWNED, *answer.shape), LOW)]
+        + [pltpu.VMEM(low_block.shape, LOW)] * 4
+        + [pltpu.SemaphoreType.DMA((4,))],
+        in_hbm=4,
+    )
     return attended, query_grad, key_grad, value_grad, gain_grad
 
 

time: 31 us -> 31.7 us (1.023)
  Pallas kernels: 7.77 us -> 8.81 us
  other arithmetic: 0.61 us -> 0.01 us
    pallas_call x5, Pallas kernels: 7.77 us -> 8.81 us  [call(): pl.pallas_call(kernel, out_shape=results, in_specs=[SMEM_SPEC if block.dt...]
    add x1 -> x0, other arithmetic: 0.61 us -> none  [one_segment_shards(): gain_grad = (gain_sum + gain_rest).reshape(width)]
  transfers between devices with their start and end apart: 9 -> 9, of which waited for: 3 -> 3; matrix products, arithmetic and copies ran while one was open for 0% -> 0% of each run, Pallas kernels for 12% -> 4%
where the time goes in v9:
time: 31.7 us; the launch traced here: 31.4 us
  starting transfers between devices  12.5 us (39%)
  Pallas kernels  8.81 us (28%)
  waiting for transfers between devices  6.77 us (21%)
  local copies, waits for them, and re-layouts  2.61 us (8%)
  between operations  0.74 us (2%)
    ppermute x9, starting transfers between devices, across(): return lax.ppermute(block, axis, route)  12.5 us
    pallas_call x5, Pallas kernels, call(): pl.pallas_call(kernel, out_shape=results, in_specs=[SMEM_SPEC if block.dt...  8.81 us
    ppermute x9, waiting for transfers between devices, across(): return lax.ppermute(block, axis, route)  6.77 us
    unnamed x22, local copies, waits for them, and re-layouts  2.61 us
  transfers between devices with their start and end apart: 9, of which 3 were waited for; matrix products, arithmetic and copies ran while one was open for 0% of the time, Pallas kernels for 4%

profile of v9, /device:TPU:0, one launch (start us, length us, event | category | flops | bytes accessed | tf_op | source)
XLA Modules:
  0.0 31.4 jit_solution(1178273409504899648)
XLA Ops:
  0.6 3.1 %pack.1 = (bf16[352,128]{1,0:T(8,128)(2,1)}, bf16[352,128]{1,0:T(8,128)(2,1)}, bf16[352,128]{1,0:T(8,128)(2,1)}, bf16[352,128]{1,0:T(8,128)(2,1)}, f32[16,128]{1...) custom-call(s32[2,5]{1,0:T(2,128)} %offsets_ref.7, bf16[1,128,640]{2,1,0:T(8,128)(2,1)} %q_ref.5, ...), custom_call_target="tpu_custom_call" | custom-call | flops 1000000000 | tf_op jit(solution)/shard_map/pack/pallas_call | solution.py:694
  3.8 0.0 copy-start.10
  3.8 5.1 %collective-permute-start = (bf16[352,128]{1,0:T(8,128)(2,1)}, bf16[352,128]{1,0:T(8,128)(2,1)S(1)}, u32[]{:S(2)}, u32[]{:S(2)}) collective-permute-start(bf16[352,128]{1,0:T(8,128)(2,1)} %get-tuple-element.43), channel_id=1, source_target_pairs={{0,12},{4,8},{8,4},{12,0},{1,13},{5,9},{9,5},{13,1},{2,14},{6,10},... | collective-permute-start | bytes 270344 | tf_op jit(solution)/shard_map/ppermute | solution.py:684
  8.9 0.0 collective-permute-start.1
  8.9 0.6 %collective-permute-start.2 = (bf16[352,128]{1,0:T(8,128)(2,1)}, bf16[352,128]{1,0:T(8,128)(2,1)S(1)}, u32[]{:S(2)}, u32[]{:S(2)}) collective-permute-start(bf16[352,128]{1,0:T(8,128)(2,1)} %get-tuple-element.45), channel_id=1, source_target_pairs={{0,4},{4,0},{8,12},{12,8},{1,5},{5,1},{9,13},{13,9},{2,6},{6,2},{1... | collective-permute-start | bytes 270344 | tf_op jit(solution)/shard_map/ppermute | solution.py:684
  9.5 0.0 copy-done.10
  9.5 0.7 %copy-done.4 = s32[2,5]{1,0:T(2,128)S(1)} copy-done((s32[2,5]{1,0:T(2,128)S(1)}, s32[2,5]{1,0:T(2,128)}, u32[]{:S(2)}) %copy-start.4) | copy-done | bytes 64
  10.2 0.9 %copy-done = bf16[1,128,640]{2,1,0:T(8,128)(2,1)S(1)} copy-done((bf16[1,128,640]{2,1,0:T(8,128)(2,1)S(1)}, bf16[1,128,640]{2,1,0:T(8,128)(2,1)}, u32[]{:S(2)}) %copy-start) | copy-done | bytes 163864
  11.1 1.0 %copy-done.5 = f32[128,640]{1,0:T(8,128)S(1)} copy-done((f32[128,640]{1,0:T(8,128)S(1)}, f32[128,640]{1,0:T(8,128)}, u32[]{:S(2)}) %copy-start.5) | copy-done | bytes 327704
  12.1 1.0 %prepare.1 = (f32[128,640]{1,0:T(8,128)S(1)}, f32[1,640]{1,0:T(1,128)S(1)}, bf16[128,1280]{1,0:T(8,128)(2,1)S(1)}, bf16[128,1024]{1,0:T(8,128)(2,1)S(1)}) custom-call(s32[2,5]{1,0:T(2,128)S(1)} %copy-done.4, bf16[1,128,640]{2,1,0:T(8,128)(2,1)S(1)} %copy-done, f32[1,640]{1,0:T(1,128)S(1)} %reshape.13.gain_ref.refs_5_, f32[128,640]{1,0:T(8,128)S(1)} %copy-done.5), custom_call_target="tpu_custom_call" | custom-call | flops 2000000000 | tf_op jit(solution)/shard_map/prepare/pallas_call | solution.py:694
  13.1 0.0 collective-permute-done.refs_3_.refs_11_
  13.1 3.5 %collective-permute-done.1.refs_4_.refs_12_ = bf16[352,128]{1,0:T(8,128)(2,1)S(1)} collective-permute-done((bf16[352,128]{1,0:T(8,128)(2,1)}, bf16[352,128]{1,0:T(8,128)(2,1)S(1)}, u32[]{:S(2)}, u32[]{:S(2)}) %collective-permute-start.1) | collective-permute-done | bytes 90144 | tf_op jit(solution)/shard_map/ppermute | solution.py:684
  16.7 0.0 collective-permute-done.2.refs_5_.refs_13_
  16.7 0.0 copy-done.8
  16.7 0.0 copy-start.2
  16.7 0.0 copy-start.3
  16.7 0.0 copy-start.7
  16.7 1.6 %owner.1 = (f32[1,640]{1,0:T(1,128)S(1)}, f32[128,128]{1,0:T(8,128)S(1)}, bf16[128,128]{1,0:T(8,128)(2,1)S(1)}, bf16[144,128]{1,0:T(8,128)(2,1)S(1)}, f32[8,128]...) custom-call(s32[2,5]{1,0:T(2,128)S(1)} %copy-done.4, ...), custom_call_target="tpu_custom_call" | custom-call | flops 3000000000 | tf_op jit(solution)/shard_map/owner/pallas_call | solution.py:694
  18.3 0.8 %collective-permute-start.3 = (f32[1,640]{1,0:T(1,128)S(1)}, f32[1,640]{1,0:T(1,128)S(1)}, u32[]{:S(2)}, u32[]{:S(2)}) collective-permute-start(f32[1,640]{1,0:T(1,128)S(1)} %get-tuple-element.46.refs_0_), channel_id=1, source_target_pairs={{0,8},{4,12},{8,0},{12,4},{1,9},{5,13},{9,1},{13,5},{2,10},{6,14},... | collective-permute-start | bytes 7688 | tf_op jit(solution)/shard_map/ppermute | solution.py:684
  19.1 2.3 %collective-permute-start.6 = (bf16[304,128]{1,0:T(8,128)(2,1)S(1)}, bf16[304,128]{1,0:T(8,128)(2,1)S(1)}, u32[]{:S(2)}, u32[]{:S(2)}) collective-permute-start(bf16[304,128]{1,0:T(8,128)(2,1)S(1)} %get-tuple-element.57), channel_id=1, source_target_pairs={{0,12},{4,8},{8,4},{12,0},{1,13},{5,9},{9,5},{13,1},{2,14},{6,10},... | collective-permute-start | bytes 233480 | tf_op jit(solution)/shard_map/ppermute | solution.py:684
  21.4 1.6 %collective-permute-start.7 = (bf16[304,128]{1,0:T(8,128)(2,1)S(1)}, bf16[304,128]{1,0:T(8,128)(2,1)S(1)}, u32[]{:S(2)}, u32[]{:S(2)}) collective-permute-start(bf16[304,128]{1,0:T(8,128)(2,1)S(1)} %get-tuple-element.58), channel_id=1, source_target_pairs={{0,8},{4,12},{8,0},{12,4},{1,9},{5,13},{9,1},{13,5},{2,10},{6,14},... | collective-permute-start | bytes 233480 | tf_op jit(solution)/shard_map/ppermute | solution.py:684
  23.0 0.5 %collective-permute-start.8 = (bf16[304,128]{1,0:T(8,128)(2,1)S(1)}, bf16[304,128]{1,0:T(8,128)(2,1)S(1)}, u32[]{:S(2)}, u32[]{:S(2)}) collective-permute-start(bf16[304,128]{1,0:T(8,128)(2,1)S(1)} %get-tuple-element.59), channel_id=1, source_target_pairs={{0,4},{4,0},{8,12},{12,8},{1,5},{5,1},{9,13},{13,9},{2,6},{6,2},{1... | collective-permute-start | bytes 233480 | tf_op jit(solution)/shard_map/ppermute | solution.py:684
  23.5 0.0 collective-permute-done.3.refs_1_
  23.5 0.3 %last_head.1 = (bf16[128,128]{1,0:T(8,128)(2,1)S(1)}, bf16[128,128]{1,0:T(8,128)(2,1)S(1)}, f32[128,128]{1,0:T(8,128)S(1)}, f32[128,128]{1,0:T(8,128)S(1)}, f32[1,640]{1,0:T(1,128)S(1)}) custom-call(f32[1,640]{1,0:T(1,128)S(1)} %get-tuple-element.46.refs_0_, f32[1,640]{1,0:T(1,128)S(1)} %collective-permute-done.3.refs_1_, ...), custom_call_target="tpu_custom_call" | custom-call | flops 20000000000 | tf_op jit(solution)/shard_map/last_head/pallas_call | solution.py:694
  23.8 0.1 collective-permute-start.4
  23.9 1.1 %collective-permute-done.4 = f32[1,640]{1,0:T(1,128)S(1)} collective-permute-done((f32[1,640]{1,0:T(1,128)S(1)}, f32[1,640]{1,0:T(1,128)S(1)}, u32[]{:S(2)}, u32[]{:S(2)}) %collective-permute-start.4) | collective-permute-done | bytes 2592 | tf_op jit(solution)/shard_map/ppermute | solution.py:684
  25.1 1.5 %collective-permute-start.5 = (f32[1,640]{1,0:T(1,128)S(1)}, f32[1,640]{1,0:T(1,128)S(1)}, u32[]{:S(2)}, u32[]{:S(2)}) collective-permute-start(f32[1,640]{1,0:T(1,128)S(1)} %add.3.refs_4_), channel_id=1, source_target_pairs={{0,4},{4,0},{8,12},{12,8},{1,5},{5,1},{9,13},{13,9},{2,6},{6,2},{1... | collective-permute-start | bytes 7688 | tf_op jit(solution)/shard_map/ppermute | solution.py:684
  26.6 2.1 %collective-permute-done.5.refs_5_ = f32[1,640]{1,0:T(1,128)S(1)} collective-permute-done((f32[1,640]{1,0:T(1,128)S(1)}, f32[1,640]{1,0:T(1,128)S(1)}, u32[]{:S(2)}, u32[]{:S(2)}) %collective-permute-start.5) | collective-permute-done | bytes 2592 | tf_op jit(solution)/shard_map/ppermute | solution.py:684
  28.7 0.0 collective-permute-done.6.refs_11_
  28.7 0.0 collective-permute-done.7.refs_12_
  28.7 0.0 collective-permute-done.8.refs_13_
  28.7 2.8 %finish.1 = (f32[640]{0:T(1024)}, bf16[1,128,640]{2,1,0:T(8,128)(2,1)}, bf16[1,128,640]{2,1,0:T(8,128)(2,1)}, bf16[1,128,640]{2,1,0:T(8,128)(2,1)}, bf16[1,128,640]{2,1,0:T(8,128)(2,1)}) custom-call(s32[2,5]{1,0:T(2,128)S(1)} %copy-done.4, bf16[1,128,640]{2,1,0:T(8,128)(2,1)S(1)} %copy-done.1, bf16[1,128,640]{2,1,0:T(8,128)(2,1)S(1)} %copy-done.2, ...), custom_call_target="tpu_custom_call" | custom-call | flops 1000000000 | tf_op jit(solution)/shard_map/finish/pallas_call | solution.py:694
  (15 shorter events, 0.0 us)
Async XLA Ops:
  3.8 5.8 %copy-start.10 = (f32[640]{0:T(1024)S(1)}, f32[640]{0:T(1024)}, u32[]{:S(2)}) copy-start(f32[640]{0:T(1024)} %param.10) | copy-start | bytes 7684
  3.8 9.4 %collective-permute-start = (bf16[352,128]{1,0:T(8,128)(2,1)}, bf16[352,128]{1,0:T(8,128)(2,1)S(1)}, u32[]{:S(2)}, u32[]{:S(2)}) collective-permute-start(bf16[352,128]{1,0:T(8,128)(2,1)} %get-tuple-element.43), channel_id=1, source_target_pairs={{0,12},{4,8},{8,4},{12,0},{1,13},{5,9},{9,5},{13,1},{2,14},{6,10},... | collective-permute-start | bytes 270344 | tf_op jit(solution)/shard_map/ppermute | solution.py:684
  8.9 7.8 %collective-permute-start.1 = (bf16[352,128]{1,0:T(8,128)(2,1)}, bf16[352,128]{1,0:T(8,128)(2,1)S(1)}, u32[]{:S(2)}, u32[]{:S(2)}) collective-permute-start(bf16[352,128]{1,0:T(8,128)(2,1)} %get-tuple-element.44), channel_id=1, source_target_pairs={{0,8},{4,12},{8,0},{12,4},{1,9},{5,13},{9,1},{13,5},{2,10},{6,14},... | collective-permute-start | bytes 270344 | tf_op jit(solution)/shard_map/ppermute | solution.py:684
  8.9 7.8 %collective-permute-start.2 = (bf16[352,128]{1,0:T(8,128)(2,1)}, bf16[352,128]{1,0:T(8,128)(2,1)S(1)}, u32[]{:S(2)}, u32[]{:S(2)}) collective-permute-start(bf16[352,128]{1,0:T(8,128)(2,1)} %get-tuple-element.45), channel_id=1, source_target_pairs={{0,4},{4,0},{8,12},{12,8},{1,5},{5,1},{9,13},{13,9},{2,6},{6,2},{1... | collective-permute-start | bytes 270344 | tf_op jit(solution)/shard_map/ppermute | solution.py:684
  9.5 0.7 %copy-start.4 = (s32[2,5]{1,0:T(2,128)S(1)}, s32[2,5]{1,0:T(2,128)}, u32[]{:S(2)}) copy-start(s32[2,5]{1,0:T(2,128)} %offsets_ref.7) | copy-start | bytes 124
  10.2 0.9 %copy-start = (bf16[1,128,640]{2,1,0:T(8,128)(2,1)S(1)}, bf16[1,128,640]{2,1,0:T(8,128)(2,1)}, u32[]{:S(2)}) copy-start(bf16[1,128,640]{2,1,0:T(8,128)(2,1)} %grad_ref.3) | copy-start | bytes 491524
  11.1 1.0 %copy-start.5 = (f32[128,640]{1,0:T(8,128)S(1)}, f32[128,640]{1,0:T(8,128)}, u32[]{:S(2)}) copy-start(f32[128,640]{1,0:T(8,128)} %get-tuple-element.36.out_ref) | copy-start | bytes 983044
  12.1 4.6 %copy-start.1 = (bf16[1,128,640]{2,1,0:T(8,128)(2,1)S(1)}, bf16[1,128,640]{2,1,0:T(8,128)(2,1)}, u32[]{:S(2)}) copy-start(bf16[1,128,640]{2,1,0:T(8,128)(2,1)} %q_ref.5) | copy-start | bytes 491524
  12.1 4.6 %copy-start.6 = (f32[128,640]{1,0:T(8,128)S(1)}, f32[128,640]{1,0:T(8,128)}, u32[]{:S(2)}) copy-start(f32[128,640]{1,0:T(8,128)} %get-tuple-element.36.out_ref) | copy-start | bytes 983044
  12.1 4.6 %copy-start.8 = (bf16[352,128]{1,0:T(8,128)(2,1)S(1)}, bf16[352,128]{1,0:T(8,128)(2,1)}, u32[]{:S(2)}) copy-start(bf16[352,128]{1,0:T(8,128)(2,1)} %get-tuple-element.42.refs_2_) | copy-start | bytes 270340
  12.1 4.6 %copy-start.9 = (f32[16,128]{1,0:T(8,128)S(1)}, f32[16,128]{1,0:T(8,128)}, u32[]{:S(2)}) copy-start(f32[16,128]{1,0:T(8,128)} %get-tuple-element.38.refs_0_.refs_1_) | copy-start | bytes 24580
  16.7 6.8 %copy-start.2 = (bf16[1,128,640]{2,1,0:T(8,128)(2,1)S(1)}, bf16[1,128,640]{2,1,0:T(8,128)(2,1)}, u32[]{:S(2)}) copy-start(bf16[1,128,640]{2,1,0:T(8,128)(2,1)} %k_ref.3) | copy-start | bytes 491524
  16.7 6.8 %copy-start.3 = (bf16[1,128,640]{2,1,0:T(8,128)(2,1)S(1)}, bf16[1,128,640]{2,1,0:T(8,128)(2,1)}, u32[]{:S(2)}) copy-start(bf16[1,128,640]{2,1,0:T(8,128)(2,1)} %v_ref.3) | copy-start | bytes 491524
  16.7 6.8 %copy-start.7 = (bf16[128,640]{1,0:T(8,128)(2,1)S(1)}, bf16[128,640]{1,0:T(8,128)(2,1)}, u32[]{:S(2)}) copy-start(bf16[128,640]{1,0:T(8,128)(2,1)} %get-tuple-element.35.refs_6_.expo_ref) | copy-start | bytes 491524
  18.3 5.2 %collective-permute-start.3 = (f32[1,640]{1,0:T(1,128)S(1)}, f32[1,640]{1,0:T(1,128)S(1)}, u32[]{:S(2)}, u32[]{:S(2)}) collective-permute-start(f32[1,640]{1,0:T(1,128)S(1)} %get-tuple-element.46.refs_0_), channel_id=1, source_target_pairs={{0,8},{4,12},{8,0},{12,4},{1,9},{5,13},{9,1},{13,5},{2,10},{6,14},... | collective-permute-start | bytes 7688 | tf_op jit(solution)/shard_map/ppermute | solution.py:684
  19.1 9.6 %collective-permute-start.6 = (bf16[304,128]{1,0:T(8,128)(2,1)S(1)}, bf16[304,128]{1,0:T(8,128)(2,1)S(1)}, u32[]{:S(2)}, u32[]{:S(2)}) collective-permute-start(bf16[304,128]{1,0:T(8,128)(2,1)S(1)} %get-tuple-element.57), channel_id=1, source_target_pairs={{0,12},{4,8},{8,4},{12,0},{1,13},{5,9},{9,5},{13,1},{2,14},{6,10},... | collective-permute-start | bytes 233480 | tf_op jit(solution)/shard_map/ppermute | solution.py:684
  21.4 7.3 %collective-permute-start.7 = (bf16[304,128]{1,0:T(8,128)(2,1)S(1)}, bf16[304,128]{1,0:T(8,128)(2,1)S(1)}, u32[]{:S(2)}, u32[]{:S(2)}) collective-permute-start(bf16[304,128]{1,0:T(8,128)(2,1)S(1)} %get-tuple-element.58), channel_id=1, source_target_pairs={{0,8},{4,12},{8,0},{12,4},{1,9},{5,13},{9,1},{13,5},{2,10},{6,14},... | collective-permute-start | bytes 233480 | tf_op jit(solution)/shard_map/ppermute | solution.py:684
  23.0 5.7 %collective-permute-start.8 = (bf16[304,128]{1,0:T(8,128)(2,1)S(1)}, bf16[304,128]{1,0:T(8,128)(2,1)S(1)}, u32[]{:S(2)}, u32[]{:S(2)}) collective-permute-start(bf16[304,128]{1,0:T(8,128)(2,1)S(1)} %get-tuple-element.59), channel_id=1, source_target_pairs={{0,4},{4,0},{8,12},{12,8},{1,5},{5,1},{9,13},{13,9},{2,6},{6,2},{1... | collective-permute-start | bytes 233480 | tf_op jit(solution)/shard_map/ppermute | solution.py:684
  23.8 1.2 %collective-permute-start.4 = (f32[1,640]{1,0:T(1,128)S(1)}, f32[1,640]{1,0:T(1,128)S(1)}, u32[]{:S(2)}, u32[]{:S(2)}) collective-permute-start(f32[1,640]{1,0:T(1,128)S(1)} %get-tuple-element.51), channel_id=1, source_target_pairs={{0,16},{16,0},{1,17},{17,1},{2,18},{18,2},{3,19},{19,3},{4,20},{20... | collective-permute-start | bytes 7688 | tf_op jit(solution)/shard_map/ppermute | solution.py:684
  25.1 3.6 %collective-permute-start.5 = (f32[1,640]{1,0:T(1,128)S(1)}, f32[1,640]{1,0:T(1,128)S(1)}, u32[]{:S(2)}, u32[]{:S(2)}) collective-permute-start(f32[1,640]{1,0:T(1,128)S(1)} %add.3.refs_4_), channel_id=1, source_target_pairs={{0,4},{4,0},{8,12},{12,8},{1,5},{5,1},{9,13},{13,9},{2,6},{6,2},{1... | collective-permute-start | bytes 7688 | tf_op jit(solution)/shard_map/ppermute | solution.py:684

commit v10 on v8

--- a/solution.py
+++ b/solution.py
@@ -273,13 +273,20 @@
     return jnp.where(position % step == offset, 1.0, 0.0)
 
 
-def piece_rows(row):
+def piece_rows(row, others=None):
     pieces = []
     for _ in range(PIECES):
         piece = row.astype(LOW).astype(WIDE)
         pieces.append(piece)
         row = row - piece
-    return jnp.concatenate(pieces + [jnp.zeros((TILE - PIECES, row.shape[1]), WIDE)], 0)
+    if others is None:
+        others = jnp.zeros((TILE - PIECES, row.shape[1]), WIDE)
+    return jnp.concatenate(pieces + [others], 0)
+
+
+def gain_pieces(rows):
+    high = rows.astype(LOW)
+    return high, (rows - high.astype(WIDE)).astype(LOW)
 
 
 def joined_row(rows, first):
@@ -290,8 +297,7 @@
 
 
 def gain_row_of(ones, product):
-    high = product.astype(LOW)
-    rest = (product - high.astype(WIDE)).astype(LOW)
+    high, rest = gain_pieces(product)
     return (contract(ones, high, 1, 1) + contract(ones, rest, 1, 1))[:1]
 
 
@@ -357,7 +363,8 @@
         stats_ref[TILE + head : TILE + head + 1, :] = totals[head]
     for head in owned:
         outs[head] = outs[head] * (1.0 / totals[head])
-    picked_outs = [contract(picks[head], outs[head].astype(LOW), 1, 1).astype(LOW) for head in owned]
+    outs = [out.astype(LOW) for out in outs]
+    picked_outs = [contract(picks[head], outs[head], 1, 1).astype(LOW) for head in owned]
     for head in heads:
         out_ref[:, head_cols(head)] = outs[head]
     for head in owned:
@@ -401,7 +408,7 @@
         seen = jnp.maximum(
             hit_row(top_offset, top_step, tokens), hit_row(mid_offset, R1, tokens)
         )
-        attn = out_ref[:, cols]
+        attn = out_ref[:, cols].astype(WIDE)
         normed = attn * lax.rsqrt(column_mean(attn * attn) + EPS)
         product = grad_norms[head] * normed * (1.0 - seen)
         gain_part_ref[:, cols] = gain_row_of(ones, product) / gain_ref[:, cols]
@@ -418,8 +425,8 @@
 def owner_kernel(top_step, offsets_ref, q_ref, gain_ref, out_ref, grad_norm_ref, *refs):
     stats_ref, gain_base_ref = refs[:2]
     payload_refs, refs = nearest_first(refs[2 : 2 + SPAN]), refs[2 + SPAN :]
-    gain_part_ref, normed_ref, grad_low_ref, score_grad_ref, kept_ref = refs[:5]
-    return_refs = refs[5:]
+    normed_ref, grad_low_ref, score_grad_ref, kept_ref = refs[:4]
+    return_refs = refs[4:]
     tokens = q_ref.shape[1]
     heads = q_ref.shape[2] // HEAD_DIM
     top_rows, mid_rows = picked_counts(tokens, top_step)
@@ -501,7 +508,7 @@
     soft_low, soft_last_low = soft.astype(LOW), soft_last.astype(LOW)
     factor_last = factor_last * inv_last
     attn = (factor * inv_total) * base_attn + contract(v_rows, soft_low, 0, 0)
-    attn_last = factor_last * out_ref[:, cols] + contract(v_peers, soft_last_low, 0, 0)
+    attn_last = factor_last * out_ref[:, cols].astype(WIDE) + contract(v_peers, soft_last_low, 0, 0)
     _, product, grad_low, inner = norm_backward(attn, grad_norm)
     normed_last, product_last, grad_last_low, inner_last = norm_backward(
         attn_last, grad_norm_ref[:, cols]
@@ -519,10 +526,21 @@
     attn_rows = attn.T.astype(LOW)
     log_total = top_score + jnp.log(total)
     padding = jnp.zeros((1, top_all - mid_all), WIDE)
+    once = is_top + (1.0 - is_top) * (1.0 - both_flag)
+    ones_all = jnp.ones((TILE, queries), LOW)
+    own_gain = gain_row_of(ones_all, product * once) / gain_row
+    gain_rows = [
+        gain_base_ref[:, head_cols(head)] + jnp.where(me == head, 1.0, 0.0) * own_gain
+        for head in range(OWNED)
+    ]
+    gain_rows.append(gain_row_of(ones, product_last) / gain_ref[:, cols])
+    gain_high, gain_rest = gain_pieces(jnp.concatenate(gain_rows, 0))
     log_rows = jnp.concatenate(
         [
-            piece_rows(log_total[:, :top_all]),
-            piece_rows(jnp.concatenate([log_total[:, top_all:], padding], 1)),
+            piece_rows(log_total[:, :top_all], gain_high.astype(WIDE)),
+            piece_rows(
+                jnp.concatenate([log_total[:, top_all:], padding], 1), gain_rest.astype(WIDE)
+            ),
         ],
         0,
     ).astype(LOW)
@@ -540,23 +558,12 @@
     score_grad_ref[...] = score_grad_last
     kept_ref[0:1, :] = factor_last
     kept_ref[1:2, :] = inner_last
-    once = is_top + (1.0 - is_top) * (1.0 - both_flag)
-    ones_all = jnp.ones((TILE, queries), LOW)
-    own_gain = gain_row_of(ones_all, product * once) / gain_row
-    last_gain = gain_row_of(ones, product_last) / gain_ref[:, cols]
-    for head in range(OWNED):
-        gain_part_ref[:, head_cols(head)] = gain_base_ref[:, head_cols(head)] + (
-            jnp.where(me == head, 1.0, 0.0) * own_gain
-        )
-    gain_part_ref[:, cols] = last_gain
-
-
-def last_head_kernel(top_step, *refs):
-    gain_part_ref, gain_peer_ref, q_ref, k_ref, v_ref, gain_ref, expo_ref, *refs = refs
+
+
+def last_head_kernel(top_step, q_ref, k_ref, v_ref, gain_ref, expo_ref, *refs):
     normed_ref, grad_low_ref, peer_score_grad_ref, kept_ref, *peers = refs[: 4 + PEERS]
     peers = peers[::-1]
-    attended_ref, dq_ref, dk_ref, dv_ref, gain_sum_ref = refs[4 + PEERS :]
-    gain_sum_ref[...] = gain_part_ref[...] + gain_peer_ref[...]
+    attended_ref, dq_ref, dk_ref, dv_ref = refs[4 + PEERS :]
     picked = sum(picked_counts(q_ref.shape[1], top_step))
     score_scale = 1.0 / math.sqrt(HEAD_DIM)
     cols = head_cols(q_ref.shape[2] // HEAD_DIM - 1)
@@ -572,6 +579,15 @@
         contract(score_grad, k_ref[0, :, cols], 0, 0)
         + contract(peer_score_grad_ref[...], k_peers, 0, 0)
     ).astype(LOW)
+
+
+def gain_kernel(picked, *refs):
+    return_refs, gain_ref = nearest_first(refs[:SPAN]), refs[SPAN]
+    tiles = [ref[6 * picked : 6 * picked + STAT_TILES].astype(WIDE) for ref in return_refs]
+    parts = [tile[PIECES:TILE] + tile[TILE + PIECES :] for tile in tiles]
+    total = (parts[0] + parts[1]) + (parts[2] + parts[3])
+    for head in range(gain_ref.shape[1] // HEAD_DIM):
+        gain_ref[:, head_cols(head)] = total[head : head + 1]
 
 
 def finish_kernel(top_step, offsets_ref, q_ref, k_ref, v_ref, gain_ref, expo_ref, out_ref, *refs):
@@ -621,7 +637,7 @@
             top_hit > 0.5, top_log, jnp.where(mid_hit > 0.5, mid_log, top_score + jnp.log(total))
         )
         factors.append(jnp.exp(top_score - log_total))
-        attn = jnp.where(seen, attn_parts[head], out_ref[:, every[head]])
+        attn = jnp.where(seen, attn_parts[head], out_ref[:, every[head]].astype(WIDE))
         normed, _, grad_low, inner = norm_backward(attn, grad_norm_ref[:, every[head]])
         normeds.append(normed)
         grad_lows.append(grad_low)
@@ -701,7 +717,7 @@
         bind(pack_kernel, top_step),
         "pack",
         (offsets, queries, keys, values, grad_y),
-        [payload] * SPAN + [low_block, wide_block, stats_block],
+        [payload] * SPAN + [low_block, low_block, stats_block],
         1,
         vmem=PACK_VMEM,
         scratch=[pltpu.VMEM((OWNED, *payload.shape), LOW)],
@@ -714,12 +730,11 @@
         [wide_block, gain_block, shape((tokens, 2 * width), LOW), shape((tokens, 2 * OWNED * tokens), LOW)],
         2,
     )
-    gain_part, normed, grad_low, score_grad, kept, own_answer, *answers = call(
+    normed, grad_low, score_grad, kept, own_answer, *answers = call(
         bind(owner_kernel, top_step),
         "owner",
         (offsets, queries, gain_row, base_out, grad_norm, stats, gain_base, own, *received),
         [
-            gain_block,
             wide_head,
             low_head,
             shape((PEERS * picked, HEAD_DIM), LOW),
@@ -729,28 +744,15 @@
         3,
     )
     returned = to_peers(answers)
-    *last_results, gain_sum = call(
+    last_results = call(
         bind(last_head_kernel, top_step),
         "last_head",
-        (
-            gain_part,
-            across(gain_part, "ctx", 2),
-            queries,
-            keys,
-            values,
-            gain_row,
-            expo,
-            normed,
-            grad_low,
-            score_grad,
-            kept,
-            *received,
-        ),
-        [low_head, low_head, wide_head, wide_head, gain_block],
+        (queries, keys, values, gain_row, expo, normed, grad_low, score_grad, kept, *received),
+        [low_head, low_head, wide_head, wide_head],
         20,
     )
-    gain_sum = gain_sum + across(gain_sum, "dp", 1)
-    gain_rest = across(gain_sum, "ctx", 1)
+    (gain_sum,) = call(bind(gain_kernel, picked), "gain", (own_answer, *returned), [gain_block], 1)
+    gain_rest = across(gain_sum, "dp", 1)
     attended, query_grad, key_grad, value_grad, gain_sum = call(
         bind(finish_kernel, top_step),
         "finish",
@@ -779,6 +781,13 @@
     return attended, query_grad, key_grad, value_grad, gain_grad
 
 
+def shards(*operands):
+    one_segment = lax.axis_size("ctx") == SPAN
+    if one_segment and operands[0].shape[2] == (OWNED + 1) * HEAD_DIM:
+        return one_segment_shards(*operands)
+    return general_shards(*operands)
+
+
 def solution(mesh):
     in_specs = (
         P("dp", "ctx", "head"),
@@ -795,5 +804,4 @@
         P("dp", "ctx", "head"),
         P("head"),
     )
-    body = one_segment_shards if mesh.shape["ctx"] == SPAN else general_shards
-    return jax.shard_map(body, mesh=mesh, in_specs=in_specs, out_specs=out_specs, check_vma=False)
+    return jax.shard_map(shards, mesh=mesh, in_specs=in_specs, out_specs=out_specs, check_vma=False)

time: 31 us -> 30.1 us (0.971)
  starting transfers between devices: 12.5 us -> 10.2 us
  waiting for transfers between devices: 6.51 us -> 7.93 us
    ppermute x9 -> x7, starting transfers between devices: 12.5 us -> 10.2 us  [across(): return lax.ppermute(block, axis, route)]
    ppermute x9 -> x7, waiting for transfers between devices: 6.51 us -> 7.93 us  [across(): return lax.ppermute(block, axis, route)]
    pallas_call x5 -> x6, Pallas kernels: 7.77 us -> 7.82 us  [call(): pl.pallas_call(kernel, out_shape=results, in_specs=[SMEM_SPEC if block.dt...]
  transfers between devices with their start and end apart: 9 -> 7, of which waited for: 3 -> 3; matrix products, arithmetic and copies ran while one was open for 0% -> 0% of each run, Pallas kernels for 12% -> 12%
where the time goes in v10:
time: 30.1 us; the launch traced here: 29.9 us
  starting transfers between devices  10.2 us (34%)
  waiting for transfers between devices  7.93 us (26%)
  Pallas kernels  7.82 us (26%)
  local copies, waits for them, and re-layouts  2.55 us (8%)
  between operations  0.71 us (2%)
  other arithmetic  0.61 us (2%)
    ppermute x7, starting transfers between devices, across(): return lax.ppermute(block, axis, route)  10.2 us
    ppermute x7, waiting for transfers between devices, across(): return lax.ppermute(block, axis, route)  7.93 us
    pallas_call x6, Pallas kernels, call(): pl.pallas_call(kernel, out_shape=results, in_specs=[SMEM_SPEC if block.dt...  7.82 us
    unnamed x22, local copies, waits for them, and re-layouts  2.55 us
    add x1, other arithmetic, one_segment_shards(): gain_grad = (gain_sum + gain_rest).reshape(width)  0.61 us
  transfers between devices with their start and end apart: 7, of which 3 were waited for; matrix products, arithmetic and copies ran while one was open for 0% of the time, Pallas kernels for 12%

profile of v10, /device:TPU:0, one launch (start us, length us, event | category | flops | bytes accessed | tf_op | source)
XLA Modules:
  0.0 29.9 jit_solution(17177690757960516041)
XLA Ops:
  0.6 2.6 %pack.1 = (bf16[352,128]{1,0:T(8,128)(2,1)}, bf16[352,128]{1,0:T(8,128)(2,1)}, bf16[352,128]{1,0:T(8,128)(2,1)}, bf16[352,128]{1,0:T(8,128)(2,1)}, bf16[128,640]...) custom-call(s32[2,5]{1,0:T(2,128)} %offsets_ref.7, bf16[1,128,640]{2,1,0:T(8,128)(2,1)} %q_ref.7, ...), custom_call_target="tpu_custom_call" | custom-call | flops 1000000000 | tf_op jit(solution)/shard_map/pack/pallas_call | solution.py:687
  3.2 5.1 %collective-permute-start = (bf16[352,128]{1,0:T(8,128)(2,1)}, bf16[352,128]{1,0:T(8,128)(2,1)S(1)}, u32[]{:S(2)}, u32[]{:S(2)}) collective-permute-start(bf16[352,128]{1,0:T(8,128)(2,1)} %get-tuple-element.41), channel_id=1, source_target_pairs={{0,12},{4,8},{8,4},{12,0},{1,13},{5,9},{9,5},{13,1},{2,14},{6,10},... | collective-permute-start | bytes 270344 | tf_op jit(solution)/shard_map/ppermute | solution.py:679
  8.4 0.0 collective-permute-start.1
  8.4 0.6 %collective-permute-start.2 = (bf16[352,128]{1,0:T(8,128)(2,1)}, bf16[352,128]{1,0:T(8,128)(2,1)S(1)}, u32[]{:S(2)}, u32[]{:S(2)}) collective-permute-start(bf16[352,128]{1,0:T(8,128)(2,1)} %get-tuple-element.43), channel_id=1, source_target_pairs={{0,4},{4,0},{8,12},{12,8},{1,5},{5,1},{9,13},{13,9},{2,6},{6,2},{1... | collective-permute-start | bytes 270344 | tf_op jit(solution)/shard_map/ppermute | solution.py:679
  9.0 0.0 copy-done.10
  9.0 0.7 %copy-done.4 = s32[2,5]{1,0:T(2,128)S(1)} copy-done((s32[2,5]{1,0:T(2,128)S(1)}, s32[2,5]{1,0:T(2,128)}, u32[]{:S(2)}) %copy-start.4) | copy-done | bytes 64
  9.7 0.9 %copy-done = bf16[1,128,640]{2,1,0:T(8,128)(2,1)S(1)} copy-done((bf16[1,128,640]{2,1,0:T(8,128)(2,1)S(1)}, bf16[1,128,640]{2,1,0:T(8,128)(2,1)}, u32[]{:S(2)}) %copy-start) | copy-done | bytes 163864
  10.6 0.9 %copy-done.6 = bf16[128,640]{1,0:T(8,128)(2,1)S(1)} copy-done((bf16[128,640]{1,0:T(8,128)(2,1)S(1)}, bf16[128,640]{1,0:T(8,128)(2,1)}, u32[]{:S(2)}) %copy-start.6) | copy-done | bytes 163864
  11.5 1.0 %prepare.1 = (f32[128,640]{1,0:T(8,128)S(1)}, f32[1,640]{1,0:T(1,128)S(1)}, bf16[128,1280]{1,0:T(8,128)(2,1)S(1)}, bf16[128,1024]{1,0:T(8,128)(2,1)S(1)}) custom-call(s32[2,5]{1,0:T(2,128)S(1)} %copy-done.4, bf16[1,128,640]{2,1,0:T(8,128)(2,1)S(1)} %copy-done, f32[1,640]{1,0:T(1,128)S(1)} %reshape.16.gain_ref, bf16[128,640]{1,0:T(8,128)(2,1)S(1)} %copy-done.6), custom_call_target="tpu_custom_call" | custom-call | flops 2000000000 | tf_op jit(solution)/shard_map/prepare/pallas_call | solution.py:687
  12.6 0.0 collective-permute-done.refs_3_.refs_4_
  12.6 3.6 %collective-permute-done.1.refs_4_.refs_5_ = bf16[352,128]{1,0:T(8,128)(2,1)S(1)} collective-permute-done((bf16[352,128]{1,0:T(8,128)(2,1)}, bf16[352,128]{1,0:T(8,128)(2,1)S(1)}, u32[]{:S(2)}, u32[]{:S(2)}) %collective-permute-start.1) | collective-permute-done | bytes 90144 | tf_op jit(solution)/shard_map/ppermute | solution.py:679
  16.1 0.0 collective-permute-done.2.refs_5_.refs_6_
  16.1 0.0 copy-done.1
  16.1 0.0 copy-done.7
  16.1 0.0 copy-done.8
  16.1 0.0 copy-done.9
  16.2 0.0 copy-start.2
  16.2 0.0 copy-start.3
  16.2 0.0 copy-start.5
  16.2 1.6 %owner.1 = (f32[128,128]{1,0:T(8,128)S(1)}, bf16[128,128]{1,0:T(8,128)(2,1)S(1)}, bf16[144,128]{1,0:T(8,128)(2,1)S(1)}, f32[8,128]{1,0:T(8,128)S(1)}, bf16[304,1...) custom-call(s32[2,5]{1,0:T(2,128)S(1)} %copy-done.4, ...), custom_call_target="tpu_custom_call" | custom-call | flops 3000000000 | tf_op jit(solution)/shard_map/owner/pallas_call | solution.py:687
  17.8 2.6 %collective-permute-start.3 = (bf16[304,128]{1,0:T(8,128)(2,1)S(1)}, bf16[304,128]{1,0:T(8,128)(2,1)S(1)}, u32[]{:S(2)}, u32[]{:S(2)}) collective-permute-start(bf16[304,128]{1,0:T(8,128)(2,1)S(1)} %get-tuple-element.45), channel_id=1, source_target_pairs={{0,12},{4,8},{8,4},{12,0},{1,13},{5,9},{9,5},{13,1},{2,14},{6,10},... | collective-permute-start | bytes 233480 | tf_op jit(solution)/shard_map/ppermute | solution.py:679
  20.4 0.0 collective-permute-start.4
  20.4 1.8 %collective-permute-start.5 = (bf16[304,128]{1,0:T(8,128)(2,1)S(1)}, bf16[304,128]{1,0:T(8,128)(2,1)S(1)}, u32[]{:S(2)}, u32[]{:S(2)}) collective-permute-start(bf16[304,128]{1,0:T(8,128)(2,1)S(1)} %get-tuple-element.47), channel_id=1, source_target_pairs={{0,4},{4,0},{8,12},{12,8},{1,5},{5,1},{9,13},{13,9},{2,6},{6,2},{1... | collective-permute-start | bytes 233480 | tf_op jit(solution)/shard_map/ppermute | solution.py:679
  22.2 0.0 copy-done.2
  22.2 0.3 %last_head.1 = (bf16[128,128]{1,0:T(8,128)(2,1)S(1)}, bf16[128,128]{1,0:T(8,128)(2,1)S(1)}, f32[128,128]{1,0:T(8,128)S(1)}, f32[128,128]{1,0:T(8,128)S(1)}) custom-call(bf16[1,128,640]{2,1,0:T(8,128)(2,1)S(1)} %copy-done.1, bf16[1,128,640]{2,1,0:T(8,128)(2,1)S(1)} %copy-done.2, bf16[1,128,640]{2,1,0:T(8,128)(2,1)S(1)} %copy-done.3, ...), custom_call_target="tpu_custom_call" | custom-call | flops 20000000000 | tf_op jit(solution)/shard_map/last_head/pallas_call | solution.py:687
  22.6 1.9 %collective-permute-done.3.refs_1_.refs_10_ = bf16[304,128]{1,0:T(8,128)(2,1)S(1)} collective-permute-done((bf16[304,128]{1,0:T(8,128)(2,1)S(1)}, bf16[304,128]{1,0:T(8,128)(2,1)S(1)}, u32[]{:S(2)}, u32[]{:S(2)}) %collective-permute-start.3) | collective-permute-done | bytes 77856 | tf_op jit(solution)/shard_map/ppermute | solution.py:679
  24.5 2.4 %collective-permute-done.4.refs_2_.refs_11_ = bf16[304,128]{1,0:T(8,128)(2,1)S(1)} collective-permute-done((bf16[304,128]{1,0:T(8,128)(2,1)S(1)}, bf16[304,128]{1,0:T(8,128)(2,1)S(1)}, u32[]{:S(2)}, u32[]{:S(2)}) %collective-permute-start.4) | collective-permute-done | bytes 77856 | tf_op jit(solution)/shard_map/ppermute | solution.py:679
  26.9 0.0 collective-permute-done.5.refs_3_.refs_12_
  26.9 0.1 collective-permute-start.6
  27.0 2.3 %finish.1 = (bf16[1,128,640]{2,1,0:T(8,128)(2,1)}, bf16[1,128,640]{2,1,0:T(8,128)(2,1)}, bf16[1,128,640]{2,1,0:T(8,128)(2,1)}, bf16[1,128,640]{2,1,0:T(8,128)(2,1)}, f32[1,640]{1,0:T(1,128)S(1)}) custom-call(s32[2,5]{1,0:T(2,128)S(1)} %copy-done.4, bf16[1,128,640]{2,1,0:T(8,128)(2,1)S(1)} %copy-done.1, bf16[1,128,640]{2,1,0:T(8,128)(2,1)S(1)} %copy-done.2, ...), custom_call_target="tpu_custom_call" | custom-call | flops 1000000000 | tf_op jit(solution)/shard_map/finish/pallas_call | solution.py:687
  29.3 0.0 collective-permute-done.6
  29.3 0.6 %add_reduce_fusion = f32[640]{0:T(1024)} fusion(f32[1,640]{1,0:T(1,128)S(1)} %get-tuple-element.60, f32[1,640]{1,0:T(1,128)S(1)} %collective-permute-done.6), kind=kLoop, calls=%fused_computation | loop fusion | flops 640 | bytes 7680 | tf_op jit(solution)/shard_map/add | solution.py:780
  (12 shorter events, 0.0 us)
Async XLA Ops:
  3.2 5.8 %copy-start.10 = (f32[640]{0:T(1024)S(1)}, f32[640]{0:T(1024)}, u32[]{:S(2)}) copy-start(f32[640]{0:T(1024)} %param.10) | copy-start | bytes 7684
  3.2 9.3 %collective-permute-start = (bf16[352,128]{1,0:T(8,128)(2,1)}, bf16[352,128]{1,0:T(8,128)(2,1)S(1)}, u32[]{:S(2)}, u32[]{:S(2)}) collective-permute-start(bf16[352,128]{1,0:T(8,128)(2,1)} %get-tuple-element.41), channel_id=1, source_target_pairs={{0,12},{4,8},{8,4},{12,0},{1,13},{5,9},{9,5},{13,1},{2,14},{6,10},... | collective-permute-start | bytes 270344 | tf_op jit(solution)/shard_map/ppermute | solution.py:679
  8.4 7.8 %collective-permute-start.1 = (bf16[352,128]{1,0:T(8,128)(2,1)}, bf16[352,128]{1,0:T(8,128)(2,1)S(1)}, u32[]{:S(2)}, u32[]{:S(2)}) collective-permute-start(bf16[352,128]{1,0:T(8,128)(2,1)} %get-tuple-element.42), channel_id=1, source_target_pairs={{0,8},{4,12},{8,0},{12,4},{1,9},{5,13},{9,1},{13,5},{2,10},{6,14},... | collective-permute-start | bytes 270344 | tf_op jit(solution)/shard_map/ppermute | solution.py:679
  8.4 7.8 %collective-permute-start.2 = (bf16[352,128]{1,0:T(8,128)(2,1)}, bf16[352,128]{1,0:T(8,128)(2,1)S(1)}, u32[]{:S(2)}, u32[]{:S(2)}) collective-permute-start(bf16[352,128]{1,0:T(8,128)(2,1)} %get-tuple-element.43), channel_id=1, source_target_pairs={{0,4},{4,0},{8,12},{12,8},{1,5},{5,1},{9,13},{13,9},{2,6},{6,2},{1... | collective-permute-start | bytes 270344 | tf_op jit(solution)/shard_map/ppermute | solution.py:679
  9.0 0.7 %copy-start.4 = (s32[2,5]{1,0:T(2,128)S(1)}, s32[2,5]{1,0:T(2,128)}, u32[]{:S(2)}) copy-start(s32[2,5]{1,0:T(2,128)} %offsets_ref.7) | copy-start | bytes 124
  9.7 0.9 %copy-start = (bf16[1,128,640]{2,1,0:T(8,128)(2,1)S(1)}, bf16[1,128,640]{2,1,0:T(8,128)(2,1)}, u32[]{:S(2)}) copy-start(bf16[1,128,640]{2,1,0:T(8,128)(2,1)} %grad_ref.3) | copy-start | bytes 491524
  10.6 0.9 %copy-start.6 = (bf16[128,640]{1,0:T(8,128)(2,1)S(1)}, bf16[128,640]{1,0:T(8,128)(2,1)}, u32[]{:S(2)}) copy-start(bf16[128,640]{1,0:T(8,128)(2,1)} %get-tuple-element.34.out_ref) | copy-start | bytes 491524
  11.5 4.6 %copy-start.1 = (bf16[1,128,640]{2,1,0:T(8,128)(2,1)S(1)}, bf16[1,128,640]{2,1,0:T(8,128)(2,1)}, u32[]{:S(2)}) copy-start(bf16[1,128,640]{2,1,0:T(8,128)(2,1)} %q_ref.7) | copy-start | bytes 491524
  11.5 4.6 %copy-start.7 = (bf16[128,640]{1,0:T(8,128)(2,1)S(1)}, bf16[128,640]{1,0:T(8,128)(2,1)}, u32[]{:S(2)}) copy-start(bf16[128,640]{1,0:T(8,128)(2,1)} %get-tuple-element.34.out_ref) | copy-start | bytes 491524
  11.5 4.6 %copy-start.8 = (bf16[352,128]{1,0:T(8,128)(2,1)S(1)}, bf16[352,128]{1,0:T(8,128)(2,1)}, u32[]{:S(2)}) copy-start(bf16[352,128]{1,0:T(8,128)(2,1)} %get-tuple-element.40.refs_2_) | copy-start | bytes 270340
  11.5 4.6 %copy-start.9 = (f32[16,128]{1,0:T(8,128)S(1)}, f32[16,128]{1,0:T(8,128)}, u32[]{:S(2)}) copy-start(f32[16,128]{1,0:T(8,128)} %get-tuple-element.36.refs_0_.refs_1_) | copy-start | bytes 24580
  16.2 6.1 %copy-start.2 = (bf16[1,128,640]{2,1,0:T(8,128)(2,1)S(1)}, bf16[1,128,640]{2,1,0:T(8,128)(2,1)}, u32[]{:S(2)}) copy-start(bf16[1,128,640]{2,1,0:T(8,128)(2,1)} %k_ref.5) | copy-start | bytes 491524
  16.2 6.0 %copy-start.3 = (bf16[1,128,640]{2,1,0:T(8,128)(2,1)S(1)}, bf16[1,128,640]{2,1,0:T(8,128)(2,1)}, u32[]{:S(2)}) copy-start(bf16[1,128,640]{2,1,0:T(8,128)(2,1)} %v_ref.5) | copy-start | bytes 491524
  16.2 6.0 %copy-start.5 = (bf16[128,640]{1,0:T(8,128)(2,1)S(1)}, bf16[128,640]{1,0:T(8,128)(2,1)}, u32[]{:S(2)}) copy-start(bf16[128,640]{1,0:T(8,128)(2,1)} %get-tuple-element.33.expo_ref) | copy-start | bytes 491524
  17.8 6.7 %collective-permute-start.3 = (bf16[304,128]{1,0:T(8,128)(2,1)S(1)}, bf16[304,128]{1,0:T(8,128)(2,1)S(1)}, u32[]{:S(2)}, u32[]{:S(2)}) collective-permute-start(bf16[304,128]{1,0:T(8,128)(2,1)S(1)} %get-tuple-element.45), channel_id=1, source_target_pairs={{0,12},{4,8},{8,4},{12,0},{1,13},{5,9},{9,5},{13,1},{2,14},{6,10},... | collective-permute-start | bytes 233480 | tf_op jit(solution)/shard_map/ppermute | solution.py:679
  20.4 6.5 %collective-permute-start.4 = (bf16[304,128]{1,0:T(8,128)(2,1)S(1)}, bf16[304,128]{1,0:T(8,128)(2,1)S(1)}, u32[]{:S(2)}, u32[]{:S(2)}) collective-permute-start(bf16[304,128]{1,0:T(8,128)(2,1)S(1)} %get-tuple-element.46), channel_id=1, source_target_pairs={{0,8},{4,12},{8,0},{12,4},{1,9},{5,13},{9,1},{13,5},{2,10},{6,14},... | collective-permute-start | bytes 233480 | tf_op jit(solution)/shard_map/ppermute | solution.py:679
  20.4 6.5 %collective-permute-start.5 = (bf16[304,128]{1,0:T(8,128)(2,1)S(1)}, bf16[304,128]{1,0:T(8,128)(2,1)S(1)}, u32[]{:S(2)}, u32[]{:S(2)}) collective-permute-start(bf16[304,128]{1,0:T(8,128)(2,1)S(1)} %get-tuple-element.47), channel_id=1, source_target_pairs={{0,4},{4,0},{8,12},{12,8},{1,5},{5,1},{9,13},{13,9},{2,6},{6,2},{1... | collective-permute-start | bytes 233480 | tf_op jit(solution)/shard_map/ppermute | solution.py:679
  26.9 2.3 %collective-permute-start.6 = (f32[1,640]{1,0:T(1,128)S(1)}, f32[1,640]{1,0:T(1,128)S(1)}, u32[]{:S(2)}, u32[]{:S(2)}) collective-permute-start(f32[1,640]{1,0:T(1,128)S(1)} %gain.1.refs_4_), channel_id=1, source_target_pairs={{0,16},{16,0},{1,17},{17,1},{2,18},{18,2},{3,19},{19,3},{4,20},{20... | collective-permute-start | bytes 7688 | tf_op jit(solution)/shard_map/ppermute | solution.py:679

commit v11 on v10

--- a/solution.py
+++ b/solution.py
@@ -248,10 +248,9 @@
 
 
 def pick_matrix(offsets_ref, head, tokens, top_step, picked_axis):
-    top_rows, mid_rows = picked_counts(tokens, top_step)
-    shape = (top_rows + mid_rows, tokens) if picked_axis == 0 else (tokens, top_rows + mid_rows)
-    row = lax.broadcasted_iota(jnp.int32, shape, picked_axis)
-    position = lax.broadcasted_iota(jnp.int32, shape, 1 - picked_axis)
+    top_rows, _ = picked_counts(tokens, top_step)
+    row = lax.broadcasted_iota(jnp.int32, (tokens, tokens), picked_axis)
+    position = lax.broadcasted_iota(jnp.int32, (tokens, tokens), 1 - picked_axis)
     wanted = jnp.where(
         row < top_rows,
         row * top_step + offsets_ref[1, head],
@@ -260,12 +259,13 @@
     return jnp.where(position == wanted, 1.0, 0.0).astype(LOW)
 
 
-def slot_matrix(offset, step, slot, tokens):
-    count = tokens // step
-    position = lax.broadcasted_iota(jnp.int32, (tokens, tokens), 0)
-    index = lax.broadcasted_iota(jnp.int32, (tokens, tokens), 1) - slot * count
-    inside = (index >= 0) & (index < count)
-    return jnp.where(inside & (position == index * step + offset), 1.0, 0.0).astype(LOW)
+def rolled(row, shift):
+    return pltpu.roll(row, shift % row.shape[1], 1)
+
+
+def lane_window(row, start, count):
+    lane = lax.broadcasted_iota(jnp.int32, row.shape, 1)
+    return jnp.where((lane >= start) & (lane < start + count), row, 0.0)
 
 
 def hit_row(offset, step, tokens):
@@ -333,7 +333,7 @@
     scores = [contract(k_rows[head], q_rows[head], 1, 1) * score_scale for head in heads]
     moved = [
         contract(
-            picks[head],
+            picks[head][:picked],
             jnp.concatenate([q_rows[head], k_rows[head], v_rows[head], grad_rows[head]], 1),
             1,
             0,
@@ -341,7 +341,9 @@
         for head in owned
     ]
     shared = [
-        contract(picks[head], jnp.concatenate([k_rows[head], v_rows[head]], 1), 1, 0).astype(LOW)
+        contract(
+            picks[head][:picked], jnp.concatenate([k_rows[head], v_rows[head]], 1), 1, 0
+        ).astype(LOW)
         for head in heads[OWNED:]
     ]
     top_scores = [jnp.max(block, axis=0, keepdims=True) for block in scores]
@@ -364,34 +366,30 @@
     for head in owned:
         outs[head] = outs[head] * (1.0 / totals[head])
     outs = [out.astype(LOW) for out in outs]
-    picked_outs = [contract(picks[head], outs[head], 1, 1).astype(LOW) for head in owned]
+    picked_outs = [
+        contract(picks[head][:picked], outs[head], 1, 1).astype(LOW) for head in owned
+    ]
     for head in heads:
         out_ref[:, head_cols(head)] = outs[head]
     for head in owned:
         pieces = piece_rows(top_scores[head] + jnp.log(totals[head])).astype(LOW)
-        slot = me ^ head
-        stat_rows = [
-            contract(pieces, slot_matrix(offsets_ref[level, head], step, slot, tokens), 1, 0)
-            for level, step in ((1, top_step), (0, R1))
-        ]
+        stat_rows = contract(pieces, picks[head], 1, 1)
         blocks = [moved[head][:, block * HEAD_DIM : (block + 1) * HEAD_DIM] for block in range(4)]
         blocks.append(picked_outs[head])
         blocks += [shared[0][:, :HEAD_DIM], shared[0][:, HEAD_DIM:]]
-        blocks.append(jnp.concatenate(stat_rows, 0).astype(LOW))
+        blocks.append(jnp.concatenate([stat_rows, jnp.zeros_like(stat_rows)], 0).astype(LOW))
         held_ref[head] = jnp.concatenate(blocks, 0)
     for distance, payload_ref in enumerate(payload_refs):
         payload_ref[...] = held_ref[me ^ distance]
 
 
 def prepare_kernel(top_step, offsets_ref, grad_ref, gain_ref, out_ref, *refs):
-    grad_norm_ref, gain_part_ref, place_ref, slots_ref = refs
+    grad_norm_ref, gain_part_ref, place_ref = refs
     tokens, width = grad_ref.shape[1:]
     heads = range(width // HEAD_DIM)
-    me = lax.axis_index("ctx")
-    picked = sum(picked_counts(tokens, top_step))
     top_rows = tokens // top_step
     ones = jnp.ones((TILE, tokens), LOW)
-    column = lax.broadcasted_iota(jnp.int32, (tokens, picked), 1)
+    column = lax.broadcasted_iota(jnp.int32, (tokens, tokens), 1)
     gain_part_ref[...] = jnp.zeros(gain_part_ref.shape, WIDE)
     grad_norms = [
         (grad_ref[0, :, head_cols(head)].astype(WIDE) * gain_ref[:, head_cols(head)]).T
@@ -401,7 +399,7 @@
         cols = head_cols(head)
         grad_norm_ref[:, cols] = grad_norms[head]
         picks = pick_matrix(offsets_ref, head, tokens, top_step, 1)
-        place_ref[:, pl.ds(head * HEAD_DIM, picked)] = picks
+        place_ref[:, cols] = picks
     for head in range(OWNED):
         cols = head_cols(head)
         mid_offset, top_offset = offsets_ref[0, head], offsets_ref[1, head]
@@ -415,11 +413,7 @@
         both = mid_offset % top_step == top_offset
         kept = jnp.where(column < top_rows, 1.0, jnp.where(both, 0.0, 1.0)).astype(LOW)
         picks = pick_matrix(offsets_ref, head, tokens, top_step, 1)
-        place_ref[:, pl.ds(width + head * HEAD_DIM, picked)] = picks * kept
-        for index, (offset, step) in enumerate(((top_offset, top_step), (mid_offset, R1))):
-            slots_ref[:, head_cols(2 * head + index)] = slot_matrix(
-                offset, step, me ^ head, tokens
-            )
+        place_ref[:, head_cols(len(heads) + head)] = picks * kept
 
 
 def owner_kernel(top_step, offsets_ref, q_ref, gain_ref, out_ref, grad_norm_ref, *refs):
@@ -456,12 +450,18 @@
 
     q_rows, k_rows, v_rows, grad_rows, base_rows = [by_level(block) for block in range(5)]
     stat_start = 7 * picked
-    stat_rows = sum(
-        ref[stat_start : stat_start + STAT_TILES].astype(WIDE) for ref in payload_refs
-    )
-    base_log = jnp.concatenate(
-        [joined_row(stat_rows, 0), joined_row(stat_rows, TILE)[:, :mid_all]], 1
-    )
+    logs = [
+        joined_row(ref[stat_start : stat_start + STAT_TILES].astype(WIDE), 0)
+        for ref in payload_refs
+    ]
+    base_top_log = sum(
+        rolled(lane_window(log, 0, top_rows), slot * top_rows) for slot, log in enumerate(logs)
+    )
+    base_mid_log = sum(
+        rolled(lane_window(log, top_rows, mid_rows), slot * mid_rows - top_rows)
+        for slot, log in enumerate(logs)
+    )
+    base_log = jnp.concatenate([base_top_log, base_mid_log[:, :mid_all]], 1)
     gain_row = jnp.zeros((1, HEAD_DIM), WIDE)
     for head in range(OWNED):
         gain_row = gain_row + jnp.where(me == head, 1.0, 0.0) * gain_ref[:, head_cols(head)]
@@ -474,7 +474,6 @@
     sees_top = is_top + (1.0 - is_top) * both_flag
     sees_mid = is_top * top_in_mid + (1.0 - is_top)
     bias = per_level((1.0 - sees_top) * NEVER, (1.0 - sees_mid) * NEVER)
-    same_level = per_level(is_top, 1.0 - is_top)
     last = heads - 1
     cols = head_cols(last)
     peers = payload_refs[1:]
@@ -513,17 +512,29 @@
     normed_last, product_last, grad_last_low, inner_last = norm_backward(
         attn_last, grad_norm_ref[:, cols]
     )
-    prob_grad = contract(v_rows, grad_low, 1, 0)
+    spans = (slice(0, top_all), slice(top_all, queries))
+    prob_grads = [contract(v_rows[span], grad_low[:, span], 1, 0) for span in spans]
     prob_grad_last = contract(v_peers, grad_last_low, 1, 0)
-    soft = soft * same_level
-    score_grad = (soft * (prob_grad - inner) * score_scale).astype(LOW)
+    score_grads = [
+        (soft[span, span] * (prob_grad - inner[:, span]) * score_scale).astype(LOW)
+        for span, prob_grad in zip(spans, prob_grads)
+    ]
     score_grad_last = (soft_last * (prob_grad_last - inner_last) * score_scale).astype(LOW)
-    dk = contract(score_grad, q_rows, 1, 0).astype(LOW)
+    dks = [
+        contract(score_grad, q_rows[span], 1, 0).astype(LOW)
+        for span, score_grad in zip(spans, score_grads)
+    ]
     dk_last = contract(score_grad_last, q_last, 1, 0).astype(LOW)
-    dv = contract(soft.astype(LOW), grad_low, 1, 1).astype(LOW)
+    dvs = [
+        contract(soft_low[span, span], grad_low[:, span], 1, 1).astype(LOW) for span in spans
+    ]
     dv_last = contract(soft_last_low, grad_last_low, 1, 1).astype(LOW)
-    dq = contract(score_grad, k_rows, 0, 0).astype(LOW)
+    dqs = [
+        contract(score_grad, k_rows[span], 0, 0).astype(LOW)
+        for span, score_grad in zip(spans, score_grads)
+    ]
     attn_rows = attn.T.astype(LOW)
+    attn_parts = [attn_rows[span] for span in spans]
     log_total = top_score + jnp.log(total)
     padding = jnp.zeros((1, top_all - mid_all), WIDE)
     once = is_top + (1.0 - is_top) * (1.0 - both_flag)
@@ -534,24 +545,25 @@
         for head in range(OWNED)
     ]
     gain_rows.append(gain_row_of(ones, product_last) / gain_ref[:, cols])
-    gain_high, gain_rest = gain_pieces(jnp.concatenate(gain_rows, 0))
-    log_rows = jnp.concatenate(
-        [
-            piece_rows(log_total[:, :top_all], gain_high.astype(WIDE)),
-            piece_rows(
-                jnp.concatenate([log_total[:, top_all:], padding], 1), gain_rest.astype(WIDE)
-            ),
-        ],
-        0,
-    ).astype(LOW)
+    gain_high, gain_rest = [
+        rows.astype(WIDE) for rows in gain_pieces(jnp.concatenate(gain_rows, 0))
+    ]
+    top_log, mid_log = log_total[:, :top_all], jnp.concatenate(
+        [log_total[:, top_all:], padding], 1
+    )
+    empty = jnp.zeros((PIECES, HEAD_DIM), WIDE)
     for distance, return_ref in enumerate(return_refs):
         blocks = []
-        for rows in (dq, dk, dv, attn_rows):
-            mid_start = top_all + distance * mid_rows
-            blocks.append(rows[distance * top_rows : (distance + 1) * top_rows])
-            blocks.append(rows[mid_start : mid_start + mid_rows])
+        for top_block, mid_block in (dqs, dks, dvs, attn_parts):
+            blocks.append(top_block[distance * top_rows : (distance + 1) * top_rows])
+            blocks.append(mid_block[distance * mid_rows : (distance + 1) * mid_rows])
         start = max(distance - 1, 0) * picked
-        blocks += [dk_last[start : start + picked], dv_last[start : start + picked], log_rows]
+        blocks += [dk_last[start : start + picked], dv_last[start : start + picked]]
+        log_row = lane_window(rolled(top_log, -distance * top_rows), 0, top_rows) + lane_window(
+            rolled(mid_log, top_rows - distance * mid_rows), top_rows, mid_rows
+        )
+        log_rows = [piece_rows(log_row, gain_high), empty, gain_rest]
+        blocks.append(jnp.concatenate(log_rows, 0).astype(LOW))
         return_ref[...] = jnp.concatenate(blocks, 0)
     normed_ref[...] = normed_last
     grad_low_ref[...] = grad_last_low
@@ -590,40 +602,26 @@
         gain_ref[:, head_cols(head)] = total[head : head + 1]
 
 
-def finish_kernel(top_step, offsets_ref, q_ref, k_ref, v_ref, gain_ref, expo_ref, out_ref, *refs):
-    grad_norm_ref, stats_ref, place_ref, slots_ref = refs[:4]
-    gain_in_ref, last_attended_ref, last_dq_ref, last_dk_ref, last_dv_ref = refs[4:9]
-    return_refs, refs = nearest_first(refs[9 : 9 + SPAN]), refs[9 + SPAN :]
-    attended_ref, dq_ref, dk_ref, dv_ref, gain_out_ref, held_ref = refs
-    gain_out_ref[...] = gain_in_ref[...]
-    tokens, width = q_ref.shape[1:]
+def mix_kernel(top_step, offsets_ref, v_ref, gain_ref, expo_ref, out_ref, *refs):
+    grad_norm_ref, stats_ref, place_ref = refs[:3]
+    return_refs, refs = nearest_first(refs[3 : 3 + SPAN]), refs[3 + SPAN :]
+    attended_ref, grad_low_ref, soft_ref, score_grad_ref, placed_ref = refs
+    tokens, width = v_ref.shape[1:]
+    count = width // HEAD_DIM
     picked = sum(picked_counts(tokens, top_step))
     score_scale = 1.0 / math.sqrt(HEAD_DIM)
     me = lax.axis_index("ctx")
     heads = range(OWNED)
     every = [head_cols(head) for head in heads]
     for distance, return_ref in enumerate(return_refs):
-        held_ref[me ^ distance] = return_ref[...]
-    blocks = [
-        [held_ref[head, block * picked : (block + 1) * picked] for block in range(4)]
+        placed_ref[me ^ distance] = return_ref[...]
+    once = [place_ref[:, head_cols(count + head)] for head in heads]
+    attn_parts = [
+        contract(placed_ref[head, 3 * picked : 4 * picked], once[head][:, :picked], 0, 1)
         for head in heads
     ]
-    log_rows = [held_ref[head, 6 * picked : 6 * picked + STAT_TILES] for head in heads]
-    attn_parts = [
-        contract(blocks[head][3], place_ref[:, pl.ds(width + head * HEAD_DIM, picked)], 0, 1)
-        for head in heads
-    ]
     log_parts = [
-        [contract(log_rows[head], slots_ref[:, head_cols(2 * head + level)], 1, 1) for level in (0, 1)]
-        for head in heads
-    ]
-    placed = [
-        contract(
-            place_ref[:, pl.ds(head * HEAD_DIM, picked)],
-            jnp.concatenate(blocks[head][:3], 1),
-            1,
-            0,
-        )
+        contract(placed_ref[head, 6 * picked : 6 * picked + STAT_TILES], once[head], 1, 1)
         for head in heads
     ]
     factors, normeds, grad_lows, inners = [], [], [], []
@@ -631,11 +629,8 @@
         top_hit = hit_row(offsets_ref[1, head], top_step, tokens)
         mid_hit = hit_row(offsets_ref[0, head], R1, tokens)
         seen = jnp.maximum(top_hit, mid_hit) > 0.5
-        top_log, mid_log = joined_row(log_parts[head][0], 0), joined_row(log_parts[head][1], TILE)
         top_score, total = stats_ref[head : head + 1, :], stats_ref[TILE + head : TILE + head + 1, :]
-        log_total = jnp.where(
-            top_hit > 0.5, top_log, jnp.where(mid_hit > 0.5, mid_log, top_score + jnp.log(total))
-        )
+        log_total = jnp.where(seen, joined_row(log_parts[head], 0), top_score + jnp.log(total))
         factors.append(jnp.exp(top_score - log_total))
         attn = jnp.where(seen, attn_parts[head], out_ref[:, every[head]].astype(WIDE))
         normed, _, grad_low, inner = norm_backward(attn, grad_norm_ref[:, every[head]])
@@ -644,23 +639,43 @@
         inners.append(inner)
     prob_grads = [contract(v_ref[0, :, every[head]], grad_lows[head], 1, 0) for head in heads]
     softs = [expo_ref[:, every[head]].astype(WIDE) * factors[head] for head in heads]
-    dvs = [contract(softs[head].astype(LOW), grad_lows[head], 1, 1) for head in heads]
-    score_grads = [
-        (softs[head] * (prob_grads[head] - inners[head]) * score_scale).astype(LOW)
-        for head in heads
-    ]
-    dks = [contract(score_grads[head], q_ref[0, :, every[head]], 1, 0) for head in heads]
-    dqs = [contract(score_grads[head], k_ref[0, :, every[head]], 0, 0) for head in heads]
     for head in heads:
         cols = every[head]
-        attended_ref[0, :, cols] = (normeds[head].T * gain_ref[:, cols]).astype(LOW)
-        for which, (block, out_block_ref) in enumerate(
-            ((dqs[head], dq_ref), (dks[head], dk_ref), (dvs[head], dv_ref))
-        ):
-            part = placed[head][:, which * HEAD_DIM : (which + 1) * HEAD_DIM]
-            out_block_ref[0, :, cols] = (block + part).astype(LOW)
+        grad_low_ref[:, cols] = grad_lows[head]
+        soft_ref[:, cols] = softs[head].astype(LOW)
+        score_grad_ref[:, cols] = (
+            softs[head] * (prob_grads[head] - inners[head]) * score_scale
+        ).astype(LOW)
+        attended_ref[:, cols] = (normeds[head].T * gain_ref[:, cols]).astype(LOW)
+
+
+def finish_kernel(top_step, *refs):
+    gain_refs, (q_ref, k_ref, place_ref), refs = refs[:2], refs[2:5], refs[5:]
+    mixed_refs, (last_attended_ref, last_dq_ref, last_dk_ref, last_dv_ref) = refs[:5], refs[5:9]
+    return_refs, refs = nearest_first(refs[9 : 9 + SPAN]), refs[9 + SPAN :]
+    mixed_ref, grad_low_ref, soft_ref, score_grad_ref, returned_ref = mixed_refs
+    attended_ref, dq_ref, dk_ref, dv_ref, gain_out_ref = refs
+    tokens, width = q_ref.shape[1:]
+    picked = sum(picked_counts(tokens, top_step))
+    heads = range(OWNED)
+    every = [head_cols(head) for head in heads]
+    gain_out_ref[...] = (gain_refs[0][...] + gain_refs[1][...]).reshape(gain_out_ref.shape)
+    score_grads = [score_grad_ref[:, cols] for cols in every]
+    dqs = [contract(score_grads[head], k_ref[0, :, every[head]], 0, 0) for head in heads]
+    placed = [
+        contract(
+            place_ref[:, pl.ds(head * HEAD_DIM, picked)],
+            jnp.concatenate(
+                [returned_ref[head, block * picked : (block + 1) * picked] for block in range(3)], 1
+            ),
+            1,
+            0,
+        )
+        for head in heads
+    ]
+    dks = [contract(score_grads[head], q_ref[0, :, every[head]], 1, 0) for head in heads]
+    dvs = [contract(soft_ref[:, cols], grad_low_ref[:, cols], 1, 1) for cols in every]
     last = width // HEAD_DIM - 1
-    cols = head_cols(last)
     total = sum(ref[4 * picked : 6 * picked].astype(WIDE) for ref in return_refs[1:]).astype(LOW)
     rows = contract(
         place_ref[:, pl.ds(last * HEAD_DIM, picked)],
@@ -668,6 +683,15 @@
         1,
         0,
     )
+    for head in heads:
+        cols = every[head]
+        attended_ref[0, :, cols] = mixed_ref[:, cols]
+        for which, (block, out_block_ref) in enumerate(
+            ((dqs[head], dq_ref), (dks[head], dk_ref), (dvs[head], dv_ref))
+        ):
+            part = placed[head][:, which * HEAD_DIM : (which + 1) * HEAD_DIM]
+            out_block_ref[0, :, cols] = (block + part).astype(LOW)
+    cols = head_cols(last)
     attended_ref[0, :, cols] = last_attended_ref[...]
     dq_ref[0, :, cols] = last_dq_ref[...]
     dk_ref[0, :, cols] = (last_dk_ref[...] + rows[:, :HEAD_DIM]).astype(LOW)
@@ -723,11 +747,11 @@
         scratch=[pltpu.VMEM((OWNED, *payload.shape), LOW)],
     )
     received = to_peers(sent)
-    grad_norm, gain_base, place, slots = call(
+    grad_norm, gain_base, place = call(
         bind(prepare_kernel, top_step),
         "prepare",
         (offsets, grad_y, gain_row, base_out),
-        [wide_block, gain_block, shape((tokens, 2 * width), LOW), shape((tokens, 2 * OWNED * tokens), LOW)],
+        [wide_block, gain_block, shape((tokens, 2 * width), LOW)],
         2,
     )
     normed, grad_low, score_grad, kept, own_answer, *answers = call(
@@ -753,13 +777,12 @@
     )
     (gain_sum,) = call(bind(gain_kernel, picked), "gain", (own_answer, *returned), [gain_block], 1)
     gain_rest = across(gain_sum, "dp", 1)
-    attended, query_grad, key_grad, value_grad, gain_sum = call(
-        bind(finish_kernel, top_step),
-        "finish",
+    mixed_block = shape((tokens, OWNED * HEAD_DIM), LOW)
+    mixed = call(
+        bind(mix_kernel, top_step),
+        "mix",
         (
             offsets,
-            queries,
-            keys,
             values,
             gain_row,
             expo,
@@ -767,17 +790,29 @@
             grad_norm,
             stats,
             place,
-            slots,
+            own_answer,
+            *returned,
+        ),
+        [mixed_block] * 4 + [shape((OWNED, *answer.shape), LOW)],
+        20,
+    )
+    attended, query_grad, key_grad, value_grad, gain_grad = call(
+        bind(finish_kernel, top_step),
+        "finish",
+        (
             gain_sum,
+            gain_rest,
+            queries,
+            keys,
+            place,
+            *mixed,
             *last_results,
             own_answer,
             *returned,
         ),
-        [row_block] * 4 + [gain_block],
+        [row_block] * 4 + [shape((width,), WIDE)],
         1,
-        scratch=[pltpu.VMEM((OWNED, *answer.shape), LOW)],
-    )
-    gain_grad = (gain_sum + gain_rest).reshape(width)
+    )
     return attended, query_grad, key_grad, value_grad, gain_grad
 
 

time: 30.1 us -> 29.5 us (0.980)
  other arithmetic: 0.61 us -> 0 us
    add x1 -> x0, other arithmetic: 0.61 us -> none  [one_segment_shards(): gain_grad = (gain_sum + gain_rest).reshape(width)]
    pallas_call x6 -> x7, Pallas kernels: 7.82 us -> 7.67 us  [call(): pl.pallas_call(kernel, out_shape=results, in_specs=[SMEM_SPEC if block.dt...]
  transfers between devices with their start and end apart: 7 -> 7, of which waited for: 3 -> 3; matrix products, arithmetic and copies ran while one was open for 0% -> 0% of each run, Pallas kernels for 12% -> 8%
where the time goes in v11:
time: 29.5 us; the launch traced here: 29.3 us
  starting transfers between devices  10.3 us (35%)
  waiting for transfers between devices  8.1 us (27%)
  Pallas kernels  7.67 us (26%)
  local copies, waits for them, and re-layouts  2.55 us (9%)
  between operations  0.72 us (2%)
    ppermute x7, starting transfers between devices, across(): return lax.ppermute(block, axis, route)  10.3 us
    ppermute x7, waiting for transfers between devices, across(): return lax.ppermute(block, axis, route)  8.1 us
    pallas_call x7, Pallas kernels, call(): pl.pallas_call(kernel, out_shape=results, in_specs=[SMEM_SPEC if block.dt...  7.67 us
    unnamed x22, local copies, waits for them, and re-layouts  2.55 us
  transfers between devices with their start and end apart: 7, of which 3 were waited for; matrix products, arithmetic and copies ran while one was open for 0% of the time, Pallas kernels for 8%

profile of v11, /device:TPU:0, one launch (start us, length us, event | category | flops | bytes accessed | tf_op | source)
XLA Modules:
  0.0 29.3 jit_solution(2793658473970916942)
XLA Ops:
  0.6 2.6 %pack.1 = (bf16[352,128]{1,0:T(8,128)(2,1)}, bf16[352,128]{1,0:T(8,128)(2,1)}, bf16[352,128]{1,0:T(8,128)(2,1)}, bf16[352,128]{1,0:T(8,128)(2,1)}, bf16[128,640]...) custom-call(s32[2,5]{1,0:T(2,128)} %offsets_ref.7, bf16[1,128,640]{2,1,0:T(8,128)(2,1)} %refs_2_.1, ...), custom_call_target="tpu_custom_call" | custom-call | flops 1000000000 | tf_op jit(solution)/shard_map/pack/pallas_call | solution.py:711
  3.2 5.1 %collective-permute-start = (bf16[352,128]{1,0:T(8,128)(2,1)}, bf16[352,128]{1,0:T(8,128)(2,1)S(1)}, u32[]{:S(2)}, u32[]{:S(2)}) collective-permute-start(bf16[352,128]{1,0:T(8,128)(2,1)} %get-tuple-element.37), channel_id=1, source_target_pairs={{0,12},{4,8},{8,4},{12,0},{1,13},{5,9},{9,5},{13,1},{2,14},{6,10},... | collective-permute-start | bytes 270344 | tf_op jit(solution)/shard_map/ppermute | solution.py:703
  8.3 0.0 collective-permute-start.1
  8.3 0.6 %collective-permute-start.2 = (bf16[352,128]{1,0:T(8,128)(2,1)}, bf16[352,128]{1,0:T(8,128)(2,1)S(1)}, u32[]{:S(2)}, u32[]{:S(2)}) collective-permute-start(bf16[352,128]{1,0:T(8,128)(2,1)} %get-tuple-element.39), channel_id=1, source_target_pairs={{0,4},{4,0},{8,12},{12,8},{1,5},{5,1},{9,13},{13,9},{2,6},{6,2},{1... | collective-permute-start | bytes 270344 | tf_op jit(solution)/shard_map/ppermute | solution.py:703
  9.0 0.0 copy-done.10
  9.0 0.7 %copy-done.4 = s32[2,5]{1,0:T(2,128)S(1)} copy-done((s32[2,5]{1,0:T(2,128)S(1)}, s32[2,5]{1,0:T(2,128)}, u32[]{:S(2)}) %copy-start.4) | copy-done | bytes 64
  9.7 0.9 %copy-done = bf16[1,128,640]{2,1,0:T(8,128)(2,1)S(1)} copy-done((bf16[1,128,640]{2,1,0:T(8,128)(2,1)S(1)}, bf16[1,128,640]{2,1,0:T(8,128)(2,1)}, u32[]{:S(2)}) %copy-start) | copy-done | bytes 163864
  10.6 0.9 %copy-done.6 = bf16[128,640]{1,0:T(8,128)(2,1)S(1)} copy-done((bf16[128,640]{1,0:T(8,128)(2,1)S(1)}, bf16[128,640]{1,0:T(8,128)(2,1)}, u32[]{:S(2)}) %copy-start.6) | copy-done | bytes 163864
  11.5 0.9 %prepare.1 = (f32[128,640]{1,0:T(8,128)S(1)}, f32[1,640]{1,0:T(1,128)S(1)}, bf16[128,1280]{1,0:T(8,128)(2,1)S(1)}) custom-call(s32[2,5]{1,0:T(2,128)S(1)} %copy-done.4, bf16[1,128,640]{2,1,0:T(8,128)(2,1)S(1)} %copy-done, f32[1,640]{1,0:T(1,128)S(1)} %reshape.13.gain_ref, bf16[128,640]{1,0:T(8,128)(2,1)S(1)} %copy-done.6), custom_call_target="tpu_custom_call" | custom-call | flops 2000000000 | tf_op jit(solution)/shard_map/prepare/pallas_call | solution.py:711
  12.4 0.0 collective-permute-done.refs_3_.refs_4_
  12.4 3.7 %collective-permute-done.1.refs_4_.refs_5_ = bf16[352,128]{1,0:T(8,128)(2,1)S(1)} collective-permute-done((bf16[352,128]{1,0:T(8,128)(2,1)}, bf16[352,128]{1,0:T(8,128)(2,1)S(1)}, u32[]{:S(2)}, u32[]{:S(2)}) %collective-permute-start.1) | collective-permute-done | bytes 90144 | tf_op jit(solution)/shard_map/ppermute | solution.py:703
  16.1 0.0 collective-permute-done.2.refs_5_.refs_6_
  16.1 0.0 copy-done.2
  16.1 0.0 copy-done.7
  16.1 0.0 copy-done.8
  16.1 0.0 copy-done.9
  16.1 0.0 copy-start.1
  16.2 0.0 copy-start.3
  16.2 0.0 copy-start.5
  16.2 1.5 %owner.1 = (f32[128,128]{1,0:T(8,128)S(1)}, bf16[128,128]{1,0:T(8,128)(2,1)S(1)}, bf16[144,128]{1,0:T(8,128)(2,1)S(1)}, f32[8,128]{1,0:T(8,128)S(1)}, bf16[304,1...) custom-call(s32[2,5]{1,0:T(2,128)S(1)} %copy-done.4, ...), custom_call_target="tpu_custom_call" | custom-call | flops 3000000000 | tf_op jit(solution)/shard_map/owner/pallas_call | solution.py:711
  17.7 2.7 %collective-permute-start.3 = (bf16[304,128]{1,0:T(8,128)(2,1)S(1)}, bf16[304,128]{1,0:T(8,128)(2,1)S(1)}, u32[]{:S(2)}, u32[]{:S(2)}) collective-permute-start(bf16[304,128]{1,0:T(8,128)(2,1)S(1)} %get-tuple-element.41), channel_id=1, source_target_pairs={{0,12},{4,8},{8,4},{12,0},{1,13},{5,9},{9,5},{13,1},{2,14},{6,10},... | collective-permute-start | bytes 233480 | tf_op jit(solution)/shard_map/ppermute | solution.py:703
  20.4 0.0 collective-permute-start.4
  20.4 1.8 %collective-permute-start.5 = (bf16[304,128]{1,0:T(8,128)(2,1)S(1)}, bf16[304,128]{1,0:T(8,128)(2,1)S(1)}, u32[]{:S(2)}, u32[]{:S(2)}) collective-permute-start(bf16[304,128]{1,0:T(8,128)(2,1)S(1)} %get-tuple-element.43), channel_id=1, source_target_pairs={{0,4},{4,0},{8,12},{12,8},{1,5},{5,1},{9,13},{13,9},{2,6},{6,2},{1... | collective-permute-start | bytes 233480 | tf_op jit(solution)/shard_map/ppermute | solution.py:703
  22.2 0.0 copy-done.1
  22.2 0.3 %last_head.1 = (bf16[128,128]{1,0:T(8,128)(2,1)S(1)}, bf16[128,128]{1,0:T(8,128)(2,1)S(1)}, f32[128,128]{1,0:T(8,128)S(1)}, f32[128,128]{1,0:T(8,128)S(1)}) custom-call(bf16[1,128,640]{2,1,0:T(8,128)(2,1)S(1)} %copy-done.2, bf16[1,128,640]{2,1,0:T(8,128)(2,1)S(1)} %copy-done.3, bf16[1,128,640]{2,1,0:T(8,128)(2,1)S(1)} %copy-done.1, ...), custom_call_target="tpu_custom_call" | custom-call | flops 20000000000 | tf_op jit(solution)/shard_map/last_head/pallas_call | solution.py:711
  22.5 1.9 %collective-permute-done.3.refs_1_.refs_4_.refs_15_ = bf16[304,128]{1,0:T(8,128)(2,1)S(1)} collective-permute-done((bf16[304,128]{1,0:T(8,128)(2,1)S(1)}, bf16[304,128]{1,0:T(8,128)(2,1)S(1)}, u32[]{:S(2)}, u32[]{:S(2)}) %collective-permute-start.3) | collective-permute-done | bytes 77856 | tf_op jit(solution)/shard_map/ppermute | solution.py:703
  24.5 2.4 %collective-permute-done.4.refs_2_.refs_5_.refs_16_ = bf16[304,128]{1,0:T(8,128)(2,1)S(1)} collective-permute-done((bf16[304,128]{1,0:T(8,128)(2,1)S(1)}, bf16[304,128]{1,0:T(8,128)(2,1)S(1)}, u32[]{:S(2)}, u32[]{:S(2)}) %collective-permute-start.4) | collective-permute-done | bytes 77856 | tf_op jit(solution)/shard_map/ppermute | solution.py:703
  26.9 0.0 collective-permute-done.5.refs_3_.refs_6_.refs_17_
  26.9 0.1 collective-permute-start.6
  27.0 1.1 %mix.1 = (bf16[128,512]{1,0:T(8,128)(2,1)S(1)}, bf16[128,512]{1,0:T(8,128)(2,1)S(1)}, bf16[128,512]{1,0:T(8,128)(2,1)S(1)}, bf16[128,512]{1,0:T(8,128)(2,1)S(1)}, bf16[4,304,128]{2,1,0:T(8,128)(2,1)S(1)}) custom-call(s32[2,5]{1,0:T(2,128)S(1)} %copy-done.4, bf16[1,128,640]{2,1,0:T(8,128)(2,1)S(1)} %copy-done.1, f32[1,640]{1,0:T(1,128)S(1)} %reshape.13.gain_ref, ...), custom_call_target="tpu_custom_call" | custom-call | flops 20000000000 | tf_op jit(solution)/shard_map/mix/pallas_call | solution.py:711
  28.1 0.0 collective-permute-done.6.refs_1_
  28.1 1.2 %finish.1 = (bf16[1,128,640]{2,1,0:T(8,128)(2,1)}, bf16[1,128,640]{2,1,0:T(8,128)(2,1)}, bf16[1,128,640]{2,1,0:T(8,128)(2,1)}, bf16[1,128,640]{2,1,0:T(8,128)(2,1)}, f32[640]{0:T(1024)}) custom-call(f32[1,640]{1,0:T(1,128)S(1)} %gain.1.refs_0_, f32[1,640]{1,0:T(1,128)S(1)} %collective-permute-done.6.refs_1_, bf16[1,128,640]{2,1,0:T(8,128)(2,1)S(1)} %copy-done.2, ...), custom_call_target="tpu_custom_call" | custom-call | flops 1000000000 | tf_op jit(solution)/shard_map/finish/pallas_call | solution.py:711
  (12 shorter events, 0.0 us)
Async XLA Ops:
  3.2 5.8 %copy-start.10 = (f32[640]{0:T(1024)S(1)}, f32[640]{0:T(1024)}, u32[]{:S(2)}) copy-start(f32[640]{0:T(1024)} %param.10) | copy-start | bytes 7684
  3.2 9.2 %collective-permute-start = (bf16[352,128]{1,0:T(8,128)(2,1)}, bf16[352,128]{1,0:T(8,128)(2,1)S(1)}, u32[]{:S(2)}, u32[]{:S(2)}) collective-permute-start(bf16[352,128]{1,0:T(8,128)(2,1)} %get-tuple-element.37), channel_id=1, source_target_pairs={{0,12},{4,8},{8,4},{12,0},{1,13},{5,9},{9,5},{13,1},{2,14},{6,10},... | collective-permute-start | bytes 270344 | tf_op jit(solution)/shard_map/ppermute | solution.py:703
  8.3 7.8 %collective-permute-start.1 = (bf16[352,128]{1,0:T(8,128)(2,1)}, bf16[352,128]{1,0:T(8,128)(2,1)S(1)}, u32[]{:S(2)}, u32[]{:S(2)}) collective-permute-start(bf16[352,128]{1,0:T(8,128)(2,1)} %get-tuple-element.38), channel_id=1, source_target_pairs={{0,8},{4,12},{8,0},{12,4},{1,9},{5,13},{9,1},{13,5},{2,10},{6,14},... | collective-permute-start | bytes 270344 | tf_op jit(solution)/shard_map/ppermute | solution.py:703
  8.3 7.8 %collective-permute-start.2 = (bf16[352,128]{1,0:T(8,128)(2,1)}, bf16[352,128]{1,0:T(8,128)(2,1)S(1)}, u32[]{:S(2)}, u32[]{:S(2)}) collective-permute-start(bf16[352,128]{1,0:T(8,128)(2,1)} %get-tuple-element.39), channel_id=1, source_target_pairs={{0,4},{4,0},{8,12},{12,8},{1,5},{5,1},{9,13},{13,9},{2,6},{6,2},{1... | collective-permute-start | bytes 270344 | tf_op jit(solution)/shard_map/ppermute | solution.py:703
  9.0 0.7 %copy-start.4 = (s32[2,5]{1,0:T(2,128)S(1)}, s32[2,5]{1,0:T(2,128)}, u32[]{:S(2)}) copy-start(s32[2,5]{1,0:T(2,128)} %offsets_ref.7) | copy-start | bytes 124
  9.7 0.9 %copy-start = (bf16[1,128,640]{2,1,0:T(8,128)(2,1)S(1)}, bf16[1,128,640]{2,1,0:T(8,128)(2,1)}, u32[]{:S(2)}) copy-start(bf16[1,128,640]{2,1,0:T(8,128)(2,1)} %grad_ref.3) | copy-start | bytes 491524
  10.6 0.9 %copy-start.6 = (bf16[128,640]{1,0:T(8,128)(2,1)S(1)}, bf16[128,640]{1,0:T(8,128)(2,1)}, u32[]{:S(2)}) copy-start(bf16[128,640]{1,0:T(8,128)(2,1)} %get-tuple-element.32.out_ref) | copy-start | bytes 491524
  11.5 4.6 %copy-start.2 = (bf16[1,128,640]{2,1,0:T(8,128)(2,1)S(1)}, bf16[1,128,640]{2,1,0:T(8,128)(2,1)}, u32[]{:S(2)}) copy-start(bf16[1,128,640]{2,1,0:T(8,128)(2,1)} %refs_2_.1) | copy-start | bytes 491524
  11.5 4.6 %copy-start.7 = (bf16[128,640]{1,0:T(8,128)(2,1)S(1)}, bf16[128,640]{1,0:T(8,128)(2,1)}, u32[]{:S(2)}) copy-start(bf16[128,640]{1,0:T(8,128)(2,1)} %get-tuple-element.32.out_ref) | copy-start | bytes 491524
  11.5 4.6 %copy-start.8 = (bf16[352,128]{1,0:T(8,128)(2,1)S(1)}, bf16[352,128]{1,0:T(8,128)(2,1)}, u32[]{:S(2)}) copy-start(bf16[352,128]{1,0:T(8,128)(2,1)} %get-tuple-element.36.refs_2_) | copy-start | bytes 270340
  11.5 4.6 %copy-start.9 = (f32[16,128]{1,0:T(8,128)S(1)}, f32[16,128]{1,0:T(8,128)}, u32[]{:S(2)}) copy-start(f32[16,128]{1,0:T(8,128)} %get-tuple-element.34.refs_0_.refs_1_) | copy-start | bytes 24580
  16.1 6.0 %copy-start.1 = (bf16[1,128,640]{2,1,0:T(8,128)(2,1)S(1)}, bf16[1,128,640]{2,1,0:T(8,128)(2,1)}, u32[]{:S(2)}) copy-start(bf16[1,128,640]{2,1,0:T(8,128)(2,1)} %v_ref.5) | copy-start | bytes 491524
  16.2 6.0 %copy-start.3 = (bf16[1,128,640]{2,1,0:T(8,128)(2,1)S(1)}, bf16[1,128,640]{2,1,0:T(8,128)(2,1)}, u32[]{:S(2)}) copy-start(bf16[1,128,640]{2,1,0:T(8,128)(2,1)} %refs_3_.1) | copy-start | bytes 491524
  16.2 6.0 %copy-start.5 = (bf16[128,640]{1,0:T(8,128)(2,1)S(1)}, bf16[128,640]{1,0:T(8,128)(2,1)}, u32[]{:S(2)}) copy-start(bf16[128,640]{1,0:T(8,128)(2,1)} %get-tuple-element.45.expo_ref) | copy-start | bytes 491524
  17.7 6.7 %collective-permute-start.3 = (bf16[304,128]{1,0:T(8,128)(2,1)S(1)}, bf16[304,128]{1,0:T(8,128)(2,1)S(1)}, u32[]{:S(2)}, u32[]{:S(2)}) collective-permute-start(bf16[304,128]{1,0:T(8,128)(2,1)S(1)} %get-tuple-element.41), channel_id=1, source_target_pairs={{0,12},{4,8},{8,4},{12,0},{1,13},{5,9},{9,5},{13,1},{2,14},{6,10},... | collective-permute-start | bytes 233480 | tf_op jit(solution)/shard_map/ppermute | solution.py:703
  20.4 6.5 %collective-permute-start.4 = (bf16[304,128]{1,0:T(8,128)(2,1)S(1)}, bf16[304,128]{1,0:T(8,128)(2,1)S(1)}, u32[]{:S(2)}, u32[]{:S(2)}) collective-permute-start(bf16[304,128]{1,0:T(8,128)(2,1)S(1)} %get-tuple-element.42), channel_id=1, source_target_pairs={{0,8},{4,12},{8,0},{12,4},{1,9},{5,13},{9,1},{13,5},{2,10},{6,14},... | collective-permute-start | bytes 233480 | tf_op jit(solution)/shard_map/ppermute | solution.py:703
  20.4 6.5 %collective-permute-start.5 = (bf16[304,128]{1,0:T(8,128)(2,1)S(1)}, bf16[304,128]{1,0:T(8,128)(2,1)S(1)}, u32[]{:S(2)}, u32[]{:S(2)}) collective-permute-start(bf16[304,128]{1,0:T(8,128)(2,1)S(1)} %get-tuple-element.43), channel_id=1, source_target_pairs={{0,4},{4,0},{8,12},{12,8},{1,5},{5,1},{9,13},{13,9},{2,6},{6,2},{1... | collective-permute-start | bytes 233480 | tf_op jit(solution)/shard_map/ppermute | solution.py:703
  26.9 1.2 %collective-permute-start.6 = (f32[1,640]{1,0:T(1,128)S(1)}, f32[1,640]{1,0:T(1,128)S(1)}, u32[]{:S(2)}, u32[]{:S(2)}) collective-permute-start(f32[1,640]{1,0:T(1,128)S(1)} %gain.1.refs_0_), channel_id=1, source_target_pairs={{0,16},{16,0},{1,17},{17,1},{2,18},{18,2},{3,19},{19,3},{4,20},{20... | collective-permute-start | bytes 7688 | tf_op jit(solution)/shard_map/ppermute | solution.py:703

commit v12 on v11

--- a/solution.py
+++ b/solution.py
@@ -227,6 +227,7 @@
 STAT_TILES = 2 * TILE
 PIECES = 3
 NEVER = -1e30
+START_ORDER = (3, 1, 2)
 LOW = jnp.bfloat16
 WIDE = jnp.float32
 PACK_VMEM = 65408 * 1024
@@ -315,7 +316,8 @@
 
 
 def nearest_first(refs):
-    return [refs[0], *refs[:0:-1]]
+    by_distance = dict(zip(START_ORDER, refs[1:]))
+    return [refs[0], *[by_distance[distance] for distance in range(1, SPAN)]]
 
 
 def pack_kernel(top_step, offsets_ref, q_ref, k_ref, v_ref, grad_ref, *refs):
@@ -574,7 +576,7 @@
 
 def last_head_kernel(top_step, q_ref, k_ref, v_ref, gain_ref, expo_ref, *refs):
     normed_ref, grad_low_ref, peer_score_grad_ref, kept_ref, *peers = refs[: 4 + PEERS]
-    peers = peers[::-1]
+    peers = nearest_first([None, *peers])[1:]
     attended_ref, dq_ref, dk_ref, dv_ref = refs[4 + PEERS :]
     picked = sum(picked_counts(q_ref.shape[1], top_step))
     score_scale = 1.0 / math.sqrt(HEAD_DIM)
@@ -704,7 +706,7 @@
 
 
 def to_peers(blocks):
-    return [across(blocks[distance - 1], "ctx", distance) for distance in range(PEERS, 0, -1)]
+    return [across(blocks[distance - 1], "ctx", distance) for distance in START_ORDER]
 
 
 def call(kernel, name, operands, results, microseconds, vmem=PLAIN_VMEM, scratch=()):

time: 29.5 us -> 28.6 us (0.969)
  waiting for transfers between devices: 8.1 us -> 7.21 us
    ppermute x7, waiting for transfers between devices: 8.1 us -> 7.21 us  [across(): return lax.ppermute(block, axis, route)]
  transfers between devices with their start and end apart: 7 -> 7, of which waited for: 3 -> 5; matrix products, arithmetic and copies ran while one was open for 0% -> 0% of each run, Pallas kernels for 8% -> 8%
where the time goes in v12:
time: 28.6 us; the launch traced here: 28.4 us
  starting transfers between devices  10.3 us (36%)
  Pallas kernels  7.68 us (27%)
  waiting for transfers between devices  7.21 us (25%)
  local copies, waits for them, and re-layouts  2.55 us (9%)
  between operations  0.72 us (3%)
    ppermute x7, starting transfers between devices, across(): return lax.ppermute(block, axis, route)  10.3 us
    pallas_call x7, Pallas kernels, call(): pl.pallas_call(kernel, out_shape=results, in_specs=[SMEM_SPEC if block.dt...  7.68 us
    ppermute x7, waiting for transfers between devices, across(): return lax.ppermute(block, axis, route)  7.21 us
    unnamed x22, local copies, waits for them, and re-layouts  2.55 us
  transfers between devices with their start and end apart: 7, of which 5 were waited for; matrix products, arithmetic and copies ran while one was open for 0% of the time, Pallas kernels for 8%

profile of v12, /device:TPU:0, one launch (start us, length us, event | category | flops | bytes accessed | tf_op | source)
XLA Modules:
  0.0 28.4 jit_solution(18297411727314242865)
XLA Ops:
  0.6 2.6 %pack.1 = (bf16[352,128]{1,0:T(8,128)(2,1)}, bf16[352,128]{1,0:T(8,128)(2,1)}, bf16[352,128]{1,0:T(8,128)(2,1)}, bf16[352,128]{1,0:T(8,128)(2,1)}, bf16[128,640]...) custom-call(s32[2,5]{1,0:T(2,128)} %offsets_ref.7, bf16[1,128,640]{2,1,0:T(8,128)(2,1)} %refs_2_.1, ...), custom_call_target="tpu_custom_call" | custom-call | flops 1000000000 | tf_op jit(solution)/shard_map/pack/pallas_call | solution.py:713
  3.2 5.1 %collective-permute-start = (bf16[352,128]{1,0:T(8,128)(2,1)}, bf16[352,128]{1,0:T(8,128)(2,1)S(1)}, u32[]{:S(2)}, u32[]{:S(2)}) collective-permute-start(bf16[352,128]{1,0:T(8,128)(2,1)} %get-tuple-element.37), channel_id=1, source_target_pairs={{0,12},{4,8},{8,4},{12,0},{1,13},{5,9},{9,5},{13,1},{2,14},{6,10},... | collective-permute-start | bytes 270344 | tf_op jit(solution)/shard_map/ppermute | solution.py:705
  8.3 0.0 collective-permute-start.1
  8.3 0.6 %collective-permute-start.2 = (bf16[352,128]{1,0:T(8,128)(2,1)}, bf16[352,128]{1,0:T(8,128)(2,1)S(1)}, u32[]{:S(2)}, u32[]{:S(2)}) collective-permute-start(bf16[352,128]{1,0:T(8,128)(2,1)} %get-tuple-element.39), channel_id=1, source_target_pairs={{0,8},{4,12},{8,0},{12,4},{1,9},{5,13},{9,1},{13,5},{2,10},{6,14},... | collective-permute-start | bytes 270344 | tf_op jit(solution)/shard_map/ppermute | solution.py:705
  9.0 0.0 copy-done.10
  9.0 0.7 %copy-done.4 = s32[2,5]{1,0:T(2,128)S(1)} copy-done((s32[2,5]{1,0:T(2,128)S(1)}, s32[2,5]{1,0:T(2,128)}, u32[]{:S(2)}) %copy-start.4) | copy-done | bytes 64
  9.7 0.9 %copy-done = bf16[1,128,640]{2,1,0:T(8,128)(2,1)S(1)} copy-done((bf16[1,128,640]{2,1,0:T(8,128)(2,1)S(1)}, bf16[1,128,640]{2,1,0:T(8,128)(2,1)}, u32[]{:S(2)}) %copy-start) | copy-done | bytes 163864
  10.6 0.9 %copy-done.6 = bf16[128,640]{1,0:T(8,128)(2,1)S(1)} copy-done((bf16[128,640]{1,0:T(8,128)(2,1)S(1)}, bf16[128,640]{1,0:T(8,128)(2,1)}, u32[]{:S(2)}) %copy-start.6) | copy-done | bytes 163864
  11.5 0.9 %prepare.1 = (f32[128,640]{1,0:T(8,128)S(1)}, f32[1,640]{1,0:T(1,128)S(1)}, bf16[128,1280]{1,0:T(8,128)(2,1)S(1)}) custom-call(s32[2,5]{1,0:T(2,128)S(1)} %copy-done.4, bf16[1,128,640]{2,1,0:T(8,128)(2,1)S(1)} %copy-done, f32[1,640]{1,0:T(1,128)S(1)} %reshape.13.gain_ref, bf16[128,640]{1,0:T(8,128)(2,1)S(1)} %copy-done.6), custom_call_target="tpu_custom_call" | custom-call | flops 2000000000 | tf_op jit(solution)/shard_map/prepare/pallas_call | solution.py:713
  12.4 0.0 collective-permute-done.refs_3_.refs_4_
  12.4 1.9 %collective-permute-done.1.refs_4_.refs_5_ = bf16[352,128]{1,0:T(8,128)(2,1)S(1)} collective-permute-done((bf16[352,128]{1,0:T(8,128)(2,1)}, bf16[352,128]{1,0:T(8,128)(2,1)S(1)}, u32[]{:S(2)}, u32[]{:S(2)}) %collective-permute-start.1) | collective-permute-done | bytes 90144 | tf_op jit(solution)/shard_map/ppermute | solution.py:705
  14.3 1.8 %collective-permute-done.2.refs_5_.refs_6_ = bf16[352,128]{1,0:T(8,128)(2,1)S(1)} collective-permute-done((bf16[352,128]{1,0:T(8,128)(2,1)}, bf16[352,128]{1,0:T(8,128)(2,1)S(1)}, u32[]{:S(2)}, u32[]{:S(2)}) %collective-permute-start.2) | collective-permute-done | bytes 90144 | tf_op jit(solution)/shard_map/ppermute | solution.py:705
  16.1 0.0 copy-done.2
  16.1 0.0 copy-done.7
  16.1 0.0 copy-done.8
  16.1 0.0 copy-done.9
  16.1 0.0 copy-start.1
  16.1 0.0 copy-start.3
  16.2 0.0 copy-start.5
  16.2 1.5 %owner.1 = (f32[128,128]{1,0:T(8,128)S(1)}, bf16[128,128]{1,0:T(8,128)(2,1)S(1)}, bf16[144,128]{1,0:T(8,128)(2,1)S(1)}, f32[8,128]{1,0:T(8,128)S(1)}, bf16[304,1...) custom-call(s32[2,5]{1,0:T(2,128)S(1)} %copy-done.4, ...), custom_call_target="tpu_custom_call" | custom-call | flops 3000000000 | tf_op jit(solution)/shard_map/owner/pallas_call | solution.py:713
  17.7 2.7 %collective-permute-start.3 = (bf16[304,128]{1,0:T(8,128)(2,1)S(1)}, bf16[304,128]{1,0:T(8,128)(2,1)S(1)}, u32[]{:S(2)}, u32[]{:S(2)}) collective-permute-start(bf16[304,128]{1,0:T(8,128)(2,1)S(1)} %get-tuple-element.41), channel_id=1, source_target_pairs={{0,12},{4,8},{8,4},{12,0},{1,13},{5,9},{9,5},{13,1},{2,14},{6,10},... | collective-permute-start | bytes 233480 | tf_op jit(solution)/shard_map/ppermute | solution.py:705
  20.4 0.0 collective-permute-start.4
  20.4 1.7 %collective-permute-start.5 = (bf16[304,128]{1,0:T(8,128)(2,1)S(1)}, bf16[304,128]{1,0:T(8,128)(2,1)S(1)}, u32[]{:S(2)}, u32[]{:S(2)}) collective-permute-start(bf16[304,128]{1,0:T(8,128)(2,1)S(1)} %get-tuple-element.43), channel_id=1, source_target_pairs={{0,8},{4,12},{8,0},{12,4},{1,9},{5,13},{9,1},{13,5},{2,10},{6,14},... | collective-permute-start | bytes 233480 | tf_op jit(solution)/shard_map/ppermute | solution.py:705
  22.2 0.0 copy-done.3
  22.2 0.3 %last_head.1 = (bf16[128,128]{1,0:T(8,128)(2,1)S(1)}, bf16[128,128]{1,0:T(8,128)(2,1)S(1)}, f32[128,128]{1,0:T(8,128)S(1)}, f32[128,128]{1,0:T(8,128)S(1)}) custom-call(bf16[1,128,640]{2,1,0:T(8,128)(2,1)S(1)} %copy-done.2, bf16[1,128,640]{2,1,0:T(8,128)(2,1)S(1)} %copy-done.3, bf16[1,128,640]{2,1,0:T(8,128)(2,1)S(1)} %copy-done.1, ...), custom_call_target="tpu_custom_call" | custom-call | flops 20000000000 | tf_op jit(solution)/shard_map/last_head/pallas_call | solution.py:713
  22.5 1.9 %collective-permute-done.3.refs_1_.refs_4_.refs_15_ = bf16[304,128]{1,0:T(8,128)(2,1)S(1)} collective-permute-done((bf16[304,128]{1,0:T(8,128)(2,1)S(1)}, bf16[304,128]{1,0:T(8,128)(2,1)S(1)}, u32[]{:S(2)}, u32[]{:S(2)}) %collective-permute-start.3) | collective-permute-done | bytes 77856 | tf_op jit(solution)/shard_map/ppermute | solution.py:705
  24.4 1.0 %collective-permute-done.4.refs_2_.refs_5_.refs_16_ = bf16[304,128]{1,0:T(8,128)(2,1)S(1)} collective-permute-done((bf16[304,128]{1,0:T(8,128)(2,1)S(1)}, bf16[304,128]{1,0:T(8,128)(2,1)S(1)}, u32[]{:S(2)}, u32[]{:S(2)}) %collective-permute-start.4) | collective-permute-done | bytes 77856 | tf_op jit(solution)/shard_map/ppermute | solution.py:705
  25.4 0.6 %collective-permute-done.5.refs_3_.refs_6_.refs_17_ = bf16[304,128]{1,0:T(8,128)(2,1)S(1)} collective-permute-done((bf16[304,128]{1,0:T(8,128)(2,1)S(1)}, bf16[304,128]{1,0:T(8,128)(2,1)S(1)}, u32[]{:S(2)}, u32[]{:S(2)}) %collective-permute-start.5) | collective-permute-done | bytes 77856 | tf_op jit(solution)/shard_map/ppermute | solution.py:705
  26.0 0.1 collective-permute-start.6
  26.1 1.1 %mix.1 = (bf16[128,512]{1,0:T(8,128)(2,1)S(1)}, bf16[128,512]{1,0:T(8,128)(2,1)S(1)}, bf16[128,512]{1,0:T(8,128)(2,1)S(1)}, bf16[128,512]{1,0:T(8,128)(2,1)S(1)}, bf16[4,304,128]{2,1,0:T(8,128)(2,1)S(1)}) custom-call(s32[2,5]{1,0:T(2,128)S(1)} %copy-done.4, bf16[1,128,640]{2,1,0:T(8,128)(2,1)S(1)} %copy-done.1, f32[1,640]{1,0:T(1,128)S(1)} %reshape.13.gain_ref, ...), custom_call_target="tpu_custom_call" | custom-call | flops 20000000000 | tf_op jit(solution)/shard_map/mix/pallas_call | solution.py:713
  27.2 0.0 collective-permute-done.6.refs_1_
  27.2 1.2 %finish.1 = (bf16[1,128,640]{2,1,0:T(8,128)(2,1)}, bf16[1,128,640]{2,1,0:T(8,128)(2,1)}, bf16[1,128,640]{2,1,0:T(8,128)(2,1)}, bf16[1,128,640]{2,1,0:T(8,128)(2,1)}, f32[640]{0:T(1024)}) custom-call(f32[1,640]{1,0:T(1,128)S(1)} %gain.1.refs_0_, f32[1,640]{1,0:T(1,128)S(1)} %collective-permute-done.6.refs_1_, bf16[1,128,640]{2,1,0:T(8,128)(2,1)S(1)} %copy-done.2, ...), custom_call_target="tpu_custom_call" | custom-call | flops 1000000000 | tf_op jit(solution)/shard_map/finish/pallas_call | solution.py:713
  (12 shorter events, 0.0 us)
Async XLA Ops:
  3.2 5.8 %copy-start.10 = (f32[640]{0:T(1024)S(1)}, f32[640]{0:T(1024)}, u32[]{:S(2)}) copy-start(f32[640]{0:T(1024)} %param.10) | copy-start | bytes 7684
  3.2 9.2 %collective-permute-start = (bf16[352,128]{1,0:T(8,128)(2,1)}, bf16[352,128]{1,0:T(8,128)(2,1)S(1)}, u32[]{:S(2)}, u32[]{:S(2)}) collective-permute-start(bf16[352,128]{1,0:T(8,128)(2,1)} %get-tuple-element.37), channel_id=1, source_target_pairs={{0,12},{4,8},{8,4},{12,0},{1,13},{5,9},{9,5},{13,1},{2,14},{6,10},... | collective-permute-start | bytes 270344 | tf_op jit(solution)/shard_map/ppermute | solution.py:705
  8.3 6.0 %collective-permute-start.1 = (bf16[352,128]{1,0:T(8,128)(2,1)}, bf16[352,128]{1,0:T(8,128)(2,1)S(1)}, u32[]{:S(2)}, u32[]{:S(2)}) collective-permute-start(bf16[352,128]{1,0:T(8,128)(2,1)} %get-tuple-element.38), channel_id=1, source_target_pairs={{0,4},{4,0},{8,12},{12,8},{1,5},{5,1},{9,13},{13,9},{2,6},{6,2},{1... | collective-permute-start | bytes 270344 | tf_op jit(solution)/shard_map/ppermute | solution.py:705
  8.3 7.8 %collective-permute-start.2 = (bf16[352,128]{1,0:T(8,128)(2,1)}, bf16[352,128]{1,0:T(8,128)(2,1)S(1)}, u32[]{:S(2)}, u32[]{:S(2)}) collective-permute-start(bf16[352,128]{1,0:T(8,128)(2,1)} %get-tuple-element.39), channel_id=1, source_target_pairs={{0,8},{4,12},{8,0},{12,4},{1,9},{5,13},{9,1},{13,5},{2,10},{6,14},... | collective-permute-start | bytes 270344 | tf_op jit(solution)/shard_map/ppermute | solution.py:705
  9.0 0.7 %copy-start.4 = (s32[2,5]{1,0:T(2,128)S(1)}, s32[2,5]{1,0:T(2,128)}, u32[]{:S(2)}) copy-start(s32[2,5]{1,0:T(2,128)} %offsets_ref.7) | copy-start | bytes 124
  9.7 0.9 %copy-start = (bf16[1,128,640]{2,1,0:T(8,128)(2,1)S(1)}, bf16[1,128,640]{2,1,0:T(8,128)(2,1)}, u32[]{:S(2)}) copy-start(bf16[1,128,640]{2,1,0:T(8,128)(2,1)} %grad_ref.3) | copy-start | bytes 491524
  10.6 0.9 %copy-start.6 = (bf16[128,640]{1,0:T(8,128)(2,1)S(1)}, bf16[128,640]{1,0:T(8,128)(2,1)}, u32[]{:S(2)}) copy-start(bf16[128,640]{1,0:T(8,128)(2,1)} %get-tuple-element.32.out_ref) | copy-start | bytes 491524
  11.5 4.6 %copy-start.2 = (bf16[1,128,640]{2,1,0:T(8,128)(2,1)S(1)}, bf16[1,128,640]{2,1,0:T(8,128)(2,1)}, u32[]{:S(2)}) copy-start(bf16[1,128,640]{2,1,0:T(8,128)(2,1)} %refs_2_.1) | copy-start | bytes 491524
  11.5 4.6 %copy-start.7 = (bf16[128,640]{1,0:T(8,128)(2,1)S(1)}, bf16[128,640]{1,0:T(8,128)(2,1)}, u32[]{:S(2)}) copy-start(bf16[128,640]{1,0:T(8,128)(2,1)} %get-tuple-element.32.out_ref) | copy-start | bytes 491524
  11.5 4.6 %copy-start.8 = (bf16[352,128]{1,0:T(8,128)(2,1)S(1)}, bf16[352,128]{1,0:T(8,128)(2,1)}, u32[]{:S(2)}) copy-start(bf16[352,128]{1,0:T(8,128)(2,1)} %get-tuple-element.36.refs_2_) | copy-start | bytes 270340
  11.5 4.6 %copy-start.9 = (f32[16,128]{1,0:T(8,128)S(1)}, f32[16,128]{1,0:T(8,128)}, u32[]{:S(2)}) copy-start(f32[16,128]{1,0:T(8,128)} %get-tuple-element.34.refs_0_.refs_1_) | copy-start | bytes 24580
  16.1 6.0 %copy-start.1 = (bf16[1,128,640]{2,1,0:T(8,128)(2,1)S(1)}, bf16[1,128,640]{2,1,0:T(8,128)(2,1)}, u32[]{:S(2)}) copy-start(bf16[1,128,640]{2,1,0:T(8,128)(2,1)} %v_ref.5) | copy-start | bytes 491524
  16.1 6.0 %copy-start.3 = (bf16[1,128,640]{2,1,0:T(8,128)(2,1)S(1)}, bf16[1,128,640]{2,1,0:T(8,128)(2,1)}, u32[]{:S(2)}) copy-start(bf16[1,128,640]{2,1,0:T(8,128)(2,1)} %refs_3_.1) | copy-start | bytes 491524
  16.2 6.0 %copy-start.5 = (bf16[128,640]{1,0:T(8,128)(2,1)S(1)}, bf16[128,640]{1,0:T(8,128)(2,1)}, u32[]{:S(2)}) copy-start(bf16[128,640]{1,0:T(8,128)(2,1)} %get-tuple-element.45.expo_ref) | copy-start | bytes 491524
  17.7 6.7 %collective-permute-start.3 = (bf16[304,128]{1,0:T(8,128)(2,1)S(1)}, bf16[304,128]{1,0:T(8,128)(2,1)S(1)}, u32[]{:S(2)}, u32[]{:S(2)}) collective-permute-start(bf16[304,128]{1,0:T(8,128)(2,1)S(1)} %get-tuple-element.41), channel_id=1, source_target_pairs={{0,12},{4,8},{8,4},{12,0},{1,13},{5,9},{9,5},{13,1},{2,14},{6,10},... | collective-permute-start | bytes 233480 | tf_op jit(solution)/shard_map/ppermute | solution.py:705
  20.4 5.0 %collective-permute-start.4 = (bf16[304,128]{1,0:T(8,128)(2,1)S(1)}, bf16[304,128]{1,0:T(8,128)(2,1)S(1)}, u32[]{:S(2)}, u32[]{:S(2)}) collective-permute-start(bf16[304,128]{1,0:T(8,128)(2,1)S(1)} %get-tuple-element.42), channel_id=1, source_target_pairs={{0,4},{4,0},{8,12},{12,8},{1,5},{5,1},{9,13},{13,9},{2,6},{6,2},{1... | collective-permute-start | bytes 233480 | tf_op jit(solution)/shard_map/ppermute | solution.py:705
  20.4 5.6 %collective-permute-start.5 = (bf16[304,128]{1,0:T(8,128)(2,1)S(1)}, bf16[304,128]{1,0:T(8,128)(2,1)S(1)}, u32[]{:S(2)}, u32[]{:S(2)}) collective-permute-start(bf16[304,128]{1,0:T(8,128)(2,1)S(1)} %get-tuple-element.43), channel_id=1, source_target_pairs={{0,8},{4,12},{8,0},{12,4},{1,9},{5,13},{9,1},{13,5},{2,10},{6,14},... | collective-permute-start | bytes 233480 | tf_op jit(solution)/shard_map/ppermute | solution.py:705
  26.0 1.2 %collective-permute-start.6 = (f32[1,640]{1,0:T(1,128)S(1)}, f32[1,640]{1,0:T(1,128)S(1)}, u32[]{:S(2)}, u32[]{:S(2)}) collective-permute-start(f32[1,640]{1,0:T(1,128)S(1)} %gain.1.refs_0_), channel_id=1, source_target_pairs={{0,16},{16,0},{1,17},{17,1},{2,18},{18,2},{3,19},{19,3},{4,20},{20... | collective-permute-start | bytes 7688 | tf_op jit(solution)/shard_map/ppermute | solution.py:705

commit v13 on v12

--- a/solution.py
+++ b/solution.py
@@ -227,7 +227,7 @@
 STAT_TILES = 2 * TILE
 PIECES = 3
 NEVER = -1e30
-START_ORDER = (3, 1, 2)
+START_ORDER = (2, 1, 3)
 LOW = jnp.bfloat16
 WIDE = jnp.float32
 PACK_VMEM = 65408 * 1024

time: 28.6 us -> 29.6 us (1.035)
  waiting for transfers between devices: 7.21 us -> 8.04 us
    ppermute x7, waiting for transfers between devices: 7.21 us -> 8.04 us  [across(): return lax.ppermute(block, axis, route)]
  transfers between devices with their start and end apart: 7 -> 7, of which waited for: 5 -> 4; matrix products, arithmetic and copies ran while one was open for 0% -> 0% of each run, Pallas kernels for 8% -> 8%
where the time goes in v13:
time: 29.6 us; the launch traced here: 29.4 us
  starting transfers between devices  10.4 us (35%)
  waiting for transfers between devices  8.04 us (27%)
  Pallas kernels  7.66 us (26%)
  local copies, waits for them, and re-layouts  2.54 us (9%)
  between operations  0.73 us (2%)
    ppermute x7, starting transfers between devices, across(): return lax.ppermute(block, axis, route)  10.4 us
    ppermute x7, waiting for transfers between devices, across(): return lax.ppermute(block, axis, route)  8.04 us
    pallas_call x7, Pallas kernels, call(): pl.pallas_call(kernel, out_shape=results, in_specs=[SMEM_SPEC if block.dt...  7.66 us
    unnamed x22, local copies, waits for them, and re-layouts  2.54 us
  transfers between devices with their start and end apart: 7, of which 4 were waited for; matrix products, arithmetic and copies ran while one was open for 0% of the time, Pallas kernels for 8%

profile of v13, /device:TPU:0, one launch (start us, length us, event | category | flops | bytes accessed | tf_op | source)
XLA Modules:
  0.0 29.4 jit_solution(9284665632604016750)
XLA Ops:
  0.6 2.6 %pack.1 = (bf16[352,128]{1,0:T(8,128)(2,1)}, bf16[352,128]{1,0:T(8,128)(2,1)}, bf16[352,128]{1,0:T(8,128)(2,1)}, bf16[352,128]{1,0:T(8,128)(2,1)}, bf16[128,640]...) custom-call(s32[2,5]{1,0:T(2,128)} %offsets_ref.7, bf16[1,128,640]{2,1,0:T(8,128)(2,1)} %refs_2_.1, ...), custom_call_target="tpu_custom_call" | custom-call | flops 1000000000 | tf_op jit(solution)/shard_map/pack/pallas_call | solution.py:713
  3.2 4.1 %collective-permute-start = (bf16[352,128]{1,0:T(8,128)(2,1)}, bf16[352,128]{1,0:T(8,128)(2,1)S(1)}, u32[]{:S(2)}, u32[]{:S(2)}) collective-permute-start(bf16[352,128]{1,0:T(8,128)(2,1)} %get-tuple-element.37), channel_id=1, source_target_pairs={{0,8},{4,12},{8,0},{12,4},{1,9},{5,13},{9,1},{13,5},{2,10},{6,14},... | collective-permute-start | bytes 270344 | tf_op jit(solution)/shard_map/ppermute | solution.py:705
  7.3 1.6 %collective-permute-start.1 = (bf16[352,128]{1,0:T(8,128)(2,1)}, bf16[352,128]{1,0:T(8,128)(2,1)S(1)}, u32[]{:S(2)}, u32[]{:S(2)}) collective-permute-start(bf16[352,128]{1,0:T(8,128)(2,1)} %get-tuple-element.38), channel_id=1, source_target_pairs={{0,4},{4,0},{8,12},{12,8},{1,5},{5,1},{9,13},{13,9},{2,6},{6,2},{1... | collective-permute-start | bytes 270344 | tf_op jit(solution)/shard_map/ppermute | solution.py:705
  8.9 0.0 collective-permute-start.2
  8.9 0.0 copy-done.10
  8.9 0.0 copy-start.4
  8.9 0.7 %copy-done.4 = s32[2,5]{1,0:T(2,128)S(1)} copy-done((s32[2,5]{1,0:T(2,128)S(1)}, s32[2,5]{1,0:T(2,128)}, u32[]{:S(2)}) %copy-start.4) | copy-done | bytes 64
  9.6 0.9 %copy-done = bf16[1,128,640]{2,1,0:T(8,128)(2,1)S(1)} copy-done((bf16[1,128,640]{2,1,0:T(8,128)(2,1)S(1)}, bf16[1,128,640]{2,1,0:T(8,128)(2,1)}, u32[]{:S(2)}) %copy-start) | copy-done | bytes 163864
  10.5 0.9 %copy-done.6 = bf16[128,640]{1,0:T(8,128)(2,1)S(1)} copy-done((bf16[128,640]{1,0:T(8,128)(2,1)S(1)}, bf16[128,640]{1,0:T(8,128)(2,1)}, u32[]{:S(2)}) %copy-start.6) | copy-done | bytes 163864
  11.4 0.9 %prepare.1 = (f32[128,640]{1,0:T(8,128)S(1)}, f32[1,640]{1,0:T(1,128)S(1)}, bf16[128,1280]{1,0:T(8,128)(2,1)S(1)}) custom-call(s32[2,5]{1,0:T(2,128)S(1)} %copy-done.4, bf16[1,128,640]{2,1,0:T(8,128)(2,1)S(1)} %copy-done, f32[1,640]{1,0:T(1,128)S(1)} %reshape.13.gain_ref, bf16[128,640]{1,0:T(8,128)(2,1)S(1)} %copy-done.6), custom_call_target="tpu_custom_call" | custom-call | flops 2000000000 | tf_op jit(solution)/shard_map/prepare/pallas_call | solution.py:713
  12.3 0.1 collective-permute-done.refs_3_.refs_4_
  12.5 0.0 collective-permute-done.1.refs_4_.refs_5_
  12.5 3.0 %collective-permute-done.2.refs_5_.refs_6_ = bf16[352,128]{1,0:T(8,128)(2,1)S(1)} collective-permute-done((bf16[352,128]{1,0:T(8,128)(2,1)}, bf16[352,128]{1,0:T(8,128)(2,1)S(1)}, u32[]{:S(2)}, u32[]{:S(2)}) %collective-permute-start.2) | collective-permute-done | bytes 90144 | tf_op jit(solution)/shard_map/ppermute | solution.py:705
  15.5 0.0 copy-done.2
  15.5 0.0 copy-done.7
  15.5 0.0 copy-done.8
  15.5 0.0 copy-done.9
  15.5 0.0 copy-start.1
  15.5 0.0 copy-start.3
  15.5 0.0 copy-start.5
  15.6 1.5 %owner.1 = (f32[128,128]{1,0:T(8,128)S(1)}, bf16[128,128]{1,0:T(8,128)(2,1)S(1)}, bf16[144,128]{1,0:T(8,128)(2,1)S(1)}, f32[8,128]{1,0:T(8,128)S(1)}, bf16[304,1...) custom-call(s32[2,5]{1,0:T(2,128)S(1)} %copy-done.4, ...), custom_call_target="tpu_custom_call" | custom-call | flops 3000000000 | tf_op jit(solution)/shard_map/owner/pallas_call | solution.py:713
  17.1 3.2 %collective-permute-start.3 = (bf16[304,128]{1,0:T(8,128)(2,1)S(1)}, bf16[304,128]{1,0:T(8,128)(2,1)S(1)}, u32[]{:S(2)}, u32[]{:S(2)}) collective-permute-start(bf16[304,128]{1,0:T(8,128)(2,1)S(1)} %get-tuple-element.41), channel_id=1, source_target_pairs={{0,8},{4,12},{8,0},{12,4},{1,9},{5,13},{9,1},{13,5},{2,10},{6,14},... | collective-permute-start | bytes 233480 | tf_op jit(solution)/shard_map/ppermute | solution.py:705
  20.3 0.0 collective-permute-start.4
  20.3 1.5 %collective-permute-start.5 = (bf16[304,128]{1,0:T(8,128)(2,1)S(1)}, bf16[304,128]{1,0:T(8,128)(2,1)S(1)}, u32[]{:S(2)}, u32[]{:S(2)}) collective-permute-start(bf16[304,128]{1,0:T(8,128)(2,1)S(1)} %get-tuple-element.43), channel_id=1, source_target_pairs={{0,12},{4,8},{8,4},{12,0},{1,13},{5,9},{9,5},{13,1},{2,14},{6,10},... | collective-permute-start | bytes 233480 | tf_op jit(solution)/shard_map/ppermute | solution.py:705
  21.8 0.3 %last_head.1 = (bf16[128,128]{1,0:T(8,128)(2,1)S(1)}, bf16[128,128]{1,0:T(8,128)(2,1)S(1)}, f32[128,128]{1,0:T(8,128)S(1)}, f32[128,128]{1,0:T(8,128)S(1)}) custom-call(bf16[1,128,640]{2,1,0:T(8,128)(2,1)S(1)} %copy-done.2, bf16[1,128,640]{2,1,0:T(8,128)(2,1)S(1)} %copy-done.3, bf16[1,128,640]{2,1,0:T(8,128)(2,1)S(1)} %copy-done.1, ...), custom_call_target="tpu_custom_call" | custom-call | flops 20000000000 | tf_op jit(solution)/shard_map/last_head/pallas_call | solution.py:713
  22.1 2.9 %collective-permute-done.3.refs_1_.refs_4_.refs_15_ = bf16[304,128]{1,0:T(8,128)(2,1)S(1)} collective-permute-done((bf16[304,128]{1,0:T(8,128)(2,1)S(1)}, bf16[304,128]{1,0:T(8,128)(2,1)S(1)}, u32[]{:S(2)}, u32[]{:S(2)}) %collective-permute-start.3) | collective-permute-done | bytes 77856 | tf_op jit(solution)/shard_map/ppermute | solution.py:705
  25.0 2.0 %collective-permute-done.4.refs_2_.refs_5_.refs_16_ = bf16[304,128]{1,0:T(8,128)(2,1)S(1)} collective-permute-done((bf16[304,128]{1,0:T(8,128)(2,1)S(1)}, bf16[304,128]{1,0:T(8,128)(2,1)S(1)}, u32[]{:S(2)}, u32[]{:S(2)}) %collective-permute-start.4) | collective-permute-done | bytes 77856 | tf_op jit(solution)/shard_map/ppermute | solution.py:705
  27.0 0.0 collective-permute-done.5.refs_3_.refs_6_.refs_17_
  27.0 0.1 collective-permute-start.6
  27.1 1.1 %mix.1 = (bf16[128,512]{1,0:T(8,128)(2,1)S(1)}, bf16[128,512]{1,0:T(8,128)(2,1)S(1)}, bf16[128,512]{1,0:T(8,128)(2,1)S(1)}, bf16[128,512]{1,0:T(8,128)(2,1)S(1)}, bf16[4,304,128]{2,1,0:T(8,128)(2,1)S(1)}) custom-call(s32[2,5]{1,0:T(2,128)S(1)} %copy-done.4, bf16[1,128,640]{2,1,0:T(8,128)(2,1)S(1)} %copy-done.1, f32[1,640]{1,0:T(1,128)S(1)} %reshape.13.gain_ref, ...), custom_call_target="tpu_custom_call" | custom-call | flops 20000000000 | tf_op jit(solution)/shard_map/mix/pallas_call | solution.py:713
  28.2 0.0 collective-permute-done.6.refs_1_
  28.2 1.2 %finish.1 = (bf16[1,128,640]{2,1,0:T(8,128)(2,1)}, bf16[1,128,640]{2,1,0:T(8,128)(2,1)}, bf16[1,128,640]{2,1,0:T(8,128)(2,1)}, bf16[1,128,640]{2,1,0:T(8,128)(2,1)}, f32[640]{0:T(1024)}) custom-call(f32[1,640]{1,0:T(1,128)S(1)} %gain.1.refs_0_, f32[1,640]{1,0:T(1,128)S(1)} %collective-permute-done.6.refs_1_, bf16[1,128,640]{2,1,0:T(8,128)(2,1)S(1)} %copy-done.2, ...), custom_call_target="tpu_custom_call" | custom-call | flops 1000000000 | tf_op jit(solution)/shard_map/finish/pallas_call | solution.py:713
  (12 shorter events, 0.0 us)
Async XLA Ops:
  3.2 5.7 %copy-start.10 = (f32[640]{0:T(1024)S(1)}, f32[640]{0:T(1024)}, u32[]{:S(2)}) copy-start(f32[640]{0:T(1024)} %param.10) | copy-start | bytes 7684
  3.2 9.3 %collective-permute-start = (bf16[352,128]{1,0:T(8,128)(2,1)}, bf16[352,128]{1,0:T(8,128)(2,1)S(1)}, u32[]{:S(2)}, u32[]{:S(2)}) collective-permute-start(bf16[352,128]{1,0:T(8,128)(2,1)} %get-tuple-element.37), channel_id=1, source_target_pairs={{0,8},{4,12},{8,0},{12,4},{1,9},{5,13},{9,1},{13,5},{2,10},{6,14},... | collective-permute-start | bytes 270344 | tf_op jit(solution)/shard_map/ppermute | solution.py:705
  7.3 5.2 %collective-permute-start.1 = (bf16[352,128]{1,0:T(8,128)(2,1)}, bf16[352,128]{1,0:T(8,128)(2,1)S(1)}, u32[]{:S(2)}, u32[]{:S(2)}) collective-permute-start(bf16[352,128]{1,0:T(8,128)(2,1)} %get-tuple-element.38), channel_id=1, source_target_pairs={{0,4},{4,0},{8,12},{12,8},{1,5},{5,1},{9,13},{13,9},{2,6},{6,2},{1... | collective-permute-start | bytes 270344 | tf_op jit(solution)/shard_map/ppermute | solution.py:705
  8.9 6.6 %collective-permute-start.2 = (bf16[352,128]{1,0:T(8,128)(2,1)}, bf16[352,128]{1,0:T(8,128)(2,1)S(1)}, u32[]{:S(2)}, u32[]{:S(2)}) collective-permute-start(bf16[352,128]{1,0:T(8,128)(2,1)} %get-tuple-element.39), channel_id=1, source_target_pairs={{0,12},{4,8},{8,4},{12,0},{1,13},{5,9},{9,5},{13,1},{2,14},{6,10},... | collective-permute-start | bytes 270344 | tf_op jit(solution)/shard_map/ppermute | solution.py:705
  8.9 0.7 %copy-start.4 = (s32[2,5]{1,0:T(2,128)S(1)}, s32[2,5]{1,0:T(2,128)}, u32[]{:S(2)}) copy-start(s32[2,5]{1,0:T(2,128)} %offsets_ref.7) | copy-start | bytes 124
  9.6 0.9 %copy-start = (bf16[1,128,640]{2,1,0:T(8,128)(2,1)S(1)}, bf16[1,128,640]{2,1,0:T(8,128)(2,1)}, u32[]{:S(2)}) copy-start(bf16[1,128,640]{2,1,0:T(8,128)(2,1)} %grad_ref.3) | copy-start | bytes 491524
  10.5 0.9 %copy-start.6 = (bf16[128,640]{1,0:T(8,128)(2,1)S(1)}, bf16[128,640]{1,0:T(8,128)(2,1)}, u32[]{:S(2)}) copy-start(bf16[128,640]{1,0:T(8,128)(2,1)} %get-tuple-element.32.out_ref) | copy-start | bytes 491524
  11.4 4.1 %copy-start.2 = (bf16[1,128,640]{2,1,0:T(8,128)(2,1)S(1)}, bf16[1,128,640]{2,1,0:T(8,128)(2,1)}, u32[]{:S(2)}) copy-start(bf16[1,128,640]{2,1,0:T(8,128)(2,1)} %refs_2_.1) | copy-start | bytes 491524
  11.4 4.1 %copy-start.7 = (bf16[128,640]{1,0:T(8,128)(2,1)S(1)}, bf16[128,640]{1,0:T(8,128)(2,1)}, u32[]{:S(2)}) copy-start(bf16[128,640]{1,0:T(8,128)(2,1)} %get-tuple-element.32.out_ref) | copy-start | bytes 491524
  11.4 4.1 %copy-start.8 = (bf16[352,128]{1,0:T(8,128)(2,1)S(1)}, bf16[352,128]{1,0:T(8,128)(2,1)}, u32[]{:S(2)}) copy-start(bf16[352,128]{1,0:T(8,128)(2,1)} %get-tuple-element.36.refs_2_) | copy-start | bytes 270340
  11.4 4.1 %copy-start.9 = (f32[16,128]{1,0:T(8,128)S(1)}, f32[16,128]{1,0:T(8,128)}, u32[]{:S(2)}) copy-start(f32[16,128]{1,0:T(8,128)} %get-tuple-element.34.refs_0_.refs_1_) | copy-start | bytes 24580
  15.5 6.3 %copy-start.1 = (bf16[1,128,640]{2,1,0:T(8,128)(2,1)S(1)}, bf16[1,128,640]{2,1,0:T(8,128)(2,1)}, u32[]{:S(2)}) copy-start(bf16[1,128,640]{2,1,0:T(8,128)(2,1)} %v_ref.5) | copy-start | bytes 491524
  15.5 6.3 %copy-start.3 = (bf16[1,128,640]{2,1,0:T(8,128)(2,1)S(1)}, bf16[1,128,640]{2,1,0:T(8,128)(2,1)}, u32[]{:S(2)}) copy-start(bf16[1,128,640]{2,1,0:T(8,128)(2,1)} %refs_3_.1) | copy-start | bytes 491524
  15.5 6.3 %copy-start.5 = (bf16[128,640]{1,0:T(8,128)(2,1)S(1)}, bf16[128,640]{1,0:T(8,128)(2,1)}, u32[]{:S(2)}) copy-start(bf16[128,640]{1,0:T(8,128)(2,1)} %get-tuple-element.45.expo_ref) | copy-start | bytes 491524
  17.1 7.9 %collective-permute-start.3 = (bf16[304,128]{1,0:T(8,128)(2,1)S(1)}, bf16[304,128]{1,0:T(8,128)(2,1)S(1)}, u32[]{:S(2)}, u32[]{:S(2)}) collective-permute-start(bf16[304,128]{1,0:T(8,128)(2,1)S(1)} %get-tuple-element.41), channel_id=1, source_target_pairs={{0,8},{4,12},{8,0},{12,4},{1,9},{5,13},{9,1},{13,5},{2,10},{6,14},... | collective-permute-start | bytes 233480 | tf_op jit(solution)/shard_map/ppermute | solution.py:705
  20.3 6.7 %collective-permute-start.4 = (bf16[304,128]{1,0:T(8,128)(2,1)S(1)}, bf16[304,128]{1,0:T(8,128)(2,1)S(1)}, u32[]{:S(2)}, u32[]{:S(2)}) collective-permute-start(bf16[304,128]{1,0:T(8,128)(2,1)S(1)} %get-tuple-element.42), channel_id=1, source_target_pairs={{0,4},{4,0},{8,12},{12,8},{1,5},{5,1},{9,13},{13,9},{2,6},{6,2},{1... | collective-permute-start | bytes 233480 | tf_op jit(solution)/shard_map/ppermute | solution.py:705
  20.3 6.7 %collective-permute-start.5 = (bf16[304,128]{1,0:T(8,128)(2,1)S(1)}, bf16[304,128]{1,0:T(8,128)(2,1)S(1)}, u32[]{:S(2)}, u32[]{:S(2)}) collective-permute-start(bf16[304,128]{1,0:T(8,128)(2,1)S(1)} %get-tuple-element.43), channel_id=1, source_target_pairs={{0,12},{4,8},{8,4},{12,0},{1,13},{5,9},{9,5},{13,1},{2,14},{6,10},... | collective-permute-start | bytes 233480 | tf_op jit(solution)/shard_map/ppermute | solution.py:705
  27.0 1.2 %collective-permute-start.6 = (f32[1,640]{1,0:T(1,128)S(1)}, f32[1,640]{1,0:T(1,128)S(1)}, u32[]{:S(2)}, u32[]{:S(2)}) collective-permute-start(f32[1,640]{1,0:T(1,128)S(1)} %gain.1.refs_0_), channel_id=1, source_target_pairs={{0,16},{16,0},{1,17},{17,1},{2,18},{18,2},{3,19},{19,3},{4,20},{20... | collective-permute-start | bytes 7688 | tf_op jit(solution)/shard_map/ppermute | solution.py:705

commit v14 on v11

--- a/solution.py
+++ b/solution.py
@@ -314,17 +314,22 @@
     return normed, product, grad_attn.astype(LOW), inner
 
 
-def nearest_first(refs):
-    return [refs[0], *refs[:0:-1]]
+def last_owner_of(dp_place):
+    return 1 + dp_place % 2
+
+
+def last_owner():
+    return last_owner_of(lax.axis_index("dp"))
 
 
 def pack_kernel(top_step, offsets_ref, q_ref, k_ref, v_ref, grad_ref, *refs):
-    payload_refs, (expo_ref, out_ref, stats_ref, held_ref) = refs[:SPAN], refs[SPAN:]
+    long_refs, short_refs, refs = refs[:SPAN], refs[SPAN : SPAN + 2], refs[SPAN + 2 :]
+    expo_ref, out_ref, stats_ref, held_ref = refs
     tokens, width = q_ref.shape[1:]
     heads = range(width // HEAD_DIM)
-    owned = range(OWNED)
     me = lax.axis_index("ctx")
     picked = sum(picked_counts(tokens, top_step))
+    rows = held_ref.shape[1]
     score_scale = 1.0 / math.sqrt(HEAD_DIM)
     q_rows, k_rows, v_rows, grad_rows = [
         [ref[0, :, head_cols(head)] for head in heads] for ref in (q_ref, k_ref, v_ref, grad_ref)
@@ -338,24 +343,10 @@
             1,
             0,
         ).astype(LOW)
-        for head in owned
-    ]
-    shared = [
-        contract(
-            picks[head][:picked], jnp.concatenate([k_rows[head], v_rows[head]], 1), 1, 0
-        ).astype(LOW)
-        for head in heads[OWNED:]
+        for head in heads
     ]
     top_scores = [jnp.max(block, axis=0, keepdims=True) for block in scores]
     expos = [jnp.exp(scores[head] - top_scores[head]) for head in heads]
-    for head in heads[OWNED:]:
-        key_row = lax.broadcasted_iota(jnp.int32, (tokens, 1), 0)
-        times = 1.0
-        for level, step in ((0, R1), (1, top_step)):
-            offset = offsets_ref[level, head]
-            hit_column = jnp.where(key_row % step == offset, 1.0, 0.0)
-            times = times + hit_column * hit_row(offset, step, tokens)
-        expos[head] = times * expos[head]
     expo_lows = [expo.astype(LOW) for expo in expos]
     outs = [contract(v_rows[head], expo_lows[head], 0, 0) for head in heads]
     totals = [jnp.sum(expo, axis=0, keepdims=True) for expo in expos]
@@ -363,24 +354,24 @@
         expo_ref[:, head_cols(head)] = expo_lows[head]
         stats_ref[head : head + 1, :] = top_scores[head]
         stats_ref[TILE + head : TILE + head + 1, :] = totals[head]
-    for head in owned:
-        outs[head] = outs[head] * (1.0 / totals[head])
-    outs = [out.astype(LOW) for out in outs]
+    outs = [(outs[head] * (1.0 / totals[head])).astype(LOW) for head in heads]
     picked_outs = [
-        contract(picks[head][:picked], outs[head], 1, 1).astype(LOW) for head in owned
+        contract(picks[head][:picked], outs[head], 1, 1).astype(LOW) for head in heads
     ]
     for head in heads:
         out_ref[:, head_cols(head)] = outs[head]
-    for head in owned:
+    for head in heads:
         pieces = piece_rows(top_scores[head] + jnp.log(totals[head])).astype(LOW)
         stat_rows = contract(pieces, picks[head], 1, 1)
         blocks = [moved[head][:, block * HEAD_DIM : (block + 1) * HEAD_DIM] for block in range(4)]
         blocks.append(picked_outs[head])
-        blocks += [shared[0][:, :HEAD_DIM], shared[0][:, HEAD_DIM:]]
         blocks.append(jnp.concatenate([stat_rows, jnp.zeros_like(stat_rows)], 0).astype(LOW))
         held_ref[head] = jnp.concatenate(blocks, 0)
-    for distance, payload_ref in enumerate(payload_refs):
-        payload_ref[...] = held_ref[me ^ distance]
+    for distance, long_ref in enumerate(long_refs):
+        long_ref[:rows] = held_ref[me ^ distance]
+        long_ref[rows:] = held_ref[heads[-1]]
+    for distance, short_ref in zip((2, 3), short_refs):
+        short_ref[...] = held_ref[me ^ distance]
 
 
 def prepare_kernel(top_step, offsets_ref, grad_ref, gain_ref, out_ref, *refs):
@@ -400,7 +391,7 @@
         grad_norm_ref[:, cols] = grad_norms[head]
         picks = pick_matrix(offsets_ref, head, tokens, top_step, 1)
         place_ref[:, cols] = picks
-    for head in range(OWNED):
+    for head in heads:
         cols = head_cols(head)
         mid_offset, top_offset = offsets_ref[0, head], offsets_ref[1, head]
         seen = jnp.maximum(
@@ -416,26 +407,48 @@
         place_ref[:, head_cols(len(heads) + head)] = picks * kept
 
 
-def owner_kernel(top_step, offsets_ref, q_ref, gain_ref, out_ref, grad_norm_ref, *refs):
-    stats_ref, gain_base_ref = refs[:2]
-    payload_refs, refs = nearest_first(refs[2 : 2 + SPAN]), refs[2 + SPAN :]
-    normed_ref, grad_low_ref, score_grad_ref, kept_ref = refs[:4]
-    return_refs = refs[4:]
-    tokens = q_ref.shape[1]
-    heads = q_ref.shape[2] // HEAD_DIM
-    top_rows, mid_rows = picked_counts(tokens, top_step)
+def owner_kernel(top_step, offsets_ref, gain_ref, gain_base_ref, *refs):
+    own_ref, far_long, far_short, near, middle_long, middle_short = refs[:6]
+    answer_refs, short_refs = refs[6 : 6 + SPAN], refs[6 + SPAN : 8 + SPAN]
+    far_ref, middle_ref = refs[8 + SPAN :]
+    heads = gain_ref.shape[1] // HEAD_DIM
+    last = heads - 1
+    top_rows, mid_rows = picked_counts(HEAD_DIM, top_step)
     picked = top_rows + mid_rows
     top_all, mid_all = SPAN * top_rows, SPAN * mid_rows
     queries = top_all + mid_all
+    rows = far_short.shape[0]
     score_scale = 1.0 / math.sqrt(HEAD_DIM)
     me = lax.axis_index("ctx")
-    ones = jnp.ones((TILE, tokens), LOW)
-
-    def by_level(block):
+    owns_last = me == last_owner()
+
+    @pl.when(owns_last)
+    def _():
+        far_ref[...] = far_long[:rows]
+        middle_ref[...] = middle_long[:rows]
+
+    @pl.when(jnp.logical_not(owns_last))
+    def _():
+        far_ref[...] = far_short[...]
+        middle_ref[...] = middle_short[...]
+
+    sources = (
+        ((own_ref, 0), (near, 0), (middle_ref, 0), (far_ref, 0)),
+        ((own_ref, rows), (near, rows), (middle_long, rows), (far_long, rows)),
+    )
+    both_heads = range(2)
+    gain_row = jnp.zeros((1, HEAD_DIM), WIDE)
+    for head in range(OWNED):
+        gain_row = gain_row + jnp.where(me == head, 1.0, 0.0) * gain_ref[:, head_cols(head)]
+    gain_rows = [gain_row, gain_ref[:, head_cols(last)]]
+    lane = lax.broadcasted_iota(jnp.int32, (1, queries), 1)
+    is_top = jnp.where(lane < top_all, 1.0, 0.0)
+
+    def by_level(which, block):
         start = block * picked
         return jnp.concatenate(
-            [ref[start : start + top_rows] for ref in payload_refs]
-            + [ref[start + top_rows : start + picked] for ref in payload_refs],
+            [ref[at + start : at + start + top_rows] for ref, at in sources[which]]
+            + [ref[at + start + top_rows : at + start + picked] for ref, at in sources[which]],
             0,
         )
 
@@ -448,180 +461,182 @@
             0,
         )
 
-    q_rows, k_rows, v_rows, grad_rows, base_rows = [by_level(block) for block in range(5)]
-    stat_start = 7 * picked
-    logs = [
-        joined_row(ref[stat_start : stat_start + STAT_TILES].astype(WIDE), 0)
-        for ref in payload_refs
-    ]
-    base_top_log = sum(
-        rolled(lane_window(log, 0, top_rows), slot * top_rows) for slot, log in enumerate(logs)
-    )
-    base_mid_log = sum(
-        rolled(lane_window(log, top_rows, mid_rows), slot * mid_rows - top_rows)
-        for slot, log in enumerate(logs)
-    )
-    base_log = jnp.concatenate([base_top_log, base_mid_log[:, :mid_all]], 1)
-    gain_row = jnp.zeros((1, HEAD_DIM), WIDE)
-    for head in range(OWNED):
-        gain_row = gain_row + jnp.where(me == head, 1.0, 0.0) * gain_ref[:, head_cols(head)]
-    mid_offset, top_offset = offsets_ref[0, me], offsets_ref[1, me]
-    both = mid_offset % top_step == top_offset
-    lane = lax.broadcasted_iota(jnp.int32, (1, queries), 1)
-    is_top = jnp.where(lane < top_all, 1.0, 0.0)
-    top_in_mid = jnp.where(((lane % top_rows) * top_step + top_offset) % R1 == mid_offset, 1.0, 0.0)
-    both_flag = jnp.where(both, 1.0, 0.0)
-    sees_top = is_top + (1.0 - is_top) * both_flag
-    sees_mid = is_top * top_in_mid + (1.0 - is_top)
-    bias = per_level((1.0 - sees_top) * NEVER, (1.0 - sees_mid) * NEVER)
-    last = heads - 1
-    cols = head_cols(last)
-    peers = payload_refs[1:]
-    q_last = q_ref[0, :, cols]
-    k_peers = jnp.concatenate([ref[5 * picked : 6 * picked] for ref in peers], 0)
-    v_peers = jnp.concatenate([ref[6 * picked : 7 * picked] for ref in peers], 0)
-    last_biases = [
-        jnp.broadcast_to((1.0 - hit_row(offsets_ref[level, last], step, tokens)) * NEVER, shape)
-        for level, step, shape in (
-            (1, top_step, (top_rows, tokens)),
-            (0, R1, (mid_rows, tokens)),
+    def base_log_of(which):
+        start = 5 * picked
+        logs = [
+            joined_row(ref[at + start : at + start + STAT_TILES].astype(WIDE), 0)
+            for ref, at in sources[which]
+        ]
+        top_log = sum(
+            rolled(lane_window(log, 0, top_rows), slot * top_rows) for slot, log in enumerate(logs)
         )
-    ]
-    scores = contract(k_rows, q_rows, 1, 1) * score_scale + bias
-    scores_last = contract(k_peers, q_last, 1, 1) * score_scale + jnp.concatenate(
-        last_biases * PEERS, 0
-    )
-    base_attn = base_rows.astype(WIDE).T
-    grad_norm = (grad_rows.astype(WIDE) * gain_row).T
-    top_score = jnp.maximum(base_log, jnp.max(scores, axis=0, keepdims=True))
-    base_top, base_total = stats_ref[last : last + 1, :], stats_ref[TILE + last : TILE + last + 1, :]
-    top_last = jnp.maximum(base_top, jnp.max(scores_last, axis=0, keepdims=True))
-    expo = jnp.exp(scores - top_score)
-    expo_last = jnp.exp(scores_last - top_last)
-    factor = jnp.exp(base_log - top_score)
-    factor_last = jnp.exp(base_top - top_last)
-    total = factor + jnp.sum(expo, axis=0, keepdims=True)
-    total_last = factor_last * base_total + jnp.sum(expo_last, axis=0, keepdims=True)
-    inv_total, inv_last = 1.0 / total, 1.0 / total_last
-    soft, soft_last = expo * inv_total, expo_last * inv_last
-    soft_low, soft_last_low = soft.astype(LOW), soft_last.astype(LOW)
-    factor_last = factor_last * inv_last
-    attn = (factor * inv_total) * base_attn + contract(v_rows, soft_low, 0, 0)
-    attn_last = factor_last * out_ref[:, cols].astype(WIDE) + contract(v_peers, soft_last_low, 0, 0)
-    _, product, grad_low, inner = norm_backward(attn, grad_norm)
-    normed_last, product_last, grad_last_low, inner_last = norm_backward(
-        attn_last, grad_norm_ref[:, cols]
+        mid_log = sum(
+            rolled(lane_window(log, top_rows, mid_rows), slot * mid_rows - top_rows)
+            for slot, log in enumerate(logs)
+        )
+        return jnp.concatenate([top_log, mid_log[:, :mid_all]], 1)
+
+    def masks(head):
+        mid_offset, top_offset = offsets_ref[0, head], offsets_ref[1, head]
+        top_in_mid = ((lane % top_rows) * top_step + top_offset) % R1 == mid_offset
+        both = jnp.where(mid_offset % top_step == top_offset, 1.0, 0.0)
+        sees_top = is_top + (1.0 - is_top) * both
+        sees_mid = is_top * jnp.where(top_in_mid, 1.0, 0.0) + (1.0 - is_top)
+        once = is_top + (1.0 - is_top) * (1.0 - both)
+        return per_level((1.0 - sees_top) * NEVER, (1.0 - sees_mid) * NEVER), once
+
+    q_rows, k_rows, v_rows, grad_rows, base_rows = [
+        [by_level(which, block) for which in both_heads] for block in range(5)
+    ]
+    biases, onces = zip(*[masks(head) for head in (me, last)])
+    scores = [
+        contract(k_rows[which], q_rows[which], 1, 1) * score_scale + biases[which]
+        for which in both_heads
+    ]
+    base_logs = [base_log_of(which) for which in both_heads]
+    base_attns = [block.astype(WIDE).T for block in base_rows]
+    grad_norms = [
+        (grad_rows[which].astype(WIDE) * gain_rows[which]).T for which in both_heads
+    ]
+    top_scores = [
+        jnp.maximum(base_logs[which], jnp.max(scores[which], axis=0, keepdims=True))
+        for which in both_heads
+    ]
+    expos = [jnp.exp(scores[which] - top_scores[which]) for which in both_heads]
+    factors = [jnp.exp(base_logs[which] - top_scores[which]) for which in both_heads]
+    totals = [
+        factors[which] + jnp.sum(expos[which], axis=0, keepdims=True) for which in both_heads
+    ]
+    inv_totals = [1.0 / total for total in totals]
+    softs = [expos[which] * inv_totals[which] for which in both_heads]
+    soft_lows = [soft.astype(LOW) for soft in softs]
+    attns = [
+        (factors[which] * inv_totals[which]) * base_attns[which]
+        + contract(v_rows[which], soft_lows[which], 0, 0)
+        for which in both_heads
+    ]
+    _, products, grad_lows, inners = zip(
+        *[norm_backward(attns[which], grad_norms[which]) for which in both_heads]
     )
     spans = (slice(0, top_all), slice(top_all, queries))
-    prob_grads = [contract(v_rows[span], grad_low[:, span], 1, 0) for span in spans]
-    prob_grad_last = contract(v_peers, grad_last_low, 1, 0)
+    cases = [(which, span) for which in both_heads for span in spans]
+    prob_grads = [
+        contract(v_rows[which][span], grad_lows[which][:, span], 1, 0) for which, span in cases
+    ]
+    dvs = [
+        contract(soft_lows[which][span, span], grad_lows[which][:, span], 1, 1).astype(LOW)
+        for which, span in cases
+    ]
     score_grads = [
-        (soft[span, span] * (prob_grad - inner[:, span]) * score_scale).astype(LOW)
-        for span, prob_grad in zip(spans, prob_grads)
-    ]
-    score_grad_last = (soft_last * (prob_grad_last - inner_last) * score_scale).astype(LOW)
+        (softs[which][span, span] * (prob_grad - inners[which][:, span]) * score_scale).astype(LOW)
+        for (which, span), prob_grad in zip(cases, prob_grads)
+    ]
     dks = [
-        contract(score_grad, q_rows[span], 1, 0).astype(LOW)
-        for span, score_grad in zip(spans, score_grads)
-    ]
-    dk_last = contract(score_grad_last, q_last, 1, 0).astype(LOW)
-    dvs = [
-        contract(soft_low[span, span], grad_low[:, span], 1, 1).astype(LOW) for span in spans
-    ]
-    dv_last = contract(soft_last_low, grad_last_low, 1, 1).astype(LOW)
+        contract(score_grad, q_rows[which][span], 1, 0).astype(LOW)
+        for (which, span), score_grad in zip(cases, score_grads)
+    ]
     dqs = [
-        contract(score_grad, k_rows[span], 0, 0).astype(LOW)
-        for span, score_grad in zip(spans, score_grads)
-    ]
-    attn_rows = attn.T.astype(LOW)
-    attn_parts = [attn_rows[span] for span in spans]
-    log_total = top_score + jnp.log(total)
+        contract(score_grad, k_rows[which][span], 0, 0).astype(LOW)
+        for (which, span), score_grad in zip(cases, score_grads)
+    ]
+    attn_rows = [attn.T.astype(LOW) for attn in attns]
+    attn_parts = [attn_rows[which][span] for which, span in cases]
+    ones = jnp.ones((TILE, queries), LOW)
+    own_gains = [
+        gain_row_of(ones, products[which] * onces[which]) / gain_rows[which]
+        for which in both_heads
+    ]
+    gains = [
+        gain_base_ref[:, head_cols(head)] + jnp.where(me == head, 1.0, 0.0) * own_gains[0]
+        for head in range(OWNED)
+    ]
+    gains.append(
+        gain_base_ref[:, head_cols(last)] + jnp.where(owns_last, 1.0, 0.0) * own_gains[1]
+    )
+    gain_high, gain_rest = [
+        block.astype(WIDE) for block in gain_pieces(jnp.concatenate(gains, 0))
+    ]
     padding = jnp.zeros((1, top_all - mid_all), WIDE)
-    once = is_top + (1.0 - is_top) * (1.0 - both_flag)
-    ones_all = jnp.ones((TILE, queries), LOW)
-    own_gain = gain_row_of(ones_all, product * once) / gain_row
-    gain_rows = [
-        gain_base_ref[:, head_cols(head)] + jnp.where(me == head, 1.0, 0.0) * own_gain
-        for head in range(OWNED)
-    ]
-    gain_rows.append(gain_row_of(ones, product_last) / gain_ref[:, cols])
-    gain_high, gain_rest = [
-        rows.astype(WIDE) for rows in gain_pieces(jnp.concatenate(gain_rows, 0))
-    ]
-    top_log, mid_log = log_total[:, :top_all], jnp.concatenate(
-        [log_total[:, top_all:], padding], 1
-    )
     empty = jnp.zeros((PIECES, HEAD_DIM), WIDE)
-    for distance, return_ref in enumerate(return_refs):
-        blocks = []
-        for top_block, mid_block in (dqs, dks, dvs, attn_parts):
-            blocks.append(top_block[distance * top_rows : (distance + 1) * top_rows])
-            blocks.append(mid_block[distance * mid_rows : (distance + 1) * mid_rows])
-        start = max(distance - 1, 0) * picked
-        blocks += [dk_last[start : start + picked], dv_last[start : start + picked]]
-        log_row = lane_window(rolled(top_log, -distance * top_rows), 0, top_rows) + lane_window(
-            rolled(mid_log, top_rows - distance * mid_rows), top_rows, mid_rows
-        )
-        log_rows = [piece_rows(log_row, gain_high), empty, gain_rest]
-        blocks.append(jnp.concatenate(log_rows, 0).astype(LOW))
-        return_ref[...] = jnp.concatenate(blocks, 0)
-    normed_ref[...] = normed_last
-    grad_low_ref[...] = grad_last_low
-    score_grad_ref[...] = score_grad_last
-    kept_ref[0:1, :] = factor_last
-    kept_ref[1:2, :] = inner_last
-
-
-def last_head_kernel(top_step, q_ref, k_ref, v_ref, gain_ref, expo_ref, *refs):
-    normed_ref, grad_low_ref, peer_score_grad_ref, kept_ref, *peers = refs[: 4 + PEERS]
-    peers = peers[::-1]
-    attended_ref, dq_ref, dk_ref, dv_ref = refs[4 + PEERS :]
-    picked = sum(picked_counts(q_ref.shape[1], top_step))
-    score_scale = 1.0 / math.sqrt(HEAD_DIM)
-    cols = head_cols(q_ref.shape[2] // HEAD_DIM - 1)
-    attended_ref[...] = (normed_ref[...].T * gain_ref[:, cols]).astype(LOW)
-    k_peers = jnp.concatenate([ref[5 * picked : 6 * picked] for ref in peers], 0)
-    grad_low = grad_low_ref[...]
-    soft = expo_ref[:, cols].astype(WIDE) * kept_ref[0:1, :]
-    prob_grad = contract(v_ref[0, :, cols], grad_low, 1, 0)
-    score_grad = (soft * (prob_grad - kept_ref[1:2, :]) * score_scale).astype(LOW)
-    dk_ref[...] = contract(score_grad, q_ref[0, :, cols], 1, 0)
-    dv_ref[...] = contract(soft.astype(LOW), grad_low, 1, 1)
-    dq_ref[...] = (
-        contract(score_grad, k_ref[0, :, cols], 0, 0)
-        + contract(peer_score_grad_ref[...], k_peers, 0, 0)
-    ).astype(LOW)
-
-
-def gain_kernel(picked, *refs):
-    return_refs, gain_ref = nearest_first(refs[:SPAN]), refs[SPAN]
-    tiles = [ref[6 * picked : 6 * picked + STAT_TILES].astype(WIDE) for ref in return_refs]
-    parts = [tile[PIECES:TILE] + tile[TILE + PIECES :] for tile in tiles]
-    total = (parts[0] + parts[1]) + (parts[2] + parts[3])
+    answers = []
+    for which in both_heads:
+        log_total = top_scores[which] + jnp.log(totals[which])
+        top_log = log_total[:, :top_all]
+        mid_log = jnp.concatenate([log_total[:, top_all:], padding], 1)
+        answers.append([])
+        for distance in range(SPAN):
+            blocks = []
+            for block in (dqs, dks, dvs, attn_parts):
+                top_block, mid_block = block[2 * which : 2 * which + 2]
+                blocks.append(top_block[distance * top_rows : (distance + 1) * top_rows])
+                blocks.append(mid_block[distance * mid_rows : (distance + 1) * mid_rows])
+            log_row = lane_window(
+                rolled(top_log, -distance * top_rows), 0, top_rows
+            ) + lane_window(
+                rolled(mid_log, top_rows - distance * mid_rows), top_rows, mid_rows
+            )
+            log_rows = [piece_rows(log_row, gain_high), empty, gain_rest]
+            blocks.append(jnp.concatenate(log_rows, 0).astype(LOW))
+            answers[-1].append(jnp.concatenate(blocks, 0))
+    rows = answers[0][0].shape[0]
+    for distance, answer_ref in enumerate(answer_refs):
+        answer_ref[:rows] = answers[0][distance]
+        answer_ref[rows:] = answers[1][distance]
+    for distance, short_ref in zip((2, 3), short_refs):
+        short_ref[...] = answers[0][distance]
+
+
+def gain_kernel(picked, own_ref, far_long, far_short, near, middle_long, middle_short, gain_ref):
+    me = lax.axis_index("ctx")
+
+    def part(ref):
+        tile = ref[4 * picked : 4 * picked + STAT_TILES].astype(WIDE)
+        return tile[PIECES:TILE] + tile[TILE + PIECES :]
+
+    far = jnp.where(me ^ 3 == last_owner(), part(far_long), part(far_short))
+    middle = jnp.where(me ^ 2 == last_owner(), part(middle_long), part(middle_short))
+    total = (part(own_ref) + part(near)) + (middle + far)
     for head in range(gain_ref.shape[1] // HEAD_DIM):
         gain_ref[:, head_cols(head)] = total[head : head + 1]
 
 
 def mix_kernel(top_step, offsets_ref, v_ref, gain_ref, expo_ref, out_ref, *refs):
     grad_norm_ref, stats_ref, place_ref = refs[:3]
-    return_refs, refs = nearest_first(refs[3 : 3 + SPAN]), refs[3 + SPAN :]
-    attended_ref, grad_low_ref, soft_ref, score_grad_ref, placed_ref = refs
+    own_ref, far_long, far_short, near, middle_long, middle_short = refs[3:9]
+    attended_ref, grad_low_ref, soft_ref, score_grad_ref, placed_ref = refs[9:]
     tokens, width = v_ref.shape[1:]
     count = width // HEAD_DIM
     picked = sum(picked_counts(tokens, top_step))
     score_scale = 1.0 / math.sqrt(HEAD_DIM)
     me = lax.axis_index("ctx")
-    heads = range(OWNED)
+    heads = range(count)
     every = [head_cols(head) for head in heads]
-    for distance, return_ref in enumerate(return_refs):
-        placed_ref[me ^ distance] = return_ref[...]
+    rows = far_short.shape[0]
+    placed_ref[me] = own_ref[:rows]
+    placed_ref[me ^ 1] = near[:rows]
+    for distance, long_ref, short_ref in ((2, middle_long, middle_short), (3, far_long, far_short)):
+
+        @pl.when(me ^ distance == last_owner())
+        def _():
+            placed_ref[me ^ distance] = long_ref[:rows]
+
+        @pl.when(me ^ distance != last_owner())
+        def _():
+            placed_ref[me ^ distance] = short_ref[...]
+
+    for distance, long_ref in enumerate((own_ref, near, middle_long, far_long)):
+
+        @pl.when(me ^ distance == last_owner())
+        def _():
+            placed_ref[count - 1] = long_ref[rows:]
+
     once = [place_ref[:, head_cols(count + head)] for head in heads]
     attn_parts = [
         contract(placed_ref[head, 3 * picked : 4 * picked], once[head][:, :picked], 0, 1)
         for head in heads
     ]
     log_parts = [
-        contract(placed_ref[head, 6 * picked : 6 * picked + STAT_TILES], once[head], 1, 1)
+        contract(placed_ref[head, 4 * picked : 4 * picked + STAT_TILES], once[head], 1, 1)
         for head in heads
     ]
     factors, normeds, grad_lows, inners = [], [], [], []
@@ -649,17 +664,30 @@
         attended_ref[:, cols] = (normeds[head].T * gain_ref[:, cols]).astype(LOW)
 
 
-def finish_kernel(top_step, *refs):
-    gain_refs, (q_ref, k_ref, place_ref), refs = refs[:2], refs[2:5], refs[5:]
-    mixed_refs, (last_attended_ref, last_dq_ref, last_dk_ref, last_dv_ref) = refs[:5], refs[5:9]
-    return_refs, refs = nearest_first(refs[9 : 9 + SPAN]), refs[9 + SPAN :]
-    mixed_ref, grad_low_ref, soft_ref, score_grad_ref, returned_ref = mixed_refs
-    attended_ref, dq_ref, dk_ref, dv_ref, gain_out_ref = refs
+def finish_kernel(
+    top_step,
+    gain_ref,
+    gain_rest_ref,
+    q_ref,
+    k_ref,
+    place_ref,
+    mixed_ref,
+    grad_low_ref,
+    soft_ref,
+    score_grad_ref,
+    returned_ref,
+    attended_ref,
+    dq_ref,
+    dk_ref,
+    dv_ref,
+    gain_out_ref,
+):
     tokens, width = q_ref.shape[1:]
     picked = sum(picked_counts(tokens, top_step))
-    heads = range(OWNED)
+    heads = range(width // HEAD_DIM)
     every = [head_cols(head) for head in heads]
-    gain_out_ref[...] = (gain_refs[0][...] + gain_refs[1][...]).reshape(gain_out_ref.shape)
+    gain_out_ref[...] = (gain_ref[...] + gain_rest_ref[...]).reshape(gain_out_ref.shape)
+    attended_ref[0] = mixed_ref[...]
     score_grads = [score_grad_ref[:, cols] for cols in every]
     dqs = [contract(score_grads[head], k_ref[0, :, every[head]], 0, 0) for head in heads]
     placed = [
@@ -675,27 +703,12 @@
     ]
     dks = [contract(score_grads[head], q_ref[0, :, every[head]], 1, 0) for head in heads]
     dvs = [contract(soft_ref[:, cols], grad_low_ref[:, cols], 1, 1) for cols in every]
-    last = width // HEAD_DIM - 1
-    total = sum(ref[4 * picked : 6 * picked].astype(WIDE) for ref in return_refs[1:]).astype(LOW)
-    rows = contract(
-        place_ref[:, pl.ds(last * HEAD_DIM, picked)],
-        jnp.concatenate([total[:picked], total[picked:]], 1),
-        1,
-        0,
-    )
     for head in heads:
-        cols = every[head]
-        attended_ref[0, :, cols] = mixed_ref[:, cols]
         for which, (block, out_block_ref) in enumerate(
             ((dqs[head], dq_ref), (dks[head], dk_ref), (dvs[head], dv_ref))
         ):
             part = placed[head][:, which * HEAD_DIM : (which + 1) * HEAD_DIM]
-            out_block_ref[0, :, cols] = (block + part).astype(LOW)
-    cols = head_cols(last)
-    attended_ref[0, :, cols] = last_attended_ref[...]
-    dq_ref[0, :, cols] = last_dq_ref[...]
-    dk_ref[0, :, cols] = (last_dk_ref[...] + rows[:, :HEAD_DIM]).astype(LOW)
-    dv_ref[0, :, cols] = (last_dv_ref[...] + rows[:, HEAD_DIM:]).astype(LOW)
+            out_block_ref[0, :, every[head]] = (block + part).astype(LOW)
 
 
 def across(block, axis, distance):
@@ -703,8 +716,26 @@
     return lax.ppermute(block, axis, route)
 
 
-def to_peers(blocks):
-    return [across(blocks[distance - 1], "ctx", distance) for distance in range(PEERS, 0, -1)]
+def across_some(block, distance, chosen):
+    route = []
+    for dp_place in range(lax.axis_size("dp")):
+        for place in range(SPAN):
+            if chosen(last_owner_of(dp_place), place, place ^ distance):
+                start = dp_place * SPAN
+                route.append((start + place, start + (place ^ distance)))
+    return lax.ppermute(block, ("dp", "ctx"), route)
+
+
+def to_peers(near, middle, far, takes_long):
+    def takes_short(*ends):
+        return not takes_long(*ends)
+
+    far_pair = [across_some(far[i], 3, rule) for i, rule in enumerate((takes_long, takes_short))]
+    near_block = across(near, "ctx", 1)
+    middle_pair = [
+        across_some(middle[i], 2, rule) for i, rule in enumerate((takes_long, takes_short))
+    ]
+    return [*far_pair, near_block, *middle_pair]
 
 
 def call(kernel, name, operands, results, microseconds, vmem=PLAIN_VMEM, scratch=()):
@@ -730,23 +761,26 @@
     shape = jax.ShapeDtypeStruct
     row_block = shape((1, tokens, width), LOW)
     low_block, wide_block = shape((tokens, width), LOW), shape((tokens, width), WIDE)
-    low_head, wide_head = shape((tokens, HEAD_DIM), LOW), shape((tokens, HEAD_DIM), WIDE)
+
     gain_block = shape((1, width), WIDE)
     stats_block = shape((2 * TILE, tokens), WIDE)
-    payload = shape((7 * picked + STAT_TILES, HEAD_DIM), LOW)
-    answer = shape((6 * picked + STAT_TILES, HEAD_DIM), LOW)
+    payload_rows, answer_rows = 5 * picked + STAT_TILES, 4 * picked + STAT_TILES
+    long_payload, payload = [shape((n * payload_rows, HEAD_DIM), LOW) for n in (2, 1)]
+    long_answer, answer = [shape((n * answer_rows, HEAD_DIM), LOW) for n in (2, 1)]
     bind = functools.partial
     gain_row = out_gain.reshape(1, width)
-    own, *sent, expo, base_out, stats = call(
+    own, near, middle, far, short_middle, short_far, expo, base_out, stats = call(
         bind(pack_kernel, top_step),
         "pack",
         (offsets, queries, keys, values, grad_y),
-        [payload] * SPAN + [low_block, low_block, stats_block],
+        [long_payload] * SPAN + [payload] * 2 + [low_block, low_block, stats_block],
         1,
         vmem=PACK_VMEM,
-        scratch=[pltpu.VMEM((OWNED, *payload.shape), LOW)],
-    )
-    received = to_peers(sent)
+        scratch=[pltpu.VMEM((heads, *payload.shape), LOW)],
+    )
+    received = to_peers(
+        near, (middle, short_middle), (far, short_far), lambda owner, source, target: target == owner
+    )
     grad_norm, gain_base, place = call(
         bind(prepare_kernel, top_step),
         "prepare",
@@ -754,30 +788,19 @@
         [wide_block, gain_block, shape((tokens, 2 * width), LOW)],
         2,
     )
-    normed, grad_low, score_grad, kept, own_answer, *answers = call(
+    own, near, middle, far, short_middle, short_far = call(
         bind(owner_kernel, top_step),
         "owner",
-        (offsets, queries, gain_row, base_out, grad_norm, stats, gain_base, own, *received),
-        [
-            wide_head,
-            low_head,
-            shape((PEERS * picked, HEAD_DIM), LOW),
-            shape((TILE, tokens), WIDE),
-        ]
-        + [answer] * SPAN,
+        (offsets, gain_row, gain_base, own, *received),
+        [long_answer] * SPAN + [answer] * 2,
         3,
-    )
-    returned = to_peers(answers)
-    last_results = call(
-        bind(last_head_kernel, top_step),
-        "last_head",
-        (queries, keys, values, gain_row, expo, normed, grad_low, score_grad, kept, *received),
-        [low_head, low_head, wide_head, wide_head],
-        20,
-    )
-    (gain_sum,) = call(bind(gain_kernel, picked), "gain", (own_answer, *returned), [gain_block], 1)
+        scratch=[pltpu.VMEM(payload.shape, LOW)] * 2,
+    )
+    returned = to_peers(
+        near, (middle, short_middle), (far, short_far), lambda owner, source, target: source == owner
+    )
+    (gain_sum,) = call(bind(gain_kernel, picked), "gain", (own, *returned), [gain_block], 1)
     gain_rest = across(gain_sum, "dp", 1)
-    mixed_block = shape((tokens, OWNED * HEAD_DIM), LOW)
     mixed = call(
         bind(mix_kernel, top_step),
         "mix",
@@ -790,10 +813,10 @@
             grad_norm,
             stats,
             place,
-            own_answer,
+            own,
             *returned,
         ),
-        [mixed_block] * 4 + [shape((OWNED, *answer.shape), LOW)],
+        [low_block] * 4 + [shape((heads, *answer.shape), LOW)],
         20,
     )
     attended, query_grad, key_grad, value_grad, gain_grad = call(
@@ -806,9 +829,6 @@
             keys,
             place,
             *mixed,
-            *last_results,
-            own_answer,
-            *returned,
         ),
         [row_block] * 4 + [shape((width,), WIDE)],
         1,

time: 29.5 us -> 42.1 us (1.43)
  starting transfers between devices: 10.3 us -> 24.8 us
  waiting for transfers between devices: 8.1 us -> 4.87 us
  local copies, waits for them, and re-layouts: 2.55 us -> 3.46 us
    ppermute x0 -> x8, starting transfers between devices: none -> 18 us  [across_some(): return lax.ppermute(block, ('dp', 'ctx'), route)]
    ppermute x7 -> x3, waiting for transfers between devices: 8.1 us -> 0.01 us  [across(): return lax.ppermute(block, axis, route)]
    ppermute x0 -> x8, waiting for transfers between devices: none -> 4.87 us  [across_some(): return lax.ppermute(block, ('dp', 'ctx'), route)]
    ppermute x7 -> x3, starting transfers between devices: 10.3 us -> 6.75 us  [across(): return lax.ppermute(block, axis, route)]
    unnamed x22, local copies, waits for them, and re-layouts: 2.55 us -> 3.46 us
    pallas_call x7 -> x6, Pallas kernels: 7.67 us -> 7.79 us  [call(): pl.pallas_call(kernel, out_shape=results, in_specs=[SMEM_SPEC if block.dt...]
  transfers between devices with their start and end apart: 7 -> 11, of which waited for: 3 -> 3; matrix products, arithmetic and copies ran while one was open for 0% -> 0% of each run, Pallas kernels for 8% -> 5%
where the time goes in v14:
time: 42.1 us; the launch traced here: 41.7 us
  starting transfers between devices  24.8 us (59%)
  Pallas kernels  7.79 us (19%)
  waiting for transfers between devices  4.87 us (12%)
  local copies, waits for them, and re-layouts  3.46 us (8%)
  between operations  0.83 us (2%)
    ppermute x8, starting transfers between devices, across_some(): return lax.ppermute(block, ('dp', 'ctx'), route)  18 us
    pallas_call x6, Pallas kernels, call(): pl.pallas_call(kernel, out_shape=results, in_specs=[SMEM_SPEC if block.dt...  7.79 us
    ppermute x3, starting transfers between devices, across(): return lax.ppermute(block, axis, route)  6.75 us
    ppermute x8, waiting for transfers between devices, across_some(): return lax.ppermute(block, ('dp', 'ctx'), route)  4.87 us
    unnamed x22, local copies, waits for them, and re-layouts  3.46 us
  transfers between devices with their start and end apart: 11, of which 3 were waited for; matrix products, arithmetic and copies ran while one was open for 0% of the time, Pallas kernels for 5%

profile of v14, /device:TPU:0, one launch (start us, length us, event | category | flops | bytes accessed | tf_op | source)
XLA Modules:
  0.0 41.7 jit_solution(1668523396381120109)
XLA Ops:
  0.6 2.7 %pack.1 = (bf16[512,128]{1,0:T(8,128)(2,1)}, bf16[512,128]{1,0:T(8,128)(2,1)}, bf16[512,128]{1,0:T(8,128)(2,1)}, bf16[512,128]{1,0:T(8,128)(2,1)}, bf16[256,128]...) custom-call(s32[2,5]{1,0:T(2,128)} %offsets_ref.7, ...), custom_call_target="tpu_custom_call" | custom-call | flops 1000000000 | tf_op jit(solution)/shard_map/pack/pallas_call | solution.py:742
  3.4 0.7 %collective-permute-start = (bf16[512,128]{1,0:T(8,128)(2,1)}, bf16[512,128]{1,0:T(8,128)(2,1)S(1)}, u32[]{:S(2)}, u32[]{:S(2)}) collective-permute-start(bf16[512,128]{1,0:T(8,128)(2,1)} %get-tuple-element.31), channel_id=1, source_target_pairs={{8,4},{20,24},{9,5},{21,25},{10,6},{22,26},{11,7},{23,27}} | collective-permute-start | bytes 393224 | tf_op jit(solution)/shard_map/ppermute | solution.py:726
  4.1 3.7 %collective-permute-start.2 = (bf16[512,128]{1,0:T(8,128)(2,1)}, bf16[512,128]{1,0:T(8,128)(2,1)S(1)}, u32[]{:S(2)}, u32[]{:S(2)}) collective-permute-start(bf16[512,128]{1,0:T(8,128)(2,1)} %get-tuple-element.33), channel_id=1, source_target_pairs={{0,4},{4,0},{8,12},{12,8},{1,5},{5,1},{9,13},{13,9},{2,6},{6,2},{1... | collective-permute-start | bytes 393224 | tf_op jit(solution)/shard_map/ppermute | solution.py:716
  7.8 0.7 %collective-permute-start.3 = (bf16[512,128]{1,0:T(8,128)(2,1)}, bf16[512,128]{1,0:T(8,128)(2,1)S(1)}, u32[]{:S(2)}, u32[]{:S(2)}) collective-permute-start(bf16[512,128]{1,0:T(8,128)(2,1)} %get-tuple-element.34), channel_id=1, source_target_pairs={{12,4},{16,24},{13,5},{17,25},{14,6},{18,26},{15,7},{19,27}} | collective-permute-start | bytes 393224 | tf_op jit(solution)/shard_map/ppermute | solution.py:726
  8.4 6.1 %collective-permute-start.1 = (bf16[256,128]{1,0:T(8,128)(2,1)}, bf16[256,128]{1,0:T(8,128)(2,1)S(1)}, u32[]{:S(2)}, u32[]{:S(2)}) collective-permute-start(bf16[256,128]{1,0:T(8,128)(2,1)} %get-tuple-element.32), channel_id=1, source_target_pairs={{0,12},{4,8},{12,0},{16,28},{24,20},{28,16},{1,13},{5,9},{13,1},{1... | collective-permute-start | bytes 196616 | tf_op jit(solution)/shard_map/ppermute | solution.py:726
  14.5 1.9 %collective-permute-start.4 = (bf16[256,128]{1,0:T(8,128)(2,1)}, bf16[256,128]{1,0:T(8,128)(2,1)S(1)}, u32[]{:S(2)}, u32[]{:S(2)}) collective-permute-start(bf16[256,128]{1,0:T(8,128)(2,1)} %get-tuple-element.35), channel_id=1, source_target_pairs={{0,8},{4,12},{8,0},{20,28},{24,16},{28,20},{1,9},{5,13},{9,1},{21,... | collective-permute-start | bytes 196616 | tf_op jit(solution)/shard_map/ppermute | solution.py:726
  16.5 0.0 copy-start.4
  16.5 0.7 %copy-done.4 = s32[2,5]{1,0:T(2,128)S(1)} copy-done((s32[2,5]{1,0:T(2,128)S(1)}, s32[2,5]{1,0:T(2,128)}, u32[]{:S(2)}) %copy-start.4) | copy-done | bytes 64
  17.1 0.9 %copy-done = bf16[1,128,640]{2,1,0:T(8,128)(2,1)S(1)} copy-done((bf16[1,128,640]{2,1,0:T(8,128)(2,1)S(1)}, bf16[1,128,640]{2,1,0:T(8,128)(2,1)}, u32[]{:S(2)}) %copy-start) | copy-done | bytes 163864
  18.1 0.9 %copy-done.6 = bf16[128,640]{1,0:T(8,128)(2,1)S(1)} copy-done((bf16[128,640]{1,0:T(8,128)(2,1)S(1)}, bf16[128,640]{1,0:T(8,128)(2,1)}, u32[]{:S(2)}) %copy-start.6) | copy-done | bytes 163864
  19.0 0.9 %prepare.1 = (f32[128,640]{1,0:T(8,128)S(1)}, f32[1,640]{1,0:T(1,128)S(1)}, bf16[128,1280]{1,0:T(8,128)(2,1)S(1)}) custom-call(s32[2,5]{1,0:T(2,128)S(1)} %copy-done.4, bf16[1,128,640]{2,1,0:T(8,128)(2,1)S(1)} %copy-done, f32[1,640]{1,0:T(1,128)S(1)} %reshape.13.gain_ref, bf16[128,640]{1,0:T(8,128)(2,1)S(1)} %copy-done.6), custom_call_target="tpu_custom_call" | custom-call | flops 2000000000 | tf_op jit(solution)/shard_map/prepare/pallas_call | solution.py:742
  19.9 0.0 collective-permute-done.1.refs_2_
  19.9 1.9 %collective-permute-done.4.refs_5_ = bf16[256,128]{1,0:T(8,128)(2,1)S(1)} collective-permute-done((bf16[256,128]{1,0:T(8,128)(2,1)}, bf16[256,128]{1,0:T(8,128)(2,1)S(1)}, u32[]{:S(2)}, u32[]{:S(2)}) %collective-permute-start.4) | collective-permute-done | bytes 65568 | tf_op jit(solution)/shard_map/ppermute | solution.py:726
  21.8 0.0 collective-permute-done.refs_1_
  21.8 1.7 %owner.1 = (bf16[416,128]{1,0:T(8,128)(2,1)S(1)}, bf16[416,128]{1,0:T(8,128)(2,1)S(1)}, bf16[416,128]{1,0:T(8,128)(2,1)S(1)}, bf16[416,128]{1,0:T(8,128)(2,1)S(1...) custom-call(s32[2,5]{1,0:T(2,128)S(1)} %copy-done.4, f32[1,640]{1,0:T(1,128)S(1)} %reshape.13.gain_ref, ...), custom_call_target="tpu_custom_call" | custom-call | flops 3000000000 | tf_op jit(solution)/shard_map/owner/pallas_call | solution.py:742
  23.5 0.7 %collective-permute-start.5 = (bf16[416,128]{1,0:T(8,128)(2,1)S(1)}, bf16[416,128]{1,0:T(8,128)(2,1)S(1)}, u32[]{:S(2)}, u32[]{:S(2)}) collective-permute-start(bf16[416,128]{1,0:T(8,128)(2,1)S(1)} %get-tuple-element.37), channel_id=1, source_target_pairs={{4,8},{24,20},{5,9},{25,21},{6,10},{26,22},{7,11},{27,23}} | collective-permute-start | bytes 319496 | tf_op jit(solution)/shard_map/ppermute | solution.py:726
  24.1 3.0 %collective-permute-start.7 = (bf16[416,128]{1,0:T(8,128)(2,1)S(1)}, bf16[416,128]{1,0:T(8,128)(2,1)S(1)}, u32[]{:S(2)}, u32[]{:S(2)}) collective-permute-start(bf16[416,128]{1,0:T(8,128)(2,1)S(1)} %get-tuple-element.39), channel_id=1, source_target_pairs={{0,4},{4,0},{8,12},{12,8},{1,5},{5,1},{9,13},{13,9},{2,6},{6,2},{1... | collective-permute-start | bytes 319496 | tf_op jit(solution)/shard_map/ppermute | solution.py:716
  27.1 0.7 %collective-permute-start.8 = (bf16[416,128]{1,0:T(8,128)(2,1)S(1)}, bf16[416,128]{1,0:T(8,128)(2,1)S(1)}, u32[]{:S(2)}, u32[]{:S(2)}) collective-permute-start(bf16[416,128]{1,0:T(8,128)(2,1)S(1)} %get-tuple-element.40), channel_id=1, source_target_pairs={{4,12},{24,16},{5,13},{25,17},{6,14},{26,18},{7,15},{27,19}} | collective-permute-start | bytes 319496 | tf_op jit(solution)/shard_map/ppermute | solution.py:726
  27.8 2.8 %collective-permute-start.6 = (bf16[208,128]{1,0:T(8,128)(2,1)S(1)}, bf16[208,128]{1,0:T(8,128)(2,1)S(1)}, u32[]{:S(2)}, u32[]{:S(2)}) collective-permute-start(bf16[208,128]{1,0:T(8,128)(2,1)S(1)} %get-tuple-element.38), channel_id=1, source_target_pairs={{0,12},{8,4},{12,0},{16,28},{20,24},{28,16},{1,13},{9,5},{13,1},{1... | collective-permute-start | bytes 159752 | tf_op jit(solution)/shard_map/ppermute | solution.py:726
  30.6 4.6 %collective-permute-start.9 = (bf16[208,128]{1,0:T(8,128)(2,1)S(1)}, bf16[208,128]{1,0:T(8,128)(2,1)S(1)}, u32[]{:S(2)}, u32[]{:S(2)}) collective-permute-start(bf16[208,128]{1,0:T(8,128)(2,1)S(1)} %get-tuple-element.41), channel_id=1, source_target_pairs={{0,8},{8,0},{12,4},{16,24},{20,28},{28,20},{1,9},{9,1},{13,5},{17,... | collective-permute-start | bytes 159752 | tf_op jit(solution)/shard_map/ppermute | solution.py:726
  35.2 0.6 %collective-permute-done.6.far_short.refs_5_ = bf16[208,128]{1,0:T(8,128)(2,1)S(1)} collective-permute-done((bf16[208,128]{1,0:T(8,128)(2,1)S(1)}, bf16[208,128]{1,0:T(8,128)(2,1)S(1)}, u32[]{:S(2)}, u32[]{:S(2)}) %collective-permute-start.6) | collective-permute-done | bytes 53280 | tf_op jit(solution)/shard_map/ppermute | solution.py:726
  35.7 2.4 %collective-permute-done.9.middle_short.refs_8_ = bf16[208,128]{1,0:T(8,128)(2,1)S(1)} collective-permute-done((bf16[208,128]{1,0:T(8,128)(2,1)S(1)}, bf16[208,128]{1,0:T(8,128)(2,1)S(1)}, u32[]{:S(2)}, u32[]{:S(2)}) %collective-permute-start.9) | collective-permute-done | bytes 53280 | tf_op jit(solution)/shard_map/ppermute | solution.py:726
  38.2 0.0 collective-permute-done.8.middle_long.refs_7_
  38.2 0.0 copy-start.1
  38.2 0.0 copy-start.5
  38.2 0.0 copy-start.7
  38.2 0.1 collective-permute-start.10
  38.3 0.8 %copy-done.1 = bf16[1,128,640]{2,1,0:T(8,128)(2,1)S(1)} copy-done((bf16[1,128,640]{2,1,0:T(8,128)(2,1)S(1)}, bf16[1,128,640]{2,1,0:T(8,128)(2,1)}, u32[]{:S(2)}) %copy-start.1) | copy-done | bytes 163864
  39.1 0.1 copy-done.5
  39.2 0.1 copy-done.7
  39.2 1.2 %mix.1 = (bf16[128,640]{1,0:T(8,128)(2,1)S(1)}, bf16[128,640]{1,0:T(8,128)(2,1)S(1)}, bf16[128,640]{1,0:T(8,128)(2,1)S(1)}, bf16[128,640]{1,0:T(8,128)(2,1)S(1)}, bf16[5,208,128]{2,1,0:T(8,128)(2,1)S(1)}) custom-call(s32[2,5]{1,0:T(2,128)S(1)} %copy-done.4, bf16[1,128,640]{2,1,0:T(8,128)(2,1)S(1)} %copy-done.1, f32[1,640]{1,0:T(1,128)S(1)} %reshape.13.gain_ref, ...), custom_call_target="tpu_custom_call" | custom-call | flops 20000000000 | tf_op jit(solution)/shard_map/mix/pallas_call | solution.py:742
  40.5 1.3 %finish.1 = (bf16[1,128,640]{2,1,0:T(8,128)(2,1)}, bf16[1,128,640]{2,1,0:T(8,128)(2,1)}, bf16[1,128,640]{2,1,0:T(8,128)(2,1)}, bf16[1,128,640]{2,1,0:T(8,128)(2,1)}, f32[640]{0:T(1024)}) custom-call(f32[1,640]{1,0:T(1,128)S(1)} %gain.1.gain_ref, f32[1,640]{1,0:T(1,128)S(1)} %collective-permute-done.10.gain_rest_ref, bf16[1,128,640]{2,1,0:T(8,128)(2,1)S(1)} %copy-done.2, ...), custom_call_target="tpu_custom_call" | custom-call | flops 1000000000 | tf_op jit(solution)/shard_map/finish/pallas_call | solution.py:742
  (19 shorter events, 0.1 us)
Async XLA Ops:
  3.4 13.1 %copy-start.10 = (f32[640]{0:T(1024)S(1)}, f32[640]{0:T(1024)}, u32[]{:S(2)}) copy-start(f32[640]{0:T(1024)} %param.10) | copy-start | bytes 7684
  3.4 18.4 %collective-permute-start = (bf16[512,128]{1,0:T(8,128)(2,1)}, bf16[512,128]{1,0:T(8,128)(2,1)S(1)}, u32[]{:S(2)}, u32[]{:S(2)}) collective-permute-start(bf16[512,128]{1,0:T(8,128)(2,1)} %get-tuple-element.31), channel_id=1, source_target_pairs={{8,4},{20,24},{9,5},{21,25},{10,6},{22,26},{11,7},{23,27}} | collective-permute-start | bytes 393224 | tf_op jit(solution)/shard_map/ppermute | solution.py:726
  4.1 17.7 %collective-permute-start.2 = (bf16[512,128]{1,0:T(8,128)(2,1)}, bf16[512,128]{1,0:T(8,128)(2,1)S(1)}, u32[]{:S(2)}, u32[]{:S(2)}) collective-permute-start(bf16[512,128]{1,0:T(8,128)(2,1)} %get-tuple-element.33), channel_id=1, source_target_pairs={{0,4},{4,0},{8,12},{12,8},{1,5},{5,1},{9,13},{13,9},{2,6},{6,2},{1... | collective-permute-start | bytes 393224 | tf_op jit(solution)/shard_map/ppermute | solution.py:716
  7.8 14.0 %collective-permute-start.3 = (bf16[512,128]{1,0:T(8,128)(2,1)}, bf16[512,128]{1,0:T(8,128)(2,1)S(1)}, u32[]{:S(2)}, u32[]{:S(2)}) collective-permute-start(bf16[512,128]{1,0:T(8,128)(2,1)} %get-tuple-element.34), channel_id=1, source_target_pairs={{12,4},{16,24},{13,5},{17,25},{14,6},{18,26},{15,7},{19,27}} | collective-permute-start | bytes 393224 | tf_op jit(solution)/shard_map/ppermute | solution.py:726
  8.4 11.5 %collective-permute-start.1 = (bf16[256,128]{1,0:T(8,128)(2,1)}, bf16[256,128]{1,0:T(8,128)(2,1)S(1)}, u32[]{:S(2)}, u32[]{:S(2)}) collective-permute-start(bf16[256,128]{1,0:T(8,128)(2,1)} %get-tuple-element.32), channel_id=1, source_target_pairs={{0,12},{4,8},{12,0},{16,28},{24,20},{28,16},{1,13},{5,9},{13,1},{1... | collective-permute-start | bytes 196616 | tf_op jit(solution)/shard_map/ppermute | solution.py:726
  14.5 7.3 %collective-permute-start.4 = (bf16[256,128]{1,0:T(8,128)(2,1)}, bf16[256,128]{1,0:T(8,128)(2,1)S(1)}, u32[]{:S(2)}, u32[]{:S(2)}) collective-permute-start(bf16[256,128]{1,0:T(8,128)(2,1)} %get-tuple-element.35), channel_id=1, source_target_pairs={{0,8},{4,12},{8,0},{20,28},{24,16},{28,20},{1,9},{5,13},{9,1},{21,... | collective-permute-start | bytes 196616 | tf_op jit(solution)/shard_map/ppermute | solution.py:726
  16.5 0.7 %copy-start.4 = (s32[2,5]{1,0:T(2,128)S(1)}, s32[2,5]{1,0:T(2,128)}, u32[]{:S(2)}) copy-start(s32[2,5]{1,0:T(2,128)} %offsets_ref.7) | copy-start | bytes 124
  17.1 0.9 %copy-start = (bf16[1,128,640]{2,1,0:T(8,128)(2,1)S(1)}, bf16[1,128,640]{2,1,0:T(8,128)(2,1)}, u32[]{:S(2)}) copy-start(bf16[1,128,640]{2,1,0:T(8,128)(2,1)} %grad_ref.3) | copy-start | bytes 491524
  18.1 0.9 %copy-start.6 = (bf16[128,640]{1,0:T(8,128)(2,1)S(1)}, bf16[128,640]{1,0:T(8,128)(2,1)}, u32[]{:S(2)}) copy-start(bf16[128,640]{1,0:T(8,128)(2,1)} %get-tuple-element.28.out_ref) | copy-start | bytes 491524
  19.0 2.8 %copy-start.8 = (bf16[512,128]{1,0:T(8,128)(2,1)S(1)}, bf16[512,128]{1,0:T(8,128)(2,1)}, u32[]{:S(2)}) copy-start(bf16[512,128]{1,0:T(8,128)(2,1)} %get-tuple-element.30.refs_0_) | copy-start | bytes 393220
  23.5 14.7 %collective-permute-start.5 = (bf16[416,128]{1,0:T(8,128)(2,1)S(1)}, bf16[416,128]{1,0:T(8,128)(2,1)S(1)}, u32[]{:S(2)}, u32[]{:S(2)}) collective-permute-start(bf16[416,128]{1,0:T(8,128)(2,1)S(1)} %get-tuple-element.37), channel_id=1, source_target_pairs={{4,8},{24,20},{5,9},{25,21},{6,10},{26,22},{7,11},{27,23}} | collective-permute-start | bytes 319496 | tf_op jit(solution)/shard_map/ppermute | solution.py:726
  24.1 14.0 %collective-permute-start.7 = (bf16[416,128]{1,0:T(8,128)(2,1)S(1)}, bf16[416,128]{1,0:T(8,128)(2,1)S(1)}, u32[]{:S(2)}, u32[]{:S(2)}) collective-permute-start(bf16[416,128]{1,0:T(8,128)(2,1)S(1)} %get-tuple-element.39), channel_id=1, source_target_pairs={{0,4},{4,0},{8,12},{12,8},{1,5},{5,1},{9,13},{13,9},{2,6},{6,2},{1... | collective-permute-start | bytes 319496 | tf_op jit(solution)/shard_map/ppermute | solution.py:716
  27.1 11.0 %collective-permute-start.8 = (bf16[416,128]{1,0:T(8,128)(2,1)S(1)}, bf16[416,128]{1,0:T(8,128)(2,1)S(1)}, u32[]{:S(2)}, u32[]{:S(2)}) collective-permute-start(bf16[416,128]{1,0:T(8,128)(2,1)S(1)} %get-tuple-element.40), channel_id=1, source_target_pairs={{4,12},{24,16},{5,13},{25,17},{6,14},{26,18},{7,15},{27,19}} | collective-permute-start | bytes 319496 | tf_op jit(solution)/shard_map/ppermute | solution.py:726
  27.8 7.9 %collective-permute-start.6 = (bf16[208,128]{1,0:T(8,128)(2,1)S(1)}, bf16[208,128]{1,0:T(8,128)(2,1)S(1)}, u32[]{:S(2)}, u32[]{:S(2)}) collective-permute-start(bf16[208,128]{1,0:T(8,128)(2,1)S(1)} %get-tuple-element.38), channel_id=1, source_target_pairs={{0,12},{8,4},{12,0},{16,28},{20,24},{28,16},{1,13},{9,5},{13,1},{1... | collective-permute-start | bytes 159752 | tf_op jit(solution)/shard_map/ppermute | solution.py:726
  30.6 7.6 %collective-permute-start.9 = (bf16[208,128]{1,0:T(8,128)(2,1)S(1)}, bf16[208,128]{1,0:T(8,128)(2,1)S(1)}, u32[]{:S(2)}, u32[]{:S(2)}) collective-permute-start(bf16[208,128]{1,0:T(8,128)(2,1)S(1)} %get-tuple-element.41), channel_id=1, source_target_pairs={{0,8},{8,0},{12,4},{16,24},{20,28},{28,20},{1,9},{9,1},{13,5},{17,... | collective-permute-start | bytes 159752 | tf_op jit(solution)/shard_map/ppermute | solution.py:726
  38.2 0.9 %copy-start.1 = (bf16[1,128,640]{2,1,0:T(8,128)(2,1)S(1)}, bf16[1,128,640]{2,1,0:T(8,128)(2,1)}, u32[]{:S(2)}) copy-start(bf16[1,128,640]{2,1,0:T(8,128)(2,1)} %v_ref.3) | copy-start | bytes 491524
  38.2 1.0 %copy-start.5 = (bf16[128,640]{1,0:T(8,128)(2,1)S(1)}, bf16[128,640]{1,0:T(8,128)(2,1)}, u32[]{:S(2)}) copy-start(bf16[128,640]{1,0:T(8,128)(2,1)} %get-tuple-element.43.expo_ref) | copy-start | bytes 491524
  38.2 1.1 %copy-start.7 = (bf16[128,640]{1,0:T(8,128)(2,1)S(1)}, bf16[128,640]{1,0:T(8,128)(2,1)}, u32[]{:S(2)}) copy-start(bf16[128,640]{1,0:T(8,128)(2,1)} %get-tuple-element.28.out_ref) | copy-start | bytes 491524
  38.2 1.0 %copy-start.9 = (f32[16,128]{1,0:T(8,128)S(1)}, f32[16,128]{1,0:T(8,128)}, u32[]{:S(2)}) copy-start(f32[16,128]{1,0:T(8,128)} %get-tuple-element.45.refs_1_) | copy-start | bytes 24580
  38.2 2.2 %collective-permute-start.10 = (f32[1,640]{1,0:T(1,128)S(1)}, f32[1,640]{1,0:T(1,128)S(1)}, u32[]{:S(2)}, u32[]{:S(2)}) collective-permute-start(f32[1,640]{1,0:T(1,128)S(1)} %gain.1.gain_ref), channel_id=1, source_target_pairs={{0,16},{16,0},{1,17},{17,1},{2,18},{18,2},{3,19},{19,3},{4,20},{20... | collective-permute-start | bytes 7688 | tf_op jit(solution)/shard_map/ppermute | solution.py:716
  39.2 1.2 %copy-start.2 = (bf16[1,128,640]{2,1,0:T(8,128)(2,1)S(1)}, bf16[1,128,640]{2,1,0:T(8,128)(2,1)}, u32[]{:S(2)}) copy-start(bf16[1,128,640]{2,1,0:T(8,128)(2,1)} %q_ref.3) | copy-start | bytes 491524
  39.2 1.2 %copy-start.3 = (bf16[1,128,640]{2,1,0:T(8,128)(2,1)S(1)}, bf16[1,128,640]{2,1,0:T(8,128)(2,1)}, u32[]{:S(2)}) copy-start(bf16[1,128,640]{2,1,0:T(8,128)(2,1)} %k_ref.3) | copy-start | bytes 491524

commit v15 on v12

--- a/solution.py
+++ b/solution.py
@@ -386,13 +386,30 @@
 
 
 def prepare_kernel(top_step, offsets_ref, grad_ref, gain_ref, out_ref, *refs):
-    grad_norm_ref, gain_part_ref, place_ref = refs
+    grad_norm_ref, gain_part_ref, place_ref, masks_ref = refs
     tokens, width = grad_ref.shape[1:]
     heads = range(width // HEAD_DIM)
     top_rows = tokens // top_step
     ones = jnp.ones((TILE, tokens), LOW)
     column = lax.broadcasted_iota(jnp.int32, (tokens, tokens), 1)
     gain_part_ref[...] = jnp.zeros(gain_part_ref.shape, WIDE)
+    me = lax.axis_index("ctx")
+    mid_rows = tokens // R1
+    top_all, queries = SPAN * top_rows, SPAN * (top_rows + mid_rows)
+    mid_offset, top_offset = offsets_ref[0, me], offsets_ref[1, me]
+    lane = lax.broadcasted_iota(jnp.int32, (1, queries), 1)
+    is_top = jnp.where(lane < top_all, 1.0, 0.0)
+    top_in_mid = jnp.where(((lane % top_rows) * top_step + top_offset) % R1 == mid_offset, 1.0, 0.0)
+    both_flag = jnp.where(mid_offset % top_step == top_offset, 1.0, 0.0)
+    sees_top = is_top + (1.0 - is_top) * both_flag
+    sees_mid = is_top * top_in_mid + (1.0 - is_top)
+    masks_ref[0:1, :queries] = (1.0 - sees_top) * NEVER
+    masks_ref[1:2, :queries] = (1.0 - sees_mid) * NEVER
+    masks_ref[2:3, :queries] = is_top + (1.0 - is_top) * (1.0 - both_flag)
+    last = len(heads) - 1
+    for row, (level, step) in enumerate(((1, top_step), (0, R1))):
+        hits = hit_row(offsets_ref[level, last], step, tokens)
+        masks_ref[3 + row : 4 + row, :tokens] = (1.0 - hits) * NEVER
     grad_norms = [
         (grad_ref[0, :, head_cols(head)].astype(WIDE) * gain_ref[:, head_cols(head)]).T
         for head in heads
@@ -408,6 +425,7 @@
         seen = jnp.maximum(
             hit_row(top_offset, top_step, tokens), hit_row(mid_offset, R1, tokens)
         )
+        masks_ref[TILE + head : TILE + head + 1, :tokens] = seen
         attn = out_ref[:, cols].astype(WIDE)
         normed = attn * lax.rsqrt(column_mean(attn * attn) + EPS)
         product = grad_norms[head] * normed * (1.0 - seen)
@@ -418,9 +436,9 @@
         place_ref[:, head_cols(len(heads) + head)] = picks * kept
 
 
-def owner_kernel(top_step, offsets_ref, q_ref, gain_ref, out_ref, grad_norm_ref, *refs):
-    stats_ref, gain_base_ref = refs[:2]
-    payload_refs, refs = nearest_first(refs[2 : 2 + SPAN]), refs[2 + SPAN :]
+def owner_kernel(top_step, q_ref, gain_ref, out_ref, grad_norm_ref, *refs):
+    stats_ref, gain_base_ref, masks_ref = refs[:3]
+    payload_refs, refs = nearest_first(refs[3 : 3 + SPAN]), refs[3 + SPAN :]
     normed_ref, grad_low_ref, score_grad_ref, kept_ref = refs[:4]
     return_refs = refs[4:]
     tokens = q_ref.shape[1]
@@ -467,15 +485,9 @@
     gain_row = jnp.zeros((1, HEAD_DIM), WIDE)
     for head in range(OWNED):
         gain_row = gain_row + jnp.where(me == head, 1.0, 0.0) * gain_ref[:, head_cols(head)]
-    mid_offset, top_offset = offsets_ref[0, me], offsets_ref[1, me]
-    both = mid_offset % top_step == top_offset
     lane = lax.broadcasted_iota(jnp.int32, (1, queries), 1)
     is_top = jnp.where(lane < top_all, 1.0, 0.0)
-    top_in_mid = jnp.where(((lane % top_rows) * top_step + top_offset) % R1 == mid_offset, 1.0, 0.0)
-    both_flag = jnp.where(both, 1.0, 0.0)
-    sees_top = is_top + (1.0 - is_top) * both_flag
-    sees_mid = is_top * top_in_mid + (1.0 - is_top)
-    bias = per_level((1.0 - sees_top) * NEVER, (1.0 - sees_mid) * NEVER)
+    bias = per_level(masks_ref[0:1, :queries], masks_ref[1:2, :queries])
     last = heads - 1
     cols = head_cols(last)
     peers = payload_refs[1:]
@@ -483,11 +495,8 @@
     k_peers = jnp.concatenate([ref[5 * picked : 6 * picked] for ref in peers], 0)
     v_peers = jnp.concatenate([ref[6 * picked : 7 * picked] for ref in peers], 0)
     last_biases = [
-        jnp.broadcast_to((1.0 - hit_row(offsets_ref[level, last], step, tokens)) * NEVER, shape)
-        for level, step, shape in (
-            (1, top_step, (top_rows, tokens)),
-            (0, R1, (mid_rows, tokens)),
-        )
+        jnp.broadcast_to(masks_ref[row : row + 1, :tokens], (count, tokens))
+        for row, count in ((3, top_rows), (4, mid_rows))
     ]
     scores = contract(k_rows, q_rows, 1, 1) * score_scale + bias
     scores_last = contract(k_peers, q_last, 1, 1) * score_scale + jnp.concatenate(
@@ -539,7 +548,7 @@
     attn_parts = [attn_rows[span] for span in spans]
     log_total = top_score + jnp.log(total)
     padding = jnp.zeros((1, top_all - mid_all), WIDE)
-    once = is_top + (1.0 - is_top) * (1.0 - both_flag)
+    once = masks_ref[2:3, :queries]
     ones_all = jnp.ones((TILE, queries), LOW)
     own_gain = gain_row_of(ones_all, product * once) / gain_row
     gain_rows = [
@@ -604,9 +613,9 @@
         gain_ref[:, head_cols(head)] = total[head : head + 1]
 
 
-def mix_kernel(top_step, offsets_ref, v_ref, gain_ref, expo_ref, out_ref, *refs):
-    grad_norm_ref, stats_ref, place_ref = refs[:3]
-    return_refs, refs = nearest_first(refs[3 : 3 + SPAN]), refs[3 + SPAN :]
+def mix_kernel(top_step, v_ref, gain_ref, expo_ref, out_ref, *refs):
+    grad_norm_ref, stats_ref, place_ref, masks_ref = refs[:4]
+    return_refs, refs = nearest_first(refs[4 : 4 + SPAN]), refs[4 + SPAN :]
     attended_ref, grad_low_ref, soft_ref, score_grad_ref, placed_ref = refs
     tokens, width = v_ref.shape[1:]
     count = width // HEAD_DIM
@@ -628,9 +637,7 @@
     ]
     factors, normeds, grad_lows, inners = [], [], [], []
     for head in heads:
-        top_hit = hit_row(offsets_ref[1, head], top_step, tokens)
-        mid_hit = hit_row(offsets_ref[0, head], R1, tokens)
-        seen = jnp.maximum(top_hit, mid_hit) > 0.5
+        seen = masks_ref[TILE + head : TILE + head + 1, :tokens] > 0.5
         top_score, total = stats_ref[head : head + 1, :], stats_ref[TILE + head : TILE + head + 1, :]
         log_total = jnp.where(seen, joined_row(log_parts[head], 0), top_score + jnp.log(total))
         factors.append(jnp.exp(top_score - log_total))
@@ -749,17 +756,22 @@
         scratch=[pltpu.VMEM((OWNED, *payload.shape), LOW)],
     )
     received = to_peers(sent)
-    grad_norm, gain_base, place = call(
+    grad_norm, gain_base, place, masks = call(
         bind(prepare_kernel, top_step),
         "prepare",
         (offsets, grad_y, gain_row, base_out),
-        [wide_block, gain_block, shape((tokens, 2 * width), LOW)],
+        [
+            wide_block,
+            gain_block,
+            shape((tokens, 2 * width), LOW),
+            shape((2 * TILE, 2 * tokens), WIDE),
+        ],
         2,
     )
     normed, grad_low, score_grad, kept, own_answer, *answers = call(
         bind(owner_kernel, top_step),
         "owner",
-        (offsets, queries, gain_row, base_out, grad_norm, stats, gain_base, own, *received),
+        (queries, gain_row, base_out, grad_norm, stats, gain_base, masks, own, *received),
         [
             wide_head,
             low_head,
@@ -784,7 +796,6 @@
         bind(mix_kernel, top_step),
         "mix",
         (
-            offsets,
             values,
             gain_row,
             expo,
@@ -792,6 +803,7 @@
             grad_norm,
             stats,
             place,
+            masks,
             own_answer,
             *returned,
         ),

time: 28.6 us -> 28.1 us (0.983)
  Pallas kernels: 7.68 us -> 6.57 us
  waiting for transfers between devices: 7.21 us -> 7.75 us
    pallas_call x7, Pallas kernels: 7.68 us -> 6.57 us  [call(): pl.pallas_call(kernel, out_shape=results, in_specs=[SMEM_SPEC if block.dt...]
    ppermute x7, waiting for transfers between devices: 7.21 us -> 7.75 us  [across(): return lax.ppermute(block, axis, route)]
  transfers between devices with their start and end apart: 7 -> 7, of which waited for: 5 -> 6; matrix products, arithmetic and copies ran while one was open for 0% -> 0% of each run, Pallas kernels for 8% -> 6%
where the time goes in v15:
time: 28.1 us; the launch traced here: 27.9 us
  starting transfers between devices  10.3 us (37%)
  waiting for transfers between devices  7.75 us (28%)
  Pallas kernels  6.57 us (23%)
  local copies, waits for them, and re-layouts  2.55 us (9%)
  between operations  0.72 us (3%)
    ppermute x7, starting transfers between devices, across(): return lax.ppermute(block, axis, route)  10.3 us
    ppermute x7, waiting for transfers between devices, across(): return lax.ppermute(block, axis, route)  7.75 us
    pallas_call x7, Pallas kernels, call(): pl.pallas_call(kernel, out_shape=results, in_specs=[SMEM_SPEC if block.dt...  6.57 us
    unnamed x22, local copies, waits for them, and re-layouts  2.55 us
  transfers between devices with their start and end apart: 7, of which 6 were waited for; matrix products, arithmetic and copies ran while one was open for 0% of the time, Pallas kernels for 6%

profile of v15, /device:TPU:0, one launch (start us, length us, event | category | flops | bytes accessed | tf_op | source)
XLA Modules:
  0.0 27.9 jit_solution(10014652400356447114)
XLA Ops:
  0.6 2.6 %pack.1 = (bf16[352,128]{1,0:T(8,128)(2,1)}, bf16[352,128]{1,0:T(8,128)(2,1)}, bf16[352,128]{1,0:T(8,128)(2,1)}, bf16[352,128]{1,0:T(8,128)(2,1)}, bf16[128,640]...) custom-call(s32[2,5]{1,0:T(2,128)} %offsets_ref.3, bf16[1,128,640]{2,1,0:T(8,128)(2,1)} %refs_2_.1, ...), custom_call_target="tpu_custom_call" | custom-call | flops 1000000000 | tf_op jit(solution)/shard_map/pack/pallas_call | solution.py:720
  3.2 5.1 %collective-permute-start = (bf16[352,128]{1,0:T(8,128)(2,1)}, bf16[352,128]{1,0:T(8,128)(2,1)S(1)}, u32[]{:S(2)}, u32[]{:S(2)}) collective-permute-start(bf16[352,128]{1,0:T(8,128)(2,1)} %get-tuple-element.39), channel_id=1, source_target_pairs={{0,12},{4,8},{8,4},{12,0},{1,13},{5,9},{9,5},{13,1},{2,14},{6,10},... | collective-permute-start | bytes 270344 | tf_op jit(solution)/shard_map/ppermute | solution.py:712
  8.3 0.0 collective-permute-start.1
  8.3 0.6 %collective-permute-start.2 = (bf16[352,128]{1,0:T(8,128)(2,1)}, bf16[352,128]{1,0:T(8,128)(2,1)S(1)}, u32[]{:S(2)}, u32[]{:S(2)}) collective-permute-start(bf16[352,128]{1,0:T(8,128)(2,1)} %get-tuple-element.41), channel_id=1, source_target_pairs={{0,8},{4,12},{8,0},{12,4},{1,9},{5,13},{9,1},{13,5},{2,10},{6,14},... | collective-permute-start | bytes 270344 | tf_op jit(solution)/shard_map/ppermute | solution.py:712
  9.0 0.0 copy-done.10
  9.0 0.7 %copy-done.4 = s32[2,5]{1,0:T(2,128)S(1)} copy-done((s32[2,5]{1,0:T(2,128)S(1)}, s32[2,5]{1,0:T(2,128)}, u32[]{:S(2)}) %copy-start.4) | copy-done | bytes 64
  9.7 0.9 %copy-done = bf16[1,128,640]{2,1,0:T(8,128)(2,1)S(1)} copy-done((bf16[1,128,640]{2,1,0:T(8,128)(2,1)S(1)}, bf16[1,128,640]{2,1,0:T(8,128)(2,1)}, u32[]{:S(2)}) %copy-start) | copy-done | bytes 163864
  10.6 0.9 %copy-done.6 = bf16[128,640]{1,0:T(8,128)(2,1)S(1)} copy-done((bf16[128,640]{1,0:T(8,128)(2,1)S(1)}, bf16[128,640]{1,0:T(8,128)(2,1)}, u32[]{:S(2)}) %copy-start.6) | copy-done | bytes 163864
  11.5 0.9 %prepare.1 = (f32[128,640]{1,0:T(8,128)S(1)}, f32[1,640]{1,0:T(1,128)S(1)}, bf16[128,1280]{1,0:T(8,128)(2,1)S(1)}, f32[16,256]{1,0:T(8,128)S(1)}) custom-call(s32[2,5]{1,0:T(2,128)S(1)} %copy-done.4, bf16[1,128,640]{2,1,0:T(8,128)(2,1)S(1)} %copy-done, f32[1,640]{1,0:T(1,128)S(1)} %reshape.13.gain_ref, bf16[128,640]{1,0:T(8,128)(2,1)S(1)} %copy-done.6), custom_call_target="tpu_custom_call" | custom-call | flops 2000000000 | tf_op jit(solution)/shard_map/prepare/pallas_call | solution.py:720
  12.4 0.0 collective-permute-done.refs_4_
  12.4 1.9 %collective-permute-done.1.refs_5_ = bf16[352,128]{1,0:T(8,128)(2,1)S(1)} collective-permute-done((bf16[352,128]{1,0:T(8,128)(2,1)}, bf16[352,128]{1,0:T(8,128)(2,1)S(1)}, u32[]{:S(2)}, u32[]{:S(2)}) %collective-permute-start.1) | collective-permute-done | bytes 90144 | tf_op jit(solution)/shard_map/ppermute | solution.py:712
  14.3 1.8 %collective-permute-done.2.refs_6_ = bf16[352,128]{1,0:T(8,128)(2,1)S(1)} collective-permute-done((bf16[352,128]{1,0:T(8,128)(2,1)}, bf16[352,128]{1,0:T(8,128)(2,1)S(1)}, u32[]{:S(2)}, u32[]{:S(2)}) %collective-permute-start.2) | collective-permute-done | bytes 90144 | tf_op jit(solution)/shard_map/ppermute | solution.py:712
  16.1 0.0 copy-done.2
  16.1 0.0 copy-done.7
  16.1 0.0 copy-done.8
  16.1 0.0 copy-done.9
  16.1 0.0 copy-start.1
  16.1 0.0 copy-start.3
  16.2 0.0 copy-start.5
  16.2 1.0 %owner.1 = (f32[128,128]{1,0:T(8,128)S(1)}, bf16[128,128]{1,0:T(8,128)(2,1)S(1)}, bf16[144,128]{1,0:T(8,128)(2,1)S(1)}, f32[8,128]{1,0:T(8,128)S(1)}, bf16[304,1...) custom-call(bf16[1,128,640]{2,1,0:T(8,128)(2,1)S(1)} %copy-done.2, ...), custom_call_target="tpu_custom_call" | custom-call | flops 3000000000 | tf_op jit(solution)/shard_map/owner/pallas_call | solution.py:720
  17.2 2.7 %collective-permute-start.3 = (bf16[304,128]{1,0:T(8,128)(2,1)S(1)}, bf16[304,128]{1,0:T(8,128)(2,1)S(1)}, u32[]{:S(2)}, u32[]{:S(2)}) collective-permute-start(bf16[304,128]{1,0:T(8,128)(2,1)S(1)} %get-tuple-element.43), channel_id=1, source_target_pairs={{0,12},{4,8},{8,4},{12,0},{1,13},{5,9},{9,5},{13,1},{2,14},{6,10},... | collective-permute-start | bytes 233480 | tf_op jit(solution)/shard_map/ppermute | solution.py:712
  19.9 0.0 collective-permute-start.4
  19.9 1.7 %collective-permute-start.5 = (bf16[304,128]{1,0:T(8,128)(2,1)S(1)}, bf16[304,128]{1,0:T(8,128)(2,1)S(1)}, u32[]{:S(2)}, u32[]{:S(2)}) collective-permute-start(bf16[304,128]{1,0:T(8,128)(2,1)S(1)} %get-tuple-element.45), channel_id=1, source_target_pairs={{0,8},{4,12},{8,0},{12,4},{1,9},{5,13},{9,1},{13,5},{2,10},{6,14},... | collective-permute-start | bytes 233480 | tf_op jit(solution)/shard_map/ppermute | solution.py:712
  21.6 0.0 copy-done.1
  21.6 0.3 %last_head.1 = (bf16[128,128]{1,0:T(8,128)(2,1)S(1)}, bf16[128,128]{1,0:T(8,128)(2,1)S(1)}, f32[128,128]{1,0:T(8,128)S(1)}, f32[128,128]{1,0:T(8,128)S(1)}) custom-call(bf16[1,128,640]{2,1,0:T(8,128)(2,1)S(1)} %copy-done.2, bf16[1,128,640]{2,1,0:T(8,128)(2,1)S(1)} %copy-done.3, bf16[1,128,640]{2,1,0:T(8,128)(2,1)S(1)} %copy-done.1, ...), custom_call_target="tpu_custom_call" | custom-call | flops 20000000000 | tf_op jit(solution)/shard_map/last_head/pallas_call | solution.py:720
  22.0 1.9 %collective-permute-done.3.refs_1_.refs_5_.refs_15_ = bf16[304,128]{1,0:T(8,128)(2,1)S(1)} collective-permute-done((bf16[304,128]{1,0:T(8,128)(2,1)S(1)}, bf16[304,128]{1,0:T(8,128)(2,1)S(1)}, u32[]{:S(2)}, u32[]{:S(2)}) %collective-permute-start.3) | collective-permute-done | bytes 77856 | tf_op jit(solution)/shard_map/ppermute | solution.py:712
  23.9 1.0 %collective-permute-done.4.refs_2_.refs_6_.refs_16_ = bf16[304,128]{1,0:T(8,128)(2,1)S(1)} collective-permute-done((bf16[304,128]{1,0:T(8,128)(2,1)S(1)}, bf16[304,128]{1,0:T(8,128)(2,1)S(1)}, u32[]{:S(2)}, u32[]{:S(2)}) %collective-permute-start.4) | collective-permute-done | bytes 77856 | tf_op jit(solution)/shard_map/ppermute | solution.py:712
  24.8 0.6 %collective-permute-done.5.refs_3_.refs_7_.refs_17_ = bf16[304,128]{1,0:T(8,128)(2,1)S(1)} collective-permute-done((bf16[304,128]{1,0:T(8,128)(2,1)S(1)}, bf16[304,128]{1,0:T(8,128)(2,1)S(1)}, u32[]{:S(2)}, u32[]{:S(2)}) %collective-permute-start.5) | collective-permute-done | bytes 77856 | tf_op jit(solution)/shard_map/ppermute | solution.py:712
  25.4 0.1 collective-permute-start.6
  25.5 0.5 %mix.1 = (bf16[128,512]{1,0:T(8,128)(2,1)S(1)}, bf16[128,512]{1,0:T(8,128)(2,1)S(1)}, bf16[128,512]{1,0:T(8,128)(2,1)S(1)}, bf16[128,512]{1,0:T(8,128)(2,1)S(1)}, bf16[4,304,128]{2,1,0:T(8,128)(2,1)S(1)}) custom-call(bf16[1,128,640]{2,1,0:T(8,128)(2,1)S(1)} %copy-done.1, f32[1,640]{1,0:T(1,128)S(1)} %reshape.13.gain_ref, bf16[128,640]{1,0:T(8,128)(2,1)S(1)} %copy-done.5, ...), custom_call_target="tpu_custom_call" | custom-call | flops 20000000000 | tf_op jit(solution)/shard_map/mix/pallas_call | solution.py:720
  26.1 0.6 %collective-permute-done.6.refs_1_ = f32[1,640]{1,0:T(1,128)S(1)} collective-permute-done((f32[1,640]{1,0:T(1,128)S(1)}, f32[1,640]{1,0:T(1,128)S(1)}, u32[]{:S(2)}, u32[]{:S(2)}) %collective-permute-start.6) | collective-permute-done | bytes 2592 | tf_op jit(solution)/shard_map/ppermute | solution.py:712
  26.7 1.2 %finish.1 = (bf16[1,128,640]{2,1,0:T(8,128)(2,1)}, bf16[1,128,640]{2,1,0:T(8,128)(2,1)}, bf16[1,128,640]{2,1,0:T(8,128)(2,1)}, bf16[1,128,640]{2,1,0:T(8,128)(2,1)}, f32[640]{0:T(1024)}) custom-call(f32[1,640]{1,0:T(1,128)S(1)} %gain.1.refs_0_, f32[1,640]{1,0:T(1,128)S(1)} %collective-permute-done.6.refs_1_, bf16[1,128,640]{2,1,0:T(8,128)(2,1)S(1)} %copy-done.2, ...), custom_call_target="tpu_custom_call" | custom-call | flops 1000000000 | tf_op jit(solution)/shard_map/finish/pallas_call | solution.py:720
  (12 shorter events, 0.0 us)
Async XLA Ops:
  3.2 5.8 %copy-start.10 = (f32[640]{0:T(1024)S(1)}, f32[640]{0:T(1024)}, u32[]{:S(2)}) copy-start(f32[640]{0:T(1024)} %param.10) | copy-start | bytes 7684
  3.2 9.2 %collective-permute-start = (bf16[352,128]{1,0:T(8,128)(2,1)}, bf16[352,128]{1,0:T(8,128)(2,1)S(1)}, u32[]{:S(2)}, u32[]{:S(2)}) collective-permute-start(bf16[352,128]{1,0:T(8,128)(2,1)} %get-tuple-element.39), channel_id=1, source_target_pairs={{0,12},{4,8},{8,4},{12,0},{1,13},{5,9},{9,5},{13,1},{2,14},{6,10},... | collective-permute-start | bytes 270344 | tf_op jit(solution)/shard_map/ppermute | solution.py:712
  8.3 6.0 %collective-permute-start.1 = (bf16[352,128]{1,0:T(8,128)(2,1)}, bf16[352,128]{1,0:T(8,128)(2,1)S(1)}, u32[]{:S(2)}, u32[]{:S(2)}) collective-permute-start(bf16[352,128]{1,0:T(8,128)(2,1)} %get-tuple-element.40), channel_id=1, source_target_pairs={{0,4},{4,0},{8,12},{12,8},{1,5},{5,1},{9,13},{13,9},{2,6},{6,2},{1... | collective-permute-start | bytes 270344 | tf_op jit(solution)/shard_map/ppermute | solution.py:712
  8.3 7.8 %collective-permute-start.2 = (bf16[352,128]{1,0:T(8,128)(2,1)}, bf16[352,128]{1,0:T(8,128)(2,1)S(1)}, u32[]{:S(2)}, u32[]{:S(2)}) collective-permute-start(bf16[352,128]{1,0:T(8,128)(2,1)} %get-tuple-element.41), channel_id=1, source_target_pairs={{0,8},{4,12},{8,0},{12,4},{1,9},{5,13},{9,1},{13,5},{2,10},{6,14},... | collective-permute-start | bytes 270344 | tf_op jit(solution)/shard_map/ppermute | solution.py:712
  9.0 0.7 %copy-start.4 = (s32[2,5]{1,0:T(2,128)S(1)}, s32[2,5]{1,0:T(2,128)}, u32[]{:S(2)}) copy-start(s32[2,5]{1,0:T(2,128)} %offsets_ref.3) | copy-start | bytes 124
  9.7 0.9 %copy-start = (bf16[1,128,640]{2,1,0:T(8,128)(2,1)S(1)}, bf16[1,128,640]{2,1,0:T(8,128)(2,1)}, u32[]{:S(2)}) copy-start(bf16[1,128,640]{2,1,0:T(8,128)(2,1)} %grad_ref.3) | copy-start | bytes 491524
  10.6 0.9 %copy-start.6 = (bf16[128,640]{1,0:T(8,128)(2,1)S(1)}, bf16[128,640]{1,0:T(8,128)(2,1)}, u32[]{:S(2)}) copy-start(bf16[128,640]{1,0:T(8,128)(2,1)} %get-tuple-element.33.out_ref) | copy-start | bytes 491524
  11.5 4.6 %copy-start.2 = (bf16[1,128,640]{2,1,0:T(8,128)(2,1)S(1)}, bf16[1,128,640]{2,1,0:T(8,128)(2,1)}, u32[]{:S(2)}) copy-start(bf16[1,128,640]{2,1,0:T(8,128)(2,1)} %refs_2_.1) | copy-start | bytes 491524
  11.5 4.6 %copy-start.7 = (bf16[128,640]{1,0:T(8,128)(2,1)S(1)}, bf16[128,640]{1,0:T(8,128)(2,1)}, u32[]{:S(2)}) copy-start(bf16[128,640]{1,0:T(8,128)(2,1)} %get-tuple-element.33.out_ref) | copy-start | bytes 491524
  11.5 4.6 %copy-start.8 = (bf16[352,128]{1,0:T(8,128)(2,1)S(1)}, bf16[352,128]{1,0:T(8,128)(2,1)}, u32[]{:S(2)}) copy-start(bf16[352,128]{1,0:T(8,128)(2,1)} %get-tuple-element.38.refs_3_) | copy-start | bytes 270340
  12.4 3.7 %copy-start.9 = (f32[16,128]{1,0:T(8,128)S(1)}, f32[16,128]{1,0:T(8,128)}, u32[]{:S(2)}) copy-start(f32[16,128]{1,0:T(8,128)} %get-tuple-element.35.refs_0_.refs_1_) | copy-start | bytes 24580
  16.1 5.5 %copy-start.1 = (bf16[1,128,640]{2,1,0:T(8,128)(2,1)S(1)}, bf16[1,128,640]{2,1,0:T(8,128)(2,1)}, u32[]{:S(2)}) copy-start(bf16[1,128,640]{2,1,0:T(8,128)(2,1)} %v_ref.5) | copy-start | bytes 491524
  16.1 5.5 %copy-start.3 = (bf16[1,128,640]{2,1,0:T(8,128)(2,1)S(1)}, bf16[1,128,640]{2,1,0:T(8,128)(2,1)}, u32[]{:S(2)}) copy-start(bf16[1,128,640]{2,1,0:T(8,128)(2,1)} %refs_3_.1) | copy-start | bytes 491524
  16.2 5.5 %copy-start.5 = (bf16[128,640]{1,0:T(8,128)(2,1)S(1)}, bf16[128,640]{1,0:T(8,128)(2,1)}, u32[]{:S(2)}) copy-start(bf16[128,640]{1,0:T(8,128)(2,1)} %get-tuple-element.47.expo_ref) | copy-start | bytes 491524
  17.2 6.7 %collective-permute-start.3 = (bf16[304,128]{1,0:T(8,128)(2,1)S(1)}, bf16[304,128]{1,0:T(8,128)(2,1)S(1)}, u32[]{:S(2)}, u32[]{:S(2)}) collective-permute-start(bf16[304,128]{1,0:T(8,128)(2,1)S(1)} %get-tuple-element.43), channel_id=1, source_target_pairs={{0,12},{4,8},{8,4},{12,0},{1,13},{5,9},{9,5},{13,1},{2,14},{6,10},... | collective-permute-start | bytes 233480 | tf_op jit(solution)/shard_map/ppermute | solution.py:712
  19.9 5.0 %collective-permute-start.4 = (bf16[304,128]{1,0:T(8,128)(2,1)S(1)}, bf16[304,128]{1,0:T(8,128)(2,1)S(1)}, u32[]{:S(2)}, u32[]{:S(2)}) collective-permute-start(bf16[304,128]{1,0:T(8,128)(2,1)S(1)} %get-tuple-element.44), channel_id=1, source_target_pairs={{0,4},{4,0},{8,12},{12,8},{1,5},{5,1},{9,13},{13,9},{2,6},{6,2},{1... | collective-permute-start | bytes 233480 | tf_op jit(solution)/shard_map/ppermute | solution.py:712
  19.9 5.6 %collective-permute-start.5 = (bf16[304,128]{1,0:T(8,128)(2,1)S(1)}, bf16[304,128]{1,0:T(8,128)(2,1)S(1)}, u32[]{:S(2)}, u32[]{:S(2)}) collective-permute-start(bf16[304,128]{1,0:T(8,128)(2,1)S(1)} %get-tuple-element.45), channel_id=1, source_target_pairs={{0,8},{4,12},{8,0},{12,4},{1,9},{5,13},{9,1},{13,5},{2,10},{6,14},... | collective-permute-start | bytes 233480 | tf_op jit(solution)/shard_map/ppermute | solution.py:712
  25.4 1.2 %collective-permute-start.6 = (f32[1,640]{1,0:T(1,128)S(1)}, f32[1,640]{1,0:T(1,128)S(1)}, u32[]{:S(2)}, u32[]{:S(2)}) collective-permute-start(f32[1,640]{1,0:T(1,128)S(1)} %gain.1.refs_0_), channel_id=1, source_target_pairs={{0,16},{16,0},{1,17},{17,1},{2,18},{18,2},{3,19},{19,3},{4,20},{20... | collective-permute-start | bytes 7688 | tf_op jit(solution)/shard_map/ppermute | solution.py:712

commit v16 on v15

--- a/solution.py
+++ b/solution.py
@@ -220,7 +220,6 @@
 
 
 VMEM_SPEC = pl.BlockSpec(memory_space=pltpu.VMEM)
-SMEM_SPEC = pl.BlockSpec(memory_space=pltpu.SMEM)
 PEERS = SPAN - 1
 OWNED = SPAN
 TILE = 8
@@ -248,14 +247,18 @@
     return tokens // top_step, tokens // R1
 
 
+def offset_of(offsets_ref, level, head):
+    return offsets_ref[level : level + 1, head : head + 1]
+
+
 def pick_matrix(offsets_ref, head, tokens, top_step, picked_axis):
     top_rows, _ = picked_counts(tokens, top_step)
     row = lax.broadcasted_iota(jnp.int32, (tokens, tokens), picked_axis)
     position = lax.broadcasted_iota(jnp.int32, (tokens, tokens), 1 - picked_axis)
     wanted = jnp.where(
         row < top_rows,
-        row * top_step + offsets_ref[1, head],
-        (row - top_rows) * R1 + offsets_ref[0, head],
+        row * top_step + offset_of(offsets_ref, 1, head),
+        (row - top_rows) * R1 + offset_of(offsets_ref, 0, head),
     )
     return jnp.where(position == wanted, 1.0, 0.0).astype(LOW)
 
@@ -354,7 +357,7 @@
         key_row = lax.broadcasted_iota(jnp.int32, (tokens, 1), 0)
         times = 1.0
         for level, step in ((0, R1), (1, top_step)):
-            offset = offsets_ref[level, head]
+            offset = offset_of(offsets_ref, level, head)
             hit_column = jnp.where(key_row % step == offset, 1.0, 0.0)
             times = times + hit_column * hit_row(offset, step, tokens)
         expos[head] = times * expos[head]
@@ -396,7 +399,12 @@
     me = lax.axis_index("ctx")
     mid_rows = tokens // R1
     top_all, queries = SPAN * top_rows, SPAN * (top_rows + mid_rows)
-    mid_offset, top_offset = offsets_ref[0, me], offsets_ref[1, me]
+    mid_offset, top_offset = [
+        sum(
+            jnp.where(me == head, offset_of(offsets_ref, level, head), 0) for head in range(OWNED)
+        )
+        for level in (0, 1)
+    ]
     lane = lax.broadcasted_iota(jnp.int32, (1, queries), 1)
     is_top = jnp.where(lane < top_all, 1.0, 0.0)
     top_in_mid = jnp.where(((lane % top_rows) * top_step + top_offset) % R1 == mid_offset, 1.0, 0.0)
@@ -408,7 +416,7 @@
     masks_ref[2:3, :queries] = is_top + (1.0 - is_top) * (1.0 - both_flag)
     last = len(heads) - 1
     for row, (level, step) in enumerate(((1, top_step), (0, R1))):
-        hits = hit_row(offsets_ref[level, last], step, tokens)
+        hits = hit_row(offset_of(offsets_ref, level, last), step, tokens)
         masks_ref[3 + row : 4 + row, :tokens] = (1.0 - hits) * NEVER
     grad_norms = [
         (grad_ref[0, :, head_cols(head)].astype(WIDE) * gain_ref[:, head_cols(head)]).T
@@ -421,7 +429,7 @@
         place_ref[:, cols] = picks
     for head in range(OWNED):
         cols = head_cols(head)
-        mid_offset, top_offset = offsets_ref[0, head], offsets_ref[1, head]
+        mid_offset, top_offset = [offset_of(offsets_ref, level, head) for level in (0, 1)]
         seen = jnp.maximum(
             hit_row(top_offset, top_step, tokens), hit_row(mid_offset, R1, tokens)
         )
@@ -613,10 +621,11 @@
         gain_ref[:, head_cols(head)] = total[head : head + 1]
 
 
-def mix_kernel(top_step, v_ref, gain_ref, expo_ref, out_ref, *refs):
+def mix_kernel(top_step, q_ref, k_ref, v_ref, gain_ref, expo_ref, out_ref, *refs):
     grad_norm_ref, stats_ref, place_ref, masks_ref = refs[:4]
-    return_refs, refs = nearest_first(refs[4 : 4 + SPAN]), refs[4 + SPAN :]
-    attended_ref, grad_low_ref, soft_ref, score_grad_ref, placed_ref = refs
+    last_attended_ref, last_dq_ref, last_dk_ref, last_dv_ref = refs[4:8]
+    return_refs, refs = nearest_first(refs[8 : 8 + SPAN]), refs[8 + SPAN :]
+    attended_ref, dq_ref, dk_ref, dv_ref, placed_ref = refs
     tokens, width = v_ref.shape[1:]
     count = width // HEAD_DIM
     picked = sum(picked_counts(tokens, top_step))
@@ -648,34 +657,17 @@
         inners.append(inner)
     prob_grads = [contract(v_ref[0, :, every[head]], grad_lows[head], 1, 0) for head in heads]
     softs = [expo_ref[:, every[head]].astype(WIDE) * factors[head] for head in heads]
-    for head in heads:
-        cols = every[head]
-        grad_low_ref[:, cols] = grad_lows[head]
-        soft_ref[:, cols] = softs[head].astype(LOW)
-        score_grad_ref[:, cols] = (
-            softs[head] * (prob_grads[head] - inners[head]) * score_scale
-        ).astype(LOW)
-        attended_ref[:, cols] = (normeds[head].T * gain_ref[:, cols]).astype(LOW)
-
-
-def finish_kernel(top_step, *refs):
-    gain_refs, (q_ref, k_ref, place_ref), refs = refs[:2], refs[2:5], refs[5:]
-    mixed_refs, (last_attended_ref, last_dq_ref, last_dk_ref, last_dv_ref) = refs[:5], refs[5:9]
-    return_refs, refs = nearest_first(refs[9 : 9 + SPAN]), refs[9 + SPAN :]
-    mixed_ref, grad_low_ref, soft_ref, score_grad_ref, returned_ref = mixed_refs
-    attended_ref, dq_ref, dk_ref, dv_ref, gain_out_ref = refs
-    tokens, width = q_ref.shape[1:]
-    picked = sum(picked_counts(tokens, top_step))
-    heads = range(OWNED)
-    every = [head_cols(head) for head in heads]
-    gain_out_ref[...] = (gain_refs[0][...] + gain_refs[1][...]).reshape(gain_out_ref.shape)
-    score_grads = [score_grad_ref[:, cols] for cols in every]
+    soft_lows = [soft.astype(LOW) for soft in softs]
+    score_grads = [
+        (softs[head] * (prob_grads[head] - inners[head]) * score_scale).astype(LOW)
+        for head in heads
+    ]
     dqs = [contract(score_grads[head], k_ref[0, :, every[head]], 0, 0) for head in heads]
     placed = [
         contract(
             place_ref[:, pl.ds(head * HEAD_DIM, picked)],
             jnp.concatenate(
-                [returned_ref[head, block * picked : (block + 1) * picked] for block in range(3)], 1
+                [placed_ref[head, block * picked : (block + 1) * picked] for block in range(3)], 1
             ),
             1,
             0,
@@ -683,8 +675,8 @@
         for head in heads
     ]
     dks = [contract(score_grads[head], q_ref[0, :, every[head]], 1, 0) for head in heads]
-    dvs = [contract(soft_ref[:, cols], grad_low_ref[:, cols], 1, 1) for cols in every]
-    last = width // HEAD_DIM - 1
+    dvs = [contract(soft_lows[head], grad_lows[head], 1, 1) for head in heads]
+    last = count - 1
     total = sum(ref[4 * picked : 6 * picked].astype(WIDE) for ref in return_refs[1:]).astype(LOW)
     rows = contract(
         place_ref[:, pl.ds(last * HEAD_DIM, picked)],
@@ -694,17 +686,24 @@
     )
     for head in heads:
         cols = every[head]
-        attended_ref[0, :, cols] = mixed_ref[:, cols]
+        attended_ref[:, cols] = (normeds[head].T * gain_ref[:, cols]).astype(LOW)
         for which, (block, out_block_ref) in enumerate(
             ((dqs[head], dq_ref), (dks[head], dk_ref), (dvs[head], dv_ref))
         ):
             part = placed[head][:, which * HEAD_DIM : (which + 1) * HEAD_DIM]
-            out_block_ref[0, :, cols] = (block + part).astype(LOW)
+            out_block_ref[:, cols] = (block + part).astype(LOW)
     cols = head_cols(last)
-    attended_ref[0, :, cols] = last_attended_ref[...]
-    dq_ref[0, :, cols] = last_dq_ref[...]
-    dk_ref[0, :, cols] = (last_dk_ref[...] + rows[:, :HEAD_DIM]).astype(LOW)
-    dv_ref[0, :, cols] = (last_dv_ref[...] + rows[:, HEAD_DIM:]).astype(LOW)
+    attended_ref[:, cols] = last_attended_ref[...]
+    dq_ref[:, cols] = last_dq_ref[...]
+    dk_ref[:, cols] = (last_dk_ref[...] + rows[:, :HEAD_DIM]).astype(LOW)
+    dv_ref[:, cols] = (last_dv_ref[...] + rows[:, HEAD_DIM:]).astype(LOW)
+
+
+def finish_kernel(gain_ref, gain_rest_ref, *refs):
+    block_refs, result_refs, gain_out_ref = refs[:4], refs[4:8], refs[8]
+    for block_ref, result_ref in zip(block_refs, result_refs):
+        result_ref[0] = block_ref[...]
+    gain_out_ref[...] = (gain_ref[...] + gain_rest_ref[...]).reshape(gain_out_ref.shape)
 
 
 def across(block, axis, distance):
@@ -720,7 +719,7 @@
     return pl.pallas_call(
         kernel,
         out_shape=results,
-        in_specs=[SMEM_SPEC if block.dtype == jnp.int32 else VMEM_SPEC for block in operands],
+        in_specs=[VMEM_SPEC] * len(operands),
         out_specs=[VMEM_SPEC] * len(results),
         scratch_shapes=scratch,
         compiler_params=pltpu.CompilerParams(vmem_limit_bytes=vmem),
@@ -791,11 +790,12 @@
     )
     (gain_sum,) = call(bind(gain_kernel, picked), "gain", (own_answer, *returned), [gain_block], 1)
     gain_rest = across(gain_sum, "dp", 1)
-    mixed_block = shape((tokens, OWNED * HEAD_DIM), LOW)
     mixed = call(
         bind(mix_kernel, top_step),
         "mix",
         (
+            queries,
+            keys,
             values,
             gain_row,
             expo,
@@ -804,26 +804,18 @@
             stats,
             place,
             masks,
-            own_answer,
-            *returned,
-        ),
-        [mixed_block] * 4 + [shape((OWNED, *answer.shape), LOW)],
-        20,
-    )
-    attended, query_grad, key_grad, value_grad, gain_grad = call(
-        bind(finish_kernel, top_step),
-        "finish",
-        (
-            gain_sum,
-            gain_rest,
-            queries,
-            keys,
-            place,
-            *mixed,
             *last_results,
             own_answer,
             *returned,
         ),
+        [low_block] * 4,
+        20,
+        scratch=[pltpu.VMEM((OWNED, *answer.shape), LOW)],
+    )
+    attended, query_grad, key_grad, value_grad, gain_grad = call(
+        finish_kernel,
+        "finish",
+        (gain_sum, gain_rest, *mixed),
         [row_block] * 4 + [shape((width,), WIDE)],
         1,
     )

time: 28.1 us -> 27.7 us (0.986)
  Pallas kernels: 6.57 us -> 6 us
    pallas_call x7, Pallas kernels: 6.57 us -> 6 us  [call(): pl.pallas_call(kernel, out_shape=results, in_specs=[VMEM_SPEC] * len(oper...]
  transfers between devices with their start and end apart: 7 -> 7, of which waited for: 6 -> 7; matrix products, arithmetic and copies ran while one was open for 0% -> 0% of each run, Pallas kernels for 6% -> 6%
where the time goes in v16:
time: 27.7 us; the launch traced here: 27.5 us
  starting transfers between devices  10.3 us (37%)
  waiting for transfers between devices  8.01 us (29%)
  Pallas kernels  6 us (22%)
  local copies, waits for them, and re-layouts  2.55 us (9%)
  between operations  0.72 us (3%)
    ppermute x7, starting transfers between devices, across(): return lax.ppermute(block, axis, route)  10.3 us
    ppermute x7, waiting for transfers between devices, across(): return lax.ppermute(block, axis, route)  8.01 us
    pallas_call x7, Pallas kernels, call(): pl.pallas_call(kernel, out_shape=results, in_specs=[VMEM_SPEC] * len(oper...  6 us
    unnamed x22, local copies, waits for them, and re-layouts  2.55 us
  transfers between devices with their start and end apart: 7, of which 7 were waited for; matrix products, arithmetic and copies ran while one was open for 0% of the time, Pallas kernels for 6%

profile of v16, /device:TPU:0, one launch (start us, length us, event | category | flops | bytes accessed | tf_op | source)
XLA Modules:
  0.0 27.5 jit_solution(3322977440637193037)
XLA Ops:
  0.6 2.6 %pack.1 = (bf16[352,128]{1,0:T(8,128)(2,1)}, bf16[352,128]{1,0:T(8,128)(2,1)}, bf16[352,128]{1,0:T(8,128)(2,1)}, bf16[352,128]{1,0:T(8,128)(2,1)}, bf16[128,640]...) custom-call(s32[2,5]{1,0:T(2,128)} %offsets_ref.3, bf16[1,128,640]{2,1,0:T(8,128)(2,1)} %q_ref.7, ...), custom_call_target="tpu_custom_call" | custom-call | flops 1000000000 | tf_op jit(solution)/shard_map/pack/pallas_call | solution.py:719
  3.2 5.1 %collective-permute-start = (bf16[352,128]{1,0:T(8,128)(2,1)}, bf16[352,128]{1,0:T(8,128)(2,1)S(1)}, u32[]{:S(2)}, u32[]{:S(2)}) collective-permute-start(bf16[352,128]{1,0:T(8,128)(2,1)} %get-tuple-element.38), channel_id=1, source_target_pairs={{0,12},{4,8},{8,4},{12,0},{1,13},{5,9},{9,5},{13,1},{2,14},{6,10},... | collective-permute-start | bytes 270344 | tf_op jit(solution)/shard_map/ppermute | solution.py:711
  8.3 0.0 collective-permute-start.1
  8.3 0.6 %collective-permute-start.2 = (bf16[352,128]{1,0:T(8,128)(2,1)}, bf16[352,128]{1,0:T(8,128)(2,1)S(1)}, u32[]{:S(2)}, u32[]{:S(2)}) collective-permute-start(bf16[352,128]{1,0:T(8,128)(2,1)} %get-tuple-element.40), channel_id=1, source_target_pairs={{0,8},{4,12},{8,0},{12,4},{1,9},{5,13},{9,1},{13,5},{2,10},{6,14},... | collective-permute-start | bytes 270344 | tf_op jit(solution)/shard_map/ppermute | solution.py:711
  9.0 0.0 copy-done.10
  9.0 0.7 %copy-done.4 = s32[2,5]{1,0:T(2,128)S(1)} copy-done((s32[2,5]{1,0:T(2,128)S(1)}, s32[2,5]{1,0:T(2,128)}, u32[]{:S(2)}) %copy-start.4) | copy-done | bytes 64
  9.7 0.9 %copy-done = bf16[1,128,640]{2,1,0:T(8,128)(2,1)S(1)} copy-done((bf16[1,128,640]{2,1,0:T(8,128)(2,1)S(1)}, bf16[1,128,640]{2,1,0:T(8,128)(2,1)}, u32[]{:S(2)}) %copy-start) | copy-done | bytes 163864
  10.6 0.9 %copy-done.6 = bf16[128,640]{1,0:T(8,128)(2,1)S(1)} copy-done((bf16[128,640]{1,0:T(8,128)(2,1)S(1)}, bf16[128,640]{1,0:T(8,128)(2,1)}, u32[]{:S(2)}) %copy-start.6) | copy-done | bytes 163864
  11.5 0.4 %prepare.1 = (f32[128,640]{1,0:T(8,128)S(1)}, f32[1,640]{1,0:T(1,128)S(1)}, bf16[128,1280]{1,0:T(8,128)(2,1)S(1)}, f32[16,256]{1,0:T(8,128)S(1)}) custom-call(s32[2,5]{1,0:T(2,128)S(1)} %copy-done.4, bf16[1,128,640]{2,1,0:T(8,128)(2,1)S(1)} %copy-done, f32[1,640]{1,0:T(1,128)S(1)} %reshape.13.gain_ref, bf16[128,640]{1,0:T(8,128)(2,1)S(1)} %copy-done.6), custom_call_target="tpu_custom_call" | custom-call | flops 2000000000 | tf_op jit(solution)/shard_map/prepare/pallas_call | solution.py:719
  11.9 0.0 copy-start.9
  11.9 0.2 collective-permute-done.refs_4_
  12.1 2.2 %collective-permute-done.1.refs_5_ = bf16[352,128]{1,0:T(8,128)(2,1)S(1)} collective-permute-done((bf16[352,128]{1,0:T(8,128)(2,1)}, bf16[352,128]{1,0:T(8,128)(2,1)S(1)}, u32[]{:S(2)}, u32[]{:S(2)}) %collective-permute-start.1) | collective-permute-done | bytes 90144 | tf_op jit(solution)/shard_map/ppermute | solution.py:711
  14.3 1.8 %collective-permute-done.2.refs_6_ = bf16[352,128]{1,0:T(8,128)(2,1)S(1)} collective-permute-done((bf16[352,128]{1,0:T(8,128)(2,1)}, bf16[352,128]{1,0:T(8,128)(2,1)S(1)}, u32[]{:S(2)}, u32[]{:S(2)}) %collective-permute-start.2) | collective-permute-done | bytes 90144 | tf_op jit(solution)/shard_map/ppermute | solution.py:711
  16.1 0.0 copy-done.1
  16.1 0.0 copy-done.7
  16.1 0.0 copy-done.8
  16.1 0.0 copy-start.2
  16.1 0.0 copy-start.3
  16.2 0.0 copy-start.5
  16.2 1.0 %owner.1 = (f32[128,128]{1,0:T(8,128)S(1)}, bf16[128,128]{1,0:T(8,128)(2,1)S(1)}, bf16[144,128]{1,0:T(8,128)(2,1)S(1)}, f32[8,128]{1,0:T(8,128)S(1)}, bf16[304,1...) custom-call(bf16[1,128,640]{2,1,0:T(8,128)(2,1)S(1)} %copy-done.1, ...), custom_call_target="tpu_custom_call" | custom-call | flops 3000000000 | tf_op jit(solution)/shard_map/owner/pallas_call | solution.py:719
  17.2 2.7 %collective-permute-start.3 = (bf16[304,128]{1,0:T(8,128)(2,1)S(1)}, bf16[304,128]{1,0:T(8,128)(2,1)S(1)}, u32[]{:S(2)}, u32[]{:S(2)}) collective-permute-start(bf16[304,128]{1,0:T(8,128)(2,1)S(1)} %get-tuple-element.42), channel_id=1, source_target_pairs={{0,12},{4,8},{8,4},{12,0},{1,13},{5,9},{9,5},{13,1},{2,14},{6,10},... | collective-permute-start | bytes 233480 | tf_op jit(solution)/shard_map/ppermute | solution.py:711
  19.9 0.0 collective-permute-start.4
  19.9 1.7 %collective-permute-start.5 = (bf16[304,128]{1,0:T(8,128)(2,1)S(1)}, bf16[304,128]{1,0:T(8,128)(2,1)S(1)}, u32[]{:S(2)}, u32[]{:S(2)}) collective-permute-start(bf16[304,128]{1,0:T(8,128)(2,1)S(1)} %get-tuple-element.44), channel_id=1, source_target_pairs={{0,8},{4,12},{8,0},{12,4},{1,9},{5,13},{9,1},{13,5},{2,10},{6,14},... | collective-permute-start | bytes 233480 | tf_op jit(solution)/shard_map/ppermute | solution.py:711
  21.6 0.0 copy-done.2
  21.6 0.3 %last_head.1 = (bf16[128,128]{1,0:T(8,128)(2,1)S(1)}, bf16[128,128]{1,0:T(8,128)(2,1)S(1)}, f32[128,128]{1,0:T(8,128)S(1)}, f32[128,128]{1,0:T(8,128)S(1)}) custom-call(bf16[1,128,640]{2,1,0:T(8,128)(2,1)S(1)} %copy-done.1, bf16[1,128,640]{2,1,0:T(8,128)(2,1)S(1)} %copy-done.2, bf16[1,128,640]{2,1,0:T(8,128)(2,1)S(1)} %copy-done.3, ...), custom_call_target="tpu_custom_call" | custom-call | flops 20000000000 | tf_op jit(solution)/shard_map/last_head/pallas_call | solution.py:719
  22.0 1.9 %collective-permute-done.3.refs_1_.refs_9_ = bf16[304,128]{1,0:T(8,128)(2,1)S(1)} collective-permute-done((bf16[304,128]{1,0:T(8,128)(2,1)S(1)}, bf16[304,128]{1,0:T(8,128)(2,1)S(1)}, u32[]{:S(2)}, u32[]{:S(2)}) %collective-permute-start.3) | collective-permute-done | bytes 77856 | tf_op jit(solution)/shard_map/ppermute | solution.py:711
  23.9 1.0 %collective-permute-done.4.refs_2_.refs_10_ = bf16[304,128]{1,0:T(8,128)(2,1)S(1)} collective-permute-done((bf16[304,128]{1,0:T(8,128)(2,1)S(1)}, bf16[304,128]{1,0:T(8,128)(2,1)S(1)}, u32[]{:S(2)}, u32[]{:S(2)}) %collective-permute-start.4) | collective-permute-done | bytes 77856 | tf_op jit(solution)/shard_map/ppermute | solution.py:711
  24.8 0.6 %collective-permute-done.5.refs_3_.refs_11_ = bf16[304,128]{1,0:T(8,128)(2,1)S(1)} collective-permute-done((bf16[304,128]{1,0:T(8,128)(2,1)S(1)}, bf16[304,128]{1,0:T(8,128)(2,1)S(1)}, u32[]{:S(2)}, u32[]{:S(2)}) %collective-permute-start.5) | collective-permute-done | bytes 77856 | tf_op jit(solution)/shard_map/ppermute | solution.py:711
  25.4 0.1 collective-permute-start.6
  25.5 0.8 %mix.1 = (bf16[128,640]{1,0:T(8,128)(2,1)S(1)}, bf16[128,640]{1,0:T(8,128)(2,1)S(1)}, bf16[128,640]{1,0:T(8,128)(2,1)S(1)}, bf16[128,640]{1,0:T(8,128)(2,1)S(1)}) custom-call(bf16[1,128,640]{2,1,0:T(8,128)(2,1)S(1)} %copy-done.1, bf16[1,128,640]{2,1,0:T(8,128)(2,1)S(1)} %copy-done.2, bf16[1,128,640]{2,1,0:T(8,128)(2,1)S(1)} %copy-done.3, ...), custom_call_target="tpu_custom_call" | custom-call | flops 20000000000 | tf_op jit(solution)/shard_map/mix/pallas_call | solution.py:719
  26.3 0.3 %collective-permute-done.6.gain_rest_ref = f32[1,640]{1,0:T(1,128)S(1)} collective-permute-done((f32[1,640]{1,0:T(1,128)S(1)}, f32[1,640]{1,0:T(1,128)S(1)}, u32[]{:S(2)}, u32[]{:S(2)}) %collective-permute-start.6) | collective-permute-done | bytes 2592 | tf_op jit(solution)/shard_map/ppermute | solution.py:711
  26.7 0.9 %finish.1 = (bf16[1,128,640]{2,1,0:T(8,128)(2,1)}, bf16[1,128,640]{2,1,0:T(8,128)(2,1)}, bf16[1,128,640]{2,1,0:T(8,128)(2,1)}, bf16[1,128,640]{2,1,0:T(8,128)(2,1)}, f32[640]{0:T(1024)}) custom-call(f32[1,640]{1,0:T(1,128)S(1)} %gain.1.gain_ref, f32[1,640]{1,0:T(1,128)S(1)} %collective-permute-done.6.gain_rest_ref, ...), custom_call_target="tpu_custom_call" | custom-call | flops 1000000000 | tf_op jit(solution)/shard_map/finish/pallas_call | solution.py:719
  (12 shorter events, 0.0 us)
Async XLA Ops:
  3.2 5.7 %copy-start.10 = (f32[640]{0:T(1024)S(1)}, f32[640]{0:T(1024)}, u32[]{:S(2)}) copy-start(f32[640]{0:T(1024)} %param.10) | copy-start | bytes 7684
  3.2 8.8 %collective-permute-start = (bf16[352,128]{1,0:T(8,128)(2,1)}, bf16[352,128]{1,0:T(8,128)(2,1)S(1)}, u32[]{:S(2)}, u32[]{:S(2)}) collective-permute-start(bf16[352,128]{1,0:T(8,128)(2,1)} %get-tuple-element.38), channel_id=1, source_target_pairs={{0,12},{4,8},{8,4},{12,0},{1,13},{5,9},{9,5},{13,1},{2,14},{6,10},... | collective-permute-start | bytes 270344 | tf_op jit(solution)/shard_map/ppermute | solution.py:711
  8.3 6.0 %collective-permute-start.1 = (bf16[352,128]{1,0:T(8,128)(2,1)}, bf16[352,128]{1,0:T(8,128)(2,1)S(1)}, u32[]{:S(2)}, u32[]{:S(2)}) collective-permute-start(bf16[352,128]{1,0:T(8,128)(2,1)} %get-tuple-element.39), channel_id=1, source_target_pairs={{0,4},{4,0},{8,12},{12,8},{1,5},{5,1},{9,13},{13,9},{2,6},{6,2},{1... | collective-permute-start | bytes 270344 | tf_op jit(solution)/shard_map/ppermute | solution.py:711
  8.3 7.8 %collective-permute-start.2 = (bf16[352,128]{1,0:T(8,128)(2,1)}, bf16[352,128]{1,0:T(8,128)(2,1)S(1)}, u32[]{:S(2)}, u32[]{:S(2)}) collective-permute-start(bf16[352,128]{1,0:T(8,128)(2,1)} %get-tuple-element.40), channel_id=1, source_target_pairs={{0,8},{4,12},{8,0},{12,4},{1,9},{5,13},{9,1},{13,5},{2,10},{6,14},... | collective-permute-start | bytes 270344 | tf_op jit(solution)/shard_map/ppermute | solution.py:711
  9.0 0.7 %copy-start.4 = (s32[2,5]{1,0:T(2,128)S(1)}, s32[2,5]{1,0:T(2,128)}, u32[]{:S(2)}) copy-start(s32[2,5]{1,0:T(2,128)} %offsets_ref.3) | copy-start | bytes 124
  9.7 0.9 %copy-start = (bf16[1,128,640]{2,1,0:T(8,128)(2,1)S(1)}, bf16[1,128,640]{2,1,0:T(8,128)(2,1)}, u32[]{:S(2)}) copy-start(bf16[1,128,640]{2,1,0:T(8,128)(2,1)} %grad_ref.3) | copy-start | bytes 491524
  10.6 0.9 %copy-start.6 = (bf16[128,640]{1,0:T(8,128)(2,1)S(1)}, bf16[128,640]{1,0:T(8,128)(2,1)}, u32[]{:S(2)}) copy-start(bf16[128,640]{1,0:T(8,128)(2,1)} %get-tuple-element.32.out_ref) | copy-start | bytes 491524
  11.5 4.6 %copy-start.1 = (bf16[1,128,640]{2,1,0:T(8,128)(2,1)S(1)}, bf16[1,128,640]{2,1,0:T(8,128)(2,1)}, u32[]{:S(2)}) copy-start(bf16[1,128,640]{2,1,0:T(8,128)(2,1)} %q_ref.7) | copy-start | bytes 491524
  11.5 4.6 %copy-start.7 = (bf16[128,640]{1,0:T(8,128)(2,1)S(1)}, bf16[128,640]{1,0:T(8,128)(2,1)}, u32[]{:S(2)}) copy-start(bf16[128,640]{1,0:T(8,128)(2,1)} %get-tuple-element.32.out_ref) | copy-start | bytes 491524
  11.5 4.6 %copy-start.8 = (bf16[352,128]{1,0:T(8,128)(2,1)S(1)}, bf16[352,128]{1,0:T(8,128)(2,1)}, u32[]{:S(2)}) copy-start(bf16[352,128]{1,0:T(8,128)(2,1)} %get-tuple-element.37.refs_3_) | copy-start | bytes 270340
  11.9 4.2 %copy-start.9 = (f32[16,128]{1,0:T(8,128)S(1)}, f32[16,128]{1,0:T(8,128)}, u32[]{:S(2)}) copy-start(f32[16,128]{1,0:T(8,128)} %get-tuple-element.34.refs_0_.refs_1_) | copy-start | bytes 24580
  16.1 5.5 %copy-start.2 = (bf16[1,128,640]{2,1,0:T(8,128)(2,1)S(1)}, bf16[1,128,640]{2,1,0:T(8,128)(2,1)}, u32[]{:S(2)}) copy-start(bf16[1,128,640]{2,1,0:T(8,128)(2,1)} %k_ref.5) | copy-start | bytes 491524
  16.1 5.5 %copy-start.3 = (bf16[1,128,640]{2,1,0:T(8,128)(2,1)S(1)}, bf16[1,128,640]{2,1,0:T(8,128)(2,1)}, u32[]{:S(2)}) copy-start(bf16[1,128,640]{2,1,0:T(8,128)(2,1)} %v_ref.5) | copy-start | bytes 491524
  16.2 5.5 %copy-start.5 = (bf16[128,640]{1,0:T(8,128)(2,1)S(1)}, bf16[128,640]{1,0:T(8,128)(2,1)}, u32[]{:S(2)}) copy-start(bf16[128,640]{1,0:T(8,128)(2,1)} %get-tuple-element.45.expo_ref) | copy-start | bytes 491524
  17.2 6.7 %collective-permute-start.3 = (bf16[304,128]{1,0:T(8,128)(2,1)S(1)}, bf16[304,128]{1,0:T(8,128)(2,1)S(1)}, u32[]{:S(2)}, u32[]{:S(2)}) collective-permute-start(bf16[304,128]{1,0:T(8,128)(2,1)S(1)} %get-tuple-element.42), channel_id=1, source_target_pairs={{0,12},{4,8},{8,4},{12,0},{1,13},{5,9},{9,5},{13,1},{2,14},{6,10},... | collective-permute-start | bytes 233480 | tf_op jit(solution)/shard_map/ppermute | solution.py:711
  19.9 5.0 %collective-permute-start.4 = (bf16[304,128]{1,0:T(8,128)(2,1)S(1)}, bf16[304,128]{1,0:T(8,128)(2,1)S(1)}, u32[]{:S(2)}, u32[]{:S(2)}) collective-permute-start(bf16[304,128]{1,0:T(8,128)(2,1)S(1)} %get-tuple-element.43), channel_id=1, source_target_pairs={{0,4},{4,0},{8,12},{12,8},{1,5},{5,1},{9,13},{13,9},{2,6},{6,2},{1... | collective-permute-start | bytes 233480 | tf_op jit(solution)/shard_map/ppermute | solution.py:711
  19.9 5.6 %collective-permute-start.5 = (bf16[304,128]{1,0:T(8,128)(2,1)S(1)}, bf16[304,128]{1,0:T(8,128)(2,1)S(1)}, u32[]{:S(2)}, u32[]{:S(2)}) collective-permute-start(bf16[304,128]{1,0:T(8,128)(2,1)S(1)} %get-tuple-element.44), channel_id=1, source_target_pairs={{0,8},{4,12},{8,0},{12,4},{1,9},{5,13},{9,1},{13,5},{2,10},{6,14},... | collective-permute-start | bytes 233480 | tf_op jit(solution)/shard_map/ppermute | solution.py:711
  25.4 1.2 %collective-permute-start.6 = (f32[1,640]{1,0:T(1,128)S(1)}, f32[1,640]{1,0:T(1,128)S(1)}, u32[]{:S(2)}, u32[]{:S(2)}) collective-permute-start(f32[1,640]{1,0:T(1,128)S(1)} %gain.1.gain_ref), channel_id=1, source_target_pairs={{0,16},{16,0},{1,17},{17,1},{2,18},{18,2},{3,19},{19,3},{4,20},{20... | collective-permute-start | bytes 7688 | tf_op jit(solution)/shard_map/ppermute | solution.py:711

commit v17 on v16

--- a/solution.py
+++ b/solution.py
@@ -315,7 +315,7 @@
     product = grad_norm * normed
     grad_attn = inv_rms * (grad_norm - normed * column_mean(product))
     inner = jnp.sum(grad_attn * attn, axis=0, keepdims=True)
-    return normed, product, grad_attn.astype(LOW), inner
+    return normed, product, grad_attn, inner
 
 
 def nearest_first(refs):
@@ -522,32 +522,37 @@
     total = factor + jnp.sum(expo, axis=0, keepdims=True)
     total_last = factor_last * base_total + jnp.sum(expo_last, axis=0, keepdims=True)
     inv_total, inv_last = 1.0 / total, 1.0 / total_last
-    soft, soft_last = expo * inv_total, expo_last * inv_last
-    soft_low, soft_last_low = soft.astype(LOW), soft_last.astype(LOW)
-    factor_last = factor_last * inv_last
-    attn = (factor * inv_total) * base_attn + contract(v_rows, soft_low, 0, 0)
-    attn_last = factor_last * out_ref[:, cols].astype(WIDE) + contract(v_peers, soft_last_low, 0, 0)
-    _, product, grad_low, inner = norm_backward(attn, grad_norm)
-    normed_last, product_last, grad_last_low, inner_last = norm_backward(
+    expo_low, expo_last_low = expo.astype(LOW), expo_last.astype(LOW)
+    attn = (factor * base_attn + contract(v_rows, expo_low, 0, 0)) * inv_total
+    attn_last = (
+        factor_last * out_ref[:, cols].astype(WIDE) + contract(v_peers, expo_last_low, 0, 0)
+    ) * inv_last
+    _, product, grad_attn, inner = norm_backward(attn, grad_norm)
+    normed_last, product_last, grad_attn_last, inner_last = norm_backward(
         attn_last, grad_norm_ref[:, cols]
     )
+    grad_low, inner = (grad_attn * inv_total).astype(LOW), inner * inv_total
+    grad_last_low = (grad_attn_last * inv_last).astype(LOW)
+    base_factor = factor_last * inv_last
     spans = (slice(0, top_all), slice(top_all, queries))
     prob_grads = [contract(v_rows[span], grad_low[:, span], 1, 0) for span in spans]
     prob_grad_last = contract(v_peers, grad_last_low, 1, 0)
     score_grads = [
-        (soft[span, span] * (prob_grad - inner[:, span]) * score_scale).astype(LOW)
+        (expo[span, span] * (prob_grad - inner[:, span]) * score_scale).astype(LOW)
         for span, prob_grad in zip(spans, prob_grads)
     ]
-    score_grad_last = (soft_last * (prob_grad_last - inner_last) * score_scale).astype(LOW)
+    score_grad_last = (
+        expo_last * (prob_grad_last - inner_last * inv_last) * score_scale
+    ).astype(LOW)
     dks = [
         contract(score_grad, q_rows[span], 1, 0).astype(LOW)
         for span, score_grad in zip(spans, score_grads)
     ]
     dk_last = contract(score_grad_last, q_last, 1, 0).astype(LOW)
     dvs = [
-        contract(soft_low[span, span], grad_low[:, span], 1, 1).astype(LOW) for span in spans
-    ]
-    dv_last = contract(soft_last_low, grad_last_low, 1, 1).astype(LOW)
+        contract(expo_low[span, span], grad_low[:, span], 1, 1).astype(LOW) for span in spans
+    ]
+    dv_last = contract(expo_last_low, grad_last_low, 1, 1).astype(LOW)
     dqs = [
         contract(score_grad, k_rows[span], 0, 0).astype(LOW)
         for span, score_grad in zip(spans, score_grads)
@@ -585,10 +590,9 @@
         blocks.append(jnp.concatenate(log_rows, 0).astype(LOW))
         return_ref[...] = jnp.concatenate(blocks, 0)
     normed_ref[...] = normed_last
-    grad_low_ref[...] = grad_last_low
+    grad_low_ref[...] = (grad_attn_last * base_factor).astype(LOW)
     score_grad_ref[...] = score_grad_last
-    kept_ref[0:1, :] = factor_last
-    kept_ref[1:2, :] = inner_last
+    kept_ref[0:1, :] = inner_last * base_factor
 
 
 def last_head_kernel(top_step, q_ref, k_ref, v_ref, gain_ref, expo_ref, *refs):
@@ -601,11 +605,13 @@
     attended_ref[...] = (normed_ref[...].T * gain_ref[:, cols]).astype(LOW)
     k_peers = jnp.concatenate([ref[5 * picked : 6 * picked] for ref in peers], 0)
     grad_low = grad_low_ref[...]
-    soft = expo_ref[:, cols].astype(WIDE) * kept_ref[0:1, :]
+    expo_low = expo_ref[:, cols]
     prob_grad = contract(v_ref[0, :, cols], grad_low, 1, 0)
-    score_grad = (soft * (prob_grad - kept_ref[1:2, :]) * score_scale).astype(LOW)
+    score_grad = (
+        expo_low.astype(WIDE) * (prob_grad - kept_ref[0:1, :]) * score_scale
+    ).astype(LOW)
     dk_ref[...] = contract(score_grad, q_ref[0, :, cols], 1, 0)
-    dv_ref[...] = contract(soft.astype(LOW), grad_low, 1, 1)
+    dv_ref[...] = contract(expo_low, grad_low, 1, 1)
     dq_ref[...] = (
         contract(score_grad, k_ref[0, :, cols], 0, 0)
         + contract(peer_score_grad_ref[...], k_peers, 0, 0)
@@ -644,19 +650,21 @@
         contract(placed_ref[head, 6 * picked : 6 * picked + STAT_TILES], once[head], 1, 1)
         for head in heads
     ]
-    factors, normeds, grad_lows, inners = [], [], [], []
+    normeds, grad_lows, inners, inv_totals = [], [], [], []
     for head in heads:
         seen = masks_ref[TILE + head : TILE + head + 1, :tokens] > 0.5
         top_score, total = stats_ref[head : head + 1, :], stats_ref[TILE + head : TILE + head + 1, :]
-        log_total = jnp.where(seen, joined_row(log_parts[head], 0), top_score + jnp.log(total))
-        factors.append(jnp.exp(top_score - log_total))
+        base_log = top_score + jnp.log(total)
+        log_total = jnp.where(seen, joined_row(log_parts[head], 0), base_log)
+        share = jnp.exp(base_log - log_total)
+        inv_totals.append(1.0 / total)
         attn = jnp.where(seen, attn_parts[head], out_ref[:, every[head]].astype(WIDE))
-        normed, _, grad_low, inner = norm_backward(attn, grad_norm_ref[:, every[head]])
+        normed, _, grad_attn, inner = norm_backward(attn, grad_norm_ref[:, every[head]])
         normeds.append(normed)
-        grad_lows.append(grad_low)
-        inners.append(inner)
+        grad_lows.append((share * grad_attn).astype(LOW))
+        inners.append(share * inner)
     prob_grads = [contract(v_ref[0, :, every[head]], grad_lows[head], 1, 0) for head in heads]
-    softs = [expo_ref[:, every[head]].astype(WIDE) * factors[head] for head in heads]
+    softs = [expo_ref[:, every[head]].astype(WIDE) * inv_totals[head] for head in heads]
     soft_lows = [soft.astype(LOW) for soft in softs]
     score_grads = [
         (softs[head] * (prob_grads[head] - inners[head]) * score_scale).astype(LOW)

time: 27.7 us -> 27.7 us (level)
  no operation moved by 1% of the time
where the time goes in v17:
time: 27.7 us; the launch traced here: 27.5 us
  starting transfers between devices  10.3 us (37%)
  waiting for transfers between devices  7.99 us (29%)
  Pallas kernels  6.01 us (22%)
  local copies, waits for them, and re-layouts  2.55 us (9%)
  between operations  0.72 us (3%)
    ppermute x7, starting transfers between devices, across(): return lax.ppermute(block, axis, route)  10.3 us
    ppermute x7, waiting for transfers between devices, across(): return lax.ppermute(block, axis, route)  7.99 us
    pallas_call x7, Pallas kernels, call(): pl.pallas_call(kernel, out_shape=results, in_specs=[VMEM_SPEC] * len(oper...  6.01 us
    unnamed x22, local copies, waits for them, and re-layouts  2.55 us
  transfers between devices with their start and end apart: 7, of which 7 were waited for; matrix products, arithmetic and copies ran while one was open for 0% of the time, Pallas kernels for 6%

profile of v17, /device:TPU:0, one launch (start us, length us, event | category | flops | bytes accessed | tf_op | source)
XLA Modules:
  0.0 27.5 jit_solution(7684208304342155804)
XLA Ops:
  0.6 2.6 %pack.1 = (bf16[352,128]{1,0:T(8,128)(2,1)}, bf16[352,128]{1,0:T(8,128)(2,1)}, bf16[352,128]{1,0:T(8,128)(2,1)}, bf16[352,128]{1,0:T(8,128)(2,1)}, bf16[128,640]...) custom-call(s32[2,5]{1,0:T(2,128)} %offsets_ref.3, bf16[1,128,640]{2,1,0:T(8,128)(2,1)} %q_ref.7, ...), custom_call_target="tpu_custom_call" | custom-call | flops 1000000000 | tf_op jit(solution)/shard_map/pack/pallas_call | solution.py:727
  3.2 5.1 %collective-permute-start = (bf16[352,128]{1,0:T(8,128)(2,1)}, bf16[352,128]{1,0:T(8,128)(2,1)S(1)}, u32[]{:S(2)}, u32[]{:S(2)}) collective-permute-start(bf16[352,128]{1,0:T(8,128)(2,1)} %get-tuple-element.38), channel_id=1, source_target_pairs={{0,12},{4,8},{8,4},{12,0},{1,13},{5,9},{9,5},{13,1},{2,14},{6,10},... | collective-permute-start | bytes 270344 | tf_op jit(solution)/shard_map/ppermute | solution.py:719
  8.3 0.0 collective-permute-start.1
  8.3 0.6 %collective-permute-start.2 = (bf16[352,128]{1,0:T(8,128)(2,1)}, bf16[352,128]{1,0:T(8,128)(2,1)S(1)}, u32[]{:S(2)}, u32[]{:S(2)}) collective-permute-start(bf16[352,128]{1,0:T(8,128)(2,1)} %get-tuple-element.40), channel_id=1, source_target_pairs={{0,8},{4,12},{8,0},{12,4},{1,9},{5,13},{9,1},{13,5},{2,10},{6,14},... | collective-permute-start | bytes 270344 | tf_op jit(solution)/shard_map/ppermute | solution.py:719
  9.0 0.0 copy-done.10
  9.0 0.7 %copy-done.4 = s32[2,5]{1,0:T(2,128)S(1)} copy-done((s32[2,5]{1,0:T(2,128)S(1)}, s32[2,5]{1,0:T(2,128)}, u32[]{:S(2)}) %copy-start.4) | copy-done | bytes 64
  9.7 0.9 %copy-done = bf16[1,128,640]{2,1,0:T(8,128)(2,1)S(1)} copy-done((bf16[1,128,640]{2,1,0:T(8,128)(2,1)S(1)}, bf16[1,128,640]{2,1,0:T(8,128)(2,1)}, u32[]{:S(2)}) %copy-start) | copy-done | bytes 163864
  10.6 0.9 %copy-done.6 = bf16[128,640]{1,0:T(8,128)(2,1)S(1)} copy-done((bf16[128,640]{1,0:T(8,128)(2,1)S(1)}, bf16[128,640]{1,0:T(8,128)(2,1)}, u32[]{:S(2)}) %copy-start.6) | copy-done | bytes 163864
  11.5 0.4 %prepare.1 = (f32[128,640]{1,0:T(8,128)S(1)}, f32[1,640]{1,0:T(1,128)S(1)}, bf16[128,1280]{1,0:T(8,128)(2,1)S(1)}, f32[16,256]{1,0:T(8,128)S(1)}) custom-call(s32[2,5]{1,0:T(2,128)S(1)} %copy-done.4, bf16[1,128,640]{2,1,0:T(8,128)(2,1)S(1)} %copy-done, f32[1,640]{1,0:T(1,128)S(1)} %reshape.13.gain_ref, bf16[128,640]{1,0:T(8,128)(2,1)S(1)} %copy-done.6), custom_call_target="tpu_custom_call" | custom-call | flops 2000000000 | tf_op jit(solution)/shard_map/prepare/pallas_call | solution.py:727
  11.9 0.0 copy-start.9
  11.9 0.2 collective-permute-done.refs_4_
  12.1 2.2 %collective-permute-done.1.refs_5_ = bf16[352,128]{1,0:T(8,128)(2,1)S(1)} collective-permute-done((bf16[352,128]{1,0:T(8,128)(2,1)}, bf16[352,128]{1,0:T(8,128)(2,1)S(1)}, u32[]{:S(2)}, u32[]{:S(2)}) %collective-permute-start.1) | collective-permute-done | bytes 90144 | tf_op jit(solution)/shard_map/ppermute | solution.py:719
  14.3 1.8 %collective-permute-done.2.refs_6_ = bf16[352,128]{1,0:T(8,128)(2,1)S(1)} collective-permute-done((bf16[352,128]{1,0:T(8,128)(2,1)}, bf16[352,128]{1,0:T(8,128)(2,1)S(1)}, u32[]{:S(2)}, u32[]{:S(2)}) %collective-permute-start.2) | collective-permute-done | bytes 90144 | tf_op jit(solution)/shard_map/ppermute | solution.py:719
  16.1 0.0 copy-done.1
  16.1 0.0 copy-done.7
  16.1 0.0 copy-done.9
  16.1 0.0 copy-start.2
  16.1 0.0 copy-start.3
  16.2 0.0 copy-start.5
  16.2 1.0 %owner.1 = (f32[128,128]{1,0:T(8,128)S(1)}, bf16[128,128]{1,0:T(8,128)(2,1)S(1)}, bf16[144,128]{1,0:T(8,128)(2,1)S(1)}, f32[8,128]{1,0:T(8,128)S(1)}, bf16[304,1...) custom-call(bf16[1,128,640]{2,1,0:T(8,128)(2,1)S(1)} %copy-done.1, ...), custom_call_target="tpu_custom_call" | custom-call | flops 3000000000 | tf_op jit(solution)/shard_map/owner/pallas_call | solution.py:727
  17.1 2.7 %collective-permute-start.3 = (bf16[304,128]{1,0:T(8,128)(2,1)S(1)}, bf16[304,128]{1,0:T(8,128)(2,1)S(1)}, u32[]{:S(2)}, u32[]{:S(2)}) collective-permute-start(bf16[304,128]{1,0:T(8,128)(2,1)S(1)} %get-tuple-element.42), channel_id=1, source_target_pairs={{0,12},{4,8},{8,4},{12,0},{1,13},{5,9},{9,5},{13,1},{2,14},{6,10},... | collective-permute-start | bytes 233480 | tf_op jit(solution)/shard_map/ppermute | solution.py:719
  19.9 0.0 collective-permute-start.4
  19.9 1.7 %collective-permute-start.5 = (bf16[304,128]{1,0:T(8,128)(2,1)S(1)}, bf16[304,128]{1,0:T(8,128)(2,1)S(1)}, u32[]{:S(2)}, u32[]{:S(2)}) collective-permute-start(bf16[304,128]{1,0:T(8,128)(2,1)S(1)} %get-tuple-element.44), channel_id=1, source_target_pairs={{0,8},{4,12},{8,0},{12,4},{1,9},{5,13},{9,1},{13,5},{2,10},{6,14},... | collective-permute-start | bytes 233480 | tf_op jit(solution)/shard_map/ppermute | solution.py:719
  21.6 0.0 copy-done.3
  21.6 0.3 %last_head.1 = (bf16[128,128]{1,0:T(8,128)(2,1)S(1)}, bf16[128,128]{1,0:T(8,128)(2,1)S(1)}, f32[128,128]{1,0:T(8,128)S(1)}, f32[128,128]{1,0:T(8,128)S(1)}) custom-call(bf16[1,128,640]{2,1,0:T(8,128)(2,1)S(1)} %copy-done.1, bf16[1,128,640]{2,1,0:T(8,128)(2,1)S(1)} %copy-done.2, bf16[1,128,640]{2,1,0:T(8,128)(2,1)S(1)} %copy-done.3, ...), custom_call_target="tpu_custom_call" | custom-call | flops 20000000000 | tf_op jit(solution)/shard_map/last_head/pallas_call | solution.py:727
  21.9 1.9 %collective-permute-done.3.refs_1_.refs_9_ = bf16[304,128]{1,0:T(8,128)(2,1)S(1)} collective-permute-done((bf16[304,128]{1,0:T(8,128)(2,1)S(1)}, bf16[304,128]{1,0:T(8,128)(2,1)S(1)}, u32[]{:S(2)}, u32[]{:S(2)}) %collective-permute-start.3) | collective-permute-done | bytes 77856 | tf_op jit(solution)/shard_map/ppermute | solution.py:719
  23.9 1.0 %collective-permute-done.4.refs_2_.refs_10_ = bf16[304,128]{1,0:T(8,128)(2,1)S(1)} collective-permute-done((bf16[304,128]{1,0:T(8,128)(2,1)S(1)}, bf16[304,128]{1,0:T(8,128)(2,1)S(1)}, u32[]{:S(2)}, u32[]{:S(2)}) %collective-permute-start.4) | collective-permute-done | bytes 77856 | tf_op jit(solution)/shard_map/ppermute | solution.py:719
  24.8 0.6 %collective-permute-done.5.refs_3_.refs_11_ = bf16[304,128]{1,0:T(8,128)(2,1)S(1)} collective-permute-done((bf16[304,128]{1,0:T(8,128)(2,1)S(1)}, bf16[304,128]{1,0:T(8,128)(2,1)S(1)}, u32[]{:S(2)}, u32[]{:S(2)}) %collective-permute-start.5) | collective-permute-done | bytes 77856 | tf_op jit(solution)/shard_map/ppermute | solution.py:719
  25.4 0.1 collective-permute-start.6
  25.5 0.8 %mix.1 = (bf16[128,640]{1,0:T(8,128)(2,1)S(1)}, bf16[128,640]{1,0:T(8,128)(2,1)S(1)}, bf16[128,640]{1,0:T(8,128)(2,1)S(1)}, bf16[128,640]{1,0:T(8,128)(2,1)S(1)}) custom-call(bf16[1,128,640]{2,1,0:T(8,128)(2,1)S(1)} %copy-done.1, bf16[1,128,640]{2,1,0:T(8,128)(2,1)S(1)} %copy-done.2, bf16[1,128,640]{2,1,0:T(8,128)(2,1)S(1)} %copy-done.3, ...), custom_call_target="tpu_custom_call" | custom-call | flops 20000000000 | tf_op jit(solution)/shard_map/mix/pallas_call | solution.py:727
  26.3 0.3 %collective-permute-done.6.gain_rest_ref = f32[1,640]{1,0:T(1,128)S(1)} collective-permute-done((f32[1,640]{1,0:T(1,128)S(1)}, f32[1,640]{1,0:T(1,128)S(1)}, u32[]{:S(2)}, u32[]{:S(2)}) %collective-permute-start.6) | collective-permute-done | bytes 2592 | tf_op jit(solution)/shard_map/ppermute | solution.py:719
  26.6 0.9 %finish.1 = (bf16[1,128,640]{2,1,0:T(8,128)(2,1)}, bf16[1,128,640]{2,1,0:T(8,128)(2,1)}, bf16[1,128,640]{2,1,0:T(8,128)(2,1)}, bf16[1,128,640]{2,1,0:T(8,128)(2,1)}, f32[640]{0:T(1024)}) custom-call(f32[1,640]{1,0:T(1,128)S(1)} %gain.1.gain_ref, f32[1,640]{1,0:T(1,128)S(1)} %collective-permute-done.6.gain_rest_ref, ...), custom_call_target="tpu_custom_call" | custom-call | flops 1000000000 | tf_op jit(solution)/shard_map/finish/pallas_call | solution.py:727
  (12 shorter events, 0.0 us)
Async XLA Ops:
  3.2 5.7 %copy-start.10 = (f32[640]{0:T(1024)S(1)}, f32[640]{0:T(1024)}, u32[]{:S(2)}) copy-start(f32[640]{0:T(1024)} %param.10) | copy-start | bytes 7684
  3.2 8.8 %collective-permute-start = (bf16[352,128]{1,0:T(8,128)(2,1)}, bf16[352,128]{1,0:T(8,128)(2,1)S(1)}, u32[]{:S(2)}, u32[]{:S(2)}) collective-permute-start(bf16[352,128]{1,0:T(8,128)(2,1)} %get-tuple-element.38), channel_id=1, source_target_pairs={{0,12},{4,8},{8,4},{12,0},{1,13},{5,9},{9,5},{13,1},{2,14},{6,10},... | collective-permute-start | bytes 270344 | tf_op jit(solution)/shard_map/ppermute | solution.py:719
  8.3 6.0 %collective-permute-start.1 = (bf16[352,128]{1,0:T(8,128)(2,1)}, bf16[352,128]{1,0:T(8,128)(2,1)S(1)}, u32[]{:S(2)}, u32[]{:S(2)}) collective-permute-start(bf16[352,128]{1,0:T(8,128)(2,1)} %get-tuple-element.39), channel_id=1, source_target_pairs={{0,4},{4,0},{8,12},{12,8},{1,5},{5,1},{9,13},{13,9},{2,6},{6,2},{1... | collective-permute-start | bytes 270344 | tf_op jit(solution)/shard_map/ppermute | solution.py:719
  8.3 7.8 %collective-permute-start.2 = (bf16[352,128]{1,0:T(8,128)(2,1)}, bf16[352,128]{1,0:T(8,128)(2,1)S(1)}, u32[]{:S(2)}, u32[]{:S(2)}) collective-permute-start(bf16[352,128]{1,0:T(8,128)(2,1)} %get-tuple-element.40), channel_id=1, source_target_pairs={{0,8},{4,12},{8,0},{12,4},{1,9},{5,13},{9,1},{13,5},{2,10},{6,14},... | collective-permute-start | bytes 270344 | tf_op jit(solution)/shard_map/ppermute | solution.py:719
  9.0 0.7 %copy-start.4 = (s32[2,5]{1,0:T(2,128)S(1)}, s32[2,5]{1,0:T(2,128)}, u32[]{:S(2)}) copy-start(s32[2,5]{1,0:T(2,128)} %offsets_ref.3) | copy-start | bytes 124
  9.7 0.9 %copy-start = (bf16[1,128,640]{2,1,0:T(8,128)(2,1)S(1)}, bf16[1,128,640]{2,1,0:T(8,128)(2,1)}, u32[]{:S(2)}) copy-start(bf16[1,128,640]{2,1,0:T(8,128)(2,1)} %grad_ref.3) | copy-start | bytes 491524
  10.6 0.9 %copy-start.6 = (bf16[128,640]{1,0:T(8,128)(2,1)S(1)}, bf16[128,640]{1,0:T(8,128)(2,1)}, u32[]{:S(2)}) copy-start(bf16[128,640]{1,0:T(8,128)(2,1)} %get-tuple-element.32.out_ref) | copy-start | bytes 491524
  11.5 4.6 %copy-start.1 = (bf16[1,128,640]{2,1,0:T(8,128)(2,1)S(1)}, bf16[1,128,640]{2,1,0:T(8,128)(2,1)}, u32[]{:S(2)}) copy-start(bf16[1,128,640]{2,1,0:T(8,128)(2,1)} %q_ref.7) | copy-start | bytes 491524
  11.5 4.6 %copy-start.7 = (bf16[128,640]{1,0:T(8,128)(2,1)S(1)}, bf16[128,640]{1,0:T(8,128)(2,1)}, u32[]{:S(2)}) copy-start(bf16[128,640]{1,0:T(8,128)(2,1)} %get-tuple-element.32.out_ref) | copy-start | bytes 491524
  11.5 4.6 %copy-start.8 = (bf16[352,128]{1,0:T(8,128)(2,1)S(1)}, bf16[352,128]{1,0:T(8,128)(2,1)}, u32[]{:S(2)}) copy-start(bf16[352,128]{1,0:T(8,128)(2,1)} %get-tuple-element.37.refs_3_) | copy-start | bytes 270340
  11.9 4.2 %copy-start.9 = (f32[16,128]{1,0:T(8,128)S(1)}, f32[16,128]{1,0:T(8,128)}, u32[]{:S(2)}) copy-start(f32[16,128]{1,0:T(8,128)} %get-tuple-element.34.refs_0_.refs_1_) | copy-start | bytes 24580
  16.1 5.5 %copy-start.2 = (bf16[1,128,640]{2,1,0:T(8,128)(2,1)S(1)}, bf16[1,128,640]{2,1,0:T(8,128)(2,1)}, u32[]{:S(2)}) copy-start(bf16[1,128,640]{2,1,0:T(8,128)(2,1)} %k_ref.5) | copy-start | bytes 491524
  16.1 5.5 %copy-start.3 = (bf16[1,128,640]{2,1,0:T(8,128)(2,1)S(1)}, bf16[1,128,640]{2,1,0:T(8,128)(2,1)}, u32[]{:S(2)}) copy-start(bf16[1,128,640]{2,1,0:T(8,128)(2,1)} %v_ref.5) | copy-start | bytes 491524
  16.2 5.4 %copy-start.5 = (bf16[128,640]{1,0:T(8,128)(2,1)S(1)}, bf16[128,640]{1,0:T(8,128)(2,1)}, u32[]{:S(2)}) copy-start(bf16[128,640]{1,0:T(8,128)(2,1)} %get-tuple-element.45.expo_ref) | copy-start | bytes 491524
  17.1 6.7 %collective-permute-start.3 = (bf16[304,128]{1,0:T(8,128)(2,1)S(1)}, bf16[304,128]{1,0:T(8,128)(2,1)S(1)}, u32[]{:S(2)}, u32[]{:S(2)}) collective-permute-start(bf16[304,128]{1,0:T(8,128)(2,1)S(1)} %get-tuple-element.42), channel_id=1, source_target_pairs={{0,12},{4,8},{8,4},{12,0},{1,13},{5,9},{9,5},{13,1},{2,14},{6,10},... | collective-permute-start | bytes 233480 | tf_op jit(solution)/shard_map/ppermute | solution.py:719
  19.9 5.0 %collective-permute-start.4 = (bf16[304,128]{1,0:T(8,128)(2,1)S(1)}, bf16[304,128]{1,0:T(8,128)(2,1)S(1)}, u32[]{:S(2)}, u32[]{:S(2)}) collective-permute-start(bf16[304,128]{1,0:T(8,128)(2,1)S(1)} %get-tuple-element.43), channel_id=1, source_target_pairs={{0,4},{4,0},{8,12},{12,8},{1,5},{5,1},{9,13},{13,9},{2,6},{6,2},{1... | collective-permute-start | bytes 233480 | tf_op jit(solution)/shard_map/ppermute | solution.py:719
  19.9 5.6 %collective-permute-start.5 = (bf16[304,128]{1,0:T(8,128)(2,1)S(1)}, bf16[304,128]{1,0:T(8,128)(2,1)S(1)}, u32[]{:S(2)}, u32[]{:S(2)}) collective-permute-start(bf16[304,128]{1,0:T(8,128)(2,1)S(1)} %get-tuple-element.44), channel_id=1, source_target_pairs={{0,8},{4,12},{8,0},{12,4},{1,9},{5,13},{9,1},{13,5},{2,10},{6,14},... | collective-permute-start | bytes 233480 | tf_op jit(solution)/shard_map/ppermute | solution.py:719
  25.4 1.2 %collective-permute-start.6 = (f32[1,640]{1,0:T(1,128)S(1)}, f32[1,640]{1,0:T(1,128)S(1)}, u32[]{:S(2)}, u32[]{:S(2)}) collective-permute-start(f32[1,640]{1,0:T(1,128)S(1)} %gain.1.gain_ref), channel_id=1, source_target_pairs={{0,16},{16,0},{1,17},{17,1},{2,18},{18,2},{3,19},{19,3},{4,20},{20... | collective-permute-start | bytes 7688 | tf_op jit(solution)/shard_map/ppermute | solution.py:719

commit v18 on v17

--- a/solution.py
+++ b/solution.py
@@ -229,7 +229,6 @@
 START_ORDER = (3, 1, 2)
 LOW = jnp.bfloat16
 WIDE = jnp.float32
-PACK_VMEM = 65408 * 1024
 PLAIN_VMEM = 16 * 1024 * 1024
 
 
@@ -323,7 +322,21 @@
     return [refs[0], *[by_distance[distance] for distance in range(1, SPAN)]]
 
 
-def pack_kernel(top_step, offsets_ref, q_ref, k_ref, v_ref, grad_ref, *refs):
+def picks_kernel(top_step, offsets_ref, picks_ref):
+    tokens = picks_ref.shape[0]
+    last = offsets_ref.shape[1] - 1
+    for head in range(last + 1):
+        picks_ref[:, head_cols(head)] = pick_matrix(offsets_ref, head, tokens, top_step, 0)
+    key_row = lax.broadcasted_iota(jnp.int32, (tokens, 1), 0)
+    times = 1.0
+    for level, step in ((0, R1), (1, top_step)):
+        offset = offset_of(offsets_ref, level, last)
+        hit_column = jnp.where(key_row % step == offset, 1.0, 0.0)
+        times = times + hit_column * hit_row(offset, step, tokens)
+    picks_ref[:, head_cols(last + 1)] = times.astype(LOW)
+
+
+def pack_kernel(top_step, picks_ref, q_ref, k_ref, v_ref, grad_ref, *refs):
     payload_refs, (expo_ref, out_ref, stats_ref, held_ref) = refs[:SPAN], refs[SPAN:]
     tokens, width = q_ref.shape[1:]
     heads = range(width // HEAD_DIM)
@@ -334,7 +347,7 @@
     q_rows, k_rows, v_rows, grad_rows = [
         [ref[0, :, head_cols(head)] for head in heads] for ref in (q_ref, k_ref, v_ref, grad_ref)
     ]
-    picks = [pick_matrix(offsets_ref, head, tokens, top_step, 0) for head in heads]
+    picks = [picks_ref[:, head_cols(head)] for head in heads]
     scores = [contract(k_rows[head], q_rows[head], 1, 1) * score_scale for head in heads]
     moved = [
         contract(
@@ -353,13 +366,8 @@
     ]
     top_scores = [jnp.max(block, axis=0, keepdims=True) for block in scores]
     expos = [jnp.exp(scores[head] - top_scores[head]) for head in heads]
+    times = picks_ref[:, head_cols(len(heads))].astype(WIDE)
     for head in heads[OWNED:]:
-        key_row = lax.broadcasted_iota(jnp.int32, (tokens, 1), 0)
-        times = 1.0
-        for level, step in ((0, R1), (1, top_step)):
-            offset = offset_of(offsets_ref, level, head)
-            hit_column = jnp.where(key_row % step == offset, 1.0, 0.0)
-            times = times + hit_column * hit_row(offset, step, tokens)
         expos[head] = times * expos[head]
     expo_lows = [expo.astype(LOW) for expo in expos]
     outs = [contract(v_rows[head], expo_lows[head], 0, 0) for head in heads]
@@ -753,13 +761,15 @@
     answer = shape((6 * picked + STAT_TILES, HEAD_DIM), LOW)
     bind = functools.partial
     gain_row = out_gain.reshape(1, width)
+    (picks,) = call(
+        bind(picks_kernel, top_step), "picks", (offsets,), [shape((tokens, width + tokens), LOW)], 20
+    )
     own, *sent, expo, base_out, stats = call(
         bind(pack_kernel, top_step),
         "pack",
-        (offsets, queries, keys, values, grad_y),
+        (picks, queries, keys, values, grad_y),
         [payload] * SPAN + [low_block, low_block, stats_block],
         1,
-        vmem=PACK_VMEM,
         scratch=[pltpu.VMEM((OWNED, *payload.shape), LOW)],
     )
     received = to_peers(sent)

time: 27.7 us -> 26.7 us (0.964)
  Pallas kernels: 6.01 us -> 4.17 us
  waiting for transfers between devices: 7.99 us -> 9.65 us
  local copies, waits for them, and re-layouts: 2.55 us -> 1.66 us
    pallas_call x7 -> x8, Pallas kernels: 6.01 us -> 4.17 us  [call(): pl.pallas_call(kernel, out_shape=results, in_specs=[VMEM_SPEC] * len(oper...]
    ppermute x7, waiting for transfers between devices: 7.99 us -> 9.65 us  [across(): return lax.ppermute(block, axis, route)]
    unnamed x22 -> x14, local copies, waits for them, and re-layouts: 2.55 us -> 1.66 us
where the time goes in v18:
time: 26.7 us; the launch traced here: 26.5 us
  starting transfers between devices  10.3 us (39%)
  waiting for transfers between devices  9.65 us (36%)
  Pallas kernels  4.17 us (16%)
  local copies, waits for them, and re-layouts  1.66 us (6%)
  between operations  0.74 us (3%)
    ppermute x7, starting transfers between devices, across(): return lax.ppermute(block, axis, route)  10.3 us
    ppermute x7, waiting for transfers between devices, across(): return lax.ppermute(block, axis, route)  9.65 us
    pallas_call x8, Pallas kernels, call(): pl.pallas_call(kernel, out_shape=results, in_specs=[VMEM_SPEC] * len(oper...  4.17 us
    unnamed x14, local copies, waits for them, and re-layouts  1.66 us
  transfers between devices with their start and end apart: 7, of which 7 were waited for; matrix products, arithmetic and copies ran while one was open for 0% of the time, Pallas kernels for 6%

profile of v18, /device:TPU:0, one launch (start us, length us, event | category | flops | bytes accessed | tf_op | source)
XLA Modules:
  0.0 26.5 jit_solution(13661904233183146302)
XLA Ops:
  0.6 0.0 copy-start.1
  0.6 0.0 copy-start.3
  0.7 0.0 copy-start.2
  0.7 0.0 copy-start.4
  0.7 0.7 %copy-done.4 = s32[2,5]{1,0:T(2,128)S(1)} copy-done((s32[2,5]{1,0:T(2,128)S(1)}, s32[2,5]{1,0:T(2,128)}, u32[]{:S(2)}) %copy-start.4) | copy-done | bytes 64
  1.4 0.1 picks.1.picks_ref
  1.6 0.0 copy-done.1
  1.6 0.1 copy-done.3
  1.6 0.1 copy-done.2
  1.7 0.1 copy-done
  1.8 0.7 %pack.1 = (bf16[352,128]{1,0:T(8,128)(2,1)S(1)}, bf16[352,128]{1,0:T(8,128)(2,1)S(1)}, bf16[352,128]{1,0:T(8,128)(2,1)S(1)}, bf16[352,128]{1,0:T(8,128)(2,1)S(1)...) custom-call(bf16[128,768]{1,0:T(8,128)(2,1)S(1)} %picks.1.picks_ref, ...), custom_call_target="tpu_custom_call" | custom-call | flops 1000000000 | tf_op jit(solution)/shard_map/pack/pallas_call | solution.py:735
  2.5 0.0 copy-start.6
  2.5 5.1 %collective-permute-start = (bf16[352,128]{1,0:T(8,128)(2,1)S(1)}, bf16[352,128]{1,0:T(8,128)(2,1)S(1)}, u32[]{:S(2)}, u32[]{:S(2)}) collective-permute-start(bf16[352,128]{1,0:T(8,128)(2,1)S(1)} %get-tuple-element.38), channel_id=1, source_target_pairs={{0,12},{4,8},{8,4},{12,0},{1,13},{5,9},{9,5},{13,1},{2,14},{6,10},... | collective-permute-start | bytes 270344 | tf_op jit(solution)/shard_map/ppermute | solution.py:727
  7.6 0.0 collective-permute-start.1
  7.6 0.6 %collective-permute-start.2 = (bf16[352,128]{1,0:T(8,128)(2,1)S(1)}, bf16[352,128]{1,0:T(8,128)(2,1)S(1)}, u32[]{:S(2)}, u32[]{:S(2)}) collective-permute-start(bf16[352,128]{1,0:T(8,128)(2,1)S(1)} %get-tuple-element.40), channel_id=1, source_target_pairs={{0,8},{4,12},{8,0},{12,4},{1,9},{5,13},{9,1},{13,5},{2,10},{6,14},... | collective-permute-start | bytes 270344 | tf_op jit(solution)/shard_map/ppermute | solution.py:727
  8.3 0.7 %copy-done.5 = s32[2,5]{1,0:T(2,128)S(1)} copy-done((s32[2,5]{1,0:T(2,128)S(1)}, s32[2,5]{1,0:T(2,128)}, u32[]{:S(2)}) %copy-start.5) | copy-done | bytes 64
  8.9 0.4 %prepare.1 = (f32[128,640]{1,0:T(8,128)S(1)}, f32[1,640]{1,0:T(1,128)S(1)}, bf16[128,1280]{1,0:T(8,128)(2,1)S(1)}, f32[16,256]{1,0:T(8,128)S(1)}) custom-call(s32[2,5]{1,0:T(2,128)S(1)} %copy-done.5, bf16[1,128,640]{2,1,0:T(8,128)(2,1)S(1)} %copy-done, f32[1,640]{1,0:T(1,128)S(1)} %reshape.13.gain_ref, bf16[128,640]{1,0:T(8,128)(2,1)S(1)} %get-tuple-element.32.out_ref), custom_call_target="tpu_custom_call" | custom-call | flops 2000000000 | tf_op jit(solution)/shard_map/prepare/pallas_call | solution.py:735
  9.3 1.8 %collective-permute-done.refs_4_ = bf16[352,128]{1,0:T(8,128)(2,1)S(1)} collective-permute-done((bf16[352,128]{1,0:T(8,128)(2,1)S(1)}, bf16[352,128]{1,0:T(8,128)(2,1)S(1)}, u32[]{:S(2)}, u32[]{:S(2)}) %collective-permute-start) | collective-permute-done | bytes 90144 | tf_op jit(solution)/shard_map/ppermute | solution.py:727
  11.1 2.2 %collective-permute-done.1.refs_5_ = bf16[352,128]{1,0:T(8,128)(2,1)S(1)} collective-permute-done((bf16[352,128]{1,0:T(8,128)(2,1)S(1)}, bf16[352,128]{1,0:T(8,128)(2,1)S(1)}, u32[]{:S(2)}, u32[]{:S(2)}) %collective-permute-start.1) | collective-permute-done | bytes 90144 | tf_op jit(solution)/shard_map/ppermute | solution.py:727
  13.4 1.8 %collective-permute-done.2.refs_6_ = bf16[352,128]{1,0:T(8,128)(2,1)S(1)} collective-permute-done((bf16[352,128]{1,0:T(8,128)(2,1)S(1)}, bf16[352,128]{1,0:T(8,128)(2,1)S(1)}, u32[]{:S(2)}, u32[]{:S(2)}) %collective-permute-start.2) | collective-permute-done | bytes 90144 | tf_op jit(solution)/shard_map/ppermute | solution.py:727
  15.2 1.0 %owner.1 = (f32[128,128]{1,0:T(8,128)S(1)}, bf16[128,128]{1,0:T(8,128)(2,1)S(1)}, bf16[144,128]{1,0:T(8,128)(2,1)S(1)}, f32[8,128]{1,0:T(8,128)S(1)}, bf16[304,1...) custom-call(bf16[1,128,640]{2,1,0:T(8,128)(2,1)S(1)} %copy-done.1, ...), custom_call_target="tpu_custom_call" | custom-call | flops 3000000000 | tf_op jit(solution)/shard_map/owner/pallas_call | solution.py:735
  16.1 2.7 %collective-permute-start.3 = (bf16[304,128]{1,0:T(8,128)(2,1)S(1)}, bf16[304,128]{1,0:T(8,128)(2,1)S(1)}, u32[]{:S(2)}, u32[]{:S(2)}) collective-permute-start(bf16[304,128]{1,0:T(8,128)(2,1)S(1)} %get-tuple-element.42), channel_id=1, source_target_pairs={{0,12},{4,8},{8,4},{12,0},{1,13},{5,9},{9,5},{13,1},{2,14},{6,10},... | collective-permute-start | bytes 233480 | tf_op jit(solution)/shard_map/ppermute | solution.py:727
  18.8 0.0 collective-permute-start.4
  18.8 1.7 %collective-permute-start.5 = (bf16[304,128]{1,0:T(8,128)(2,1)S(1)}, bf16[304,128]{1,0:T(8,128)(2,1)S(1)}, u32[]{:S(2)}, u32[]{:S(2)}) collective-permute-start(bf16[304,128]{1,0:T(8,128)(2,1)S(1)} %get-tuple-element.44), channel_id=1, source_target_pairs={{0,8},{4,12},{8,0},{12,4},{1,9},{5,13},{9,1},{13,5},{2,10},{6,14},... | collective-permute-start | bytes 233480 | tf_op jit(solution)/shard_map/ppermute | solution.py:727
  20.6 0.3 %last_head.1 = (bf16[128,128]{1,0:T(8,128)(2,1)S(1)}, bf16[128,128]{1,0:T(8,128)(2,1)S(1)}, f32[128,128]{1,0:T(8,128)S(1)}, f32[128,128]{1,0:T(8,128)S(1)}) custom-call(bf16[1,128,640]{2,1,0:T(8,128)(2,1)S(1)} %copy-done.1, bf16[1,128,640]{2,1,0:T(8,128)(2,1)S(1)} %copy-done.2, bf16[1,128,640]{2,1,0:T(8,128)(2,1)S(1)} %copy-done.3, ...), custom_call_target="tpu_custom_call" | custom-call | flops 20000000000 | tf_op jit(solution)/shard_map/last_head/pallas_call | solution.py:735
  20.9 1.9 %collective-permute-done.3.refs_1_.refs_9_ = bf16[304,128]{1,0:T(8,128)(2,1)S(1)} collective-permute-done((bf16[304,128]{1,0:T(8,128)(2,1)S(1)}, bf16[304,128]{1,0:T(8,128)(2,1)S(1)}, u32[]{:S(2)}, u32[]{:S(2)}) %collective-permute-start.3) | collective-permute-done | bytes 77856 | tf_op jit(solution)/shard_map/ppermute | solution.py:727
  22.8 1.0 %collective-permute-done.4.refs_2_.refs_10_ = bf16[304,128]{1,0:T(8,128)(2,1)S(1)} collective-permute-done((bf16[304,128]{1,0:T(8,128)(2,1)S(1)}, bf16[304,128]{1,0:T(8,128)(2,1)S(1)}, u32[]{:S(2)}, u32[]{:S(2)}) %collective-permute-start.4) | collective-permute-done | bytes 77856 | tf_op jit(solution)/shard_map/ppermute | solution.py:727
  23.8 0.6 %collective-permute-done.5.refs_3_.refs_11_ = bf16[304,128]{1,0:T(8,128)(2,1)S(1)} collective-permute-done((bf16[304,128]{1,0:T(8,128)(2,1)S(1)}, bf16[304,128]{1,0:T(8,128)(2,1)S(1)}, u32[]{:S(2)}, u32[]{:S(2)}) %collective-permute-start.5) | collective-permute-done | bytes 77856 | tf_op jit(solution)/shard_map/ppermute | solution.py:727
  24.4 0.1 collective-permute-start.6
  24.5 0.8 %mix.1 = (bf16[128,640]{1,0:T(8,128)(2,1)S(1)}, bf16[128,640]{1,0:T(8,128)(2,1)S(1)}, bf16[128,640]{1,0:T(8,128)(2,1)S(1)}, bf16[128,640]{1,0:T(8,128)(2,1)S(1)}) custom-call(bf16[1,128,640]{2,1,0:T(8,128)(2,1)S(1)} %copy-done.1, bf16[1,128,640]{2,1,0:T(8,128)(2,1)S(1)} %copy-done.2, bf16[1,128,640]{2,1,0:T(8,128)(2,1)S(1)} %copy-done.3, ...), custom_call_target="tpu_custom_call" | custom-call | flops 20000000000 | tf_op jit(solution)/shard_map/mix/pallas_call | solution.py:735
  25.3 0.3 %collective-permute-done.6.gain_rest_ref = f32[1,640]{1,0:T(1,128)S(1)} collective-permute-done((f32[1,640]{1,0:T(1,128)S(1)}, f32[1,640]{1,0:T(1,128)S(1)}, u32[]{:S(2)}, u32[]{:S(2)}) %collective-permute-start.6) | collective-permute-done | bytes 2592 | tf_op jit(solution)/shard_map/ppermute | solution.py:727
  25.6 0.9 %finish.1 = (bf16[1,128,640]{2,1,0:T(8,128)(2,1)}, bf16[1,128,640]{2,1,0:T(8,128)(2,1)}, bf16[1,128,640]{2,1,0:T(8,128)(2,1)}, bf16[1,128,640]{2,1,0:T(8,128)(2,1)}, f32[640]{0:T(1024)}) custom-call(f32[1,640]{1,0:T(1,128)S(1)} %gain.1.gain_ref, f32[1,640]{1,0:T(1,128)S(1)} %collective-permute-done.6.gain_rest_ref, ...), custom_call_target="tpu_custom_call" | custom-call | flops 1000000000 | tf_op jit(solution)/shard_map/finish/pallas_call | solution.py:735
  (5 shorter events, 0.0 us)
Async XLA Ops:
  0.6 0.9 %copy-start.1 = (bf16[1,128,640]{2,1,0:T(8,128)(2,1)S(1)}, bf16[1,128,640]{2,1,0:T(8,128)(2,1)}, u32[]{:S(2)}) copy-start(bf16[1,128,640]{2,1,0:T(8,128)(2,1)} %q_ref.7) | copy-start | bytes 491524
  0.6 1.0 %copy-start.3 = (bf16[1,128,640]{2,1,0:T(8,128)(2,1)S(1)}, bf16[1,128,640]{2,1,0:T(8,128)(2,1)}, u32[]{:S(2)}) copy-start(bf16[1,128,640]{2,1,0:T(8,128)(2,1)} %v_ref.5) | copy-start | bytes 491524
  0.7 1.1 %copy-start.2 = (bf16[1,128,640]{2,1,0:T(8,128)(2,1)S(1)}, bf16[1,128,640]{2,1,0:T(8,128)(2,1)}, u32[]{:S(2)}) copy-start(bf16[1,128,640]{2,1,0:T(8,128)(2,1)} %k_ref.5) | copy-start | bytes 491524
  0.7 1.1 %copy-start = (bf16[1,128,640]{2,1,0:T(8,128)(2,1)S(1)}, bf16[1,128,640]{2,1,0:T(8,128)(2,1)}, u32[]{:S(2)}) copy-start(bf16[1,128,640]{2,1,0:T(8,128)(2,1)} %grad_ref.3) | copy-start | bytes 491524
  0.7 0.7 %copy-start.4 = (s32[2,5]{1,0:T(2,128)S(1)}, s32[2,5]{1,0:T(2,128)}, u32[]{:S(2)}) copy-start(s32[2,5]{1,0:T(2,128)} %offsets_ref.3) | copy-start | bytes 124
  2.5 5.8 %copy-start.6 = (f32[640]{0:T(1024)S(1)}, f32[640]{0:T(1024)}, u32[]{:S(2)}) copy-start(f32[640]{0:T(1024)} %param.10) | copy-start | bytes 7684
  2.5 8.7 %collective-permute-start = (bf16[352,128]{1,0:T(8,128)(2,1)S(1)}, bf16[352,128]{1,0:T(8,128)(2,1)S(1)}, u32[]{:S(2)}, u32[]{:S(2)}) collective-permute-start(bf16[352,128]{1,0:T(8,128)(2,1)S(1)} %get-tuple-element.38), channel_id=1, source_target_pairs={{0,12},{4,8},{8,4},{12,0},{1,13},{5,9},{9,5},{13,1},{2,14},{6,10},... | collective-permute-start | bytes 270344 | tf_op jit(solution)/shard_map/ppermute | solution.py:727
  7.6 5.8 %collective-permute-start.1 = (bf16[352,128]{1,0:T(8,128)(2,1)S(1)}, bf16[352,128]{1,0:T(8,128)(2,1)S(1)}, u32[]{:S(2)}, u32[]{:S(2)}) collective-permute-start(bf16[352,128]{1,0:T(8,128)(2,1)S(1)} %get-tuple-element.39), channel_id=1, source_target_pairs={{0,4},{4,0},{8,12},{12,8},{1,5},{5,1},{9,13},{13,9},{2,6},{6,2},{1... | collective-permute-start | bytes 270344 | tf_op jit(solution)/shard_map/ppermute | solution.py:727
  7.6 7.6 %collective-permute-start.2 = (bf16[352,128]{1,0:T(8,128)(2,1)S(1)}, bf16[352,128]{1,0:T(8,128)(2,1)S(1)}, u32[]{:S(2)}, u32[]{:S(2)}) collective-permute-start(bf16[352,128]{1,0:T(8,128)(2,1)S(1)} %get-tuple-element.40), channel_id=1, source_target_pairs={{0,8},{4,12},{8,0},{12,4},{1,9},{5,13},{9,1},{13,5},{2,10},{6,14},... | collective-permute-start | bytes 270344 | tf_op jit(solution)/shard_map/ppermute | solution.py:727
  8.3 0.7 %copy-start.5 = (s32[2,5]{1,0:T(2,128)S(1)}, s32[2,5]{1,0:T(2,128)}, u32[]{:S(2)}) copy-start(s32[2,5]{1,0:T(2,128)} %offsets_ref.3) | copy-start | bytes 124
  16.1 6.7 %collective-permute-start.3 = (bf16[304,128]{1,0:T(8,128)(2,1)S(1)}, bf16[304,128]{1,0:T(8,128)(2,1)S(1)}, u32[]{:S(2)}, u32[]{:S(2)}) collective-permute-start(bf16[304,128]{1,0:T(8,128)(2,1)S(1)} %get-tuple-element.42), channel_id=1, source_target_pairs={{0,12},{4,8},{8,4},{12,0},{1,13},{5,9},{9,5},{13,1},{2,14},{6,10},... | collective-permute-start | bytes 233480 | tf_op jit(solution)/shard_map/ppermute | solution.py:727
  18.8 5.0 %collective-permute-start.4 = (bf16[304,128]{1,0:T(8,128)(2,1)S(1)}, bf16[304,128]{1,0:T(8,128)(2,1)S(1)}, u32[]{:S(2)}, u32[]{:S(2)}) collective-permute-start(bf16[304,128]{1,0:T(8,128)(2,1)S(1)} %get-tuple-element.43), channel_id=1, source_target_pairs={{0,4},{4,0},{8,12},{12,8},{1,5},{5,1},{9,13},{13,9},{2,6},{6,2},{1... | collective-permute-start | bytes 233480 | tf_op jit(solution)/shard_map/ppermute | solution.py:727
  18.8 5.5 %collective-permute-start.5 = (bf16[304,128]{1,0:T(8,128)(2,1)S(1)}, bf16[304,128]{1,0:T(8,128)(2,1)S(1)}, u32[]{:S(2)}, u32[]{:S(2)}) collective-permute-start(bf16[304,128]{1,0:T(8,128)(2,1)S(1)} %get-tuple-element.44), channel_id=1, source_target_pairs={{0,8},{4,12},{8,0},{12,4},{1,9},{5,13},{9,1},{13,5},{2,10},{6,14},... | collective-permute-start | bytes 233480 | tf_op jit(solution)/shard_map/ppermute | solution.py:727
  24.4 1.2 %collective-permute-start.6 = (f32[1,640]{1,0:T(1,128)S(1)}, f32[1,640]{1,0:T(1,128)S(1)}, u32[]{:S(2)}, u32[]{:S(2)}) collective-permute-start(f32[1,640]{1,0:T(1,128)S(1)} %gain.1.gain_ref), channel_id=1, source_target_pairs={{0,16},{16,0},{1,17},{17,1},{2,18},{18,2},{3,19},{19,3},{4,20},{20... | collective-permute-start | bytes 7688 | tf_op jit(solution)/shard_map/ppermute | solution.py:727

commit v19 on v18

--- a/solution.py
+++ b/solution.py
@@ -337,7 +337,7 @@
 
 
 def pack_kernel(top_step, picks_ref, q_ref, k_ref, v_ref, grad_ref, *refs):
-    payload_refs, (expo_ref, out_ref, stats_ref, held_ref) = refs[:SPAN], refs[SPAN:]
+    payload_refs, held_ref = refs[:SPAN], refs[SPAN]
     tokens, width = q_ref.shape[1:]
     heads = range(width // HEAD_DIM)
     owned = range(OWNED)
@@ -348,7 +348,7 @@
         [ref[0, :, head_cols(head)] for head in heads] for ref in (q_ref, k_ref, v_ref, grad_ref)
     ]
     picks = [picks_ref[:, head_cols(head)] for head in heads]
-    scores = [contract(k_rows[head], q_rows[head], 1, 1) * score_scale for head in heads]
+    scores = [contract(k_rows[head], q_rows[head], 1, 1) * score_scale for head in owned]
     moved = [
         contract(
             picks[head][:picked],
@@ -365,25 +365,14 @@
         for head in heads[OWNED:]
     ]
     top_scores = [jnp.max(block, axis=0, keepdims=True) for block in scores]
-    expos = [jnp.exp(scores[head] - top_scores[head]) for head in heads]
-    times = picks_ref[:, head_cols(len(heads))].astype(WIDE)
-    for head in heads[OWNED:]:
-        expos[head] = times * expos[head]
+    expos = [jnp.exp(scores[head] - top_scores[head]) for head in owned]
     expo_lows = [expo.astype(LOW) for expo in expos]
-    outs = [contract(v_rows[head], expo_lows[head], 0, 0) for head in heads]
+    outs = [contract(v_rows[head], expo_lows[head], 0, 0) for head in owned]
     totals = [jnp.sum(expo, axis=0, keepdims=True) for expo in expos]
-    for head in heads:
-        expo_ref[:, head_cols(head)] = expo_lows[head]
-        stats_ref[head : head + 1, :] = top_scores[head]
-        stats_ref[TILE + head : TILE + head + 1, :] = totals[head]
-    for head in owned:
-        outs[head] = outs[head] * (1.0 / totals[head])
-    outs = [out.astype(LOW) for out in outs]
+    outs = [(outs[head] * (1.0 / totals[head])).astype(LOW) for head in owned]
     picked_outs = [
         contract(picks[head][:picked], outs[head], 1, 1).astype(LOW) for head in owned
     ]
-    for head in heads:
-        out_ref[:, head_cols(head)] = outs[head]
     for head in owned:
         pieces = piece_rows(top_scores[head] + jnp.log(totals[head])).astype(LOW)
         stat_rows = contract(pieces, picks[head], 1, 1)
@@ -396,10 +385,31 @@
         payload_ref[...] = held_ref[me ^ distance]
 
 
-def prepare_kernel(top_step, offsets_ref, grad_ref, gain_ref, out_ref, *refs):
-    grad_norm_ref, gain_part_ref, place_ref, masks_ref = refs
+def prepare_kernel(top_step, offsets_ref, q_ref, k_ref, v_ref, grad_ref, gain_ref, *refs):
+    picks_ref, grad_norm_ref, gain_part_ref, place_ref, masks_ref, expo_ref, out_ref, stats_ref = refs
     tokens, width = grad_ref.shape[1:]
     heads = range(width // HEAD_DIM)
+    score_scale = 1.0 / math.sqrt(HEAD_DIM)
+    every = [head_cols(head) for head in heads]
+    scores = [
+        contract(k_ref[0, :, cols], q_ref[0, :, cols], 1, 1) * score_scale for cols in every
+    ]
+    top_scores = [jnp.max(block, axis=0, keepdims=True) for block in scores]
+    expos = [jnp.exp(scores[head] - top_scores[head]) for head in heads]
+    times = picks_ref[:, head_cols(len(heads))].astype(WIDE)
+    for head in heads[OWNED:]:
+        expos[head] = times * expos[head]
+    expo_lows = [expo.astype(LOW) for expo in expos]
+    outs = [contract(v_ref[0, :, cols], expo_lows[head], 0, 0) for head, cols in enumerate(every)]
+    totals = [jnp.sum(expo, axis=0, keepdims=True) for expo in expos]
+    for head in range(OWNED):
+        outs[head] = outs[head] * (1.0 / totals[head])
+    outs = [out.astype(LOW) for out in outs]
+    for head, cols in enumerate(every):
+        expo_ref[:, cols] = expo_lows[head]
+        out_ref[:, cols] = outs[head]
+        stats_ref[head : head + 1, :] = top_scores[head]
+        stats_ref[TILE + head : TILE + head + 1, :] = totals[head]
     top_rows = tokens // top_step
     ones = jnp.ones((TILE, tokens), LOW)
     column = lax.broadcasted_iota(jnp.int32, (tokens, tokens), 1)
@@ -442,7 +452,7 @@
             hit_row(top_offset, top_step, tokens), hit_row(mid_offset, R1, tokens)
         )
         masks_ref[TILE + head : TILE + head + 1, :tokens] = seen
-        attn = out_ref[:, cols].astype(WIDE)
+        attn = outs[head].astype(WIDE)
         normed = attn * lax.rsqrt(column_mean(attn * attn) + EPS)
         product = grad_norms[head] * normed * (1.0 - seen)
         gain_part_ref[:, cols] = gain_row_of(ones, product) / gain_ref[:, cols]
@@ -764,24 +774,27 @@
     (picks,) = call(
         bind(picks_kernel, top_step), "picks", (offsets,), [shape((tokens, width + tokens), LOW)], 20
     )
-    own, *sent, expo, base_out, stats = call(
+    own, *sent = call(
         bind(pack_kernel, top_step),
         "pack",
         (picks, queries, keys, values, grad_y),
-        [payload] * SPAN + [low_block, low_block, stats_block],
+        [payload] * SPAN,
         1,
         scratch=[pltpu.VMEM((OWNED, *payload.shape), LOW)],
     )
     received = to_peers(sent)
-    grad_norm, gain_base, place, masks = call(
+    grad_norm, gain_base, place, masks, expo, base_out, stats = call(
         bind(prepare_kernel, top_step),
         "prepare",
-        (offsets, grad_y, gain_row, base_out),
+        (offsets, queries, keys, values, grad_y, gain_row, picks),
         [
             wide_block,
             gain_block,
             shape((tokens, 2 * width), LOW),
             shape((2 * TILE, 2 * tokens), WIDE),
+            low_block,
+            low_block,
+            stats_block,
         ],
         2,
     )

time: 26.7 us -> 26.7 us (level)
  local copies, waits for them, and re-layouts: 1.66 us -> 1.01 us
  waiting for transfers between devices: 9.65 us -> 9.99 us
  Pallas kernels: 4.17 us -> 4.49 us
    unnamed x14, local copies, waits for them, and re-layouts: 1.66 us -> 1.01 us
    ppermute x7, waiting for transfers between devices: 9.65 us -> 9.99 us  [across(): return lax.ppermute(block, axis, route)]
    pallas_call x8, Pallas kernels: 4.17 us -> 4.49 us  [call(): pl.pallas_call(kernel, out_shape=results, in_specs=[VMEM_SPEC] * len(oper...]
  transfers between devices with their start and end apart: 7 -> 7, of which waited for: 7 -> 7; matrix products, arithmetic and copies ran while one was open for 0% -> 0% of each run, Pallas kernels for 6% -> 7%
where the time goes in v19:
time: 26.7 us; the launch traced here: 26.5 us
  starting transfers between devices  10.3 us (39%)
  waiting for transfers between devices  9.99 us (37%)
  Pallas kernels  4.49 us (17%)
  local copies, waits for them, and re-layouts  1.01 us (4%)
  between operations  0.74 us (3%)
    ppermute x7, starting transfers between devices, across(): return lax.ppermute(block, axis, route)  10.3 us
    ppermute x7, waiting for transfers between devices, across(): return lax.ppermute(block, axis, route)  9.99 us
    pallas_call x8, Pallas kernels, call(): pl.pallas_call(kernel, out_shape=results, in_specs=[VMEM_SPEC] * len(oper...  4.49 us
    unnamed x14, local copies, waits for them, and re-layouts  1.01 us
  transfers between devices with their start and end apart: 7, of which 7 were waited for; matrix products, arithmetic and copies ran while one was open for 0% of the time, Pallas kernels for 7%

profile of v19, /device:TPU:0, one launch (start us, length us, event | category | flops | bytes accessed | tf_op | source)
XLA Modules:
  0.0 26.5 jit_solution(3770369348725842472)
XLA Ops:
  0.6 0.0 copy-start.1
  0.6 0.0 copy-start.3
  0.7 0.0 copy-start.2
  0.7 0.0 copy-start.4
  0.7 0.7 %copy-done.4 = s32[2,5]{1,0:T(2,128)S(1)} copy-done((s32[2,5]{1,0:T(2,128)S(1)}, s32[2,5]{1,0:T(2,128)}, u32[]{:S(2)}) %copy-start.4) | copy-done | bytes 64
  1.4 0.1 picks.1.refs_0_.picks_ref
  1.6 0.0 copy-done.1
  1.6 0.1 copy-done.3
  1.6 0.1 copy-done.2
  1.7 0.1 copy-done
  1.8 0.7 %pack.1 = (bf16[352,128]{1,0:T(8,128)(2,1)S(1)}, bf16[352,128]{1,0:T(8,128)(2,1)S(1)}, bf16[352,128]{1,0:T(8,128)(2,1)S(1)}, bf16[352,128]{1,0:T(8,128)(2,1)S(1)}) custom-call(bf16[128,768]{1,0:T(8,128)(2,1)S(1)} %picks.1.refs_0_.picks_ref, bf16[1,128,640]{2,1,0:T(8,128)(2,1)S(1)} %copy-done.1, bf16[1,128,640]{2,1,0:T(8,128)(2,1)S(1)} %copy-done.2, ...), custom_call_target="tpu_custom_call" | custom-call | flops 1000000000 | tf_op jit(solution)/shard_map/pack/pallas_call | solution.py:745
  2.5 0.0 copy-start.6
  2.5 5.1 %collective-permute-start = (bf16[352,128]{1,0:T(8,128)(2,1)S(1)}, bf16[352,128]{1,0:T(8,128)(2,1)S(1)}, u32[]{:S(2)}, u32[]{:S(2)}) collective-permute-start(bf16[352,128]{1,0:T(8,128)(2,1)S(1)} %get-tuple-element.38), channel_id=1, source_target_pairs={{0,12},{4,8},{8,4},{12,0},{1,13},{5,9},{9,5},{13,1},{2,14},{6,10},... | collective-permute-start | bytes 270344 | tf_op jit(solution)/shard_map/ppermute | solution.py:737
  7.6 0.0 collective-permute-start.1
  7.6 0.6 %collective-permute-start.2 = (bf16[352,128]{1,0:T(8,128)(2,1)S(1)}, bf16[352,128]{1,0:T(8,128)(2,1)S(1)}, u32[]{:S(2)}, u32[]{:S(2)}) collective-permute-start(bf16[352,128]{1,0:T(8,128)(2,1)S(1)} %get-tuple-element.40), channel_id=1, source_target_pairs={{0,8},{4,12},{8,0},{12,4},{1,9},{5,13},{9,1},{13,5},{2,10},{6,14},... | collective-permute-start | bytes 270344 | tf_op jit(solution)/shard_map/ppermute | solution.py:737
  8.2 0.0 copy-done.5
  8.3 0.7 %prepare.1 = (f32[128,640]{1,0:T(8,128)S(1)}, f32[1,640]{1,0:T(1,128)S(1)}, bf16[128,1280]{1,0:T(8,128)(2,1)S(1)}, f32[16,256]{1,0:T(8,128)S(1)}, bf16[128,640]{...) custom-call(s32[2,5]{1,0:T(2,128)S(1)} %copy-done.5, bf16[1,128,640]{2,1,0:T(8,128)(2,1)S(1)} %copy-done.1, ...), custom_call_target="tpu_custom_call" | custom-call | flops 2000000000 | tf_op jit(solution)/shard_map/prepare/pallas_call | solution.py:745
  9.0 2.1 %collective-permute-done.refs_4_ = bf16[352,128]{1,0:T(8,128)(2,1)S(1)} collective-permute-done((bf16[352,128]{1,0:T(8,128)(2,1)S(1)}, bf16[352,128]{1,0:T(8,128)(2,1)S(1)}, u32[]{:S(2)}, u32[]{:S(2)}) %collective-permute-start) | collective-permute-done | bytes 90144 | tf_op jit(solution)/shard_map/ppermute | solution.py:737
  11.1 2.2 %collective-permute-done.1.refs_5_ = bf16[352,128]{1,0:T(8,128)(2,1)S(1)} collective-permute-done((bf16[352,128]{1,0:T(8,128)(2,1)S(1)}, bf16[352,128]{1,0:T(8,128)(2,1)S(1)}, u32[]{:S(2)}, u32[]{:S(2)}) %collective-permute-start.1) | collective-permute-done | bytes 90144 | tf_op jit(solution)/shard_map/ppermute | solution.py:737
  13.4 1.8 %collective-permute-done.2.refs_6_ = bf16[352,128]{1,0:T(8,128)(2,1)S(1)} collective-permute-done((bf16[352,128]{1,0:T(8,128)(2,1)S(1)}, bf16[352,128]{1,0:T(8,128)(2,1)S(1)}, u32[]{:S(2)}, u32[]{:S(2)}) %collective-permute-start.2) | collective-permute-done | bytes 90144 | tf_op jit(solution)/shard_map/ppermute | solution.py:737
  15.2 1.0 %owner.1 = (f32[128,128]{1,0:T(8,128)S(1)}, bf16[128,128]{1,0:T(8,128)(2,1)S(1)}, bf16[144,128]{1,0:T(8,128)(2,1)S(1)}, f32[8,128]{1,0:T(8,128)S(1)}, bf16[304,1...) custom-call(bf16[1,128,640]{2,1,0:T(8,128)(2,1)S(1)} %copy-done.1, ...), custom_call_target="tpu_custom_call" | custom-call | flops 3000000000 | tf_op jit(solution)/shard_map/owner/pallas_call | solution.py:745
  16.1 2.7 %collective-permute-start.3 = (bf16[304,128]{1,0:T(8,128)(2,1)S(1)}, bf16[304,128]{1,0:T(8,128)(2,1)S(1)}, u32[]{:S(2)}, u32[]{:S(2)}) collective-permute-start(bf16[304,128]{1,0:T(8,128)(2,1)S(1)} %get-tuple-element.42), channel_id=1, source_target_pairs={{0,12},{4,8},{8,4},{12,0},{1,13},{5,9},{9,5},{13,1},{2,14},{6,10},... | collective-permute-start | bytes 233480 | tf_op jit(solution)/shard_map/ppermute | solution.py:737
  18.8 0.0 collective-permute-start.4
  18.8 1.7 %collective-permute-start.5 = (bf16[304,128]{1,0:T(8,128)(2,1)S(1)}, bf16[304,128]{1,0:T(8,128)(2,1)S(1)}, u32[]{:S(2)}, u32[]{:S(2)}) collective-permute-start(bf16[304,128]{1,0:T(8,128)(2,1)S(1)} %get-tuple-element.44), channel_id=1, source_target_pairs={{0,8},{4,12},{8,0},{12,4},{1,9},{5,13},{9,1},{13,5},{2,10},{6,14},... | collective-permute-start | bytes 233480 | tf_op jit(solution)/shard_map/ppermute | solution.py:737
  20.6 0.3 %last_head.1 = (bf16[128,128]{1,0:T(8,128)(2,1)S(1)}, bf16[128,128]{1,0:T(8,128)(2,1)S(1)}, f32[128,128]{1,0:T(8,128)S(1)}, f32[128,128]{1,0:T(8,128)S(1)}) custom-call(bf16[1,128,640]{2,1,0:T(8,128)(2,1)S(1)} %copy-done.1, bf16[1,128,640]{2,1,0:T(8,128)(2,1)S(1)} %copy-done.2, bf16[1,128,640]{2,1,0:T(8,128)(2,1)S(1)} %copy-done.3, ...), custom_call_target="tpu_custom_call" | custom-call | flops 20000000000 | tf_op jit(solution)/shard_map/last_head/pallas_call | solution.py:745
  20.9 1.9 %collective-permute-done.3.refs_1_.refs_9_ = bf16[304,128]{1,0:T(8,128)(2,1)S(1)} collective-permute-done((bf16[304,128]{1,0:T(8,128)(2,1)S(1)}, bf16[304,128]{1,0:T(8,128)(2,1)S(1)}, u32[]{:S(2)}, u32[]{:S(2)}) %collective-permute-start.3) | collective-permute-done | bytes 77856 | tf_op jit(solution)/shard_map/ppermute | solution.py:737
  22.8 1.0 %collective-permute-done.4.refs_2_.refs_10_ = bf16[304,128]{1,0:T(8,128)(2,1)S(1)} collective-permute-done((bf16[304,128]{1,0:T(8,128)(2,1)S(1)}, bf16[304,128]{1,0:T(8,128)(2,1)S(1)}, u32[]{:S(2)}, u32[]{:S(2)}) %collective-permute-start.4) | collective-permute-done | bytes 77856 | tf_op jit(solution)/shard_map/ppermute | solution.py:737
  23.8 0.6 %collective-permute-done.5.refs_3_.refs_11_ = bf16[304,128]{1,0:T(8,128)(2,1)S(1)} collective-permute-done((bf16[304,128]{1,0:T(8,128)(2,1)S(1)}, bf16[304,128]{1,0:T(8,128)(2,1)S(1)}, u32[]{:S(2)}, u32[]{:S(2)}) %collective-permute-start.5) | collective-permute-done | bytes 77856 | tf_op jit(solution)/shard_map/ppermute | solution.py:737
  24.4 0.1 collective-permute-start.6
  24.5 0.8 %mix.1 = (bf16[128,640]{1,0:T(8,128)(2,1)S(1)}, bf16[128,640]{1,0:T(8,128)(2,1)S(1)}, bf16[128,640]{1,0:T(8,128)(2,1)S(1)}, bf16[128,640]{1,0:T(8,128)(2,1)S(1)}) custom-call(bf16[1,128,640]{2,1,0:T(8,128)(2,1)S(1)} %copy-done.1, bf16[1,128,640]{2,1,0:T(8,128)(2,1)S(1)} %copy-done.2, bf16[1,128,640]{2,1,0:T(8,128)(2,1)S(1)} %copy-done.3, ...), custom_call_target="tpu_custom_call" | custom-call | flops 20000000000 | tf_op jit(solution)/shard_map/mix/pallas_call | solution.py:745
  25.3 0.3 %collective-permute-done.6.gain_rest_ref = f32[1,640]{1,0:T(1,128)S(1)} collective-permute-done((f32[1,640]{1,0:T(1,128)S(1)}, f32[1,640]{1,0:T(1,128)S(1)}, u32[]{:S(2)}, u32[]{:S(2)}) %collective-permute-start.6) | collective-permute-done | bytes 2592 | tf_op jit(solution)/shard_map/ppermute | solution.py:737
  25.6 0.9 %finish.1 = (bf16[1,128,640]{2,1,0:T(8,128)(2,1)}, bf16[1,128,640]{2,1,0:T(8,128)(2,1)}, bf16[1,128,640]{2,1,0:T(8,128)(2,1)}, bf16[1,128,640]{2,1,0:T(8,128)(2,1)}, f32[640]{0:T(1024)}) custom-call(f32[1,640]{1,0:T(1,128)S(1)} %gain.1.gain_ref, f32[1,640]{1,0:T(1,128)S(1)} %collective-permute-done.6.gain_rest_ref, ...), custom_call_target="tpu_custom_call" | custom-call | flops 1000000000 | tf_op jit(solution)/shard_map/finish/pallas_call | solution.py:745
  (5 shorter events, 0.0 us)
Async XLA Ops:
  0.6 0.9 %copy-start.1 = (bf16[1,128,640]{2,1,0:T(8,128)(2,1)S(1)}, bf16[1,128,640]{2,1,0:T(8,128)(2,1)}, u32[]{:S(2)}) copy-start(bf16[1,128,640]{2,1,0:T(8,128)(2,1)} %q_ref.9) | copy-start | bytes 491524
  0.6 1.0 %copy-start.3 = (bf16[1,128,640]{2,1,0:T(8,128)(2,1)S(1)}, bf16[1,128,640]{2,1,0:T(8,128)(2,1)}, u32[]{:S(2)}) copy-start(bf16[1,128,640]{2,1,0:T(8,128)(2,1)} %v_ref.7) | copy-start | bytes 491524
  0.7 1.1 %copy-start.2 = (bf16[1,128,640]{2,1,0:T(8,128)(2,1)S(1)}, bf16[1,128,640]{2,1,0:T(8,128)(2,1)}, u32[]{:S(2)}) copy-start(bf16[1,128,640]{2,1,0:T(8,128)(2,1)} %k_ref.7) | copy-start | bytes 491524
  0.7 1.1 %copy-start = (bf16[1,128,640]{2,1,0:T(8,128)(2,1)S(1)}, bf16[1,128,640]{2,1,0:T(8,128)(2,1)}, u32[]{:S(2)}) copy-start(bf16[1,128,640]{2,1,0:T(8,128)(2,1)} %grad_ref.3) | copy-start | bytes 491524
  0.7 0.7 %copy-start.4 = (s32[2,5]{1,0:T(2,128)S(1)}, s32[2,5]{1,0:T(2,128)}, u32[]{:S(2)}) copy-start(s32[2,5]{1,0:T(2,128)} %offsets_ref.3) | copy-start | bytes 124
  2.5 5.8 %copy-start.6 = (f32[640]{0:T(1024)S(1)}, f32[640]{0:T(1024)}, u32[]{:S(2)}) copy-start(f32[640]{0:T(1024)} %param.10) | copy-start | bytes 7684
  2.5 8.6 %collective-permute-start = (bf16[352,128]{1,0:T(8,128)(2,1)S(1)}, bf16[352,128]{1,0:T(8,128)(2,1)S(1)}, u32[]{:S(2)}, u32[]{:S(2)}) collective-permute-start(bf16[352,128]{1,0:T(8,128)(2,1)S(1)} %get-tuple-element.38), channel_id=1, source_target_pairs={{0,12},{4,8},{8,4},{12,0},{1,13},{5,9},{9,5},{13,1},{2,14},{6,10},... | collective-permute-start | bytes 270344 | tf_op jit(solution)/shard_map/ppermute | solution.py:737
  7.6 5.8 %collective-permute-start.1 = (bf16[352,128]{1,0:T(8,128)(2,1)S(1)}, bf16[352,128]{1,0:T(8,128)(2,1)S(1)}, u32[]{:S(2)}, u32[]{:S(2)}) collective-permute-start(bf16[352,128]{1,0:T(8,128)(2,1)S(1)} %get-tuple-element.39), channel_id=1, source_target_pairs={{0,4},{4,0},{8,12},{12,8},{1,5},{5,1},{9,13},{13,9},{2,6},{6,2},{1... | collective-permute-start | bytes 270344 | tf_op jit(solution)/shard_map/ppermute | solution.py:737
  7.6 0.7 %copy-start.5 = (s32[2,5]{1,0:T(2,128)S(1)}, s32[2,5]{1,0:T(2,128)}, u32[]{:S(2)}) copy-start(s32[2,5]{1,0:T(2,128)} %offsets_ref.3) | copy-start | bytes 124
  7.6 7.6 %collective-permute-start.2 = (bf16[352,128]{1,0:T(8,128)(2,1)S(1)}, bf16[352,128]{1,0:T(8,128)(2,1)S(1)}, u32[]{:S(2)}, u32[]{:S(2)}) collective-permute-start(bf16[352,128]{1,0:T(8,128)(2,1)S(1)} %get-tuple-element.40), channel_id=1, source_target_pairs={{0,8},{4,12},{8,0},{12,4},{1,9},{5,13},{9,1},{13,5},{2,10},{6,14},... | collective-permute-start | bytes 270344 | tf_op jit(solution)/shard_map/ppermute | solution.py:737
  16.1 6.7 %collective-permute-start.3 = (bf16[304,128]{1,0:T(8,128)(2,1)S(1)}, bf16[304,128]{1,0:T(8,128)(2,1)S(1)}, u32[]{:S(2)}, u32[]{:S(2)}) collective-permute-start(bf16[304,128]{1,0:T(8,128)(2,1)S(1)} %get-tuple-element.42), channel_id=1, source_target_pairs={{0,12},{4,8},{8,4},{12,0},{1,13},{5,9},{9,5},{13,1},{2,14},{6,10},... | collective-permute-start | bytes 233480 | tf_op jit(solution)/shard_map/ppermute | solution.py:737
  18.8 5.0 %collective-permute-start.4 = (bf16[304,128]{1,0:T(8,128)(2,1)S(1)}, bf16[304,128]{1,0:T(8,128)(2,1)S(1)}, u32[]{:S(2)}, u32[]{:S(2)}) collective-permute-start(bf16[304,128]{1,0:T(8,128)(2,1)S(1)} %get-tuple-element.43), channel_id=1, source_target_pairs={{0,4},{4,0},{8,12},{12,8},{1,5},{5,1},{9,13},{13,9},{2,6},{6,2},{1... | collective-permute-start | bytes 233480 | tf_op jit(solution)/shard_map/ppermute | solution.py:737
  18.8 5.6 %collective-permute-start.5 = (bf16[304,128]{1,0:T(8,128)(2,1)S(1)}, bf16[304,128]{1,0:T(8,128)(2,1)S(1)}, u32[]{:S(2)}, u32[]{:S(2)}) collective-permute-start(bf16[304,128]{1,0:T(8,128)(2,1)S(1)} %get-tuple-element.44), channel_id=1, source_target_pairs={{0,8},{4,12},{8,0},{12,4},{1,9},{5,13},{9,1},{13,5},{2,10},{6,14},... | collective-permute-start | bytes 233480 | tf_op jit(solution)/shard_map/ppermute | solution.py:737
  24.4 1.2 %collective-permute-start.6 = (f32[1,640]{1,0:T(1,128)S(1)}, f32[1,640]{1,0:T(1,128)S(1)}, u32[]{:S(2)}, u32[]{:S(2)}) collective-permute-start(f32[1,640]{1,0:T(1,128)S(1)} %gain.1.gain_ref), channel_id=1, source_target_pairs={{0,16},{16,0},{1,17},{17,1},{2,18},{18,2},{3,19},{19,3},{4,20},{20... | collective-permute-start | bytes 7688 | tf_op jit(solution)/shard_map/ppermute | solution.py:737

commit v20 on v19

--- a/solution.py
+++ b/solution.py
@@ -336,53 +336,56 @@
     picks_ref[:, head_cols(last + 1)] = times.astype(LOW)
 
 
-def pack_kernel(top_step, picks_ref, q_ref, k_ref, v_ref, grad_ref, *refs):
-    payload_refs, held_ref = refs[:SPAN], refs[SPAN]
+def pack_kernel(top_step, picks_ref, q_ref, k_ref, v_ref, grad_ref, *payload_refs):
     tokens, width = q_ref.shape[1:]
-    heads = range(width // HEAD_DIM)
-    owned = range(OWNED)
     me = lax.axis_index("ctx")
     picked = sum(picked_counts(tokens, top_step))
     score_scale = 1.0 / math.sqrt(HEAD_DIM)
+    places = range(SPAN)
+    sent_cols = [
+        pl.ds(pl.multiple_of((me ^ distance) * HEAD_DIM, HEAD_DIM), HEAD_DIM) for distance in places
+    ]
+    last_cols = head_cols(width // HEAD_DIM - 1)
     q_rows, k_rows, v_rows, grad_rows = [
-        [ref[0, :, head_cols(head)] for head in heads] for ref in (q_ref, k_ref, v_ref, grad_ref)
-    ]
-    picks = [picks_ref[:, head_cols(head)] for head in heads]
-    scores = [contract(k_rows[head], q_rows[head], 1, 1) * score_scale for head in owned]
+        [ref[0, :, cols] for cols in sent_cols] for ref in (q_ref, k_ref, v_ref, grad_ref)
+    ]
+    picks = [picks_ref[:, cols] for cols in sent_cols]
+    scores = [contract(k_rows[i], q_rows[i], 1, 1) * score_scale for i in places]
     moved = [
         contract(
-            picks[head][:picked],
-            jnp.concatenate([q_rows[head], k_rows[head], v_rows[head], grad_rows[head]], 1),
+            picks[i][:picked],
+            jnp.concatenate([q_rows[i], k_rows[i], v_rows[i], grad_rows[i]], 1),
             1,
             0,
         ).astype(LOW)
-        for head in owned
-    ]
-    shared = [
-        contract(
-            picks[head][:picked], jnp.concatenate([k_rows[head], v_rows[head]], 1), 1, 0
+        for i in places
+    ]
+    shared = contract(
+        picks_ref[:picked, last_cols],
+        jnp.concatenate([k_ref[0, :, last_cols], v_ref[0, :, last_cols]], 1),
+        1,
+        0,
+    ).astype(LOW)
+    top_scores = [jnp.max(block, axis=0, keepdims=True) for block in scores]
+    expos = [jnp.exp(scores[i] - top_scores[i]) for i in places]
+    expo_lows = [expo.astype(LOW) for expo in expos]
+    outs = [contract(v_rows[i], expo_lows[i], 0, 0) for i in places]
+    totals = [jnp.sum(expo, axis=0, keepdims=True) for expo in expos]
+    outs = [(outs[i] * (1.0 / totals[i])).astype(LOW) for i in places]
+    picked_outs = [contract(picks[i][:picked], outs[i], 1, 1).astype(LOW) for i in places]
+    pieces = [piece_rows(top_scores[i] + jnp.log(totals[i])).astype(LOW) for i in places]
+    stat_rows = [contract(pieces[i], picks[i], 1, 1) for i in places]
+    for i, payload_ref in enumerate(payload_refs):
+        for block in range(4):
+            payload_ref[block * picked : (block + 1) * picked] = moved[i][
+                :, block * HEAD_DIM : (block + 1) * HEAD_DIM
+            ]
+        payload_ref[4 * picked : 5 * picked] = picked_outs[i]
+        payload_ref[5 * picked : 6 * picked] = shared[:, :HEAD_DIM]
+        payload_ref[6 * picked : 7 * picked] = shared[:, HEAD_DIM:]
+        payload_ref[7 * picked :] = jnp.concatenate(
+            [stat_rows[i], jnp.zeros_like(stat_rows[i])], 0
         ).astype(LOW)
-        for head in heads[OWNED:]
-    ]
-    top_scores = [jnp.max(block, axis=0, keepdims=True) for block in scores]
-    expos = [jnp.exp(scores[head] - top_scores[head]) for head in owned]
-    expo_lows = [expo.astype(LOW) for expo in expos]
-    outs = [contract(v_rows[head], expo_lows[head], 0, 0) for head in owned]
-    totals = [jnp.sum(expo, axis=0, keepdims=True) for expo in expos]
-    outs = [(outs[head] * (1.0 / totals[head])).astype(LOW) for head in owned]
-    picked_outs = [
-        contract(picks[head][:picked], outs[head], 1, 1).astype(LOW) for head in owned
-    ]
-    for head in owned:
-        pieces = piece_rows(top_scores[head] + jnp.log(totals[head])).astype(LOW)
-        stat_rows = contract(pieces, picks[head], 1, 1)
-        blocks = [moved[head][:, block * HEAD_DIM : (block + 1) * HEAD_DIM] for block in range(4)]
-        blocks.append(picked_outs[head])
-        blocks += [shared[0][:, :HEAD_DIM], shared[0][:, HEAD_DIM:]]
-        blocks.append(jnp.concatenate([stat_rows, jnp.zeros_like(stat_rows)], 0).astype(LOW))
-        held_ref[head] = jnp.concatenate(blocks, 0)
-    for distance, payload_ref in enumerate(payload_refs):
-        payload_ref[...] = held_ref[me ^ distance]
 
 
 def prepare_kernel(top_step, offsets_ref, q_ref, k_ref, v_ref, grad_ref, gain_ref, *refs):
@@ -780,7 +783,6 @@
         (picks, queries, keys, values, grad_y),
         [payload] * SPAN,
         1,
-        scratch=[pltpu.VMEM((OWNED, *payload.shape), LOW)],
     )
     received = to_peers(sent)
     grad_norm, gain_base, place, masks, expo, base_out, stats = call(

time: 26.7 us -> 26.6 us (level)
  no operation moved by 1% of the time
where the time goes in v20:
time: 26.6 us; the launch traced here: 26.4 us
  starting transfers between devices  10.3 us (39%)
  waiting for transfers between devices  9.98 us (38%)
  Pallas kernels  4.47 us (17%)
  local copies, waits for them, and re-layouts  1.01 us (4%)
  between operations  0.73 us (3%)
    ppermute x7, starting transfers between devices, across(): return lax.ppermute(block, axis, route)  10.3 us
    ppermute x7, waiting for transfers between devices, across(): return lax.ppermute(block, axis, route)  9.98 us
    pallas_call x8, Pallas kernels, call(): pl.pallas_call(kernel, out_shape=results, in_specs=[VMEM_SPEC] * len(oper...  4.47 us
    unnamed x14, local copies, waits for them, and re-layouts  1.01 us
  transfers between devices with their start and end apart: 7, of which 7 were waited for; matrix products, arithmetic and copies ran while one was open for 0% of the time, Pallas kernels for 7%

profile of v20, /device:TPU:0, one launch (start us, length us, event | category | flops | bytes accessed | tf_op | source)
XLA Modules:
  0.0 26.4 jit_solution(10007610241270039228)
XLA Ops:
  0.6 0.0 copy-start.1
  0.6 0.0 copy-start.3
  0.7 0.0 copy-start.2
  0.7 0.0 copy-start
  0.7 0.0 copy-start.4
  0.7 0.7 %copy-done.4 = s32[2,5]{1,0:T(2,128)S(1)} copy-done((s32[2,5]{1,0:T(2,128)S(1)}, s32[2,5]{1,0:T(2,128)}, u32[]{:S(2)}) %copy-start.4) | copy-done | bytes 64
  1.4 0.1 picks.1.refs_0_.picks_ref
  1.6 0.0 copy-done.1
  1.6 0.1 copy-done.3
  1.6 0.1 copy-done.2
  1.7 0.1 copy-done
  1.8 0.6 %pack.1 = (bf16[352,128]{1,0:T(8,128)(2,1)S(1)}, bf16[352,128]{1,0:T(8,128)(2,1)S(1)}, bf16[352,128]{1,0:T(8,128)(2,1)S(1)}, bf16[352,128]{1,0:T(8,128)(2,1)S(1)}) custom-call(bf16[128,768]{1,0:T(8,128)(2,1)S(1)} %picks.1.refs_0_.picks_ref, bf16[1,128,640]{2,1,0:T(8,128)(2,1)S(1)} %copy-done.1, bf16[1,128,640]{2,1,0:T(8,128)(2,1)S(1)} %copy-done.2, ...), custom_call_target="tpu_custom_call" | custom-call | flops 1000000000 | tf_op jit(solution)/shard_map/pack/pallas_call | solution.py:748
  2.4 5.1 %collective-permute-start = (bf16[352,128]{1,0:T(8,128)(2,1)S(1)}, bf16[352,128]{1,0:T(8,128)(2,1)S(1)}, u32[]{:S(2)}, u32[]{:S(2)}) collective-permute-start(bf16[352,128]{1,0:T(8,128)(2,1)S(1)} %get-tuple-element.38), channel_id=1, source_target_pairs={{0,12},{4,8},{8,4},{12,0},{1,13},{5,9},{9,5},{13,1},{2,14},{6,10},... | collective-permute-start | bytes 270344 | tf_op jit(solution)/shard_map/ppermute | solution.py:740
  7.5 0.0 collective-permute-start.1
  7.5 0.6 %collective-permute-start.2 = (bf16[352,128]{1,0:T(8,128)(2,1)S(1)}, bf16[352,128]{1,0:T(8,128)(2,1)S(1)}, u32[]{:S(2)}, u32[]{:S(2)}) collective-permute-start(bf16[352,128]{1,0:T(8,128)(2,1)S(1)} %get-tuple-element.40), channel_id=1, source_target_pairs={{0,8},{4,12},{8,0},{12,4},{1,9},{5,13},{9,1},{13,5},{2,10},{6,14},... | collective-permute-start | bytes 270344 | tf_op jit(solution)/shard_map/ppermute | solution.py:740
  8.2 0.0 copy-done.5
  8.2 0.7 %prepare.1 = (f32[128,640]{1,0:T(8,128)S(1)}, f32[1,640]{1,0:T(1,128)S(1)}, bf16[128,1280]{1,0:T(8,128)(2,1)S(1)}, f32[16,256]{1,0:T(8,128)S(1)}, bf16[128,640]{...) custom-call(s32[2,5]{1,0:T(2,128)S(1)} %copy-done.5, bf16[1,128,640]{2,1,0:T(8,128)(2,1)S(1)} %copy-done.1, ...), custom_call_target="tpu_custom_call" | custom-call | flops 2000000000 | tf_op jit(solution)/shard_map/prepare/pallas_call | solution.py:748
  8.9 2.1 %collective-permute-done.refs_4_ = bf16[352,128]{1,0:T(8,128)(2,1)S(1)} collective-permute-done((bf16[352,128]{1,0:T(8,128)(2,1)S(1)}, bf16[352,128]{1,0:T(8,128)(2,1)S(1)}, u32[]{:S(2)}, u32[]{:S(2)}) %collective-permute-start) | collective-permute-done | bytes 90144 | tf_op jit(solution)/shard_map/ppermute | solution.py:740
  11.1 2.2 %collective-permute-done.1.refs_5_ = bf16[352,128]{1,0:T(8,128)(2,1)S(1)} collective-permute-done((bf16[352,128]{1,0:T(8,128)(2,1)S(1)}, bf16[352,128]{1,0:T(8,128)(2,1)S(1)}, u32[]{:S(2)}, u32[]{:S(2)}) %collective-permute-start.1) | collective-permute-done | bytes 90144 | tf_op jit(solution)/shard_map/ppermute | solution.py:740
  13.3 1.8 %collective-permute-done.2.refs_6_ = bf16[352,128]{1,0:T(8,128)(2,1)S(1)} collective-permute-done((bf16[352,128]{1,0:T(8,128)(2,1)S(1)}, bf16[352,128]{1,0:T(8,128)(2,1)S(1)}, u32[]{:S(2)}, u32[]{:S(2)}) %collective-permute-start.2) | collective-permute-done | bytes 90144 | tf_op jit(solution)/shard_map/ppermute | solution.py:740
  15.1 1.0 %owner.1 = (f32[128,128]{1,0:T(8,128)S(1)}, bf16[128,128]{1,0:T(8,128)(2,1)S(1)}, bf16[144,128]{1,0:T(8,128)(2,1)S(1)}, f32[8,128]{1,0:T(8,128)S(1)}, bf16[304,1...) custom-call(bf16[1,128,640]{2,1,0:T(8,128)(2,1)S(1)} %copy-done.1, ...), custom_call_target="tpu_custom_call" | custom-call | flops 3000000000 | tf_op jit(solution)/shard_map/owner/pallas_call | solution.py:748
  16.1 2.7 %collective-permute-start.3 = (bf16[304,128]{1,0:T(8,128)(2,1)S(1)}, bf16[304,128]{1,0:T(8,128)(2,1)S(1)}, u32[]{:S(2)}, u32[]{:S(2)}) collective-permute-start(bf16[304,128]{1,0:T(8,128)(2,1)S(1)} %get-tuple-element.42), channel_id=1, source_target_pairs={{0,12},{4,8},{8,4},{12,0},{1,13},{5,9},{9,5},{13,1},{2,14},{6,10},... | collective-permute-start | bytes 233480 | tf_op jit(solution)/shard_map/ppermute | solution.py:740
  18.8 0.0 collective-permute-start.4
  18.8 1.7 %collective-permute-start.5 = (bf16[304,128]{1,0:T(8,128)(2,1)S(1)}, bf16[304,128]{1,0:T(8,128)(2,1)S(1)}, u32[]{:S(2)}, u32[]{:S(2)}) collective-permute-start(bf16[304,128]{1,0:T(8,128)(2,1)S(1)} %get-tuple-element.44), channel_id=1, source_target_pairs={{0,8},{4,12},{8,0},{12,4},{1,9},{5,13},{9,1},{13,5},{2,10},{6,14},... | collective-permute-start | bytes 233480 | tf_op jit(solution)/shard_map/ppermute | solution.py:740
  20.5 0.3 %last_head.1 = (bf16[128,128]{1,0:T(8,128)(2,1)S(1)}, bf16[128,128]{1,0:T(8,128)(2,1)S(1)}, f32[128,128]{1,0:T(8,128)S(1)}, f32[128,128]{1,0:T(8,128)S(1)}) custom-call(bf16[1,128,640]{2,1,0:T(8,128)(2,1)S(1)} %copy-done.1, bf16[1,128,640]{2,1,0:T(8,128)(2,1)S(1)} %copy-done.2, bf16[1,128,640]{2,1,0:T(8,128)(2,1)S(1)} %copy-done.3, ...), custom_call_target="tpu_custom_call" | custom-call | flops 20000000000 | tf_op jit(solution)/shard_map/last_head/pallas_call | solution.py:748
  20.9 1.9 %collective-permute-done.3.refs_1_.refs_9_ = bf16[304,128]{1,0:T(8,128)(2,1)S(1)} collective-permute-done((bf16[304,128]{1,0:T(8,128)(2,1)S(1)}, bf16[304,128]{1,0:T(8,128)(2,1)S(1)}, u32[]{:S(2)}, u32[]{:S(2)}) %collective-permute-start.3) | collective-permute-done | bytes 77856 | tf_op jit(solution)/shard_map/ppermute | solution.py:740
  22.8 0.9 %collective-permute-done.4.refs_2_.refs_10_ = bf16[304,128]{1,0:T(8,128)(2,1)S(1)} collective-permute-done((bf16[304,128]{1,0:T(8,128)(2,1)S(1)}, bf16[304,128]{1,0:T(8,128)(2,1)S(1)}, u32[]{:S(2)}, u32[]{:S(2)}) %collective-permute-start.4) | collective-permute-done | bytes 77856 | tf_op jit(solution)/shard_map/ppermute | solution.py:740
  23.7 0.6 %collective-permute-done.5.refs_3_.refs_11_ = bf16[304,128]{1,0:T(8,128)(2,1)S(1)} collective-permute-done((bf16[304,128]{1,0:T(8,128)(2,1)S(1)}, bf16[304,128]{1,0:T(8,128)(2,1)S(1)}, u32[]{:S(2)}, u32[]{:S(2)}) %collective-permute-start.5) | collective-permute-done | bytes 77856 | tf_op jit(solution)/shard_map/ppermute | solution.py:740
  24.3 0.1 collective-permute-start.6
  24.4 0.8 %mix.1 = (bf16[128,640]{1,0:T(8,128)(2,1)S(1)}, bf16[128,640]{1,0:T(8,128)(2,1)S(1)}, bf16[128,640]{1,0:T(8,128)(2,1)S(1)}, bf16[128,640]{1,0:T(8,128)(2,1)S(1)}) custom-call(bf16[1,128,640]{2,1,0:T(8,128)(2,1)S(1)} %copy-done.1, bf16[1,128,640]{2,1,0:T(8,128)(2,1)S(1)} %copy-done.2, bf16[1,128,640]{2,1,0:T(8,128)(2,1)S(1)} %copy-done.3, ...), custom_call_target="tpu_custom_call" | custom-call | flops 20000000000 | tf_op jit(solution)/shard_map/mix/pallas_call | solution.py:748
  25.2 0.3 %collective-permute-done.6.gain_rest_ref = f32[1,640]{1,0:T(1,128)S(1)} collective-permute-done((f32[1,640]{1,0:T(1,128)S(1)}, f32[1,640]{1,0:T(1,128)S(1)}, u32[]{:S(2)}, u32[]{:S(2)}) %collective-permute-start.6) | collective-permute-done | bytes 2592 | tf_op jit(solution)/shard_map/ppermute | solution.py:740
  25.6 0.9 %finish.1 = (bf16[1,128,640]{2,1,0:T(8,128)(2,1)}, bf16[1,128,640]{2,1,0:T(8,128)(2,1)}, bf16[1,128,640]{2,1,0:T(8,128)(2,1)}, bf16[1,128,640]{2,1,0:T(8,128)(2,1)}, f32[640]{0:T(1024)}) custom-call(f32[1,640]{1,0:T(1,128)S(1)} %gain.1.gain_ref, f32[1,640]{1,0:T(1,128)S(1)} %collective-permute-done.6.gain_rest_ref, ...), custom_call_target="tpu_custom_call" | custom-call | flops 1000000000 | tf_op jit(solution)/shard_map/finish/pallas_call | solution.py:748
  (5 shorter events, 0.0 us)
Async XLA Ops:
  0.6 0.9 %copy-start.1 = (bf16[1,128,640]{2,1,0:T(8,128)(2,1)S(1)}, bf16[1,128,640]{2,1,0:T(8,128)(2,1)}, u32[]{:S(2)}) copy-start(bf16[1,128,640]{2,1,0:T(8,128)(2,1)} %q_ref.9) | copy-start | bytes 491524
  0.6 1.0 %copy-start.3 = (bf16[1,128,640]{2,1,0:T(8,128)(2,1)S(1)}, bf16[1,128,640]{2,1,0:T(8,128)(2,1)}, u32[]{:S(2)}) copy-start(bf16[1,128,640]{2,1,0:T(8,128)(2,1)} %v_ref.7) | copy-start | bytes 491524
  0.7 1.1 %copy-start.2 = (bf16[1,128,640]{2,1,0:T(8,128)(2,1)S(1)}, bf16[1,128,640]{2,1,0:T(8,128)(2,1)}, u32[]{:S(2)}) copy-start(bf16[1,128,640]{2,1,0:T(8,128)(2,1)} %k_ref.7) | copy-start | bytes 491524
  0.7 1.1 %copy-start = (bf16[1,128,640]{2,1,0:T(8,128)(2,1)S(1)}, bf16[1,128,640]{2,1,0:T(8,128)(2,1)}, u32[]{:S(2)}) copy-start(bf16[1,128,640]{2,1,0:T(8,128)(2,1)} %grad_ref.3) | copy-start | bytes 491524
  0.7 0.7 %copy-start.4 = (s32[2,5]{1,0:T(2,128)S(1)}, s32[2,5]{1,0:T(2,128)}, u32[]{:S(2)}) copy-start(s32[2,5]{1,0:T(2,128)} %offsets_ref.3) | copy-start | bytes 124
  2.4 5.7 %copy-start.6 = (f32[640]{0:T(1024)S(1)}, f32[640]{0:T(1024)}, u32[]{:S(2)}) copy-start(f32[640]{0:T(1024)} %param.10) | copy-start | bytes 7684
  2.4 8.6 %collective-permute-start = (bf16[352,128]{1,0:T(8,128)(2,1)S(1)}, bf16[352,128]{1,0:T(8,128)(2,1)S(1)}, u32[]{:S(2)}, u32[]{:S(2)}) collective-permute-start(bf16[352,128]{1,0:T(8,128)(2,1)S(1)} %get-tuple-element.38), channel_id=1, source_target_pairs={{0,12},{4,8},{8,4},{12,0},{1,13},{5,9},{9,5},{13,1},{2,14},{6,10},... | collective-permute-start | bytes 270344 | tf_op jit(solution)/shard_map/ppermute | solution.py:740
  7.5 5.8 %collective-permute-start.1 = (bf16[352,128]{1,0:T(8,128)(2,1)S(1)}, bf16[352,128]{1,0:T(8,128)(2,1)S(1)}, u32[]{:S(2)}, u32[]{:S(2)}) collective-permute-start(bf16[352,128]{1,0:T(8,128)(2,1)S(1)} %get-tuple-element.39), channel_id=1, source_target_pairs={{0,4},{4,0},{8,12},{12,8},{1,5},{5,1},{9,13},{13,9},{2,6},{6,2},{1... | collective-permute-start | bytes 270344 | tf_op jit(solution)/shard_map/ppermute | solution.py:740
  7.5 0.7 %copy-start.5 = (s32[2,5]{1,0:T(2,128)S(1)}, s32[2,5]{1,0:T(2,128)}, u32[]{:S(2)}) copy-start(s32[2,5]{1,0:T(2,128)} %offsets_ref.3) | copy-start | bytes 124
  7.5 7.6 %collective-permute-start.2 = (bf16[352,128]{1,0:T(8,128)(2,1)S(1)}, bf16[352,128]{1,0:T(8,128)(2,1)S(1)}, u32[]{:S(2)}, u32[]{:S(2)}) collective-permute-start(bf16[352,128]{1,0:T(8,128)(2,1)S(1)} %get-tuple-element.40), channel_id=1, source_target_pairs={{0,8},{4,12},{8,0},{12,4},{1,9},{5,13},{9,1},{13,5},{2,10},{6,14},... | collective-permute-start | bytes 270344 | tf_op jit(solution)/shard_map/ppermute | solution.py:740
  16.1 6.7 %collective-permute-start.3 = (bf16[304,128]{1,0:T(8,128)(2,1)S(1)}, bf16[304,128]{1,0:T(8,128)(2,1)S(1)}, u32[]{:S(2)}, u32[]{:S(2)}) collective-permute-start(bf16[304,128]{1,0:T(8,128)(2,1)S(1)} %get-tuple-element.42), channel_id=1, source_target_pairs={{0,12},{4,8},{8,4},{12,0},{1,13},{5,9},{9,5},{13,1},{2,14},{6,10},... | collective-permute-start | bytes 233480 | tf_op jit(solution)/shard_map/ppermute | solution.py:740
  18.8 5.0 %collective-permute-start.4 = (bf16[304,128]{1,0:T(8,128)(2,1)S(1)}, bf16[304,128]{1,0:T(8,128)(2,1)S(1)}, u32[]{:S(2)}, u32[]{:S(2)}) collective-permute-start(bf16[304,128]{1,0:T(8,128)(2,1)S(1)} %get-tuple-element.43), channel_id=1, source_target_pairs={{0,4},{4,0},{8,12},{12,8},{1,5},{5,1},{9,13},{13,9},{2,6},{6,2},{1... | collective-permute-start | bytes 233480 | tf_op jit(solution)/shard_map/ppermute | solution.py:740
  18.8 5.5 %collective-permute-start.5 = (bf16[304,128]{1,0:T(8,128)(2,1)S(1)}, bf16[304,128]{1,0:T(8,128)(2,1)S(1)}, u32[]{:S(2)}, u32[]{:S(2)}) collective-permute-start(bf16[304,128]{1,0:T(8,128)(2,1)S(1)} %get-tuple-element.44), channel_id=1, source_target_pairs={{0,8},{4,12},{8,0},{12,4},{1,9},{5,13},{9,1},{13,5},{2,10},{6,14},... | collective-permute-start | bytes 233480 | tf_op jit(solution)/shard_map/ppermute | solution.py:740
  24.3 1.2 %collective-permute-start.6 = (f32[1,640]{1,0:T(1,128)S(1)}, f32[1,640]{1,0:T(1,128)S(1)}, u32[]{:S(2)}, u32[]{:S(2)}) collective-permute-start(f32[1,640]{1,0:T(1,128)S(1)} %gain.1.gain_ref), channel_id=1, source_target_pairs={{0,16},{16,0},{1,17},{17,1},{2,18},{18,2},{3,19},{19,3},{4,20},{20... | collective-permute-start | bytes 7688 | tf_op jit(solution)/shard_map/ppermute | solution.py:740

commit v21 on v19

--- a/solution.py
+++ b/solution.py
@@ -727,8 +727,10 @@
 
 def finish_kernel(gain_ref, gain_rest_ref, *refs):
     block_refs, result_refs, gain_out_ref = refs[:4], refs[4:8], refs[8]
+    half = result_refs[0].shape[1]
+    rows = pl.ds(pl.multiple_of(pl.program_id(0) * half, half), half)
     for block_ref, result_ref in zip(block_refs, result_refs):
-        result_ref[0] = block_ref[...]
+        result_ref[0] = block_ref[rows, :]
     gain_out_ref[...] = (gain_ref[...] + gain_rest_ref[...]).reshape(gain_out_ref.shape)
 
 
@@ -741,12 +743,22 @@
     return [across(blocks[distance - 1], "ctx", distance) for distance in START_ORDER]
 
 
-def call(kernel, name, operands, results, microseconds, vmem=PLAIN_VMEM, scratch=()):
+def row_spec(block, row_steps):
+    if not row_steps or len(block.shape) < 3:
+        return VMEM_SPEC
+    count, rows, width = block.shape
+    return pl.BlockSpec((count, rows // row_steps, width), lambda step: (0, step, 0))
+
+
+def call(
+    kernel, name, operands, results, microseconds, vmem=PLAIN_VMEM, scratch=(), row_steps=0
+):
     return pl.pallas_call(
         kernel,
         out_shape=results,
         in_specs=[VMEM_SPEC] * len(operands),
-        out_specs=[VMEM_SPEC] * len(results),
+        out_specs=[row_spec(block, row_steps) for block in results],
+        grid=(row_steps,) if row_steps else (),
         scratch_shapes=scratch,
         compiler_params=pltpu.CompilerParams(vmem_limit_bytes=vmem),
         cost_estimate=pl.CostEstimate(
@@ -849,6 +861,7 @@
         (gain_sum, gain_rest, *mixed),
         [row_block] * 4 + [shape((width,), WIDE)],
         1,
+        row_steps=2,
     )
     return attended, query_grad, key_grad, value_grad, gain_grad
 

time: 26.7 us -> 26.7 us (level)
  no operation moved by 1% of the time
where the time goes in v21:
time: 26.7 us; the launch traced here: 26.5 us
  starting transfers between devices  10.3 us (39%)
  waiting for transfers between devices  9.99 us (37%)
  Pallas kernels  4.47 us (17%)
  local copies, waits for them, and re-layouts  1.01 us (4%)
  between operations  0.74 us (3%)
    ppermute x7, starting transfers between devices, across(): return lax.ppermute(block, axis, route)  10.3 us
    ppermute x7, waiting for transfers between devices, across(): return lax.ppermute(block, axis, route)  9.99 us
    pallas_call x8, Pallas kernels, call(): pl.pallas_call(kernel, out_shape=results, in_specs=[VMEM_SPEC] * len(oper...  4.47 us
    unnamed x14, local copies, waits for them, and re-layouts  1.01 us
  transfers between devices with their start and end apart: 7, of which 7 were waited for; matrix products, arithmetic and copies ran while one was open for 0% of the time, Pallas kernels for 7%

profile of v21, /device:TPU:0, one launch (start us, length us, event | category | flops | bytes accessed | tf_op | source)
XLA Modules:
  0.0 26.5 jit_solution(2847728598999660185)
XLA Ops:
  0.6 0.0 copy-start.1
  0.6 0.0 copy-start.3
  0.7 0.0 copy-start.2
  0.7 0.0 copy-start
  0.7 0.0 copy-start.4
  0.7 0.7 %copy-done.4 = s32[2,5]{1,0:T(2,128)S(1)} copy-done((s32[2,5]{1,0:T(2,128)S(1)}, s32[2,5]{1,0:T(2,128)}, u32[]{:S(2)}) %copy-start.4) | copy-done | bytes 64
  1.4 0.1 picks.1.refs_0_.picks_ref
  1.6 0.1 copy-done.3
  1.6 0.1 copy-done.2
  1.7 0.1 copy-done
  1.8 0.7 %pack.1 = (bf16[352,128]{1,0:T(8,128)(2,1)S(1)}, bf16[352,128]{1,0:T(8,128)(2,1)S(1)}, bf16[352,128]{1,0:T(8,128)(2,1)S(1)}, bf16[352,128]{1,0:T(8,128)(2,1)S(1)}) custom-call(bf16[128,768]{1,0:T(8,128)(2,1)S(1)} %picks.1.refs_0_.picks_ref, bf16[1,128,640]{2,1,0:T(8,128)(2,1)S(1)} %copy-done.1, bf16[1,128,640]{2,1,0:T(8,128)(2,1)S(1)} %copy-done.2, ...), custom_call_target="tpu_custom_call" | custom-call | flops 1000000000 | tf_op jit(solution)/shard_map/pack/pallas_call | solution.py:756
  2.5 0.0 copy-start.6
  2.5 5.1 %collective-permute-start = (bf16[352,128]{1,0:T(8,128)(2,1)S(1)}, bf16[352,128]{1,0:T(8,128)(2,1)S(1)}, u32[]{:S(2)}, u32[]{:S(2)}) collective-permute-start(bf16[352,128]{1,0:T(8,128)(2,1)S(1)} %get-tuple-element.38), channel_id=1, source_target_pairs={{0,12},{4,8},{8,4},{12,0},{1,13},{5,9},{9,5},{13,1},{2,14},{6,10},... | collective-permute-start | bytes 270344 | tf_op jit(solution)/shard_map/ppermute | solution.py:739
  7.6 0.0 collective-permute-start.1
  7.6 0.6 %collective-permute-start.2 = (bf16[352,128]{1,0:T(8,128)(2,1)S(1)}, bf16[352,128]{1,0:T(8,128)(2,1)S(1)}, u32[]{:S(2)}, u32[]{:S(2)}) collective-permute-start(bf16[352,128]{1,0:T(8,128)(2,1)S(1)} %get-tuple-element.40), channel_id=1, source_target_pairs={{0,8},{4,12},{8,0},{12,4},{1,9},{5,13},{9,1},{13,5},{2,10},{6,14},... | collective-permute-start | bytes 270344 | tf_op jit(solution)/shard_map/ppermute | solution.py:739
  8.2 0.0 copy-done.5
  8.3 0.7 %prepare.1 = (f32[128,640]{1,0:T(8,128)S(1)}, f32[1,640]{1,0:T(1,128)S(1)}, bf16[128,1280]{1,0:T(8,128)(2,1)S(1)}, f32[16,256]{1,0:T(8,128)S(1)}, bf16[128,640]{...) custom-call(s32[2,5]{1,0:T(2,128)S(1)} %copy-done.5, bf16[1,128,640]{2,1,0:T(8,128)(2,1)S(1)} %copy-done.1, ...), custom_call_target="tpu_custom_call" | custom-call | flops 2000000000 | tf_op jit(solution)/shard_map/prepare/pallas_call | solution.py:756
  9.0 2.1 %collective-permute-done.refs_4_ = bf16[352,128]{1,0:T(8,128)(2,1)S(1)} collective-permute-done((bf16[352,128]{1,0:T(8,128)(2,1)S(1)}, bf16[352,128]{1,0:T(8,128)(2,1)S(1)}, u32[]{:S(2)}, u32[]{:S(2)}) %collective-permute-start) | collective-permute-done | bytes 90144 | tf_op jit(solution)/shard_map/ppermute | solution.py:739
  11.1 2.2 %collective-permute-done.1.refs_5_ = bf16[352,128]{1,0:T(8,128)(2,1)S(1)} collective-permute-done((bf16[352,128]{1,0:T(8,128)(2,1)S(1)}, bf16[352,128]{1,0:T(8,128)(2,1)S(1)}, u32[]{:S(2)}, u32[]{:S(2)}) %collective-permute-start.1) | collective-permute-done | bytes 90144 | tf_op jit(solution)/shard_map/ppermute | solution.py:739
  13.4 1.8 %collective-permute-done.2.refs_6_ = bf16[352,128]{1,0:T(8,128)(2,1)S(1)} collective-permute-done((bf16[352,128]{1,0:T(8,128)(2,1)S(1)}, bf16[352,128]{1,0:T(8,128)(2,1)S(1)}, u32[]{:S(2)}, u32[]{:S(2)}) %collective-permute-start.2) | collective-permute-done | bytes 90144 | tf_op jit(solution)/shard_map/ppermute | solution.py:739
  15.2 1.0 %owner.1 = (f32[128,128]{1,0:T(8,128)S(1)}, bf16[128,128]{1,0:T(8,128)(2,1)S(1)}, bf16[144,128]{1,0:T(8,128)(2,1)S(1)}, f32[8,128]{1,0:T(8,128)S(1)}, bf16[304,1...) custom-call(bf16[1,128,640]{2,1,0:T(8,128)(2,1)S(1)} %copy-done.1, ...), custom_call_target="tpu_custom_call" | custom-call | flops 3000000000 | tf_op jit(solution)/shard_map/owner/pallas_call | solution.py:756
  16.1 2.7 %collective-permute-start.3 = (bf16[304,128]{1,0:T(8,128)(2,1)S(1)}, bf16[304,128]{1,0:T(8,128)(2,1)S(1)}, u32[]{:S(2)}, u32[]{:S(2)}) collective-permute-start(bf16[304,128]{1,0:T(8,128)(2,1)S(1)} %get-tuple-element.42), channel_id=1, source_target_pairs={{0,12},{4,8},{8,4},{12,0},{1,13},{5,9},{9,5},{13,1},{2,14},{6,10},... | collective-permute-start | bytes 233480 | tf_op jit(solution)/shard_map/ppermute | solution.py:739
  18.8 0.0 collective-permute-start.4
  18.8 1.7 %collective-permute-start.5 = (bf16[304,128]{1,0:T(8,128)(2,1)S(1)}, bf16[304,128]{1,0:T(8,128)(2,1)S(1)}, u32[]{:S(2)}, u32[]{:S(2)}) collective-permute-start(bf16[304,128]{1,0:T(8,128)(2,1)S(1)} %get-tuple-element.44), channel_id=1, source_target_pairs={{0,8},{4,12},{8,0},{12,4},{1,9},{5,13},{9,1},{13,5},{2,10},{6,14},... | collective-permute-start | bytes 233480 | tf_op jit(solution)/shard_map/ppermute | solution.py:739
  20.6 0.3 %last_head.1 = (bf16[128,128]{1,0:T(8,128)(2,1)S(1)}, bf16[128,128]{1,0:T(8,128)(2,1)S(1)}, f32[128,128]{1,0:T(8,128)S(1)}, f32[128,128]{1,0:T(8,128)S(1)}) custom-call(bf16[1,128,640]{2,1,0:T(8,128)(2,1)S(1)} %copy-done.1, bf16[1,128,640]{2,1,0:T(8,128)(2,1)S(1)} %copy-done.2, bf16[1,128,640]{2,1,0:T(8,128)(2,1)S(1)} %copy-done.3, ...), custom_call_target="tpu_custom_call" | custom-call | flops 20000000000 | tf_op jit(solution)/shard_map/last_head/pallas_call | solution.py:756
  20.9 1.9 %collective-permute-done.3.refs_1_.refs_9_ = bf16[304,128]{1,0:T(8,128)(2,1)S(1)} collective-permute-done((bf16[304,128]{1,0:T(8,128)(2,1)S(1)}, bf16[304,128]{1,0:T(8,128)(2,1)S(1)}, u32[]{:S(2)}, u32[]{:S(2)}) %collective-permute-start.3) | collective-permute-done | bytes 77856 | tf_op jit(solution)/shard_map/ppermute | solution.py:739
  22.8 1.0 %collective-permute-done.4.refs_2_.refs_10_ = bf16[304,128]{1,0:T(8,128)(2,1)S(1)} collective-permute-done((bf16[304,128]{1,0:T(8,128)(2,1)S(1)}, bf16[304,128]{1,0:T(8,128)(2,1)S(1)}, u32[]{:S(2)}, u32[]{:S(2)}) %collective-permute-start.4) | collective-permute-done | bytes 77856 | tf_op jit(solution)/shard_map/ppermute | solution.py:739
  23.8 0.6 %collective-permute-done.5.refs_3_.refs_11_ = bf16[304,128]{1,0:T(8,128)(2,1)S(1)} collective-permute-done((bf16[304,128]{1,0:T(8,128)(2,1)S(1)}, bf16[304,128]{1,0:T(8,128)(2,1)S(1)}, u32[]{:S(2)}, u32[]{:S(2)}) %collective-permute-start.5) | collective-permute-done | bytes 77856 | tf_op jit(solution)/shard_map/ppermute | solution.py:739
  24.4 0.1 collective-permute-start.6
  24.5 0.8 %mix.1 = (bf16[128,640]{1,0:T(8,128)(2,1)S(1)}, bf16[128,640]{1,0:T(8,128)(2,1)S(1)}, bf16[128,640]{1,0:T(8,128)(2,1)S(1)}, bf16[128,640]{1,0:T(8,128)(2,1)S(1)}) custom-call(bf16[1,128,640]{2,1,0:T(8,128)(2,1)S(1)} %copy-done.1, bf16[1,128,640]{2,1,0:T(8,128)(2,1)S(1)} %copy-done.2, bf16[1,128,640]{2,1,0:T(8,128)(2,1)S(1)} %copy-done.3, ...), custom_call_target="tpu_custom_call" | custom-call | flops 20000000000 | tf_op jit(solution)/shard_map/mix/pallas_call | solution.py:756
  25.3 0.3 %collective-permute-done.6.gain_rest_ref = f32[1,640]{1,0:T(1,128)S(1)} collective-permute-done((f32[1,640]{1,0:T(1,128)S(1)}, f32[1,640]{1,0:T(1,128)S(1)}, u32[]{:S(2)}, u32[]{:S(2)}) %collective-permute-start.6) | collective-permute-done | bytes 2592 | tf_op jit(solution)/shard_map/ppermute | solution.py:739
  25.6 0.9 %finish.1 = (bf16[1,128,640]{2,1,0:T(8,128)(2,1)}, bf16[1,128,640]{2,1,0:T(8,128)(2,1)}, bf16[1,128,640]{2,1,0:T(8,128)(2,1)}, bf16[1,128,640]{2,1,0:T(8,128)(2,1)}, f32[640]{0:T(1024)}) custom-call(f32[1,640]{1,0:T(1,128)S(1)} %gain.1.gain_ref, f32[1,640]{1,0:T(1,128)S(1)} %collective-permute-done.6.gain_rest_ref, ...), custom_call_target="tpu_custom_call" | custom-call | flops 1000000000 | tf_op jit(solution)/shard_map/finish/pallas_call | solution.py:756
  (5 shorter events, 0.0 us)
Async XLA Ops:
  0.6 0.9 %copy-start.1 = (bf16[1,128,640]{2,1,0:T(8,128)(2,1)S(1)}, bf16[1,128,640]{2,1,0:T(8,128)(2,1)}, u32[]{:S(2)}) copy-start(bf16[1,128,640]{2,1,0:T(8,128)(2,1)} %q_ref.9) | copy-start | bytes 491524
  0.6 1.0 %copy-start.3 = (bf16[1,128,640]{2,1,0:T(8,128)(2,1)S(1)}, bf16[1,128,640]{2,1,0:T(8,128)(2,1)}, u32[]{:S(2)}) copy-start(bf16[1,128,640]{2,1,0:T(8,128)(2,1)} %v_ref.7) | copy-start | bytes 491524
  0.7 1.1 %copy-start.2 = (bf16[1,128,640]{2,1,0:T(8,128)(2,1)S(1)}, bf16[1,128,640]{2,1,0:T(8,128)(2,1)}, u32[]{:S(2)}) copy-start(bf16[1,128,640]{2,1,0:T(8,128)(2,1)} %k_ref.7) | copy-start | bytes 491524
  0.7 1.1 %copy-start = (bf16[1,128,640]{2,1,0:T(8,128)(2,1)S(1)}, bf16[1,128,640]{2,1,0:T(8,128)(2,1)}, u32[]{:S(2)}) copy-start(bf16[1,128,640]{2,1,0:T(8,128)(2,1)} %grad_ref.3) | copy-start | bytes 491524
  0.7 0.7 %copy-start.4 = (s32[2,5]{1,0:T(2,128)S(1)}, s32[2,5]{1,0:T(2,128)}, u32[]{:S(2)}) copy-start(s32[2,5]{1,0:T(2,128)} %offsets_ref.3) | copy-start | bytes 124
  2.5 5.8 %copy-start.6 = (f32[640]{0:T(1024)S(1)}, f32[640]{0:T(1024)}, u32[]{:S(2)}) copy-start(f32[640]{0:T(1024)} %param.10) | copy-start | bytes 7684
  2.5 8.6 %collective-permute-start = (bf16[352,128]{1,0:T(8,128)(2,1)S(1)}, bf16[352,128]{1,0:T(8,128)(2,1)S(1)}, u32[]{:S(2)}, u32[]{:S(2)}) collective-permute-start(bf16[352,128]{1,0:T(8,128)(2,1)S(1)} %get-tuple-element.38), channel_id=1, source_target_pairs={{0,12},{4,8},{8,4},{12,0},{1,13},{5,9},{9,5},{13,1},{2,14},{6,10},... | collective-permute-start | bytes 270344 | tf_op jit(solution)/shard_map/ppermute | solution.py:739
  7.6 5.8 %collective-permute-start.1 = (bf16[352,128]{1,0:T(8,128)(2,1)S(1)}, bf16[352,128]{1,0:T(8,128)(2,1)S(1)}, u32[]{:S(2)}, u32[]{:S(2)}) collective-permute-start(bf16[352,128]{1,0:T(8,128)(2,1)S(1)} %get-tuple-element.39), channel_id=1, source_target_pairs={{0,4},{4,0},{8,12},{12,8},{1,5},{5,1},{9,13},{13,9},{2,6},{6,2},{1... | collective-permute-start | bytes 270344 | tf_op jit(solution)/shard_map/ppermute | solution.py:739
  7.6 0.7 %copy-start.5 = (s32[2,5]{1,0:T(2,128)S(1)}, s32[2,5]{1,0:T(2,128)}, u32[]{:S(2)}) copy-start(s32[2,5]{1,0:T(2,128)} %offsets_ref.3) | copy-start | bytes 124
  7.6 7.6 %collective-permute-start.2 = (bf16[352,128]{1,0:T(8,128)(2,1)S(1)}, bf16[352,128]{1,0:T(8,128)(2,1)S(1)}, u32[]{:S(2)}, u32[]{:S(2)}) collective-permute-start(bf16[352,128]{1,0:T(8,128)(2,1)S(1)} %get-tuple-element.40), channel_id=1, source_target_pairs={{0,8},{4,12},{8,0},{12,4},{1,9},{5,13},{9,1},{13,5},{2,10},{6,14},... | collective-permute-start | bytes 270344 | tf_op jit(solution)/shard_map/ppermute | solution.py:739
  16.1 6.7 %collective-permute-start.3 = (bf16[304,128]{1,0:T(8,128)(2,1)S(1)}, bf16[304,128]{1,0:T(8,128)(2,1)S(1)}, u32[]{:S(2)}, u32[]{:S(2)}) collective-permute-start(bf16[304,128]{1,0:T(8,128)(2,1)S(1)} %get-tuple-element.42), channel_id=1, source_target_pairs={{0,12},{4,8},{8,4},{12,0},{1,13},{5,9},{9,5},{13,1},{2,14},{6,10},... | collective-permute-start | bytes 233480 | tf_op jit(solution)/shard_map/ppermute | solution.py:739
  18.8 5.0 %collective-permute-start.4 = (bf16[304,128]{1,0:T(8,128)(2,1)S(1)}, bf16[304,128]{1,0:T(8,128)(2,1)S(1)}, u32[]{:S(2)}, u32[]{:S(2)}) collective-permute-start(bf16[304,128]{1,0:T(8,128)(2,1)S(1)} %get-tuple-element.43), channel_id=1, source_target_pairs={{0,4},{4,0},{8,12},{12,8},{1,5},{5,1},{9,13},{13,9},{2,6},{6,2},{1... | collective-permute-start | bytes 233480 | tf_op jit(solution)/shard_map/ppermute | solution.py:739
  18.8 5.6 %collective-permute-start.5 = (bf16[304,128]{1,0:T(8,128)(2,1)S(1)}, bf16[304,128]{1,0:T(8,128)(2,1)S(1)}, u32[]{:S(2)}, u32[]{:S(2)}) collective-permute-start(bf16[304,128]{1,0:T(8,128)(2,1)S(1)} %get-tuple-element.44), channel_id=1, source_target_pairs={{0,8},{4,12},{8,0},{12,4},{1,9},{5,13},{9,1},{13,5},{2,10},{6,14},... | collective-permute-start | bytes 233480 | tf_op jit(solution)/shard_map/ppermute | solution.py:739
  24.4 1.2 %collective-permute-start.6 = (f32[1,640]{1,0:T(1,128)S(1)}, f32[1,640]{1,0:T(1,128)S(1)}, u32[]{:S(2)}, u32[]{:S(2)}) collective-permute-start(f32[1,640]{1,0:T(1,128)S(1)} %gain.1.gain_ref), channel_id=1, source_target_pairs={{0,16},{16,0},{1,17},{17,1},{2,18},{18,2},{3,19},{19,3},{4,20},{20... | collective-permute-start | bytes 7688 | tf_op jit(solution)/shard_map/ppermute | solution.py:739

commit v22 on v20

--- a/solution.py
+++ b/solution.py
@@ -730,8 +730,10 @@
 
 def finish_kernel(gain_ref, gain_rest_ref, *refs):
     block_refs, result_refs, gain_out_ref = refs[:4], refs[4:8], refs[8]
+    half = result_refs[0].shape[1]
+    rows = pl.ds(pl.multiple_of(pl.program_id(0) * half, half), half)
     for block_ref, result_ref in zip(block_refs, result_refs):
-        result_ref[0] = block_ref[...]
+        result_ref[0] = block_ref[rows, :]
     gain_out_ref[...] = (gain_ref[...] + gain_rest_ref[...]).reshape(gain_out_ref.shape)
 
 
@@ -744,12 +746,22 @@
     return [across(blocks[distance - 1], "ctx", distance) for distance in START_ORDER]
 
 
-def call(kernel, name, operands, results, microseconds, vmem=PLAIN_VMEM, scratch=()):
+def row_spec(block, row_steps):
+    if not row_steps or len(block.shape) < 3:
+        return VMEM_SPEC
+    count, rows, width = block.shape
+    return pl.BlockSpec((count, rows // row_steps, width), lambda step: (0, step, 0))
+
+
+def call(
+    kernel, name, operands, results, microseconds, vmem=PLAIN_VMEM, scratch=(), row_steps=0
+):
     return pl.pallas_call(
         kernel,
         out_shape=results,
         in_specs=[VMEM_SPEC] * len(operands),
-        out_specs=[VMEM_SPEC] * len(results),
+        out_specs=[row_spec(block, row_steps) for block in results],
+        grid=(row_steps,) if row_steps else (),
         scratch_shapes=scratch,
         compiler_params=pltpu.CompilerParams(vmem_limit_bytes=vmem),
         cost_estimate=pl.CostEstimate(
@@ -851,6 +863,7 @@
         (gain_sum, gain_rest, *mixed),
         [row_block] * 4 + [shape((width,), WIDE)],
         1,
+        row_steps=2,
     )
     return attended, query_grad, key_grad, value_grad, gain_grad
 

time: 26.6 us -> 26.6 us (level)
  no operation moved by 1% of the time
where the time goes in v22:
time: 26.6 us; the launch traced here: 26.4 us
  starting transfers between devices  10.3 us (39%)
  waiting for transfers between devices  9.98 us (38%)
  Pallas kernels  4.45 us (17%)
  local copies, waits for them, and re-layouts  1.01 us (4%)
  between operations  0.73 us (3%)
    ppermute x7, starting transfers between devices, across(): return lax.ppermute(block, axis, route)  10.3 us
    ppermute x7, waiting for transfers between devices, across(): return lax.ppermute(block, axis, route)  9.98 us
    pallas_call x8, Pallas kernels, call(): pl.pallas_call(kernel, out_shape=results, in_specs=[VMEM_SPEC] * len(oper...  4.45 us
    unnamed x14, local copies, waits for them, and re-layouts  1.01 us
  transfers between devices with their start and end apart: 7, of which 7 were waited for; matrix products, arithmetic and copies ran while one was open for 0% of the time, Pallas kernels for 7%

profile of v22, /device:TPU:0, one launch (start us, length us, event | category | flops | bytes accessed | tf_op | source)
XLA Modules:
  0.0 26.4 jit_solution(10751705036756232679)
XLA Ops:
  0.6 0.0 copy-start.1
  0.6 0.0 copy-start.3
  0.7 0.0 copy-start.2
  0.7 0.0 copy-start
  0.7 0.0 copy-start.4
  0.7 0.7 %copy-done.4 = s32[2,5]{1,0:T(2,128)S(1)} copy-done((s32[2,5]{1,0:T(2,128)S(1)}, s32[2,5]{1,0:T(2,128)}, u32[]{:S(2)}) %copy-start.4) | copy-done | bytes 64
  1.4 0.1 picks.1.refs_0_.picks_ref
  1.6 0.0 copy-done.1
  1.6 0.1 copy-done.3
  1.6 0.1 copy-done.2
  1.7 0.1 copy-done
  1.8 0.6 %pack.1 = (bf16[352,128]{1,0:T(8,128)(2,1)S(1)}, bf16[352,128]{1,0:T(8,128)(2,1)S(1)}, bf16[352,128]{1,0:T(8,128)(2,1)S(1)}, bf16[352,128]{1,0:T(8,128)(2,1)S(1)}) custom-call(bf16[128,768]{1,0:T(8,128)(2,1)S(1)} %picks.1.refs_0_.picks_ref, bf16[1,128,640]{2,1,0:T(8,128)(2,1)S(1)} %copy-done.1, bf16[1,128,640]{2,1,0:T(8,128)(2,1)S(1)} %copy-done.2, ...), custom_call_target="tpu_custom_call" | custom-call | flops 1000000000 | tf_op jit(solution)/shard_map/pack/pallas_call | solution.py:759
  2.4 5.1 %collective-permute-start = (bf16[352,128]{1,0:T(8,128)(2,1)S(1)}, bf16[352,128]{1,0:T(8,128)(2,1)S(1)}, u32[]{:S(2)}, u32[]{:S(2)}) collective-permute-start(bf16[352,128]{1,0:T(8,128)(2,1)S(1)} %get-tuple-element.38), channel_id=1, source_target_pairs={{0,12},{4,8},{8,4},{12,0},{1,13},{5,9},{9,5},{13,1},{2,14},{6,10},... | collective-permute-start | bytes 270344 | tf_op jit(solution)/shard_map/ppermute | solution.py:742
  7.5 0.0 collective-permute-start.1
  7.5 0.6 %collective-permute-start.2 = (bf16[352,128]{1,0:T(8,128)(2,1)S(1)}, bf16[352,128]{1,0:T(8,128)(2,1)S(1)}, u32[]{:S(2)}, u32[]{:S(2)}) collective-permute-start(bf16[352,128]{1,0:T(8,128)(2,1)S(1)} %get-tuple-element.40), channel_id=1, source_target_pairs={{0,8},{4,12},{8,0},{12,4},{1,9},{5,13},{9,1},{13,5},{2,10},{6,14},... | collective-permute-start | bytes 270344 | tf_op jit(solution)/shard_map/ppermute | solution.py:742
  8.2 0.0 copy-done.5
  8.2 0.7 %prepare.1 = (f32[128,640]{1,0:T(8,128)S(1)}, f32[1,640]{1,0:T(1,128)S(1)}, bf16[128,1280]{1,0:T(8,128)(2,1)S(1)}, f32[16,256]{1,0:T(8,128)S(1)}, bf16[128,640]{...) custom-call(s32[2,5]{1,0:T(2,128)S(1)} %copy-done.5, bf16[1,128,640]{2,1,0:T(8,128)(2,1)S(1)} %copy-done.1, ...), custom_call_target="tpu_custom_call" | custom-call | flops 2000000000 | tf_op jit(solution)/shard_map/prepare/pallas_call | solution.py:759
  8.9 2.1 %collective-permute-done.refs_4_ = bf16[352,128]{1,0:T(8,128)(2,1)S(1)} collective-permute-done((bf16[352,128]{1,0:T(8,128)(2,1)S(1)}, bf16[352,128]{1,0:T(8,128)(2,1)S(1)}, u32[]{:S(2)}, u32[]{:S(2)}) %collective-permute-start) | collective-permute-done | bytes 90144 | tf_op jit(solution)/shard_map/ppermute | solution.py:742
  11.1 2.2 %collective-permute-done.1.refs_5_ = bf16[352,128]{1,0:T(8,128)(2,1)S(1)} collective-permute-done((bf16[352,128]{1,0:T(8,128)(2,1)S(1)}, bf16[352,128]{1,0:T(8,128)(2,1)S(1)}, u32[]{:S(2)}, u32[]{:S(2)}) %collective-permute-start.1) | collective-permute-done | bytes 90144 | tf_op jit(solution)/shard_map/ppermute | solution.py:742
  13.3 1.8 %collective-permute-done.2.refs_6_ = bf16[352,128]{1,0:T(8,128)(2,1)S(1)} collective-permute-done((bf16[352,128]{1,0:T(8,128)(2,1)S(1)}, bf16[352,128]{1,0:T(8,128)(2,1)S(1)}, u32[]{:S(2)}, u32[]{:S(2)}) %collective-permute-start.2) | collective-permute-done | bytes 90144 | tf_op jit(solution)/shard_map/ppermute | solution.py:742
  15.1 1.0 %owner.1 = (f32[128,128]{1,0:T(8,128)S(1)}, bf16[128,128]{1,0:T(8,128)(2,1)S(1)}, bf16[144,128]{1,0:T(8,128)(2,1)S(1)}, f32[8,128]{1,0:T(8,128)S(1)}, bf16[304,1...) custom-call(bf16[1,128,640]{2,1,0:T(8,128)(2,1)S(1)} %copy-done.1, ...), custom_call_target="tpu_custom_call" | custom-call | flops 3000000000 | tf_op jit(solution)/shard_map/owner/pallas_call | solution.py:759
  16.1 2.7 %collective-permute-start.3 = (bf16[304,128]{1,0:T(8,128)(2,1)S(1)}, bf16[304,128]{1,0:T(8,128)(2,1)S(1)}, u32[]{:S(2)}, u32[]{:S(2)}) collective-permute-start(bf16[304,128]{1,0:T(8,128)(2,1)S(1)} %get-tuple-element.42), channel_id=1, source_target_pairs={{0,12},{4,8},{8,4},{12,0},{1,13},{5,9},{9,5},{13,1},{2,14},{6,10},... | collective-permute-start | bytes 233480 | tf_op jit(solution)/shard_map/ppermute | solution.py:742
  18.8 0.0 collective-permute-start.4
  18.8 1.7 %collective-permute-start.5 = (bf16[304,128]{1,0:T(8,128)(2,1)S(1)}, bf16[304,128]{1,0:T(8,128)(2,1)S(1)}, u32[]{:S(2)}, u32[]{:S(2)}) collective-permute-start(bf16[304,128]{1,0:T(8,128)(2,1)S(1)} %get-tuple-element.44), channel_id=1, source_target_pairs={{0,8},{4,12},{8,0},{12,4},{1,9},{5,13},{9,1},{13,5},{2,10},{6,14},... | collective-permute-start | bytes 233480 | tf_op jit(solution)/shard_map/ppermute | solution.py:742
  20.5 0.3 %last_head.1 = (bf16[128,128]{1,0:T(8,128)(2,1)S(1)}, bf16[128,128]{1,0:T(8,128)(2,1)S(1)}, f32[128,128]{1,0:T(8,128)S(1)}, f32[128,128]{1,0:T(8,128)S(1)}) custom-call(bf16[1,128,640]{2,1,0:T(8,128)(2,1)S(1)} %copy-done.1, bf16[1,128,640]{2,1,0:T(8,128)(2,1)S(1)} %copy-done.2, bf16[1,128,640]{2,1,0:T(8,128)(2,1)S(1)} %copy-done.3, ...), custom_call_target="tpu_custom_call" | custom-call | flops 20000000000 | tf_op jit(solution)/shard_map/last_head/pallas_call | solution.py:759
  20.9 1.9 %collective-permute-done.3.refs_1_.refs_9_ = bf16[304,128]{1,0:T(8,128)(2,1)S(1)} collective-permute-done((bf16[304,128]{1,0:T(8,128)(2,1)S(1)}, bf16[304,128]{1,0:T(8,128)(2,1)S(1)}, u32[]{:S(2)}, u32[]{:S(2)}) %collective-permute-start.3) | collective-permute-done | bytes 77856 | tf_op jit(solution)/shard_map/ppermute | solution.py:742
  22.8 0.9 %collective-permute-done.4.refs_2_.refs_10_ = bf16[304,128]{1,0:T(8,128)(2,1)S(1)} collective-permute-done((bf16[304,128]{1,0:T(8,128)(2,1)S(1)}, bf16[304,128]{1,0:T(8,128)(2,1)S(1)}, u32[]{:S(2)}, u32[]{:S(2)}) %collective-permute-start.4) | collective-permute-done | bytes 77856 | tf_op jit(solution)/shard_map/ppermute | solution.py:742
  23.7 0.6 %collective-permute-done.5.refs_3_.refs_11_ = bf16[304,128]{1,0:T(8,128)(2,1)S(1)} collective-permute-done((bf16[304,128]{1,0:T(8,128)(2,1)S(1)}, bf16[304,128]{1,0:T(8,128)(2,1)S(1)}, u32[]{:S(2)}, u32[]{:S(2)}) %collective-permute-start.5) | collective-permute-done | bytes 77856 | tf_op jit(solution)/shard_map/ppermute | solution.py:742
  24.3 0.1 collective-permute-start.6
  24.4 0.8 %mix.1 = (bf16[128,640]{1,0:T(8,128)(2,1)S(1)}, bf16[128,640]{1,0:T(8,128)(2,1)S(1)}, bf16[128,640]{1,0:T(8,128)(2,1)S(1)}, bf16[128,640]{1,0:T(8,128)(2,1)S(1)}) custom-call(bf16[1,128,640]{2,1,0:T(8,128)(2,1)S(1)} %copy-done.1, bf16[1,128,640]{2,1,0:T(8,128)(2,1)S(1)} %copy-done.2, bf16[1,128,640]{2,1,0:T(8,128)(2,1)S(1)} %copy-done.3, ...), custom_call_target="tpu_custom_call" | custom-call | flops 20000000000 | tf_op jit(solution)/shard_map/mix/pallas_call | solution.py:759
  25.2 0.3 %collective-permute-done.6.gain_rest_ref = f32[1,640]{1,0:T(1,128)S(1)} collective-permute-done((f32[1,640]{1,0:T(1,128)S(1)}, f32[1,640]{1,0:T(1,128)S(1)}, u32[]{:S(2)}, u32[]{:S(2)}) %collective-permute-start.6) | collective-permute-done | bytes 2592 | tf_op jit(solution)/shard_map/ppermute | solution.py:742
  25.6 0.9 %finish.1 = (bf16[1,128,640]{2,1,0:T(8,128)(2,1)}, bf16[1,128,640]{2,1,0:T(8,128)(2,1)}, bf16[1,128,640]{2,1,0:T(8,128)(2,1)}, bf16[1,128,640]{2,1,0:T(8,128)(2,1)}, f32[640]{0:T(1024)}) custom-call(f32[1,640]{1,0:T(1,128)S(1)} %gain.1.gain_ref, f32[1,640]{1,0:T(1,128)S(1)} %collective-permute-done.6.gain_rest_ref, ...), custom_call_target="tpu_custom_call" | custom-call | flops 1000000000 | tf_op jit(solution)/shard_map/finish/pallas_call | solution.py:759
  (5 shorter events, 0.0 us)
Async XLA Ops:
  0.6 0.9 %copy-start.1 = (bf16[1,128,640]{2,1,0:T(8,128)(2,1)S(1)}, bf16[1,128,640]{2,1,0:T(8,128)(2,1)}, u32[]{:S(2)}) copy-start(bf16[1,128,640]{2,1,0:T(8,128)(2,1)} %q_ref.9) | copy-start | bytes 491524
  0.6 1.0 %copy-start.3 = (bf16[1,128,640]{2,1,0:T(8,128)(2,1)S(1)}, bf16[1,128,640]{2,1,0:T(8,128)(2,1)}, u32[]{:S(2)}) copy-start(bf16[1,128,640]{2,1,0:T(8,128)(2,1)} %v_ref.7) | copy-start | bytes 491524
  0.7 1.1 %copy-start.2 = (bf16[1,128,640]{2,1,0:T(8,128)(2,1)S(1)}, bf16[1,128,640]{2,1,0:T(8,128)(2,1)}, u32[]{:S(2)}) copy-start(bf16[1,128,640]{2,1,0:T(8,128)(2,1)} %k_ref.7) | copy-start | bytes 491524
  0.7 1.1 %copy-start = (bf16[1,128,640]{2,1,0:T(8,128)(2,1)S(1)}, bf16[1,128,640]{2,1,0:T(8,128)(2,1)}, u32[]{:S(2)}) copy-start(bf16[1,128,640]{2,1,0:T(8,128)(2,1)} %grad_ref.3) | copy-start | bytes 491524
  0.7 0.7 %copy-start.4 = (s32[2,5]{1,0:T(2,128)S(1)}, s32[2,5]{1,0:T(2,128)}, u32[]{:S(2)}) copy-start(s32[2,5]{1,0:T(2,128)} %offsets_ref.3) | copy-start | bytes 124
  2.4 5.7 %copy-start.6 = (f32[640]{0:T(1024)S(1)}, f32[640]{0:T(1024)}, u32[]{:S(2)}) copy-start(f32[640]{0:T(1024)} %param.10) | copy-start | bytes 7684
  2.4 8.6 %collective-permute-start = (bf16[352,128]{1,0:T(8,128)(2,1)S(1)}, bf16[352,128]{1,0:T(8,128)(2,1)S(1)}, u32[]{:S(2)}, u32[]{:S(2)}) collective-permute-start(bf16[352,128]{1,0:T(8,128)(2,1)S(1)} %get-tuple-element.38), channel_id=1, source_target_pairs={{0,12},{4,8},{8,4},{12,0},{1,13},{5,9},{9,5},{13,1},{2,14},{6,10},... | collective-permute-start | bytes 270344 | tf_op jit(solution)/shard_map/ppermute | solution.py:742
  7.5 5.8 %collective-permute-start.1 = (bf16[352,128]{1,0:T(8,128)(2,1)S(1)}, bf16[352,128]{1,0:T(8,128)(2,1)S(1)}, u32[]{:S(2)}, u32[]{:S(2)}) collective-permute-start(bf16[352,128]{1,0:T(8,128)(2,1)S(1)} %get-tuple-element.39), channel_id=1, source_target_pairs={{0,4},{4,0},{8,12},{12,8},{1,5},{5,1},{9,13},{13,9},{2,6},{6,2},{1... | collective-permute-start | bytes 270344 | tf_op jit(solution)/shard_map/ppermute | solution.py:742
  7.5 0.7 %copy-start.5 = (s32[2,5]{1,0:T(2,128)S(1)}, s32[2,5]{1,0:T(2,128)}, u32[]{:S(2)}) copy-start(s32[2,5]{1,0:T(2,128)} %offsets_ref.3) | copy-start | bytes 124
  7.5 7.6 %collective-permute-start.2 = (bf16[352,128]{1,0:T(8,128)(2,1)S(1)}, bf16[352,128]{1,0:T(8,128)(2,1)S(1)}, u32[]{:S(2)}, u32[]{:S(2)}) collective-permute-start(bf16[352,128]{1,0:T(8,128)(2,1)S(1)} %get-tuple-element.40), channel_id=1, source_target_pairs={{0,8},{4,12},{8,0},{12,4},{1,9},{5,13},{9,1},{13,5},{2,10},{6,14},... | collective-permute-start | bytes 270344 | tf_op jit(solution)/shard_map/ppermute | solution.py:742
  16.1 6.7 %collective-permute-start.3 = (bf16[304,128]{1,0:T(8,128)(2,1)S(1)}, bf16[304,128]{1,0:T(8,128)(2,1)S(1)}, u32[]{:S(2)}, u32[]{:S(2)}) collective-permute-start(bf16[304,128]{1,0:T(8,128)(2,1)S(1)} %get-tuple-element.42), channel_id=1, source_target_pairs={{0,12},{4,8},{8,4},{12,0},{1,13},{5,9},{9,5},{13,1},{2,14},{6,10},... | collective-permute-start | bytes 233480 | tf_op jit(solution)/shard_map/ppermute | solution.py:742
  18.8 5.0 %collective-permute-start.4 = (bf16[304,128]{1,0:T(8,128)(2,1)S(1)}, bf16[304,128]{1,0:T(8,128)(2,1)S(1)}, u32[]{:S(2)}, u32[]{:S(2)}) collective-permute-start(bf16[304,128]{1,0:T(8,128)(2,1)S(1)} %get-tuple-element.43), channel_id=1, source_target_pairs={{0,4},{4,0},{8,12},{12,8},{1,5},{5,1},{9,13},{13,9},{2,6},{6,2},{1... | collective-permute-start | bytes 233480 | tf_op jit(solution)/shard_map/ppermute | solution.py:742
  18.8 5.5 %collective-permute-start.5 = (bf16[304,128]{1,0:T(8,128)(2,1)S(1)}, bf16[304,128]{1,0:T(8,128)(2,1)S(1)}, u32[]{:S(2)}, u32[]{:S(2)}) collective-permute-start(bf16[304,128]{1,0:T(8,128)(2,1)S(1)} %get-tuple-element.44), channel_id=1, source_target_pairs={{0,8},{4,12},{8,0},{12,4},{1,9},{5,13},{9,1},{13,5},{2,10},{6,14},... | collective-permute-start | bytes 233480 | tf_op jit(solution)/shard_map/ppermute | solution.py:742
  24.3 1.2 %collective-permute-start.6 = (f32[1,640]{1,0:T(1,128)S(1)}, f32[1,640]{1,0:T(1,128)S(1)}, u32[]{:S(2)}, u32[]{:S(2)}) collective-permute-start(f32[1,640]{1,0:T(1,128)S(1)} %gain.1.gain_ref), channel_id=1, source_target_pairs={{0,16},{16,0},{1,17},{17,1},{2,18},{18,2},{3,19},{19,3},{4,20},{20... | collective-permute-start | bytes 7688 | tf_op jit(solution)/shard_map/ppermute | solution.py:742
